TPU v7x, 32 devices: a whole 2x2x4 slice. The times are simulated.
32 devices in a mesh: leaf: 16 (over z, x, core), probe: 2 (over y).
Axes of the slice: x: 2, y: 2, z: 4, core: 2. Of those that a mesh axis runs over, the one named last changes fastest.
Arguments:
- coef_fine: bfloat16 [64, 65536], P('probe', 'leaf'), may hold values from -0.59765625 to 0.59765625
- points_fine: float32 [3, 65536], P(None, 'leaf'), may hold values from -1 to 1
- points_coarse: float32 [3, 32768], P(None, 'leaf'), may hold values from -1 to 1
- transfer: bfloat16 [64, 65536], P(None, 'leaf'), may hold values from -0.5 to 0.5
- send_fine: int32 [16, 16, 16], P('leaf'), may hold values from 0 to 63, as said below
- slots_fine: int32 [1024, 64], P('leaf'), may hold values from 0 to 319, as said below
- counts_fine: int32 [1024], P('leaf'), may hold values from 1 to 64, as said below
- send_coarse: int32 [16, 16, 8], P('leaf'), may hold values from 0 to 31, as said below
- slots_coarse: int32 [512, 64], P('leaf'), may hold values from 0 to 159, as said below
- counts_coarse: int32 [512], P('leaf'), may hold values from 1 to 64, as said below
Outputs:
- far_field: float32 [64, 65536], P('probe', 'leaf')
- probe_gram: float32 [64, 64], P('probe')
Inputs may be any that keep to these rules, and one draw needn't show every extreme that they name: `send_fine`: entry [e, d, i] is the local index of a cluster of device e that device e sends to device d; every device sends exactly 16 distinct clusters to every device, itself included. `slots_fine`: A slot value v below 64 names the owning device's own cluster v; a value of 64 or more names entry [(v - 64) // 16, owner, (v - 64) % 16] of send_fine. Only the first counts_fine[c] slots of cluster c are live; every device has a cluster with all 64 slots live. `send_coarse`: entry [e, d, i] is the local index of a cluster of device e that device e sends to device d; every device sends exactly 8 distinct clusters to every device, itself included. `slots_coarse`: A slot value v below 32 names the owning device's own cluster v; a value of 32 or more names entry [(v - 32) // 8, owner, (v - 32) % 8] of send_coarse. Only the first counts_coarse[q] slots of cluster q are live; every device has a cluster with all 64 slots live.
All inputs are finite; a program needn't handle non-finite values.
Results may differ from a plain program's by a relative error of at most 0.0036.
Values may be sent and summed in bfloat16 or wider, within the bound.
No kernel may reach another device: no remote copies, remote signals or barrier semaphores. Data moves between devices by JAX's collectives and lax.ppermute only.
A program may use at most 64 MiB of HBM per device.

v0:
```python
import functools
import math

import jax
import jax.numpy as jnp
from jax import lax
from jax.experimental import pallas as pl
from jax.experimental.pallas import tpu as pltpu
from jax.sharding import PartitionSpec as P

KERNEL_RATE = 1.5
POINT_SCALE = math.sqrt(2.0 * KERNEL_RATE * math.log2(math.e))
LANES = 128
TARGETS = 4
CHUNK = 8
FAR_AWAY = -30000.0
VMEM = 56 * 1024 * 1024

NT = (((1,), (1,)), ((), ()))
NN = (((1,), (0,)), ((), ()))


def bdot(a, b, dims):
    return lax.dot_general(a, b, dims, preferred_element_type=jnp.float32)


def split_rows(points):
    v = points * POINT_SCALE
    norm = -0.5 * (v[0:1] * v[0:1] + v[1:2] * v[1:2] + v[2:3] * v[2:3])
    full = jnp.concatenate([v, norm], axis=0)
    high = full.astype(jnp.bfloat16).astype(jnp.float32)
    rest = (full - high).astype(jnp.bfloat16).astype(jnp.float32)
    return jnp.concatenate([high, rest], axis=0)


def source_features(rows):
    place = lax.broadcasted_iota(jnp.int32, rows.shape, 0)
    one = jnp.where((place == 3) | (place == 7), 1.0, 0.0)
    return jnp.concatenate([rows, jnp.where(place < 3, rows, one)], axis=0)


def target_features(rows):
    place = lax.broadcasted_iota(jnp.int32, rows.shape, 0)
    turned = jnp.concatenate([rows[4:8], rows[0:4]], axis=0)
    one = jnp.where((place == 3) | (place == 7), 1.0, jnp.where(place < 3, rows, turned))
    return jnp.concatenate([one, turned], axis=0)


def halves(tile):
    lane = lax.broadcasted_iota(jnp.int32, tile.shape, 1)
    turned = pltpu.roll(tile, LANES // 2, 1)
    low = lane < LANES // 2
    return jnp.where(low, tile, turned), jnp.where(low, turned, tile)


def lane_tile(index):
    return pl.ds(pl.multiple_of(index * LANES, LANES), LANES)


def pack_send(send_ref, out_ref, dup_coef, dup_rows, owners, capacity, px):
    pairs = capacity // 2
    lane = lax.broadcasted_iota(jnp.int32, (px, LANES), 1) < LANES // 2
    lane8 = lax.broadcasted_iota(jnp.int32, (8, LANES), 1) < LANES // 2

    def one_owner(owner, carry):
        before = None
        for pair in range(pairs):
            first = send_ref[owner, 2 * pair]
            second = send_ref[owner, 2 * pair + 1]
            out_ref[owner, pair * px:(pair + 1) * px, :] = jnp.where(
                lane, dup_coef[first], dup_coef[second]
            ).astype(jnp.bfloat16)
            rows = jnp.where(lane8, dup_rows[first], dup_rows[second])
            if pair % 2 == 0:
                before = rows
            else:
                start = pairs * px + (pair - 1) * 8
                out_ref[owner, start:start + 16, :] = jnp.concatenate(
                    [before, rows], axis=0
                ).astype(jnp.bfloat16)
        return carry

    lax.fori_loop(0, owners, one_owner, 0)


def pack_fine_kernel(send_ref, coef_ref, points_ref, out_ref, rows_ref, dup_coef, dup_rows):
    owners, capacity = send_ref.shape
    px = coef_ref.shape[0]
    rows_ref[...] = split_rows(points_ref[...])

    def one_tile(index, carry):
        a, b = halves(coef_ref[:, lane_tile(index)].astype(jnp.float32))
        dup_coef[2 * index] = a
        dup_coef[2 * index + 1] = b
        a, b = halves(rows_ref[:, lane_tile(index)])
        dup_rows[2 * index] = a
        dup_rows[2 * index + 1] = b
        return carry

    lax.fori_loop(0, coef_ref.shape[1] // LANES, one_tile, 0, unroll=4)
    pack_send(send_ref, out_ref, dup_coef, dup_rows, owners, capacity, px)


def pack_coarse_kernel(
    send_ref, coef_ref, transfer_ref, points_ref, out_ref, rows_ref, coarse_ref, dup_coef, dup_rows
):
    owners, capacity = send_ref.shape
    px = coef_ref.shape[0]
    rows_ref[...] = split_rows(points_ref[...])

    def one_tile(index, carry):
        doubled = []
        for part in range(2):
            q = 2 * index + part
            a, b = halves(transfer_ref[:, lane_tile(q)].astype(jnp.float32))
            matrix = jnp.concatenate([a, b], axis=0).astype(jnp.bfloat16)
            block = bdot(coef_ref[:, lane_tile(q)], matrix, NN)
            dup_coef[q] = block
            doubled.append(block)
        lane = lax.broadcasted_iota(jnp.int32, (px, LANES), 1) < LANES // 2
        coarse_ref[:, lane_tile(index)] = jnp.where(lane, doubled[0], doubled[1]).astype(jnp.bfloat16)
        a, b = halves(rows_ref[:, lane_tile(index)])
        dup_rows[2 * index] = a
        dup_rows[2 * index + 1] = b
        return carry

    lax.fori_loop(0, coef_ref.shape[1] // (2 * LANES), one_tile, 0, unroll=2)
    pack_send(send_ref, out_ref, dup_coef, dup_rows, owners, capacity, px)


def build_tables(recv_ref, coef_ref, rows_ref, coef_table, feature_table):
    owners, recv_rows, _ = recv_ref.shape
    px = coef_ref.shape[0]
    pairs = recv_rows // (px + 8)
    own_tiles = coef_ref.shape[1] // LANES
    own = 2 * own_tiles
    row = lax.broadcasted_iota(jnp.int32, (LANES, LANES), 0)
    column = lax.broadcasted_iota(jnp.int32, (LANES, LANES), 1)
    unit = jnp.where(row == column, 1.0, 0.0).astype(jnp.bfloat16)

    def put(entry, coef, rows):
        a, b = halves(coef.astype(jnp.float32))
        coef_table[entry] = a.astype(jnp.bfloat16)
        coef_table[entry + 1] = b.astype(jnp.bfloat16)
        features = source_features(rows).astype(jnp.bfloat16)
        spread = jnp.concatenate([features] * 8, axis=0)
        turned = bdot(unit, spread, NT).astype(jnp.bfloat16)
        feature_table[entry] = turned[:64]
        feature_table[entry + 1] = turned[64:]

    def one_own(index, carry):
        put(2 * index, coef_ref[:, lane_tile(index)], rows_ref[:, lane_tile(index)])
        return carry

    lax.fori_loop(0, own_tiles, one_own, 0, unroll=4)

    def one_owner(owner, carry):
        for pair in range(0, pairs, 2):
            start = pairs * px + pair * 8
            both = recv_ref[owner, start:start + 16, :].astype(jnp.float32)
            for part in range(2):
                where = pair + part
                put(
                    own + owner * (2 * pairs) + 2 * where,
                    recv_ref[owner, where * px:(where + 1) * px, :],
                    both[8 * part:8 * part + 8],
                )
        return carry

    lax.fori_loop(0, owners, one_owner, 0)
    last = own + owners * pairs * 2
    coef_table[last] = jnp.zeros((px, LANES), jnp.bfloat16)
    place = lax.broadcasted_iota(jnp.int32, (8, LANES), 0)
    nothing = source_features(jnp.where(place == 3, FAR_AWAY, 0.0)).astype(jnp.bfloat16)
    feature_table[last] = bdot(unit, jnp.concatenate([nothing] * 8, axis=0), NT)[:64].astype(jnp.bfloat16)


def sweep_group(group, index_ref, turns_ref, rows_ref, coef_table, feature_table, acc):
    px = coef_table.shape[1]
    width = TARGETS * 64
    targets = target_features(rows_ref[:, pl.ds(pl.multiple_of(group * width, width), width)])
    targets = jnp.concatenate([targets] * 16, axis=0)
    row = lax.broadcasted_iota(jnp.int32, targets.shape, 0)
    column = lax.broadcasted_iota(jnp.int32, targets.shape, 1)
    owner_of_row = (row // LANES) * 2 + jnp.where(row % LANES < 16, 0, jnp.where(row % LANES < 32, 1, 9))
    weights = jnp.where(owner_of_row == column // 64, targets, 0.0).astype(jnp.bfloat16)
    lane = lax.broadcasted_iota(jnp.int32, (64, LANES), 1) < 16
    lane_x = lax.broadcasted_iota(jnp.int32, (px, LANES), 1) < 64
    acc[...] = jnp.zeros_like(acc)

    def one_turn(turn, carry):
        slot = turn * CHUNK
        total = None
        for part in range(0, CHUNK, 4):
            ids = [
                [index_ref[group * TARGETS + s, slot + part + m] for m in range(4)]
                for s in range(TARGETS)
            ]
            moving = []
            for m in range(4):
                moving.append(
                    jnp.concatenate(
                        [
                            jnp.where(lane, feature_table[ids[s][m]], feature_table[ids[s + 1][m]])
                            for s in (0, 2)
                        ],
                        axis=1,
                    )
                )
            values = jnp.exp2(bdot(jnp.concatenate(moving, axis=0), weights, NN)).astype(jnp.bfloat16)
            coefs = jnp.concatenate(
                [
                    jnp.concatenate(
                        [
                            jnp.where(lane_x, coef_table[ids[s][m]], coef_table[ids[s][m + 1]])
                            for m in (0, 2)
                        ],
                        axis=1,
                    )
                    for s in range(TARGETS)
                ],
                axis=0,
            )
            product = bdot(coefs, values, NN)
            total = product if total is None else total + product
        acc[...] += total
        return carry

    lax.fori_loop(0, turns_ref[group], one_turn, 0)
    block = lax.broadcasted_iota(jnp.int32, (px, width), 1) // 64
    result = acc[0:px, :]
    for s in range(1, TARGETS):
        result = jnp.where(block == s, acc[s * px:(s + 1) * px, :], result)
    return result


def fine_kernel(index_ref, turns_ref, recv_ref, coef_ref, rows_ref, out_ref, coef_table, feature_table, acc):
    build_tables(recv_ref, coef_ref, rows_ref, coef_table, feature_table)
    width = TARGETS * 64

    def one_group(group, carry):
        out_ref[:, pl.ds(pl.multiple_of(group * width, width), width)] = sweep_group(
            group, index_ref, turns_ref, rows_ref, coef_table, feature_table, acc
        )
        return carry

    lax.fori_loop(0, turns_ref.shape[0], one_group, 0)


def coarse_kernel(
    index_ref,
    turns_ref,
    recv_ref,
    coef_ref,
    rows_ref,
    fine_ref,
    transfer_ref,
    probes_ref,
    out_ref,
    gram_ref,
    coef_table,
    feature_table,
    acc,
):
    build_tables(recv_ref, coef_ref, rows_ref, coef_table, feature_table)
    gram_ref[...] = jnp.zeros_like(gram_ref)
    px = coef_ref.shape[0]

    def one_group(group, carry):
        far = sweep_group(group, index_ref, turns_ref, rows_ref, coef_table, feature_table, acc)
        for part in range(TARGETS):
            q = group * TARGETS + part
            tile = far[:, (part // 2) * LANES:(part // 2 + 1) * LANES]
            twice = halves(tile)[part % 2].astype(jnp.bfloat16)
            matrix = transfer_ref[:, lane_tile(q)].astype(jnp.float32)
            low = lax.broadcasted_iota(jnp.int32, matrix.shape, 1) < 64
            matrix = jnp.concatenate(
                [jnp.where(low, matrix, 0.0), jnp.where(low, 0.0, matrix)], axis=0
            ).astype(jnp.bfloat16)
            total = fine_ref[:, lane_tile(q)] + bdot(twice, matrix, NT)
            out_ref[:, lane_tile(q)] = total
            high = total.astype(jnp.bfloat16)
            rest = (total - high.astype(jnp.float32)).astype(jnp.bfloat16)
            probes = probes_ref[:, lane_tile(q)]
            gram_ref[...] += bdot(probes, high, NT) + bdot(probes, rest, NT)
        return carry

    lax.fori_loop(0, turns_ref.shape[0], one_group, 0)


def live_index(slots, counts, nothing):
    place = lax.broadcasted_iota(jnp.int32, slots.shape, 1)
    index = jnp.where(place < counts[:, None], slots, nothing)
    turns = (jnp.max(counts.reshape(-1, TARGETS), axis=1) + CHUNK - 1) // CHUNK
    return index, turns


def shards(
    coef_fine,
    points_fine,
    points_coarse,
    transfer,
    send_fine,
    slots_fine,
    counts_fine,
    send_coarse,
    slots_coarse,
    counts_coarse,
):
    probes = coef_fine.shape[0]
    fine_count = counts_fine.shape[0]
    coarse_count = counts_coarse.shape[0]
    owners = lax.axis_size("leaf")
    groups = lax.axis_size("probe")
    px = -(-probes // 16) * 16
    coef = coef_fine if px == probes else jnp.pad(coef_fine, ((0, px - probes), (0, 0)))
    send_fine = send_fine.reshape(owners, -1)
    send_coarse = send_coarse.reshape(owners, -1)
    cap_fine = send_fine.shape[1]
    cap_coarse = send_coarse.shape[1]
    params = pltpu.CompilerParams(vmem_limit_bytes=VMEM)
    smem = pl.BlockSpec(memory_space=pltpu.SMEM)
    vmem = pl.BlockSpec(memory_space=pltpu.VMEM)
    bf16, f32 = jnp.bfloat16, jnp.float32

    all_probes = lax.all_gather(coef_fine, "probe", axis=0, tiled=True)

    fine_send, fine_rows = pl.pallas_call(
        pack_fine_kernel,
        out_shape=(
            jax.ShapeDtypeStruct((owners, (cap_fine // 2) * (px + 8), LANES), bf16),
            jax.ShapeDtypeStruct((8, points_fine.shape[1]), f32),
        ),
        in_specs=[smem, vmem, vmem],
        out_specs=[vmem, vmem],
        scratch_shapes=[
            pltpu.VMEM((fine_count, px, LANES), f32),
            pltpu.VMEM((fine_count, 8, LANES), f32),
        ],
        compiler_params=params,
        name="pack_fine",
    )(send_fine, coef, points_fine)
    fine_recv = lax.all_to_all(fine_send, "leaf", split_axis=0, concat_axis=0, tiled=True)

    coarse_send, coarse_rows, coarse_coef = pl.pallas_call(
        pack_coarse_kernel,
        out_shape=(
            jax.ShapeDtypeStruct((owners, (cap_coarse // 2) * (px + 8), LANES), bf16),
            jax.ShapeDtypeStruct((8, points_coarse.shape[1]), f32),
            jax.ShapeDtypeStruct((px, points_coarse.shape[1]), bf16),
        ),
        in_specs=[smem, vmem, vmem, vmem],
        out_specs=[vmem, vmem, vmem],
        scratch_shapes=[
            pltpu.VMEM((coarse_count, px, LANES), f32),
            pltpu.VMEM((coarse_count, 8, LANES), f32),
        ],
        compiler_params=params,
        name="pack_coarse",
    )(send_coarse, coef, transfer, points_coarse)
    coarse_recv = lax.all_to_all(coarse_send, "leaf", split_axis=0, concat_axis=0, tiled=True)

    fine_total = fine_count + owners * cap_fine
    coarse_total = coarse_count + owners * cap_coarse
    fine_index, fine_turns = live_index(slots_fine, counts_fine, fine_total)
    coarse_index, coarse_turns = live_index(slots_coarse, counts_coarse, coarse_total)

    fine_far = pl.pallas_call(
        fine_kernel,
        out_shape=jax.ShapeDtypeStruct((px, points_fine.shape[1]), f32),
        in_specs=[smem, smem, vmem, vmem, vmem],
        out_specs=vmem,
        scratch_shapes=[
            pltpu.VMEM((fine_total + 1, px, LANES), bf16),
            pltpu.VMEM((fine_total + 1, 64, LANES), bf16),
            pltpu.VMEM((TARGETS * px, TARGETS * 64), f32),
        ],
        compiler_params=params,
        name="fine_sweep",
    )(fine_index, fine_turns, fine_recv, coef, fine_rows)

    far, gram = pl.pallas_call(
        coarse_kernel,
        out_shape=(
            jax.ShapeDtypeStruct((px, points_fine.shape[1]), f32),
            jax.ShapeDtypeStruct((all_probes.shape[0], px), f32),
        ),
        in_specs=[smem, smem] + [vmem] * 6,
        out_specs=[vmem, vmem],
        scratch_shapes=[
            pltpu.VMEM((coarse_total + 1, px, LANES), bf16),
            pltpu.VMEM((coarse_total + 1, 64, LANES), bf16),
            pltpu.VMEM((TARGETS * px, TARGETS * 64), f32),
        ],
        compiler_params=params,
        name="coarse_sweep",
    )(coarse_index, coarse_turns, coarse_recv, coarse_coef, coarse_rows, fine_far, transfer, all_probes)

    far_field = far[:probes]
    blocks = gram[:, :probes].reshape(groups, probes * probes)
    blocks = jnp.broadcast_to(blocks[None], (owners, groups, probes * probes))
    blocks = blocks.reshape(owners * groups, 1, probes * probes)
    blocks = lax.all_to_all(blocks, ("leaf", "probe"), split_axis=0, concat_axis=0, tiled=True)
    total = jnp.sum(blocks.reshape(owners, groups, probes, probes), axis=0)
    gram_scale = 1.0 / math.sqrt(owners * fine_count * 64)
    probe_gram = total.transpose(1, 0, 2).reshape(probes, groups * probes) * gram_scale
    return (far_field, probe_gram)


def solution(mesh):
    return jax.shard_map(
        shards,
        mesh=mesh,
        in_specs=(
            P("probe", "leaf"),
            P(None, "leaf"),
            P(None, "leaf"),
            P(None, "leaf"),
            P("leaf", None, None),
            P("leaf", None),
            P("leaf"),
            P("leaf", None, None),
            P("leaf", None),
            P("leaf"),
        ),
        out_specs=(P("probe", "leaf"), P("probe", None)),
        check_vma=False,
    )
```

profile of v0, /device:TPU:0, one launch (start us, length us, event | category | flops | bytes accessed | tf_op | source)
XLA Modules:
  0.0 183.5 jit_solution(12847009705844119048)
XLA Ops:
  0.6 3.3 %pack_fine.1 = (bf16[16,320,128]{2,1,0:T(8,128)(2,1)}, f32[8,4096]{1,0:T(8,128)}) custom-call(s32[16,16]{1,0:T(8,128)} %bitcast.4, bf16[32,4096]{1,0:T(8,128)(2,1)} %coef_ref.5, f32[3,4096]{1,0:T(4,128)} %points_ref.3), custom_call_target="tpu_custom_call" | custom-call | tf_op jit(solution)/shard_map/pack_fine/pallas_call | solution.py:328
  3.9 0.0 copy-start.5
  3.9 7.5 %all-to-all-start.1 = ((bf16[16,320,128]{2,1,0:T(8,128)(2,1)}), bf16[16,320,128]{2,1,0:T(8,128)(2,1)S(1)}, u32[]{:S(2)}, u32[]{:S(2)}) async-start(bf16[16,320,128]{2,1,0:T(8,128)(2,1)} %get-tuple-element.12), calls=%async_computation.1 | async-start | bytes 2621440 | tf_op jit(solution)/shard_map/all_to_all | solution.py:343
  11.4 0.0 copy-start.7
  11.4 0.0 copy-start.6
  11.5 0.0 copy-start.1
  11.5 0.0 copy-done.5
  11.5 0.7 copy.16.send_ref
  12.1 0.0 copy-start.4
  12.1 0.0 copy-start.3
  12.1 4.2 %pack_coarse.1 = (bf16[16,160,128]{2,1,0:T(8,128)(2,1)}, f32[8,2048]{1,0:T(8,128)}, bf16[32,2048]{1,0:T(8,128)(2,1)}) custom-call(s32[16,8]{1,0:T(8,128)} %copy.16.send_ref, bf16[32,4096]{1,0:T(8,128)(2,1)} %coef_ref.5, bf16[64,4096]{1,0:T(8,128)(2,1)} %transfer_ref.3, f32[3,2048]{1,0:T(4,128)} %points_ref.2), custom_call_target="tpu_custom_call" | custom-call | tf_op jit(solution)/shard_map/pack_coarse/pallas_call | solution.py:345
  16.3 22.5 %all-to-all-done.1.recv_ref = bf16[16,320,128]{2,1,0:T(8,128)(2,1)S(1)} async-done(((bf16[16,320,128]{2,1,0:T(8,128)(2,1)}), bf16[16,320,128]{2,1,0:T(8,128)(2,1)S(1)}, u32[]{:S(2)}, u32[]{:S(2)}) %all-to-all-start.1) | async-done | bytes 1310752 | tf_op jit(solution)/shard_map/all_to_all | solution.py:343
  38.8 0.0 copy-start
  38.8 8.0 %all-to-all-start = ((bf16[16,160,128]{2,1,0:T(8,128)(2,1)}), bf16[16,160,128]{2,1,0:T(8,128)(2,1)S(1)}, u32[]{:S(2)}, u32[]{:S(2)}) async-start(bf16[16,160,128]{2,1,0:T(8,128)(2,1)} %get-tuple-element.9), calls=%async_computation | async-start | bytes 1310720 | tf_op jit(solution)/shard_map/all_to_all | solution.py:361
  46.9 0.0 copy-done.7
  46.9 0.1 reshape.30
  47.0 0.0 copy-done.6
  47.0 0.1 reshape.28
  47.0 0.1 reduce_max.19
  47.2 0.1 reduce_max.18
  47.3 0.0 copy-done.1
  47.3 9.4 %all_gather.3.probes_ref = bf16[64,4096]{1,0:T(8,128)(2,1)} all-gather(bf16[32,4096]{1,0:T(8,128)(2,1)S(1)} %copy-done.1), channel_id=1, replica_groups=mesh['leaf'=16,'probe'=2] {'probe'}, dimensions={0}, use_global_device_ids=true | all-gather | bytes 786432 | tf_op jit(solution)/shard_map/all_gather | solution.py:326
  56.7 0.5 and_select_fusion.turns_ref
  57.2 0.6 and_select_fusion.1.turns_ref
  57.8 0.0 copy-done.4
  57.8 0.7 fusion.1.index_ref
  58.5 0.0 copy-done.3
  58.5 0.7 fusion.index_ref
  59.2 0.0 copy-done
  59.2 65.5 %fine_sweep.1.fine_ref = f32[32,4096]{1,0:T(8,128)} custom-call(s32[64,64]{1,0:T(8,128)} %fusion.index_ref, s32[16]{0:T(128)} %and_select_fusion.turns_ref, bf16[16,320,128]{2,1,0:T(8,128)(2,1)} %copy-done, bf16[32,4096]{1,0:T(8,128)(2,1)} %coef_ref.5, f32[8,4096]{1,0:T(8,128)} %get-tuple-element.13.rows_ref), custom_call_target="tpu_custom_call" | custom-call | tf_op jit(solution)/shard_map/fine_sweep/pallas_call | solution.py:368
  124.7 0.0 all-to-all-done.recv_ref
  124.7 0.0 copy-start.2
  124.7 0.8 copy-done.2
  125.5 40.8 %coarse_sweep.1 = (f32[32,4096]{1,0:T(8,128)}, f32[64,32]{1,0:T(8,128)}) custom-call(s32[32,64]{1,0:T(8,128)} %fusion.1.index_ref, s32[8]{0:T(128)} %and_select_fusion.1.turns_ref, bf16[16,160,128]{2,1,0:T(8,128)(2,1)} %copy-done.2, bf16[32,2048]{1,0:T(8,128)(2,1)} %get-tuple-element.10.coef_ref, f32[8,2048]{1,0:T(8,128)} %get-tuple-element.11.rows_ref, ...), custom_call_target="tpu_custom_call" | custom-call | tf_op jit(solution)/shard_map/coarse_sweep/pallas_call | solution.py:382
  166.3 0.8 broadcast_in_dim.19
  167.2 0.2 reshape.32
  167.4 14.8 %all_to_all.15 = f32[32,1,1024]{2,1,0:T(1,128)S(1)} all-to-all(f32[32,1,1024]{2,1,0:T(1,128)S(1)} %reshape.32), channel_id=1, replica_groups=mesh['leaf'=16,'probe'=2] {'leaf','probe'}, dimensions={0} | all-to-all | bytes 262144 | tf_op jit(solution)/shard_map/all_to_all | solution.py:403
  182.2 0.3 reduce
  182.5 0.2 reshape.33
  182.7 0.1 reduce_sum.9
  182.8 0.7 mul.15
  (3 shorter events, 0.1 us)
Async XLA Ops:
  3.9 7.5 %copy-start.5 = (s32[1,16,8]{1,2,0:T(8,128)S(1)}, s32[1,16,8]{1,2,0:T(8,128)}, u32[]{:S(2)}) copy-start(s32[1,16,8]{1,2,0:T(8,128)} %param.17) | copy-start | bytes 1540
  3.9 34.9 %all-to-all-start.1 = ((bf16[16,320,128]{2,1,0:T(8,128)(2,1)}), bf16[16,320,128]{2,1,0:T(8,128)(2,1)S(1)}, u32[]{:S(2)}, u32[]{:S(2)}) async-start(bf16[16,320,128]{2,1,0:T(8,128)(2,1)} %get-tuple-element.12), calls=%async_computation.1 | async-start | bytes 2621440 | tf_op jit(solution)/shard_map/all_to_all | solution.py:343
  11.4 35.4 %copy-start.7 = (s32[64]{0:T(128)S(1)}, s32[64]{0:T(128)}, u32[]{:S(2)}) copy-start(s32[64]{0:T(128)} %param.16) | copy-start | bytes 772
  11.4 35.5 %copy-start.6 = (s32[32]{0:T(128)S(1)}, s32[32]{0:T(128)}, u32[]{:S(2)}) copy-start(s32[32]{0:T(128)} %param.19) | copy-start | bytes 388
  11.5 35.8 %copy-start.1 = (bf16[32,4096]{1,0:T(8,128)(2,1)S(1)}, bf16[32,4096]{1,0:T(8,128)(2,1)}, u32[]{:S(2)}) copy-start(bf16[32,4096]{1,0:T(8,128)(2,1)} %coef_ref.5) | copy-start | bytes 786436
  12.1 45.7 %copy-start.4 = (s32[32,64]{1,0:T(8,128)S(1)}, s32[32,64]{1,0:T(8,128)}, u32[]{:S(2)}) copy-start(s32[32,64]{1,0:T(8,128)} %param.18) | copy-start | bytes 24580
  12.1 46.3 %copy-start.3 = (s32[64,64]{1,0:T(8,128)S(1)}, s32[64,64]{1,0:T(8,128)}, u32[]{:S(2)}) copy-start(s32[64,64]{1,0:T(8,128)} %param.15) | copy-start | bytes 49156
  38.8 20.3 %copy-start = (bf16[16,320,128]{2,1,0:T(8,128)(2,1)}, bf16[16,320,128]{2,1,0:T(8,128)(2,1)S(1)}, u32[]{:S(2)}) copy-start(bf16[16,320,128]{2,1,0:T(8,128)(2,1)S(1)} %all-to-all-done.1.recv_ref) | copy-start | bytes 3932164
  38.8 85.8 %all-to-all-start = ((bf16[16,160,128]{2,1,0:T(8,128)(2,1)}), bf16[16,160,128]{2,1,0:T(8,128)(2,1)S(1)}, u32[]{:S(2)}, u32[]{:S(2)}) async-start(bf16[16,160,128]{2,1,0:T(8,128)(2,1)} %get-tuple-element.9), calls=%async_computation | async-start | bytes 1310720 | tf_op jit(solution)/shard_map/all_to_all | solution.py:361
  124.7 0.8 copy-start.2
where the time goes:
time: 183 us
  Pallas kernels  114 us (62%)
  blocking collectives  24.2 us (13%)
  waiting for transfers between devices  22.5 us (12%)
  starting transfers between devices  15.5 us (8%)
  local copies, waits for them, and re-layouts  3.67 us (2%)
  other arithmetic  3.04 us (2%)
    pallas_call x1, Pallas kernels, shards(): pl.pallas_call(fine_kernel, out_shape=jax.ShapeDtypeStruct((px, points_fi...  65.5 us
    pallas_call x1, Pallas kernels, shards(): pl.pallas_call(coarse_kernel, out_shape=(jax.ShapeDtypeStruct((px, points...  40.8 us
    all_to_all x1, waiting for transfers between devices, shards(): lax.all_to_all(fine_send, 'leaf', split_axis=0, concat_axis=0, tiled=True)  22.5 us
    all_to_all x1, blocking collectives, shards(): lax.all_to_all(blocks, ('leaf', 'probe'), split_axis=0, concat_axis=0, ti...  14.8 us
    all_gather x1, blocking collectives, shards(): all_probes = lax.all_gather(coef_fine, 'probe', axis=0, tiled=True)  9.43 us
    all_to_all x1, starting transfers between devices, shards(): lax.all_to_all(coarse_send, 'leaf', split_axis=0, concat_axis=0, tiled=True)  8.01 us
    all_to_all x1, starting transfers between devices, shards(): lax.all_to_all(fine_send, 'leaf', split_axis=0, concat_axis=0, tiled=True)  7.49 us
    pallas_call x1, Pallas kernels, shards(): pl.pallas_call(pack_coarse_kernel, out_shape=(jax.ShapeDtypeStruct((owner...  4.19 us
  transfers between devices with their start and end apart: 2, of which 1 were waited for; matrix products, arithmetic and copies ran while one was open for 2% of the time, Pallas kernels for 38%

commit v1 on v0

--- a/solution.py
+++ b/solution.py
@@ -128,7 +128,7 @@
     pack_send(send_ref, out_ref, dup_coef, dup_rows, owners, capacity, px)
 
 
-def build_tables(recv_ref, coef_ref, rows_ref, coef_table, feature_table):
+def build_tables(recv_ref, coef_ref, rows_ref, coef_table, feature_table, target_table):
     owners, recv_rows, _ = recv_ref.shape
     px = coef_ref.shape[0]
     pairs = recv_rows // (px + 8)
@@ -142,14 +142,18 @@
         a, b = halves(coef.astype(jnp.float32))
         coef_table[entry] = a.astype(jnp.bfloat16)
         coef_table[entry + 1] = b.astype(jnp.bfloat16)
-        features = source_features(rows).astype(jnp.bfloat16)
-        spread = jnp.concatenate([features] * 8, axis=0)
-        turned = bdot(unit, spread, NT).astype(jnp.bfloat16)
-        feature_table[entry] = turned[:64]
-        feature_table[entry + 1] = turned[64:]
+        a, b = halves(source_features(rows))
+        feature_table[entry] = a.astype(jnp.bfloat16)
+        feature_table[entry + 1] = b.astype(jnp.bfloat16)
 
     def one_own(index, carry):
-        put(2 * index, coef_ref[:, lane_tile(index)], rows_ref[:, lane_tile(index)])
+        rows = rows_ref[:, lane_tile(index)]
+        put(2 * index, coef_ref[:, lane_tile(index)], rows)
+        features = target_features(rows).astype(jnp.bfloat16)
+        turned = bdot(unit, jnp.concatenate([features] * 8, axis=0), NT)
+        place = 2 * (index % (TARGETS // 2)) + row // 64
+        turned = jnp.where(column // 16 == place, turned, 0.0)
+        target_table[index] = turned[:, :16 * TARGETS].astype(jnp.bfloat16)
         return carry
 
     lax.fori_loop(0, own_tiles, one_own, 0, unroll=4)
@@ -171,77 +175,93 @@
     last = own + owners * pairs * 2
     coef_table[last] = jnp.zeros((px, LANES), jnp.bfloat16)
     place = lax.broadcasted_iota(jnp.int32, (8, LANES), 0)
-    nothing = source_features(jnp.where(place == 3, FAR_AWAY, 0.0)).astype(jnp.bfloat16)
-    feature_table[last] = bdot(unit, jnp.concatenate([nothing] * 8, axis=0), NT)[:64].astype(jnp.bfloat16)
-
-
-def sweep_group(group, index_ref, turns_ref, rows_ref, coef_table, feature_table, acc):
+    nothing = source_features(jnp.where(place == 3, FAR_AWAY, 0.0))
+    feature_table[last] = nothing.astype(jnp.bfloat16)
+
+
+def sweep(index_ref, turns_ref, coef_table, feature_table, target_table, first_buffer, second_buffer, acc):
+    groups = turns_ref.shape[0]
     px = coef_table.shape[1]
-    width = TARGETS * 64
-    targets = target_features(rows_ref[:, pl.ds(pl.multiple_of(group * width, width), width)])
-    targets = jnp.concatenate([targets] * 16, axis=0)
-    row = lax.broadcasted_iota(jnp.int32, targets.shape, 0)
-    column = lax.broadcasted_iota(jnp.int32, targets.shape, 1)
-    owner_of_row = (row // LANES) * 2 + jnp.where(row % LANES < 16, 0, jnp.where(row % LANES < 32, 1, 9))
-    weights = jnp.where(owner_of_row == column // 64, targets, 0.0).astype(jnp.bfloat16)
-    lane = lax.broadcasted_iota(jnp.int32, (64, LANES), 1) < 16
+    slots_end = index_ref.shape[1] // CHUNK - 1
+    lane = lax.broadcasted_iota(jnp.int32, (16, LANES), 1) < 64
     lane_x = lax.broadcasted_iota(jnp.int32, (px, LANES), 1) < 64
     acc[...] = jnp.zeros_like(acc)
 
-    def one_turn(turn, carry):
-        slot = turn * CHUNK
-        total = None
+    def tiles(item, buffer):
+        group, turn = item
+        targets = target_table[pl.ds(2 * group, 2)].reshape(TARGETS * 64, 16 * TARGETS)
         for part in range(0, CHUNK, 4):
-            ids = [
-                [index_ref[group * TARGETS + s, slot + part + m] for m in range(4)]
-                for s in range(TARGETS)
-            ]
-            moving = []
-            for m in range(4):
-                moving.append(
+            sources = []
+            for s in range(TARGETS):
+                ids = [index_ref[group * TARGETS + s, turn * CHUNK + part + m] for m in range(4)]
+                sources.append(
                     jnp.concatenate(
                         [
-                            jnp.where(lane, feature_table[ids[s][m]], feature_table[ids[s + 1][m]])
-                            for s in (0, 2)
+                            jnp.where(lane, feature_table[ids[m]], feature_table[ids[m + 1]])
+                            for m in (0, 2)
                         ],
                         axis=1,
                     )
                 )
-            values = jnp.exp2(bdot(jnp.concatenate(moving, axis=0), weights, NN)).astype(jnp.bfloat16)
-            coefs = jnp.concatenate(
-                [
-                    jnp.concatenate(
-                        [
-                            jnp.where(lane_x, coef_table[ids[s][m]], coef_table[ids[s][m + 1]])
-                            for m in (0, 2)
-                        ],
-                        axis=1,
-                    )
-                    for s in range(TARGETS)
-                ],
-                axis=0,
+            power = bdot(targets, jnp.concatenate(sources, axis=0), NN)
+            buffer[:, part * 64:part * 64 + 256] = jnp.exp2(power).astype(jnp.bfloat16)
+
+    def product(item, buffer):
+        group, turn = item
+        coefs = []
+        for s in range(TARGETS):
+            ids = [index_ref[group * TARGETS + s, turn * CHUNK + m] for m in range(CHUNK)]
+            coefs.append(
+                jnp.concatenate(
+                    [
+                        jnp.where(lane_x, coef_table[ids[m]], coef_table[ids[m + 1]])
+                        for m in range(0, CHUNK, 2)
+                    ],
+                    axis=1,
+                )
             )
-            product = bdot(coefs, values, NN)
-            total = product if total is None else total + product
-        acc[...] += total
-        return carry
-
-    lax.fori_loop(0, turns_ref[group], one_turn, 0)
-    block = lax.broadcasted_iota(jnp.int32, (px, width), 1) // 64
-    result = acc[0:px, :]
+        acc[group] += bdot(jnp.concatenate(coefs, axis=0), buffer[...], NT)
+
+    def following(item):
+        group, turn = item
+        over = turn + 1 >= turns_ref[group]
+        later = jnp.where(over, group + 1, group)
+        end = later >= groups
+        turn = jnp.where(end, slots_end, jnp.where(over, 0, turn + 1))
+        return jnp.minimum(later, groups - 1), turn
+
+    def two_items(_, item):
+        second = following(item)
+        third = following(second)
+        tiles(second, second_buffer)
+        product(item, first_buffer)
+        tiles(third, first_buffer)
+        product(second, second_buffer)
+        return third
+
+    items = lax.fori_loop(0, groups, lambda g, n: n + turns_ref[g], jnp.int32(0))
+    start = (jnp.int32(0), jnp.int32(0))
+    tiles(start, first_buffer)
+    lax.fori_loop(0, (items + 1) // 2, two_items, start)
+
+
+def diagonal(block, px):
+    column = lax.broadcasted_iota(jnp.int32, (px, TARGETS * 64), 1) // 64
+    result = block[0:px]
     for s in range(1, TARGETS):
-        result = jnp.where(block == s, acc[s * px:(s + 1) * px, :], result)
+        result = jnp.where(column == s, block[s * px:(s + 1) * px], result)
     return result
 
 
-def fine_kernel(index_ref, turns_ref, recv_ref, coef_ref, rows_ref, out_ref, coef_table, feature_table, acc):
-    build_tables(recv_ref, coef_ref, rows_ref, coef_table, feature_table)
+def fine_kernel(index_ref, turns_ref, recv_ref, coef_ref, rows_ref, out_ref, *scratch):
+    tables, acc = scratch[:3], scratch[-1]
+    build_tables(recv_ref, coef_ref, rows_ref, *tables)
+    sweep(index_ref, turns_ref, *scratch)
+    px = coef_ref.shape[0]
     width = TARGETS * 64
 
     def one_group(group, carry):
-        out_ref[:, pl.ds(pl.multiple_of(group * width, width), width)] = sweep_group(
-            group, index_ref, turns_ref, rows_ref, coef_table, feature_table, acc
-        )
+        out_ref[:, pl.ds(pl.multiple_of(group * width, width), width)] = diagonal(acc[group], px)
         return carry
 
     lax.fori_loop(0, turns_ref.shape[0], one_group, 0)
@@ -258,16 +278,17 @@
     probes_ref,
     out_ref,
     gram_ref,
-    coef_table,
-    feature_table,
-    acc,
+    *scratch,
 ):
-    build_tables(recv_ref, coef_ref, rows_ref, coef_table, feature_table)
+    tables, acc = scratch[:3], scratch[-1]
+    build_tables(recv_ref, coef_ref, rows_ref, *tables)
+    sweep(index_ref, turns_ref, *scratch)
     gram_ref[...] = jnp.zeros_like(gram_ref)
     px = coef_ref.shape[0]
 
     def one_group(group, carry):
-        far = sweep_group(group, index_ref, turns_ref, rows_ref, coef_table, feature_table, acc)
+        far = diagonal(acc[group], px)
+        gram = None
         for part in range(TARGETS):
             q = group * TARGETS + part
             tile = far[:, (part // 2) * LANES:(part // 2 + 1) * LANES]
@@ -282,15 +303,29 @@
             high = total.astype(jnp.bfloat16)
             rest = (total - high.astype(jnp.float32)).astype(jnp.bfloat16)
             probes = probes_ref[:, lane_tile(q)]
-            gram_ref[...] += bdot(probes, high, NT) + bdot(probes, rest, NT)
+            term = bdot(probes, high, NT) + bdot(probes, rest, NT)
+            gram = term if gram is None else gram + term
+        gram_ref[...] += gram
         return carry
 
     lax.fori_loop(0, turns_ref.shape[0], one_group, 0)
+
+
+def sweep_scratch(total, clusters, px):
+    return [
+        pltpu.VMEM((total + 1, px, LANES), jnp.bfloat16),
+        pltpu.VMEM((total + 1, 16, LANES), jnp.bfloat16),
+        pltpu.VMEM((clusters // 2, LANES, 16 * TARGETS), jnp.bfloat16),
+        pltpu.VMEM((TARGETS * 64, CHUNK * 64), jnp.bfloat16),
+        pltpu.VMEM((TARGETS * 64, CHUNK * 64), jnp.bfloat16),
+        pltpu.VMEM((clusters // TARGETS, TARGETS * px, TARGETS * 64), jnp.float32),
+    ]
 
 
 def live_index(slots, counts, nothing):
     place = lax.broadcasted_iota(jnp.int32, slots.shape, 1)
     index = jnp.where(place < counts[:, None], slots, nothing)
+    index = jnp.pad(index, ((0, 0), (0, CHUNK)), constant_values=nothing)
     turns = (jnp.max(counts.reshape(-1, TARGETS), axis=1) + CHUNK - 1) // CHUNK
     return index, turns
 
@@ -323,7 +358,10 @@
     vmem = pl.BlockSpec(memory_space=pltpu.VMEM)
     bf16, f32 = jnp.bfloat16, jnp.float32
 
-    all_probes = lax.all_gather(coef_fine, "probe", axis=0, tiled=True)
+    turned = [coef_fine]
+    for step in range(1, groups):
+        turned.append(lax.ppermute(coef_fine, "probe", [(i, (i + step) % groups) for i in range(groups)]))
+    all_probes = jnp.concatenate(turned, axis=0)
 
     fine_send, fine_rows = pl.pallas_call(
         pack_fine_kernel,
@@ -370,11 +408,7 @@
         out_shape=jax.ShapeDtypeStruct((px, points_fine.shape[1]), f32),
         in_specs=[smem, smem, vmem, vmem, vmem],
         out_specs=vmem,
-        scratch_shapes=[
-            pltpu.VMEM((fine_total + 1, px, LANES), bf16),
-            pltpu.VMEM((fine_total + 1, 64, LANES), bf16),
-            pltpu.VMEM((TARGETS * px, TARGETS * 64), f32),
-        ],
+        scratch_shapes=sweep_scratch(fine_total, fine_count, px),
         compiler_params=params,
         name="fine_sweep",
     )(fine_index, fine_turns, fine_recv, coef, fine_rows)
@@ -387,17 +421,14 @@
         ),
         in_specs=[smem, smem] + [vmem] * 6,
         out_specs=[vmem, vmem],
-        scratch_shapes=[
-            pltpu.VMEM((coarse_total + 1, px, LANES), bf16),
-            pltpu.VMEM((coarse_total + 1, 64, LANES), bf16),
-            pltpu.VMEM((TARGETS * px, TARGETS * 64), f32),
-        ],
+        scratch_shapes=sweep_scratch(coarse_total, coarse_count, px),
         compiler_params=params,
         name="coarse_sweep",
     )(coarse_index, coarse_turns, coarse_recv, coarse_coef, coarse_rows, fine_far, transfer, all_probes)
 
     far_field = far[:probes]
     blocks = gram[:, :probes].reshape(groups, probes * probes)
+    blocks = blocks[(lax.axis_index("probe") - jnp.arange(groups)) % groups]
     blocks = jnp.broadcast_to(blocks[None], (owners, groups, probes * probes))
     blocks = blocks.reshape(owners * groups, 1, probes * probes)
     blocks = lax.all_to_all(blocks, ("leaf", "probe"), split_axis=0, concat_axis=0, tiled=True)

time: 183 us -> 129 us (0.70)
  Pallas kernels: 114 us -> 64.7 us
  blocking collectives: 24.2 us -> 17 us
  waiting for transfers between devices: 22.5 us -> 20.6 us
    pallas_call x1, Pallas kernels: 65.5 us -> 34.5 us  [shards(): pl.pallas_call(fine_kernel, out_shape=jax.ShapeDtypeStruct((px, points_fi...]
    pallas_call x1, Pallas kernels: 40.8 us -> 22.7 us  [shards(): pl.pallas_call(coarse_kernel, out_shape=(jax.ShapeDtypeStruct((px, points...]
    all_gather x1 -> x0, blocking collectives: 9.43 us -> none  [shards(): all_probes = lax.all_gather(coef_fine, 'probe', axis=0, tiled=True)]
    all_to_all x1, blocking collectives: 14.8 us -> 17 us  [shards(): lax.all_to_all(blocks, ('leaf', 'probe'), split_axis=0, concat_axis=0, ti...]
    all_to_all x1, waiting for transfers between devices: 22.5 us -> 20.6 us  [shards(): lax.all_to_all(fine_send, 'leaf', split_axis=0, concat_axis=0, tiled=True)]
  transfers between devices with their start and end apart: 2 -> 3, of which waited for: 1 -> 1; matrix products, arithmetic and copies ran while one was open for 2% -> 3% of each run, Pallas kernels for 38% -> 30%
where the time goes in v1:
time: 129 us; the launch traced here: 128 us
  Pallas kernels  64.7 us (50%)
  waiting for transfers between devices  20.6 us (16%)
  starting transfers between devices  17.1 us (13%)
  blocking collectives  17 us (13%)
  local copies, waits for them, and re-layouts  5.46 us (4%)
  other arithmetic  2.74 us (2%)
    pallas_call x1, Pallas kernels, shards(): pl.pallas_call(fine_kernel, out_shape=jax.ShapeDtypeStruct((px, points_fi...  34.5 us
    pallas_call x1, Pallas kernels, shards(): pl.pallas_call(coarse_kernel, out_shape=(jax.ShapeDtypeStruct((px, points...  22.7 us
    all_to_all x1, waiting for transfers between devices, shards(): lax.all_to_all(fine_send, 'leaf', split_axis=0, concat_axis=0, tiled=True)  20.6 us
    all_to_all x1, blocking collectives, shards(): lax.all_to_all(blocks, ('leaf', 'probe'), split_axis=0, concat_axis=0, ti...  17 us
    all_to_all x1, starting transfers between devices, shards(): lax.all_to_all(coarse_send, 'leaf', split_axis=0, concat_axis=0, tiled=True)  8.01 us
    all_to_all x1, starting transfers between devices, shards(): lax.all_to_all(fine_send, 'leaf', split_axis=0, concat_axis=0, tiled=True)  7.5 us
    pallas_call x1, Pallas kernels, shards(): pl.pallas_call(pack_coarse_kernel, out_shape=(jax.ShapeDtypeStruct((owner...  4.18 us
    pallas_call x1, Pallas kernels, shards(): pl.pallas_call(pack_fine_kernel, out_shape=(jax.ShapeDtypeStruct((owners,...  3.3 us
  transfers between devices with their start and end apart: 3, of which 1 were waited for; matrix products, arithmetic and copies ran while one was open for 3% of the time, Pallas kernels for 30%

profile of v1, /device:TPU:0, one launch (start us, length us, event | category | flops | bytes accessed | tf_op | source)
XLA Modules:
  0.0 128.4 jit_solution(6546979022850287900)
XLA Ops:
  0.6 3.3 %pack_fine.1 = (bf16[16,320,128]{2,1,0:T(8,128)(2,1)}, f32[8,4096]{1,0:T(8,128)}) custom-call(s32[16,16]{1,0:T(8,128)} %bitcast.6, bf16[32,4096]{1,0:T(8,128)(2,1)} %coef_ref.5, f32[3,4096]{1,0:T(4,128)} %points_ref.3), custom_call_target="tpu_custom_call" | custom-call | tf_op jit(solution)/shard_map/pack_fine/pallas_call | solution.py:366
  3.9 0.0 copy-start.1
  3.9 0.0 copy-start.7
  3.9 0.0 copy-start.6
  3.9 0.0 copy-start.5
  4.0 0.0 copy-start.8
  4.0 7.5 %all-to-all-start.1 = ((bf16[16,320,128]{2,1,0:T(8,128)(2,1)}), bf16[16,320,128]{2,1,0:T(8,128)(2,1)S(1)}, u32[]{:S(2)}, u32[]{:S(2)}) async-start(bf16[16,320,128]{2,1,0:T(8,128)(2,1)} %get-tuple-element.12), calls=%async_computation.1 | async-start | bytes 2621440 | tf_op jit(solution)/shard_map/all_to_all | solution.py:381
  11.5 0.0 copy-done.1
  11.5 0.0 copy-start.4
  11.5 0.0 copy-start.2
  11.5 1.6 %collective-permute-start = (bf16[32,4096]{1,0:T(8,128)(2,1)S(1)}, bf16[32,4096]{1,0:T(8,128)(2,1)S(1)}, u32[]{:S(2)}, u32[]{:S(2)}) collective-permute-start(bf16[32,4096]{1,0:T(8,128)(2,1)S(1)} %copy-done.1), channel_id=1, source_target_pairs={{0,1},{1,0},{2,3},{3,2},{4,5},{5,4},{6,7},{7,6},{8,9},{9,8},{10,11... | collective-permute-start | bytes 786440 | tf_op jit(solution)/shard_map/ppermute | solution.py:363
  13.1 0.0 copy-done.7
  13.1 0.1 reshape.82
  13.2 0.0 copy-done.6
  13.2 0.7 copy.16.send_ref
  13.9 0.1 reduce_max.19
  14.0 4.2 %pack_coarse.1 = (bf16[16,160,128]{2,1,0:T(8,128)(2,1)}, f32[8,2048]{1,0:T(8,128)}, bf16[32,2048]{1,0:T(8,128)(2,1)}) custom-call(s32[16,8]{1,0:T(8,128)} %copy.16.send_ref, bf16[32,4096]{1,0:T(8,128)(2,1)} %coef_ref.5, bf16[64,4096]{1,0:T(8,128)(2,1)} %transfer_ref.3, f32[3,2048]{1,0:T(4,128)} %points_ref.2), custom_call_target="tpu_custom_call" | custom-call | tf_op jit(solution)/shard_map/pack_coarse/pallas_call | solution.py:383
  18.2 0.0 copy-done.5
  18.2 0.0 copy-done.8
  18.2 0.1 fusion.1
  18.3 20.6 %all-to-all-done.1.recv_ref = bf16[16,320,128]{2,1,0:T(8,128)(2,1)S(1)} async-done(((bf16[16,320,128]{2,1,0:T(8,128)(2,1)}), bf16[16,320,128]{2,1,0:T(8,128)(2,1)S(1)}, u32[]{:S(2)}, u32[]{:S(2)}) %all-to-all-start.1) | async-done | bytes 1310752 | tf_op jit(solution)/shard_map/all_to_all | solution.py:381
  38.9 0.0 copy-start
  38.9 8.0 %all-to-all-start = ((bf16[16,160,128]{2,1,0:T(8,128)(2,1)}), bf16[16,160,128]{2,1,0:T(8,128)(2,1)S(1)}, u32[]{:S(2)}, u32[]{:S(2)}) async-start(bf16[16,160,128]{2,1,0:T(8,128)(2,1)} %get-tuple-element.9), calls=%async_computation | async-start | bytes 1310720 | tf_op jit(solution)/shard_map/all_to_all | solution.py:399
  46.9 0.5 and_select_fusion.1.turns_ref
  47.5 0.0 copy-done.4
  47.5 0.1 fusion
  47.5 0.1 reshape.80
  47.6 0.1 reduce_max.18
  47.7 0.6 pad.9.index_ref
  48.4 0.6 pad.8.index_ref
  49.0 0.6 and_select_fusion.2.turns_ref
  49.6 0.0 collective-permute-done
  49.6 0.0 copy-done.2
  49.6 0.8 pad_maximum_fusion.probes_ref
  50.4 0.0 copy-done
  50.4 34.5 %fine_sweep.1.fine_ref = f32[32,4096]{1,0:T(8,128)} custom-call(s32[64,72]{1,0:T(8,128)} %pad.9.index_ref, s32[16]{0:T(128)} %and_select_fusion.1.turns_ref, bf16[16,320,128]{2,1,0:T(8,128)(2,1)} %copy-done, bf16[32,4096]{1,0:T(8,128)(2,1)} %coef_ref.5, f32[8,4096]{1,0:T(8,128)} %get-tuple-element.13.rows_ref), custom_call_target="tpu_custom_call" | custom-call | tf_op jit(solution)/shard_map/fine_sweep/pallas_call | solution.py:406
  84.9 0.0 all-to-all-done.recv_ref
  84.9 0.0 copy-start.3
  84.9 0.8 copy-done.3
  85.7 22.7 %coarse_sweep.1 = (f32[32,4096]{1,0:T(8,128)}, f32[64,32]{1,0:T(8,128)}) custom-call(s32[32,72]{1,0:T(8,128)} %pad.8.index_ref, s32[8]{0:T(128)} %and_select_fusion.2.turns_ref, bf16[16,160,128]{2,1,0:T(8,128)(2,1)} %copy-done.3, bf16[32,2048]{1,0:T(8,128)(2,1)} %get-tuple-element.10.coef_ref, f32[8,2048]{1,0:T(8,128)} %get-tuple-element.11.rows_ref, ...), custom_call_target="tpu_custom_call" | custom-call | tf_op jit(solution)/shard_map/coarse_sweep/pallas_call | solution.py:416
  108.5 0.8 reshape.84
  109.3 0.6 gather_fusion
  109.9 0.2 reshape.85
  110.1 17.0 %all_to_all.15 = f32[32,1,1024]{2,1,0:T(1,128)S(1)} all-to-all(f32[32,1,1024]{2,1,0:T(1,128)S(1)} %reshape.85), channel_id=1, replica_groups=mesh['leaf'=16,'probe'=2] {'leaf','probe'}, dimensions={0} | all-to-all | bytes 262144 | tf_op jit(solution)/shard_map/all_to_all | solution.py:434
  127.1 0.3 reduce
  127.4 0.2 reshape.86
  127.6 0.1 reduce_sum.9
  127.7 0.7 mul.15
  (5 shorter events, 0.1 us)
Async XLA Ops:
  3.9 7.5 %copy-start.1 = (bf16[32,4096]{1,0:T(8,128)(2,1)S(1)}, bf16[32,4096]{1,0:T(8,128)(2,1)}, u32[]{:S(2)}) copy-start(bf16[32,4096]{1,0:T(8,128)(2,1)} %coef_ref.5) | copy-start | bytes 786436
  3.9 9.2 %copy-start.7 = (s32[64]{0:T(128)S(1)}, s32[64]{0:T(128)}, u32[]{:S(2)}) copy-start(s32[64]{0:T(128)} %param.16) | copy-start | bytes 772
  3.9 9.2 %copy-start.6 = (s32[1,16,8]{1,2,0:T(8,128)S(1)}, s32[1,16,8]{1,2,0:T(8,128)}, u32[]{:S(2)}) copy-start(s32[1,16,8]{1,2,0:T(8,128)} %param.17) | copy-start | bytes 1540
  3.9 14.2 %copy-start.5 = (s32[32,64]{1,0:T(8,128)S(1)}, s32[32,64]{1,0:T(8,128)}, u32[]{:S(2)}) copy-start(s32[32,64]{1,0:T(8,128)} %param.18) | copy-start | bytes 24580
  4.0 14.2 %copy-start.8 = (s32[32]{0:T(128)S(1)}, s32[32]{0:T(128)}, u32[]{:S(2)}) copy-start(s32[32]{0:T(128)} %param.19) | copy-start | bytes 388
  4.0 34.9 %all-to-all-start.1 = ((bf16[16,320,128]{2,1,0:T(8,128)(2,1)}), bf16[16,320,128]{2,1,0:T(8,128)(2,1)S(1)}, u32[]{:S(2)}, u32[]{:S(2)}) async-start(bf16[16,320,128]{2,1,0:T(8,128)(2,1)} %get-tuple-element.12), calls=%async_computation.1 | async-start | bytes 2621440 | tf_op jit(solution)/shard_map/all_to_all | solution.py:381
  11.5 36.0 %copy-start.4 = (s32[64,64]{1,0:T(8,128)S(1)}, s32[64,64]{1,0:T(8,128)}, u32[]{:S(2)}) copy-start(s32[64,64]{1,0:T(8,128)} %param.15) | copy-start | bytes 49156
  11.5 38.1 %copy-start.2 = (bf16[32,4096]{1,0:T(8,128)(2,1)S(1)}, bf16[32,4096]{1,0:T(8,128)(2,1)}, u32[]{:S(2)}) copy-start(bf16[32,4096]{1,0:T(8,128)(2,1)} %coef_ref.5) | copy-start | bytes 786436
  11.5 38.0 %collective-permute-start = (bf16[32,4096]{1,0:T(8,128)(2,1)S(1)}, bf16[32,4096]{1,0:T(8,128)(2,1)S(1)}, u32[]{:S(2)}, u32[]{:S(2)}) collective-permute-start(bf16[32,4096]{1,0:T(8,128)(2,1)S(1)} %copy-done.1), channel_id=1, source_target_pairs={{0,1},{1,0},{2,3},{3,2},{4,5},{5,4},{6,7},{7,6},{8,9},{9,8},{10,11... | collective-permute-start | bytes 786440 | tf_op jit(solution)/shard_map/ppermute | solution.py:363
  38.9 11.5 %copy-start = (bf16[16,320,128]{2,1,0:T(8,128)(2,1)}, bf16[16,320,128]{2,1,0:T(8,128)(2,1)S(1)}, u32[]{:S(2)}) copy-start(bf16[16,320,128]{2,1,0:T(8,128)(2,1)S(1)} %all-to-all-done.1.recv_ref) | copy-start | bytes 3932164
  38.9 46.0 %all-to-all-start = ((bf16[16,160,128]{2,1,0:T(8,128)(2,1)}), bf16[16,160,128]{2,1,0:T(8,128)(2,1)S(1)}, u32[]{:S(2)}, u32[]{:S(2)}) async-start(bf16[16,160,128]{2,1,0:T(8,128)(2,1)} %get-tuple-element.9), calls=%async_computation | async-start | bytes 1310720 | tf_op jit(solution)/shard_map/all_to_all | solution.py:399
  84.9 0.8 copy-start.3

commit v2 on v1

--- a/solution.py
+++ b/solution.py
@@ -11,7 +11,7 @@
 KERNEL_RATE = 1.5
 POINT_SCALE = math.sqrt(2.0 * KERNEL_RATE * math.log2(math.e))
 LANES = 128
-TARGETS = 4
+UNITS = 4
 CHUNK = 8
 FAR_AWAY = -30000.0
 VMEM = 56 * 1024 * 1024
@@ -150,10 +150,9 @@
         rows = rows_ref[:, lane_tile(index)]
         put(2 * index, coef_ref[:, lane_tile(index)], rows)
         features = target_features(rows).astype(jnp.bfloat16)
-        turned = bdot(unit, jnp.concatenate([features] * 8, axis=0), NT)
-        place = 2 * (index % (TARGETS // 2)) + row // 64
-        turned = jnp.where(column // 16 == place, turned, 0.0)
-        target_table[index] = turned[:, :16 * TARGETS].astype(jnp.bfloat16)
+        turned = bdot(unit, jnp.concatenate([features] * 8, axis=0), NT)[:, :16]
+        target_table[2 * index] = turned[:64].astype(jnp.bfloat16)
+        target_table[2 * index + 1] = turned[64:].astype(jnp.bfloat16)
         return carry
 
     lax.fori_loop(0, own_tiles, one_own, 0, unroll=4)
@@ -180,91 +179,72 @@
 
 
 def sweep(index_ref, turns_ref, coef_table, feature_table, target_table, first_buffer, second_buffer, acc):
-    groups = turns_ref.shape[0]
+    clusters = turns_ref.shape[0]
     px = coef_table.shape[1]
     slots_end = index_ref.shape[1] // CHUNK - 1
     lane = lax.broadcasted_iota(jnp.int32, (16, LANES), 1) < 64
     lane_x = lax.broadcasted_iota(jnp.int32, (px, LANES), 1) < 64
     acc[...] = jnp.zeros_like(acc)
 
-    def tiles(item, buffer):
-        group, turn = item
-        targets = target_table[pl.ds(2 * group, 2)].reshape(TARGETS * 64, 16 * TARGETS)
-        for part in range(0, CHUNK, 4):
-            sources = []
-            for s in range(TARGETS):
-                ids = [index_ref[group * TARGETS + s, turn * CHUNK + part + m] for m in range(4)]
-                sources.append(
-                    jnp.concatenate(
-                        [
-                            jnp.where(lane, feature_table[ids[m]], feature_table[ids[m + 1]])
-                            for m in (0, 2)
-                        ],
-                        axis=1,
-                    )
-                )
-            power = bdot(targets, jnp.concatenate(sources, axis=0), NN)
-            buffer[:, part * 64:part * 64 + 256] = jnp.exp2(power).astype(jnp.bfloat16)
-
-    def product(item, buffer):
-        group, turn = item
-        coefs = []
-        for s in range(TARGETS):
-            ids = [index_ref[group * TARGETS + s, turn * CHUNK + m] for m in range(CHUNK)]
-            coefs.append(
-                jnp.concatenate(
-                    [
-                        jnp.where(lane_x, coef_table[ids[m]], coef_table[ids[m + 1]])
-                        for m in range(0, CHUNK, 2)
-                    ],
-                    axis=1,
-                )
-            )
-        acc[group] += bdot(jnp.concatenate(coefs, axis=0), buffer[...], NT)
-
-    def following(item):
-        group, turn = item
-        over = turn + 1 >= turns_ref[group]
-        later = jnp.where(over, group + 1, group)
-        end = later >= groups
+    def pairs_of(unit, table, low):
+        target, turn = unit
+        ids = [index_ref[target, turn * CHUNK + m] for m in range(CHUNK)]
+        return jnp.concatenate(
+            [jnp.where(low, table[ids[m]], table[ids[m + 1]]) for m in range(0, CHUNK, 2)], axis=1
+        )
+
+    def tiles(units, buffer):
+        for place, unit in enumerate(units):
+            power = bdot(target_table[unit[0]], pairs_of(unit, feature_table, lane), NN)
+            buffer[place] = jnp.exp2(power).astype(jnp.bfloat16)
+
+    def products(units, buffer):
+        for place, unit in enumerate(units):
+            acc[unit[0]] += bdot(pairs_of(unit, coef_table, lane_x), buffer[place], NT)
+
+    def following(unit):
+        target, turn = unit
+        over = turn + 1 >= turns_ref[target]
+        later = jnp.where(over, target + 1, target)
+        end = later >= clusters
         turn = jnp.where(end, slots_end, jnp.where(over, 0, turn + 1))
-        return jnp.minimum(later, groups - 1), turn
-
-    def two_items(_, item):
-        second = following(item)
-        third = following(second)
+        return jnp.minimum(later, clusters - 1), turn
+
+    def next_units(unit):
+        units = []
+        for _ in range(UNITS):
+            unit = following(unit)
+            units.append(unit)
+        return tuple(units)
+
+    def two_sets(_, units):
+        second = next_units(units[-1])
+        third = next_units(second[-1])
         tiles(second, second_buffer)
-        product(item, first_buffer)
+        products(units, first_buffer)
         tiles(third, first_buffer)
-        product(second, second_buffer)
+        products(second, second_buffer)
         return third
 
-    items = lax.fori_loop(0, groups, lambda g, n: n + turns_ref[g], jnp.int32(0))
-    start = (jnp.int32(0), jnp.int32(0))
+    total = lax.fori_loop(0, clusters, lambda c, n: n + turns_ref[c], jnp.int32(0))
+    unit = (jnp.int32(0), jnp.int32(0))
+    start = (unit,) + next_units(unit)[:-1]
     tiles(start, first_buffer)
-    lax.fori_loop(0, (items + 1) // 2, two_items, start)
-
-
-def diagonal(block, px):
-    column = lax.broadcasted_iota(jnp.int32, (px, TARGETS * 64), 1) // 64
-    result = block[0:px]
-    for s in range(1, TARGETS):
-        result = jnp.where(column == s, block[s * px:(s + 1) * px], result)
-    return result
+    lax.fori_loop(0, (total + 2 * UNITS - 1) // (2 * UNITS), two_sets, start)
 
 
 def fine_kernel(index_ref, turns_ref, recv_ref, coef_ref, rows_ref, out_ref, *scratch):
     tables, acc = scratch[:3], scratch[-1]
     build_tables(recv_ref, coef_ref, rows_ref, *tables)
     sweep(index_ref, turns_ref, *scratch)
-    px = coef_ref.shape[0]
-    width = TARGETS * 64
-
-    def one_group(group, carry):
-        out_ref[:, pl.ds(pl.multiple_of(group * width, width), width)] = diagonal(acc[group], px)
-        return carry
-
-    lax.fori_loop(0, turns_ref.shape[0], one_group, 0)
+    low = lax.broadcasted_iota(jnp.int32, (coef_ref.shape[0], LANES), 1) < 64
+
+    def one_tile(index, carry):
+        pair = [jnp.concatenate([acc[2 * index + part]] * 2, axis=1) for part in range(2)]
+        out_ref[:, lane_tile(index)] = jnp.where(low, pair[0], pair[1])
+        return carry
+
+    lax.fori_loop(0, turns_ref.shape[0] // 2, one_tile, 0, unroll=4)
 
 
 def coarse_kernel(
@@ -284,15 +264,12 @@
     build_tables(recv_ref, coef_ref, rows_ref, *tables)
     sweep(index_ref, turns_ref, *scratch)
     gram_ref[...] = jnp.zeros_like(gram_ref)
-    px = coef_ref.shape[0]
 
     def one_group(group, carry):
-        far = diagonal(acc[group], px)
         gram = None
-        for part in range(TARGETS):
-            q = group * TARGETS + part
-            tile = far[:, (part // 2) * LANES:(part // 2 + 1) * LANES]
-            twice = halves(tile)[part % 2].astype(jnp.bfloat16)
+        for part in range(4):
+            q = group * 4 + part
+            twice = jnp.concatenate([acc[q]] * 2, axis=1).astype(jnp.bfloat16)
             matrix = transfer_ref[:, lane_tile(q)].astype(jnp.float32)
             low = lax.broadcasted_iota(jnp.int32, matrix.shape, 1) < 64
             matrix = jnp.concatenate(
@@ -308,17 +285,17 @@
         gram_ref[...] += gram
         return carry
 
-    lax.fori_loop(0, turns_ref.shape[0], one_group, 0)
+    lax.fori_loop(0, turns_ref.shape[0] // 4, one_group, 0)
 
 
 def sweep_scratch(total, clusters, px):
     return [
         pltpu.VMEM((total + 1, px, LANES), jnp.bfloat16),
         pltpu.VMEM((total + 1, 16, LANES), jnp.bfloat16),
-        pltpu.VMEM((clusters // 2, LANES, 16 * TARGETS), jnp.bfloat16),
-        pltpu.VMEM((TARGETS * 64, CHUNK * 64), jnp.bfloat16),
-        pltpu.VMEM((TARGETS * 64, CHUNK * 64), jnp.bfloat16),
-        pltpu.VMEM((clusters // TARGETS, TARGETS * px, TARGETS * 64), jnp.float32),
+        pltpu.VMEM((clusters, 64, 16), jnp.bfloat16),
+        pltpu.VMEM((UNITS, 64, CHUNK * 64), jnp.bfloat16),
+        pltpu.VMEM((UNITS, 64, CHUNK * 64), jnp.bfloat16),
+        pltpu.VMEM((clusters, px, 64), jnp.float32),
     ]
 
 
@@ -326,7 +303,7 @@
     place = lax.broadcasted_iota(jnp.int32, slots.shape, 1)
     index = jnp.where(place < counts[:, None], slots, nothing)
     index = jnp.pad(index, ((0, 0), (0, CHUNK)), constant_values=nothing)
-    turns = (jnp.max(counts.reshape(-1, TARGETS), axis=1) + CHUNK - 1) // CHUNK
+    turns = (counts + CHUNK - 1) // CHUNK
     return index, turns
 
 

time: 129 us -> 130 us (level)
  Pallas kernels: 64.7 us -> 66.6 us
    pallas_call x1, Pallas kernels: 22.7 us -> 24.6 us  [shards(): pl.pallas_call(coarse_kernel, out_shape=(jax.ShapeDtypeStruct((px, points...]
where the time goes in v2:
time: 130 us; the launch traced here: 129 us
  Pallas kernels  66.6 us (51%)
  waiting for transfers between devices  20.9 us (16%)
  starting transfers between devices  17.1 us (13%)
  blocking collectives  16 us (12%)
  local copies, waits for them, and re-layouts  5.3 us (4%)
  other arithmetic  2.57 us (2%)
    pallas_call x1, Pallas kernels, shards(): pl.pallas_call(fine_kernel, out_shape=jax.ShapeDtypeStruct((px, points_fi...  34.6 us
    pallas_call x1, Pallas kernels, shards(): pl.pallas_call(coarse_kernel, out_shape=(jax.ShapeDtypeStruct((px, points...  24.6 us
    all_to_all x1, waiting for transfers between devices, shards(): lax.all_to_all(fine_send, 'leaf', split_axis=0, concat_axis=0, tiled=True)  20.9 us
    all_to_all x1, blocking collectives, shards(): lax.all_to_all(blocks, ('leaf', 'probe'), split_axis=0, concat_axis=0, ti...  16 us
    all_to_all x1, starting transfers between devices, shards(): lax.all_to_all(coarse_send, 'leaf', split_axis=0, concat_axis=0, tiled=True)  8.01 us
    all_to_all x1, starting transfers between devices, shards(): lax.all_to_all(fine_send, 'leaf', split_axis=0, concat_axis=0, tiled=True)  7.5 us
    pallas_call x1, Pallas kernels, shards(): pl.pallas_call(pack_coarse_kernel, out_shape=(jax.ShapeDtypeStruct((owner...  4.15 us
    pallas_call x1, Pallas kernels, shards(): pl.pallas_call(pack_fine_kernel, out_shape=(jax.ShapeDtypeStruct((owners,...  3.33 us
  transfers between devices with their start and end apart: 3, of which 1 were waited for; matrix products, arithmetic and copies ran while one was open for 3% of the time, Pallas kernels for 30%

profile of v2, /device:TPU:0, one launch (start us, length us, event | category | flops | bytes accessed | tf_op | source)
XLA Modules:
  0.0 129.3 jit_solution(5395425849879885512)
XLA Ops:
  0.6 3.3 %pack_fine.1 = (bf16[16,320,128]{2,1,0:T(8,128)(2,1)}, f32[8,4096]{1,0:T(8,128)}) custom-call(s32[16,16]{1,0:T(8,128)} %bitcast.6, bf16[32,4096]{1,0:T(8,128)(2,1)} %coef_ref.5, f32[3,4096]{1,0:T(4,128)} %points_ref.3), custom_call_target="tpu_custom_call" | custom-call | tf_op jit(solution)/shard_map/pack_fine/pallas_call | solution.py:343
  4.0 0.0 copy-start.1
  4.0 0.0 copy-start.6
  4.0 0.0 copy-start.5
  4.0 0.0 copy-start.8
  4.0 7.5 %all-to-all-start.1 = ((bf16[16,320,128]{2,1,0:T(8,128)(2,1)}), bf16[16,320,128]{2,1,0:T(8,128)(2,1)S(1)}, u32[]{:S(2)}, u32[]{:S(2)}) async-start(bf16[16,320,128]{2,1,0:T(8,128)(2,1)} %get-tuple-element.12), calls=%async_computation.1 | async-start | bytes 2621440 | tf_op jit(solution)/shard_map/all_to_all | solution.py:358
  11.5 0.0 copy-done.1
  11.5 0.0 copy-start.7
  11.5 0.0 copy-start.4
  11.5 0.0 copy-start.2
  11.5 1.6 %collective-permute-start = (bf16[32,4096]{1,0:T(8,128)(2,1)S(1)}, bf16[32,4096]{1,0:T(8,128)(2,1)S(1)}, u32[]{:S(2)}, u32[]{:S(2)}) collective-permute-start(bf16[32,4096]{1,0:T(8,128)(2,1)S(1)} %copy-done.1), channel_id=1, source_target_pairs={{0,1},{1,0},{2,3},{3,2},{4,5},{5,4},{6,7},{7,6},{8,9},{9,8},{10,11... | collective-permute-start | bytes 786440 | tf_op jit(solution)/shard_map/ppermute | solution.py:340
  13.1 0.0 copy-done.6
  13.1 0.7 copy.16.send_ref
  13.8 4.2 %pack_coarse.1 = (bf16[16,160,128]{2,1,0:T(8,128)(2,1)}, f32[8,2048]{1,0:T(8,128)}, bf16[32,2048]{1,0:T(8,128)(2,1)}) custom-call(s32[16,8]{1,0:T(8,128)} %copy.16.send_ref, bf16[32,4096]{1,0:T(8,128)(2,1)} %coef_ref.5, bf16[64,4096]{1,0:T(8,128)(2,1)} %transfer_ref.3, f32[3,2048]{1,0:T(4,128)} %points_ref.2), custom_call_target="tpu_custom_call" | custom-call | tf_op jit(solution)/shard_map/pack_coarse/pallas_call | solution.py:360
  18.0 0.0 copy-done.5
  18.0 0.0 copy-done.8
  18.0 0.1 fusion.1
  18.1 20.9 %all-to-all-done.1.recv_ref = bf16[16,320,128]{2,1,0:T(8,128)(2,1)S(1)} async-done(((bf16[16,320,128]{2,1,0:T(8,128)(2,1)}), bf16[16,320,128]{2,1,0:T(8,128)(2,1)S(1)}, u32[]{:S(2)}, u32[]{:S(2)}) %all-to-all-start.1) | async-done | bytes 1310752 | tf_op jit(solution)/shard_map/all_to_all | solution.py:358
  38.9 0.0 copy-start
  38.9 8.0 %all-to-all-start = ((bf16[16,160,128]{2,1,0:T(8,128)(2,1)}), bf16[16,160,128]{2,1,0:T(8,128)(2,1)S(1)}, u32[]{:S(2)}, u32[]{:S(2)}) async-start(bf16[16,160,128]{2,1,0:T(8,128)(2,1)} %get-tuple-element.9), calls=%async_computation | async-start | bytes 1310720 | tf_op jit(solution)/shard_map/all_to_all | solution.py:376
  46.9 0.0 copy-done.7
  46.9 0.6 and_select_fusion.1.turns_ref
  47.5 0.0 copy-done.4
  47.5 0.1 fusion
  47.6 0.6 pad.9.index_ref
  48.2 0.6 pad.8.index_ref
  48.8 0.6 and_select_fusion.2.turns_ref
  49.4 0.0 collective-permute-done
  49.4 0.0 copy-done.2
  49.4 0.8 pad_maximum_fusion.probes_ref
  50.3 0.0 copy-done
  50.3 34.6 %fine_sweep.1.fine_ref = f32[32,4096]{1,0:T(8,128)} custom-call(s32[64,72]{1,0:T(8,128)} %pad.9.index_ref, s32[64]{0:T(128)} %and_select_fusion.1.turns_ref, bf16[16,320,128]{2,1,0:T(8,128)(2,1)} %copy-done, bf16[32,4096]{1,0:T(8,128)(2,1)} %coef_ref.5, f32[8,4096]{1,0:T(8,128)} %get-tuple-element.13.rows_ref), custom_call_target="tpu_custom_call" | custom-call | tf_op jit(solution)/shard_map/fine_sweep/pallas_call | solution.py:383
  84.9 0.0 all-to-all-done.recv_ref
  84.9 0.0 copy-start.3
  84.9 0.8 copy-done.3
  85.7 24.6 %coarse_sweep.1 = (f32[32,4096]{1,0:T(8,128)}, f32[64,32]{1,0:T(8,128)}) custom-call(s32[32,72]{1,0:T(8,128)} %pad.8.index_ref, s32[32]{0:T(128)} %and_select_fusion.2.turns_ref, bf16[16,160,128]{2,1,0:T(8,128)(2,1)} %copy-done.3, bf16[32,2048]{1,0:T(8,128)(2,1)} %get-tuple-element.10.coef_ref, f32[8,2048]{1,0:T(8,128)} %get-tuple-element.11.rows_ref, ...), custom_call_target="tpu_custom_call" | custom-call | tf_op jit(solution)/shard_map/coarse_sweep/pallas_call | solution.py:393
  110.3 0.8 reshape.76
  111.1 0.6 gather_fusion
  111.7 0.2 reshape.77
  111.9 16.0 %all_to_all.15 = f32[32,1,1024]{2,1,0:T(1,128)S(1)} all-to-all(f32[32,1,1024]{2,1,0:T(1,128)S(1)} %reshape.77), channel_id=1, replica_groups=mesh['leaf'=16,'probe'=2] {'leaf','probe'}, dimensions={0} | all-to-all | bytes 262144 | tf_op jit(solution)/shard_map/all_to_all | solution.py:411
  128.0 0.3 reduce
  128.3 0.2 reshape.78
  128.5 0.1 reduce_sum.9
  128.6 0.7 mul.15
  (5 shorter events, 0.1 us)
Async XLA Ops:
  4.0 7.5 %copy-start.1 = (bf16[32,4096]{1,0:T(8,128)(2,1)S(1)}, bf16[32,4096]{1,0:T(8,128)(2,1)}, u32[]{:S(2)}) copy-start(bf16[32,4096]{1,0:T(8,128)(2,1)} %coef_ref.5) | copy-start | bytes 786436
  4.0 9.2 %copy-start.6 = (s32[1,16,8]{1,2,0:T(8,128)S(1)}, s32[1,16,8]{1,2,0:T(8,128)}, u32[]{:S(2)}) copy-start(s32[1,16,8]{1,2,0:T(8,128)} %param.17) | copy-start | bytes 1540
  4.0 14.0 %copy-start.5 = (s32[32,64]{1,0:T(8,128)S(1)}, s32[32,64]{1,0:T(8,128)}, u32[]{:S(2)}) copy-start(s32[32,64]{1,0:T(8,128)} %param.18) | copy-start | bytes 24580
  4.0 14.0 %copy-start.8 = (s32[32]{0:T(128)S(1)}, s32[32]{0:T(128)}, u32[]{:S(2)}) copy-start(s32[32]{0:T(128)} %param.19) | copy-start | bytes 388
  4.0 34.9 %all-to-all-start.1 = ((bf16[16,320,128]{2,1,0:T(8,128)(2,1)}), bf16[16,320,128]{2,1,0:T(8,128)(2,1)S(1)}, u32[]{:S(2)}, u32[]{:S(2)}) async-start(bf16[16,320,128]{2,1,0:T(8,128)(2,1)} %get-tuple-element.12), calls=%async_computation.1 | async-start | bytes 2621440 | tf_op jit(solution)/shard_map/all_to_all | solution.py:358
  11.5 35.4 %copy-start.7 = (s32[64]{0:T(128)S(1)}, s32[64]{0:T(128)}, u32[]{:S(2)}) copy-start(s32[64]{0:T(128)} %param.16) | copy-start | bytes 772
  11.5 36.0 %copy-start.4 = (s32[64,64]{1,0:T(8,128)S(1)}, s32[64,64]{1,0:T(8,128)}, u32[]{:S(2)}) copy-start(s32[64,64]{1,0:T(8,128)} %param.15) | copy-start | bytes 49156
  11.5 37.9 %copy-start.2 = (bf16[32,4096]{1,0:T(8,128)(2,1)S(1)}, bf16[32,4096]{1,0:T(8,128)(2,1)}, u32[]{:S(2)}) copy-start(bf16[32,4096]{1,0:T(8,128)(2,1)} %coef_ref.5) | copy-start | bytes 786436
  11.5 37.9 %collective-permute-start = (bf16[32,4096]{1,0:T(8,128)(2,1)S(1)}, bf16[32,4096]{1,0:T(8,128)(2,1)S(1)}, u32[]{:S(2)}, u32[]{:S(2)}) collective-permute-start(bf16[32,4096]{1,0:T(8,128)(2,1)S(1)} %copy-done.1), channel_id=1, source_target_pairs={{0,1},{1,0},{2,3},{3,2},{4,5},{5,4},{6,7},{7,6},{8,9},{9,8},{10,11... | collective-permute-start | bytes 786440 | tf_op jit(solution)/shard_map/ppermute | solution.py:340
  38.9 11.4 %copy-start = (bf16[16,320,128]{2,1,0:T(8,128)(2,1)}, bf16[16,320,128]{2,1,0:T(8,128)(2,1)S(1)}, u32[]{:S(2)}) copy-start(bf16[16,320,128]{2,1,0:T(8,128)(2,1)S(1)} %all-to-all-done.1.recv_ref) | copy-start | bytes 3932164
  38.9 46.0 %all-to-all-start = ((bf16[16,160,128]{2,1,0:T(8,128)(2,1)}), bf16[16,160,128]{2,1,0:T(8,128)(2,1)S(1)}, u32[]{:S(2)}, u32[]{:S(2)}) async-start(bf16[16,160,128]{2,1,0:T(8,128)(2,1)} %get-tuple-element.9), calls=%async_computation | async-start | bytes 1310720 | tf_op jit(solution)/shard_map/all_to_all | solution.py:376
  84.9 0.8 copy-start.3

commit v3 on v2

--- a/solution.py
+++ b/solution.py
@@ -139,9 +139,9 @@
     unit = jnp.where(row == column, 1.0, 0.0).astype(jnp.bfloat16)
 
     def put(entry, coef, rows):
-        a, b = halves(coef.astype(jnp.float32))
-        coef_table[entry] = a.astype(jnp.bfloat16)
-        coef_table[entry + 1] = b.astype(jnp.bfloat16)
+        turned = bdot(unit, coef, NT).astype(jnp.bfloat16)
+        coef_table[entry] = turned[:64]
+        coef_table[entry + 1] = turned[64:]
         a, b = halves(source_features(rows))
         feature_table[entry] = a.astype(jnp.bfloat16)
         feature_table[entry + 1] = b.astype(jnp.bfloat16)
@@ -172,7 +172,7 @@
 
     lax.fori_loop(0, owners, one_owner, 0)
     last = own + owners * pairs * 2
-    coef_table[last] = jnp.zeros((px, LANES), jnp.bfloat16)
+    coef_table[last] = jnp.zeros((64, px), jnp.bfloat16)
     place = lax.broadcasted_iota(jnp.int32, (8, LANES), 0)
     nothing = source_features(jnp.where(place == 3, FAR_AWAY, 0.0))
     feature_table[last] = nothing.astype(jnp.bfloat16)
@@ -180,27 +180,28 @@
 
 def sweep(index_ref, turns_ref, coef_table, feature_table, target_table, first_buffer, second_buffer, acc):
     clusters = turns_ref.shape[0]
-    px = coef_table.shape[1]
     slots_end = index_ref.shape[1] // CHUNK - 1
     lane = lax.broadcasted_iota(jnp.int32, (16, LANES), 1) < 64
-    lane_x = lax.broadcasted_iota(jnp.int32, (px, LANES), 1) < 64
     acc[...] = jnp.zeros_like(acc)
 
-    def pairs_of(unit, table, low):
+    def partners(unit):
         target, turn = unit
-        ids = [index_ref[target, turn * CHUNK + m] for m in range(CHUNK)]
-        return jnp.concatenate(
-            [jnp.where(low, table[ids[m]], table[ids[m + 1]]) for m in range(0, CHUNK, 2)], axis=1
-        )
+        return [index_ref[target, turn * CHUNK + m] for m in range(CHUNK)]
 
     def tiles(units, buffer):
         for place, unit in enumerate(units):
-            power = bdot(target_table[unit[0]], pairs_of(unit, feature_table, lane), NN)
+            ids = partners(unit)
+            sources = [
+                jnp.where(lane, feature_table[ids[m]], feature_table[ids[m + 1]])
+                for m in range(0, CHUNK, 2)
+            ]
+            power = bdot(target_table[unit[0]], jnp.concatenate(sources, axis=1), NN)
             buffer[place] = jnp.exp2(power).astype(jnp.bfloat16)
 
     def products(units, buffer):
         for place, unit in enumerate(units):
-            acc[unit[0]] += bdot(pairs_of(unit, coef_table, lane_x), buffer[place], NT)
+            coefs = jnp.concatenate([coef_table[i] for i in partners(unit)], axis=0)
+            acc[unit[0]] += bdot(buffer[place], coefs, NN)
 
     def following(unit):
         target, turn = unit
@@ -237,11 +238,10 @@
     tables, acc = scratch[:3], scratch[-1]
     build_tables(recv_ref, coef_ref, rows_ref, *tables)
     sweep(index_ref, turns_ref, *scratch)
-    low = lax.broadcasted_iota(jnp.int32, (coef_ref.shape[0], LANES), 1) < 64
 
     def one_tile(index, carry):
-        pair = [jnp.concatenate([acc[2 * index + part]] * 2, axis=1) for part in range(2)]
-        out_ref[:, lane_tile(index)] = jnp.where(low, pair[0], pair[1])
+        pair = jnp.concatenate([acc[2 * index], acc[2 * index + 1]], axis=0)
+        out_ref[:, lane_tile(index)] = pair.T
         return carry
 
     lax.fori_loop(0, turns_ref.shape[0] // 2, one_tile, 0, unroll=4)
@@ -269,7 +269,7 @@
         gram = None
         for part in range(4):
             q = group * 4 + part
-            twice = jnp.concatenate([acc[q]] * 2, axis=1).astype(jnp.bfloat16)
+            twice = jnp.concatenate([acc[q]] * 2, axis=0).T.astype(jnp.bfloat16)
             matrix = transfer_ref[:, lane_tile(q)].astype(jnp.float32)
             low = lax.broadcasted_iota(jnp.int32, matrix.shape, 1) < 64
             matrix = jnp.concatenate(
@@ -290,12 +290,12 @@
 
 def sweep_scratch(total, clusters, px):
     return [
-        pltpu.VMEM((total + 1, px, LANES), jnp.bfloat16),
+        pltpu.VMEM((total + 1, 64, px), jnp.bfloat16),
         pltpu.VMEM((total + 1, 16, LANES), jnp.bfloat16),
         pltpu.VMEM((clusters, 64, 16), jnp.bfloat16),
         pltpu.VMEM((UNITS, 64, CHUNK * 64), jnp.bfloat16),
         pltpu.VMEM((UNITS, 64, CHUNK * 64), jnp.bfloat16),
-        pltpu.VMEM((clusters, px, 64), jnp.float32),
+        pltpu.VMEM((clusters, 64, px), jnp.float32),
     ]
 
 

time: 130 us -> 133 us (1.023)
  Pallas kernels: 66.6 us -> 68.6 us
  blocking collectives: 16 us -> 18 us
    all_to_all x1, blocking collectives: 16 us -> 18 us  [shards(): lax.all_to_all(blocks, ('leaf', 'probe'), split_axis=0, concat_axis=0, ti...]
where the time goes in v3:
time: 133 us
  Pallas kernels  68.6 us (52%)
  waiting for transfers between devices  20.9 us (16%)
  blocking collectives  18 us (14%)
  starting transfers between devices  17.1 us (13%)
  local copies, waits for them, and re-layouts  5.3 us (4%)
  other arithmetic  2.57 us (2%)
    pallas_call x1, Pallas kernels, shards(): pl.pallas_call(fine_kernel, out_shape=jax.ShapeDtypeStruct((px, points_fi...  35.7 us
    pallas_call x1, Pallas kernels, shards(): pl.pallas_call(coarse_kernel, out_shape=(jax.ShapeDtypeStruct((px, points...  25.5 us
    all_to_all x1, waiting for transfers between devices, shards(): lax.all_to_all(fine_send, 'leaf', split_axis=0, concat_axis=0, tiled=True)  20.9 us
    all_to_all x1, blocking collectives, shards(): lax.all_to_all(blocks, ('leaf', 'probe'), split_axis=0, concat_axis=0, ti...  18 us
    all_to_all x1, starting transfers between devices, shards(): lax.all_to_all(coarse_send, 'leaf', split_axis=0, concat_axis=0, tiled=True)  8.01 us
    all_to_all x1, starting transfers between devices, shards(): lax.all_to_all(fine_send, 'leaf', split_axis=0, concat_axis=0, tiled=True)  7.5 us
    pallas_call x1, Pallas kernels, shards(): pl.pallas_call(pack_coarse_kernel, out_shape=(jax.ShapeDtypeStruct((owner...  4.15 us
    pallas_call x1, Pallas kernels, shards(): pl.pallas_call(pack_fine_kernel, out_shape=(jax.ShapeDtypeStruct((owners,...  3.33 us
  transfers between devices with their start and end apart: 3, of which 1 were waited for; matrix products, arithmetic and copies ran while one was open for 3% of the time, Pallas kernels for 30%

profile of v3, /device:TPU:0, one launch (start us, length us, event | category | flops | bytes accessed | tf_op | source)
XLA Modules:
  0.0 133.3 jit_solution(4416082834651607852)
XLA Ops:
  0.6 3.3 %pack_fine.1 = (bf16[16,320,128]{2,1,0:T(8,128)(2,1)}, f32[8,4096]{1,0:T(8,128)}) custom-call(s32[16,16]{1,0:T(8,128)} %bitcast.6, bf16[32,4096]{1,0:T(8,128)(2,1)} %coef_ref.5, f32[3,4096]{1,0:T(4,128)} %points_ref.3), custom_call_target="tpu_custom_call" | custom-call | tf_op jit(solution)/shard_map/pack_fine/pallas_call | solution.py:343
  4.0 0.0 copy-start.1
  4.0 0.0 copy-start.6
  4.0 0.0 copy-start.5
  4.0 0.0 copy-start.8
  4.0 7.5 %all-to-all-start.1 = ((bf16[16,320,128]{2,1,0:T(8,128)(2,1)}), bf16[16,320,128]{2,1,0:T(8,128)(2,1)S(1)}, u32[]{:S(2)}, u32[]{:S(2)}) async-start(bf16[16,320,128]{2,1,0:T(8,128)(2,1)} %get-tuple-element.12), calls=%async_computation.1 | async-start | bytes 2621440 | tf_op jit(solution)/shard_map/all_to_all | solution.py:358
  11.5 0.0 copy-done.1
  11.5 0.0 copy-start.7
  11.5 0.0 copy-start.4
  11.5 0.0 copy-start.2
  11.5 1.6 %collective-permute-start = (bf16[32,4096]{1,0:T(8,128)(2,1)S(1)}, bf16[32,4096]{1,0:T(8,128)(2,1)S(1)}, u32[]{:S(2)}, u32[]{:S(2)}) collective-permute-start(bf16[32,4096]{1,0:T(8,128)(2,1)S(1)} %copy-done.1), channel_id=1, source_target_pairs={{0,1},{1,0},{2,3},{3,2},{4,5},{5,4},{6,7},{7,6},{8,9},{9,8},{10,11... | collective-permute-start | bytes 786440 | tf_op jit(solution)/shard_map/ppermute | solution.py:340
  13.1 0.0 copy-done.6
  13.1 0.7 copy.16.send_ref
  13.8 4.1 %pack_coarse.1 = (bf16[16,160,128]{2,1,0:T(8,128)(2,1)}, f32[8,2048]{1,0:T(8,128)}, bf16[32,2048]{1,0:T(8,128)(2,1)}) custom-call(s32[16,8]{1,0:T(8,128)} %copy.16.send_ref, bf16[32,4096]{1,0:T(8,128)(2,1)} %coef_ref.5, bf16[64,4096]{1,0:T(8,128)(2,1)} %transfer_ref.3, f32[3,2048]{1,0:T(4,128)} %points_ref.2), custom_call_target="tpu_custom_call" | custom-call | tf_op jit(solution)/shard_map/pack_coarse/pallas_call | solution.py:360
  18.0 0.0 copy-done.5
  18.0 0.0 copy-done.8
  18.0 0.1 fusion.1
  18.0 20.9 %all-to-all-done.1.recv_ref = bf16[16,320,128]{2,1,0:T(8,128)(2,1)S(1)} async-done(((bf16[16,320,128]{2,1,0:T(8,128)(2,1)}), bf16[16,320,128]{2,1,0:T(8,128)(2,1)S(1)}, u32[]{:S(2)}, u32[]{:S(2)}) %all-to-all-start.1) | async-done | bytes 1310752 | tf_op jit(solution)/shard_map/all_to_all | solution.py:358
  38.9 0.0 copy-start
  38.9 8.0 %all-to-all-start = ((bf16[16,160,128]{2,1,0:T(8,128)(2,1)}), bf16[16,160,128]{2,1,0:T(8,128)(2,1)S(1)}, u32[]{:S(2)}, u32[]{:S(2)}) async-start(bf16[16,160,128]{2,1,0:T(8,128)(2,1)} %get-tuple-element.9), calls=%async_computation | async-start | bytes 1310720 | tf_op jit(solution)/shard_map/all_to_all | solution.py:376
  46.9 0.0 copy-done.7
  46.9 0.6 and_select_fusion.1.turns_ref
  47.5 0.0 copy-done.4
  47.5 0.1 fusion
  47.6 0.6 pad.9.index_ref
  48.2 0.6 pad.8.index_ref
  48.8 0.6 and_select_fusion.2.turns_ref
  49.4 0.0 collective-permute-done
  49.4 0.0 copy-done.2
  49.4 0.8 pad_maximum_fusion.probes_ref
  50.3 0.0 copy-done
  50.3 35.7 %fine_sweep.1.fine_ref = f32[32,4096]{1,0:T(8,128)} custom-call(s32[64,72]{1,0:T(8,128)} %pad.9.index_ref, s32[64]{0:T(128)} %and_select_fusion.1.turns_ref, bf16[16,320,128]{2,1,0:T(8,128)(2,1)} %copy-done, bf16[32,4096]{1,0:T(8,128)(2,1)} %coef_ref.5, f32[8,4096]{1,0:T(8,128)} %get-tuple-element.13.rows_ref), custom_call_target="tpu_custom_call" | custom-call | tf_op jit(solution)/shard_map/fine_sweep/pallas_call | solution.py:383
  86.0 0.0 all-to-all-done.recv_ref
  86.0 0.0 copy-start.3
  86.0 0.8 copy-done.3
  86.8 25.5 %coarse_sweep.1 = (f32[32,4096]{1,0:T(8,128)}, f32[64,32]{1,0:T(8,128)}) custom-call(s32[32,72]{1,0:T(8,128)} %pad.8.index_ref, s32[32]{0:T(128)} %and_select_fusion.2.turns_ref, bf16[16,160,128]{2,1,0:T(8,128)(2,1)} %copy-done.3, bf16[32,2048]{1,0:T(8,128)(2,1)} %get-tuple-element.10.coef_ref, f32[8,2048]{1,0:T(8,128)} %get-tuple-element.11.rows_ref, ...), custom_call_target="tpu_custom_call" | custom-call | tf_op jit(solution)/shard_map/coarse_sweep/pallas_call | solution.py:393
  112.3 0.8 reshape.76
  113.1 0.6 gather_fusion
  113.8 0.2 reshape.77
  114.0 18.0 %all_to_all.15 = f32[32,1,1024]{2,1,0:T(1,128)S(1)} all-to-all(f32[32,1,1024]{2,1,0:T(1,128)S(1)} %reshape.77), channel_id=1, replica_groups=mesh['leaf'=16,'probe'=2] {'leaf','probe'}, dimensions={0} | all-to-all | bytes 262144 | tf_op jit(solution)/shard_map/all_to_all | solution.py:411
  132.0 0.3 reduce
  132.3 0.2 reshape.78
  132.5 0.1 reduce_sum.9
  132.6 0.7 mul.15
  (5 shorter events, 0.1 us)
Async XLA Ops:
  4.0 7.5 %copy-start.1 = (bf16[32,4096]{1,0:T(8,128)(2,1)S(1)}, bf16[32,4096]{1,0:T(8,128)(2,1)}, u32[]{:S(2)}) copy-start(bf16[32,4096]{1,0:T(8,128)(2,1)} %coef_ref.5) | copy-start | bytes 786436
  4.0 9.2 %copy-start.6 = (s32[1,16,8]{1,2,0:T(8,128)S(1)}, s32[1,16,8]{1,2,0:T(8,128)}, u32[]{:S(2)}) copy-start(s32[1,16,8]{1,2,0:T(8,128)} %param.17) | copy-start | bytes 1540
  4.0 14.0 %copy-start.5 = (s32[32,64]{1,0:T(8,128)S(1)}, s32[32,64]{1,0:T(8,128)}, u32[]{:S(2)}) copy-start(s32[32,64]{1,0:T(8,128)} %param.18) | copy-start | bytes 24580
  4.0 14.0 %copy-start.8 = (s32[32]{0:T(128)S(1)}, s32[32]{0:T(128)}, u32[]{:S(2)}) copy-start(s32[32]{0:T(128)} %param.19) | copy-start | bytes 388
  4.0 34.9 %all-to-all-start.1 = ((bf16[16,320,128]{2,1,0:T(8,128)(2,1)}), bf16[16,320,128]{2,1,0:T(8,128)(2,1)S(1)}, u32[]{:S(2)}, u32[]{:S(2)}) async-start(bf16[16,320,128]{2,1,0:T(8,128)(2,1)} %get-tuple-element.12), calls=%async_computation.1 | async-start | bytes 2621440 | tf_op jit(solution)/shard_map/all_to_all | solution.py:358
  11.5 35.4 %copy-start.7 = (s32[64]{0:T(128)S(1)}, s32[64]{0:T(128)}, u32[]{:S(2)}) copy-start(s32[64]{0:T(128)} %param.16) | copy-start | bytes 772
  11.5 36.0 %copy-start.4 = (s32[64,64]{1,0:T(8,128)S(1)}, s32[64,64]{1,0:T(8,128)}, u32[]{:S(2)}) copy-start(s32[64,64]{1,0:T(8,128)} %param.15) | copy-start | bytes 49156
  11.5 37.9 %copy-start.2 = (bf16[32,4096]{1,0:T(8,128)(2,1)S(1)}, bf16[32,4096]{1,0:T(8,128)(2,1)}, u32[]{:S(2)}) copy-start(bf16[32,4096]{1,0:T(8,128)(2,1)} %coef_ref.5) | copy-start | bytes 786436
  11.5 37.9 %collective-permute-start = (bf16[32,4096]{1,0:T(8,128)(2,1)S(1)}, bf16[32,4096]{1,0:T(8,128)(2,1)S(1)}, u32[]{:S(2)}, u32[]{:S(2)}) collective-permute-start(bf16[32,4096]{1,0:T(8,128)(2,1)S(1)} %copy-done.1), channel_id=1, source_target_pairs={{0,1},{1,0},{2,3},{3,2},{4,5},{5,4},{6,7},{7,6},{8,9},{9,8},{10,11... | collective-permute-start | bytes 786440 | tf_op jit(solution)/shard_map/ppermute | solution.py:340
  38.9 11.4 %copy-start = (bf16[16,320,128]{2,1,0:T(8,128)(2,1)}, bf16[16,320,128]{2,1,0:T(8,128)(2,1)S(1)}, u32[]{:S(2)}) copy-start(bf16[16,320,128]{2,1,0:T(8,128)(2,1)S(1)} %all-to-all-done.1.recv_ref) | copy-start | bytes 3932164
  38.9 47.1 %all-to-all-start = ((bf16[16,160,128]{2,1,0:T(8,128)(2,1)}), bf16[16,160,128]{2,1,0:T(8,128)(2,1)S(1)}, u32[]{:S(2)}, u32[]{:S(2)}) async-start(bf16[16,160,128]{2,1,0:T(8,128)(2,1)} %get-tuple-element.9), calls=%async_computation | async-start | bytes 1310720 | tf_op jit(solution)/shard_map/all_to_all | solution.py:376
  86.0 0.8 copy-start.3

commit v4 on v2

--- a/solution.py
+++ b/solution.py
@@ -11,7 +11,8 @@
 KERNEL_RATE = 1.5
 POINT_SCALE = math.sqrt(2.0 * KERNEL_RATE * math.log2(math.e))
 LANES = 128
-UNITS = 4
+UNITS = 8
+QUAD = 4
 CHUNK = 8
 FAR_AWAY = -30000.0
 VMEM = 56 * 1024 * 1024
@@ -150,7 +151,7 @@
         rows = rows_ref[:, lane_tile(index)]
         put(2 * index, coef_ref[:, lane_tile(index)], rows)
         features = target_features(rows).astype(jnp.bfloat16)
-        turned = bdot(unit, jnp.concatenate([features] * 8, axis=0), NT)[:, :16]
+        turned = bdot(unit, jnp.concatenate([features] * 8, axis=0), NT)[:, :16 * QUAD]
         target_table[2 * index] = turned[:64].astype(jnp.bfloat16)
         target_table[2 * index + 1] = turned[64:].astype(jnp.bfloat16)
         return carry
@@ -184,6 +185,8 @@
     slots_end = index_ref.shape[1] // CHUNK - 1
     lane = lax.broadcasted_iota(jnp.int32, (16, LANES), 1) < 64
     lane_x = lax.broadcasted_iota(jnp.int32, (px, LANES), 1) < 64
+    owner = lax.broadcasted_iota(jnp.int32, (64, 16 * QUAD), 1) // 16
+    blank = jnp.zeros((64, 16 * QUAD), jnp.bfloat16)
     acc[...] = jnp.zeros_like(acc)
 
     def pairs_of(unit, table, low):
@@ -194,13 +197,26 @@
         )
 
     def tiles(units, buffer):
-        for place, unit in enumerate(units):
-            power = bdot(target_table[unit[0]], pairs_of(unit, feature_table, lane), NN)
-            buffer[place] = jnp.exp2(power).astype(jnp.bfloat16)
+        for start in range(0, UNITS, QUAD):
+            quad = units[start:start + QUAD]
+            targets = jnp.concatenate(
+                [jnp.where(owner == u, target_table[quad[u][0]], blank) for u in range(QUAD)], axis=0
+            )
+            sources = jnp.concatenate([pairs_of(unit, feature_table, lane) for unit in quad], axis=0)
+            for part in range(0, CHUNK * 64, 256):
+                power = bdot(targets, sources[:, part:part + 256], NN)
+                buffer[start * 64:(start + QUAD) * 64, part:part + 256] = jnp.exp2(power).astype(
+                    jnp.bfloat16
+                )
 
     def products(units, buffer):
-        for place, unit in enumerate(units):
-            acc[unit[0]] += bdot(pairs_of(unit, coef_table, lane_x), buffer[place], NT)
+        for start in range(0, UNITS, QUAD):
+            quad = units[start:start + QUAD]
+            coefs = jnp.concatenate([pairs_of(unit, coef_table, lane_x) for unit in quad], axis=0)
+            product = bdot(coefs, buffer[start * 64:(start + QUAD) * 64], NT)
+            for u in range(QUAD):
+                side = (u // 2) * LANES
+                acc[u % 2, quad[u][0]] += product[u * px:(u + 1) * px, side:side + LANES]
 
     def following(unit):
         target, turn = unit
@@ -233,6 +249,12 @@
     lax.fori_loop(0, (total + 2 * UNITS - 1) // (2 * UNITS), two_sets, start)
 
 
+def summed(acc, target):
+    low = lax.broadcasted_iota(jnp.int32, acc.shape[2:], 1) < 64
+    here = jnp.where(low, acc[0, target], acc[1, target])
+    return here + pltpu.roll(here, 64, 1)
+
+
 def fine_kernel(index_ref, turns_ref, recv_ref, coef_ref, rows_ref, out_ref, *scratch):
     tables, acc = scratch[:3], scratch[-1]
     build_tables(recv_ref, coef_ref, rows_ref, *tables)
@@ -240,8 +262,7 @@
     low = lax.broadcasted_iota(jnp.int32, (coef_ref.shape[0], LANES), 1) < 64
 
     def one_tile(index, carry):
-        pair = [jnp.concatenate([acc[2 * index + part]] * 2, axis=1) for part in range(2)]
-        out_ref[:, lane_tile(index)] = jnp.where(low, pair[0], pair[1])
+        out_ref[:, lane_tile(index)] = jnp.where(low, summed(acc, 2 * index), summed(acc, 2 * index + 1))
         return carry
 
     lax.fori_loop(0, turns_ref.shape[0] // 2, one_tile, 0, unroll=4)
@@ -269,7 +290,7 @@
         gram = None
         for part in range(4):
             q = group * 4 + part
-            twice = jnp.concatenate([acc[q]] * 2, axis=1).astype(jnp.bfloat16)
+            twice = summed(acc, q).astype(jnp.bfloat16)
             matrix = transfer_ref[:, lane_tile(q)].astype(jnp.float32)
             low = lax.broadcasted_iota(jnp.int32, matrix.shape, 1) < 64
             matrix = jnp.concatenate(
@@ -292,10 +313,10 @@
     return [
         pltpu.VMEM((total + 1, px, LANES), jnp.bfloat16),
         pltpu.VMEM((total + 1, 16, LANES), jnp.bfloat16),
-        pltpu.VMEM((clusters, 64, 16), jnp.bfloat16),
-        pltpu.VMEM((UNITS, 64, CHUNK * 64), jnp.bfloat16),
-        pltpu.VMEM((UNITS, 64, CHUNK * 64), jnp.bfloat16),
-        pltpu.VMEM((clusters, px, 64), jnp.float32),
+        pltpu.VMEM((clusters, 64, 16 * QUAD), jnp.bfloat16),
+        pltpu.VMEM((UNITS * 64, CHUNK * 64), jnp.bfloat16),
+        pltpu.VMEM((UNITS * 64, CHUNK * 64), jnp.bfloat16),
+        pltpu.VMEM((2, clusters, px, LANES), jnp.float32),
     ]
 
 

time: 130 us -> 127 us (0.977)
  blocking collectives: 16 us -> 11.3 us
  Pallas kernels: 66.6 us -> 68.7 us
    all_to_all x1, blocking collectives: 16 us -> 11.3 us  [shards(): lax.all_to_all(blocks, ('leaf', 'probe'), split_axis=0, concat_axis=0, ti...]
    pallas_call x1, Pallas kernels: 34.6 us -> 37.2 us  [shards(): pl.pallas_call(fine_kernel, out_shape=jax.ShapeDtypeStruct((px, points_fi...]
  transfers between devices with their start and end apart: 3 -> 3, of which waited for: 1 -> 1; matrix products, arithmetic and copies ran while one was open for 3% -> 3% of each run, Pallas kernels for 30% -> 33%
where the time goes in v4:
time: 127 us
  Pallas kernels  68.7 us (54%)
  waiting for transfers between devices  20.9 us (16%)
  starting transfers between devices  17.1 us (13%)
  blocking collectives  11.3 us (9%)
  local copies, waits for them, and re-layouts  5.3 us (4%)
  other arithmetic  2.57 us (2%)
    pallas_call x1, Pallas kernels, shards(): pl.pallas_call(fine_kernel, out_shape=jax.ShapeDtypeStruct((px, points_fi...  37.2 us
    pallas_call x1, Pallas kernels, shards(): pl.pallas_call(coarse_kernel, out_shape=(jax.ShapeDtypeStruct((px, points...  24 us
    all_to_all x1, waiting for transfers between devices, shards(): lax.all_to_all(fine_send, 'leaf', split_axis=0, concat_axis=0, tiled=True)  20.9 us
    all_to_all x1, blocking collectives, shards(): lax.all_to_all(blocks, ('leaf', 'probe'), split_axis=0, concat_axis=0, ti...  11.3 us
    all_to_all x1, starting transfers between devices, shards(): lax.all_to_all(coarse_send, 'leaf', split_axis=0, concat_axis=0, tiled=True)  8.01 us
    all_to_all x1, starting transfers between devices, shards(): lax.all_to_all(fine_send, 'leaf', split_axis=0, concat_axis=0, tiled=True)  7.5 us
    pallas_call x1, Pallas kernels, shards(): pl.pallas_call(pack_coarse_kernel, out_shape=(jax.ShapeDtypeStruct((owner...  4.15 us
    pallas_call x1, Pallas kernels, shards(): pl.pallas_call(pack_fine_kernel, out_shape=(jax.ShapeDtypeStruct((owners,...  3.33 us
  transfers between devices with their start and end apart: 3, of which 1 were waited for; matrix products, arithmetic and copies ran while one was open for 3% of the time, Pallas kernels for 33%

profile of v4, /device:TPU:0, one launch (start us, length us, event | category | flops | bytes accessed | tf_op | source)
XLA Modules:
  0.0 126.6 jit_solution(2423463646350493377)
XLA Ops:
  0.6 3.3 %pack_fine.1 = (bf16[16,320,128]{2,1,0:T(8,128)(2,1)}, f32[8,4096]{1,0:T(8,128)}) custom-call(s32[16,16]{1,0:T(8,128)} %bitcast.6, bf16[32,4096]{1,0:T(8,128)(2,1)} %coef_ref.5, f32[3,4096]{1,0:T(4,128)} %points_ref.3), custom_call_target="tpu_custom_call" | custom-call | tf_op jit(solution)/shard_map/pack_fine/pallas_call | solution.py:364
  4.0 0.0 copy-start.1
  4.0 0.0 copy-start.6
  4.0 0.0 copy-start.5
  4.0 0.0 copy-start.8
  4.0 7.5 %all-to-all-start.1 = ((bf16[16,320,128]{2,1,0:T(8,128)(2,1)}), bf16[16,320,128]{2,1,0:T(8,128)(2,1)S(1)}, u32[]{:S(2)}, u32[]{:S(2)}) async-start(bf16[16,320,128]{2,1,0:T(8,128)(2,1)} %get-tuple-element.12), calls=%async_computation.1 | async-start | bytes 2621440 | tf_op jit(solution)/shard_map/all_to_all | solution.py:379
  11.5 0.0 copy-done.1
  11.5 0.0 copy-start.7
  11.5 0.0 copy-start.4
  11.5 0.0 copy-start.2
  11.5 1.6 %collective-permute-start = (bf16[32,4096]{1,0:T(8,128)(2,1)S(1)}, bf16[32,4096]{1,0:T(8,128)(2,1)S(1)}, u32[]{:S(2)}, u32[]{:S(2)}) collective-permute-start(bf16[32,4096]{1,0:T(8,128)(2,1)S(1)} %copy-done.1), channel_id=1, source_target_pairs={{0,1},{1,0},{2,3},{3,2},{4,5},{5,4},{6,7},{7,6},{8,9},{9,8},{10,11... | collective-permute-start | bytes 786440 | tf_op jit(solution)/shard_map/ppermute | solution.py:361
  13.1 0.0 copy-done.6
  13.1 0.7 copy.16.send_ref
  13.8 4.1 %pack_coarse.1 = (bf16[16,160,128]{2,1,0:T(8,128)(2,1)}, f32[8,2048]{1,0:T(8,128)}, bf16[32,2048]{1,0:T(8,128)(2,1)}) custom-call(s32[16,8]{1,0:T(8,128)} %copy.16.send_ref, bf16[32,4096]{1,0:T(8,128)(2,1)} %coef_ref.5, bf16[64,4096]{1,0:T(8,128)(2,1)} %transfer_ref.3, f32[3,2048]{1,0:T(4,128)} %points_ref.2), custom_call_target="tpu_custom_call" | custom-call | tf_op jit(solution)/shard_map/pack_coarse/pallas_call | solution.py:381
  18.0 0.0 copy-done.5
  18.0 0.0 copy-done.8
  18.0 0.1 fusion.1
  18.0 20.9 %all-to-all-done.1.recv_ref = bf16[16,320,128]{2,1,0:T(8,128)(2,1)S(1)} async-done(((bf16[16,320,128]{2,1,0:T(8,128)(2,1)}), bf16[16,320,128]{2,1,0:T(8,128)(2,1)S(1)}, u32[]{:S(2)}, u32[]{:S(2)}) %all-to-all-start.1) | async-done | bytes 1310752 | tf_op jit(solution)/shard_map/all_to_all | solution.py:379
  38.9 0.0 copy-start
  38.9 8.0 %all-to-all-start = ((bf16[16,160,128]{2,1,0:T(8,128)(2,1)}), bf16[16,160,128]{2,1,0:T(8,128)(2,1)S(1)}, u32[]{:S(2)}, u32[]{:S(2)}) async-start(bf16[16,160,128]{2,1,0:T(8,128)(2,1)} %get-tuple-element.9), calls=%async_computation | async-start | bytes 1310720 | tf_op jit(solution)/shard_map/all_to_all | solution.py:397
  46.9 0.0 copy-done.7
  46.9 0.6 and_select_fusion.1.turns_ref
  47.5 0.0 copy-done.4
  47.5 0.1 fusion
  47.6 0.6 pad.9.index_ref
  48.2 0.6 pad.8.index_ref
  48.8 0.6 and_select_fusion.2.turns_ref
  49.4 0.0 collective-permute-done
  49.4 0.0 copy-done.2
  49.4 0.8 pad_maximum_fusion.probes_ref
  50.3 0.0 copy-done
  50.3 37.2 %fine_sweep.1.fine_ref = f32[32,4096]{1,0:T(8,128)} custom-call(s32[64,72]{1,0:T(8,128)} %pad.9.index_ref, s32[64]{0:T(128)} %and_select_fusion.1.turns_ref, bf16[16,320,128]{2,1,0:T(8,128)(2,1)} %copy-done, bf16[32,4096]{1,0:T(8,128)(2,1)} %coef_ref.5, f32[8,4096]{1,0:T(8,128)} %get-tuple-element.13.rows_ref), custom_call_target="tpu_custom_call" | custom-call | tf_op jit(solution)/shard_map/fine_sweep/pallas_call | solution.py:404
  87.5 0.0 all-to-all-done.recv_ref
  87.5 0.0 copy-start.3
  87.5 0.8 copy-done.3
  88.3 24.0 %coarse_sweep.1 = (f32[32,4096]{1,0:T(8,128)}, f32[64,32]{1,0:T(8,128)}) custom-call(s32[32,72]{1,0:T(8,128)} %pad.8.index_ref, s32[32]{0:T(128)} %and_select_fusion.2.turns_ref, bf16[16,160,128]{2,1,0:T(8,128)(2,1)} %copy-done.3, bf16[32,2048]{1,0:T(8,128)(2,1)} %get-tuple-element.10.coef_ref, f32[8,2048]{1,0:T(8,128)} %get-tuple-element.11.rows_ref, ...), custom_call_target="tpu_custom_call" | custom-call | tf_op jit(solution)/shard_map/coarse_sweep/pallas_call | solution.py:414
  112.3 0.8 reshape.76
  113.2 0.6 gather_fusion
  113.8 0.2 reshape.77
  114.0 11.3 %all_to_all.15 = f32[32,1,1024]{2,1,0:T(1,128)S(1)} all-to-all(f32[32,1,1024]{2,1,0:T(1,128)S(1)} %reshape.77), channel_id=1, replica_groups=mesh['leaf'=16,'probe'=2] {'leaf','probe'}, dimensions={0} | all-to-all | bytes 262144 | tf_op jit(solution)/shard_map/all_to_all | solution.py:432
  125.3 0.3 reduce
  125.6 0.2 reshape.78
  125.8 0.1 reduce_sum.9
  125.9 0.7 mul.15
  (5 shorter events, 0.1 us)
Async XLA Ops:
  4.0 7.5 %copy-start.1 = (bf16[32,4096]{1,0:T(8,128)(2,1)S(1)}, bf16[32,4096]{1,0:T(8,128)(2,1)}, u32[]{:S(2)}) copy-start(bf16[32,4096]{1,0:T(8,128)(2,1)} %coef_ref.5) | copy-start | bytes 786436
  4.0 9.2 %copy-start.6 = (s32[1,16,8]{1,2,0:T(8,128)S(1)}, s32[1,16,8]{1,2,0:T(8,128)}, u32[]{:S(2)}) copy-start(s32[1,16,8]{1,2,0:T(8,128)} %param.17) | copy-start | bytes 1540
  4.0 14.0 %copy-start.5 = (s32[32,64]{1,0:T(8,128)S(1)}, s32[32,64]{1,0:T(8,128)}, u32[]{:S(2)}) copy-start(s32[32,64]{1,0:T(8,128)} %param.18) | copy-start | bytes 24580
  4.0 14.0 %copy-start.8 = (s32[32]{0:T(128)S(1)}, s32[32]{0:T(128)}, u32[]{:S(2)}) copy-start(s32[32]{0:T(128)} %param.19) | copy-start | bytes 388
  4.0 34.9 %all-to-all-start.1 = ((bf16[16,320,128]{2,1,0:T(8,128)(2,1)}), bf16[16,320,128]{2,1,0:T(8,128)(2,1)S(1)}, u32[]{:S(2)}, u32[]{:S(2)}) async-start(bf16[16,320,128]{2,1,0:T(8,128)(2,1)} %get-tuple-element.12), calls=%async_computation.1 | async-start | bytes 2621440 | tf_op jit(solution)/shard_map/all_to_all | solution.py:379
  11.5 35.4 %copy-start.7 = (s32[64]{0:T(128)S(1)}, s32[64]{0:T(128)}, u32[]{:S(2)}) copy-start(s32[64]{0:T(128)} %param.16) | copy-start | bytes 772
  11.5 36.0 %copy-start.4 = (s32[64,64]{1,0:T(8,128)S(1)}, s32[64,64]{1,0:T(8,128)}, u32[]{:S(2)}) copy-start(s32[64,64]{1,0:T(8,128)} %param.15) | copy-start | bytes 49156
  11.5 37.9 %copy-start.2 = (bf16[32,4096]{1,0:T(8,128)(2,1)S(1)}, bf16[32,4096]{1,0:T(8,128)(2,1)}, u32[]{:S(2)}) copy-start(bf16[32,4096]{1,0:T(8,128)(2,1)} %coef_ref.5) | copy-start | bytes 786436
  11.5 37.9 %collective-permute-start = (bf16[32,4096]{1,0:T(8,128)(2,1)S(1)}, bf16[32,4096]{1,0:T(8,128)(2,1)S(1)}, u32[]{:S(2)}, u32[]{:S(2)}) collective-permute-start(bf16[32,4096]{1,0:T(8,128)(2,1)S(1)} %copy-done.1), channel_id=1, source_target_pairs={{0,1},{1,0},{2,3},{3,2},{4,5},{5,4},{6,7},{7,6},{8,9},{9,8},{10,11... | collective-permute-start | bytes 786440 | tf_op jit(solution)/shard_map/ppermute | solution.py:361
  38.9 11.4 %copy-start = (bf16[16,320,128]{2,1,0:T(8,128)(2,1)}, bf16[16,320,128]{2,1,0:T(8,128)(2,1)S(1)}, u32[]{:S(2)}) copy-start(bf16[16,320,128]{2,1,0:T(8,128)(2,1)S(1)} %all-to-all-done.1.recv_ref) | copy-start | bytes 3932164
  38.9 48.6 %all-to-all-start = ((bf16[16,160,128]{2,1,0:T(8,128)(2,1)}), bf16[16,160,128]{2,1,0:T(8,128)(2,1)S(1)}, u32[]{:S(2)}, u32[]{:S(2)}) async-start(bf16[16,160,128]{2,1,0:T(8,128)(2,1)} %get-tuple-element.9), calls=%async_computation | async-start | bytes 1310720 | tf_op jit(solution)/shard_map/all_to_all | solution.py:397
  87.5 0.8 copy-start.3

commit v5 on v4

--- a/solution.py
+++ b/solution.py
@@ -129,34 +129,38 @@
     pack_send(send_ref, out_ref, dup_coef, dup_rows, owners, capacity, px)
 
 
-def build_tables(recv_ref, coef_ref, rows_ref, coef_table, feature_table, target_table):
+def put_pair(entry, coef, rows, coef_table, feature_table):
+    a, b = halves(coef.astype(jnp.float32))
+    coef_table[entry] = a.astype(jnp.bfloat16)
+    coef_table[entry + 1] = b.astype(jnp.bfloat16)
+    a, b = halves(source_features(rows))
+    feature_table[entry] = a.astype(jnp.bfloat16)
+    feature_table[entry + 1] = b.astype(jnp.bfloat16)
+
+
+def put_nothing(entry, coef_table, feature_table):
+    coef_table[entry] = jnp.zeros(coef_table.shape[1:], jnp.bfloat16)
+    place = lax.broadcasted_iota(jnp.int32, (8, LANES), 0)
+    nothing = source_features(jnp.where(place == 3, FAR_AWAY, 0.0))
+    feature_table[entry] = nothing.astype(jnp.bfloat16)
+
+
+def build_own(coef_ref, rows_ref, coef_table, feature_table):
+    tiles = coef_ref.shape[1] // LANES
+
+    def one_tile(index, carry):
+        tile = lane_tile(index)
+        put_pair(2 * index, coef_ref[:, tile], rows_ref[:, tile], coef_table, feature_table)
+        return carry
+
+    lax.fori_loop(0, tiles, one_tile, 0, unroll=4)
+    put_nothing(2 * tiles, coef_table, feature_table)
+
+
+def build_received(recv_ref, coef_table, feature_table):
     owners, recv_rows, _ = recv_ref.shape
-    px = coef_ref.shape[0]
+    px = coef_table.shape[1]
     pairs = recv_rows // (px + 8)
-    own_tiles = coef_ref.shape[1] // LANES
-    own = 2 * own_tiles
-    row = lax.broadcasted_iota(jnp.int32, (LANES, LANES), 0)
-    column = lax.broadcasted_iota(jnp.int32, (LANES, LANES), 1)
-    unit = jnp.where(row == column, 1.0, 0.0).astype(jnp.bfloat16)
-
-    def put(entry, coef, rows):
-        a, b = halves(coef.astype(jnp.float32))
-        coef_table[entry] = a.astype(jnp.bfloat16)
-        coef_table[entry + 1] = b.astype(jnp.bfloat16)
-        a, b = halves(source_features(rows))
-        feature_table[entry] = a.astype(jnp.bfloat16)
-        feature_table[entry + 1] = b.astype(jnp.bfloat16)
-
-    def one_own(index, carry):
-        rows = rows_ref[:, lane_tile(index)]
-        put(2 * index, coef_ref[:, lane_tile(index)], rows)
-        features = target_features(rows).astype(jnp.bfloat16)
-        turned = bdot(unit, jnp.concatenate([features] * 8, axis=0), NT)[:, :16 * QUAD]
-        target_table[2 * index] = turned[:64].astype(jnp.bfloat16)
-        target_table[2 * index + 1] = turned[64:].astype(jnp.bfloat16)
-        return carry
-
-    lax.fori_loop(0, own_tiles, one_own, 0, unroll=4)
 
     def one_owner(owner, carry):
         for pair in range(0, pairs, 2):
@@ -164,19 +168,32 @@
             both = recv_ref[owner, start:start + 16, :].astype(jnp.float32)
             for part in range(2):
                 where = pair + part
-                put(
-                    own + owner * (2 * pairs) + 2 * where,
+                put_pair(
+                    owner * (2 * pairs) + 2 * where,
                     recv_ref[owner, where * px:(where + 1) * px, :],
                     both[8 * part:8 * part + 8],
+                    coef_table,
+                    feature_table,
                 )
         return carry
 
     lax.fori_loop(0, owners, one_owner, 0)
-    last = own + owners * pairs * 2
-    coef_table[last] = jnp.zeros((px, LANES), jnp.bfloat16)
-    place = lax.broadcasted_iota(jnp.int32, (8, LANES), 0)
-    nothing = source_features(jnp.where(place == 3, FAR_AWAY, 0.0))
-    feature_table[last] = nothing.astype(jnp.bfloat16)
+    put_nothing(owners * pairs * 2, coef_table, feature_table)
+
+
+def build_targets(rows_ref, target_table):
+    row = lax.broadcasted_iota(jnp.int32, (LANES, LANES), 0)
+    column = lax.broadcasted_iota(jnp.int32, (LANES, LANES), 1)
+    unit = jnp.where(row == column, 1.0, 0.0).astype(jnp.bfloat16)
+
+    def one_tile(index, carry):
+        features = target_features(rows_ref[:, lane_tile(index)]).astype(jnp.bfloat16)
+        turned = bdot(unit, jnp.concatenate([features] * 8, axis=0), NT)[:, :16 * QUAD]
+        target_table[2 * index] = turned[:64].astype(jnp.bfloat16)
+        target_table[2 * index + 1] = turned[64:].astype(jnp.bfloat16)
+        return carry
+
+    lax.fori_loop(0, rows_ref.shape[1] // LANES, one_tile, 0, unroll=4)
 
 
 def sweep(index_ref, turns_ref, coef_table, feature_table, target_table, first_buffer, second_buffer, acc):
@@ -255,25 +272,55 @@
     return here + pltpu.roll(here, 64, 1)
 
 
-def fine_kernel(index_ref, turns_ref, recv_ref, coef_ref, rows_ref, out_ref, *scratch):
-    tables, acc = scratch[:3], scratch[-1]
-    build_tables(recv_ref, coef_ref, rows_ref, *tables)
+def put_sums(acc, clusters, out_ref, before_ref=None):
+    low = lax.broadcasted_iota(jnp.int32, acc.shape[2:], 1) < 64
+
+    def one_tile(index, carry):
+        tile = lane_tile(index)
+        sums = jnp.where(low, summed(acc, 2 * index), summed(acc, 2 * index + 1))
+        out_ref[:, tile] = sums if before_ref is None else before_ref[:, tile] + sums
+        return carry
+
+    lax.fori_loop(0, clusters // 2, one_tile, 0, unroll=4)
+
+
+def own_kernel(
+    fine_index_ref,
+    fine_turns_ref,
+    coarse_index_ref,
+    coarse_turns_ref,
+    fine_coef_ref,
+    fine_rows_ref,
+    coarse_coef_ref,
+    coarse_rows_ref,
+    fine_out_ref,
+    coarse_out_ref,
+    *scratch,
+):
+    acc = scratch[-1]
+    for index_ref, turns_ref, coef_ref, rows_ref, out_ref in (
+        (fine_index_ref, fine_turns_ref, fine_coef_ref, fine_rows_ref, fine_out_ref),
+        (coarse_index_ref, coarse_turns_ref, coarse_coef_ref, coarse_rows_ref, coarse_out_ref),
+    ):
+        build_own(coef_ref, rows_ref, *scratch[:2])
+        build_targets(rows_ref, scratch[2])
+        sweep(index_ref, turns_ref, *scratch)
+        put_sums(acc, turns_ref.shape[0], out_ref)
+
+
+def fine_kernel(index_ref, turns_ref, recv_ref, rows_ref, own_ref, out_ref, *scratch):
+    build_received(recv_ref, *scratch[:2])
+    build_targets(rows_ref, scratch[2])
     sweep(index_ref, turns_ref, *scratch)
-    low = lax.broadcasted_iota(jnp.int32, (coef_ref.shape[0], LANES), 1) < 64
-
-    def one_tile(index, carry):
-        out_ref[:, lane_tile(index)] = jnp.where(low, summed(acc, 2 * index), summed(acc, 2 * index + 1))
-        return carry
-
-    lax.fori_loop(0, turns_ref.shape[0] // 2, one_tile, 0, unroll=4)
+    put_sums(scratch[-1], turns_ref.shape[0], out_ref, own_ref)
 
 
 def coarse_kernel(
     index_ref,
     turns_ref,
     recv_ref,
-    coef_ref,
     rows_ref,
+    own_ref,
     fine_ref,
     transfer_ref,
     probes_ref,
@@ -281,8 +328,9 @@
     gram_ref,
     *scratch,
 ):
-    tables, acc = scratch[:3], scratch[-1]
-    build_tables(recv_ref, coef_ref, rows_ref, *tables)
+    acc = scratch[-1]
+    build_received(recv_ref, *scratch[:2])
+    build_targets(rows_ref, scratch[2])
     sweep(index_ref, turns_ref, *scratch)
     gram_ref[...] = jnp.zeros_like(gram_ref)
 
@@ -290,7 +338,8 @@
         gram = None
         for part in range(4):
             q = group * 4 + part
-            twice = summed(acc, q).astype(jnp.bfloat16)
+            own = halves(own_ref[:, lane_tile(group * 2 + part // 2)])[part % 2]
+            twice = (summed(acc, q) + own).astype(jnp.bfloat16)
             matrix = transfer_ref[:, lane_tile(q)].astype(jnp.float32)
             low = lax.broadcasted_iota(jnp.int32, matrix.shape, 1) < 64
             matrix = jnp.concatenate(
@@ -320,12 +369,23 @@
     ]
 
 
-def live_index(slots, counts, nothing):
-    place = lax.broadcasted_iota(jnp.int32, slots.shape, 1)
-    index = jnp.where(place < counts[:, None], slots, nothing)
-    index = jnp.pad(index, ((0, 0), (0, CHUNK)), constant_values=nothing)
-    turns = (counts + CHUNK - 1) // CHUNK
-    return index, turns
+def slot_list(slots, chosen, nothing):
+    width = slots.shape[1]
+    before = jnp.tril(jnp.ones((width, width), jnp.float32)).T
+    rank = jnp.dot(chosen.astype(jnp.float32), before).astype(jnp.int32) - 1
+    place = lax.broadcasted_iota(jnp.int32, (1, 1, width + CHUNK), 2)
+    moved = jnp.where(chosen, rank, -1)[:, :, None] == place
+    index = nothing + jnp.sum(jnp.where(moved, (slots - nothing)[:, :, None], 0), axis=1)
+    turns = (rank[:, -1] + CHUNK) // CHUNK
+    return index, jnp.maximum(turns, 1)
+
+
+def slot_lists(slots, counts, entries):
+    clusters, width = slots.shape
+    live = lax.broadcasted_iota(jnp.int32, slots.shape, 1) < counts[:, None]
+    own = slot_list(slots, live & (slots < clusters), clusters)
+    received = slot_list(slots - clusters, live & (slots >= clusters), entries)
+    return own, received
 
 
 def shards(
@@ -394,12 +454,28 @@
         compiler_params=params,
         name="pack_coarse",
     )(send_coarse, coef, transfer, points_coarse)
+    fine_total = owners * cap_fine
+    coarse_total = owners * cap_coarse
+    (fine_own, fine_own_turns), (fine_index, fine_turns) = slot_lists(slots_fine, counts_fine, fine_total)
+    (coarse_own, coarse_own_turns), (coarse_index, coarse_turns) = slot_lists(
+        slots_coarse, counts_coarse, coarse_total
+    )
+    fine_sums, coarse_sums = pl.pallas_call(
+        own_kernel,
+        out_shape=(
+            jax.ShapeDtypeStruct((px, points_fine.shape[1]), f32),
+            jax.ShapeDtypeStruct((px, points_coarse.shape[1]), f32),
+        ),
+        in_specs=[smem] * 4 + [vmem] * 4,
+        out_specs=[vmem, vmem],
+        scratch_shapes=sweep_scratch(fine_count, fine_count, px),
+        compiler_params=params,
+        cost_estimate=pl.CostEstimate(flops=10**10, bytes_accessed=10**7, transcendentals=10**7),
+        name="own_sweep",
+    )(fine_own, fine_own_turns, coarse_own, coarse_own_turns, coef, fine_rows, coarse_coef, coarse_rows)
+
+    coarse_send, coarse_sums = lax.optimization_barrier((coarse_send, coarse_sums))
     coarse_recv = lax.all_to_all(coarse_send, "leaf", split_axis=0, concat_axis=0, tiled=True)
-
-    fine_total = fine_count + owners * cap_fine
-    coarse_total = coarse_count + owners * cap_coarse
-    fine_index, fine_turns = live_index(slots_fine, counts_fine, fine_total)
-    coarse_index, coarse_turns = live_index(slots_coarse, counts_coarse, coarse_total)
 
     fine_far = pl.pallas_call(
         fine_kernel,
@@ -409,7 +485,7 @@
         scratch_shapes=sweep_scratch(fine_total, fine_count, px),
         compiler_params=params,
         name="fine_sweep",
-    )(fine_index, fine_turns, fine_recv, coef, fine_rows)
+    )(fine_index, fine_turns, fine_recv, fine_rows, fine_sums)
 
     far, gram = pl.pallas_call(
         coarse_kernel,
@@ -422,7 +498,7 @@
         scratch_shapes=sweep_scratch(coarse_total, coarse_count, px),
         compiler_params=params,
         name="coarse_sweep",
-    )(coarse_index, coarse_turns, coarse_recv, coarse_coef, coarse_rows, fine_far, transfer, all_probes)
+    )(coarse_index, coarse_turns, coarse_recv, coarse_rows, coarse_sums, fine_far, transfer, all_probes)
 
     far_field = far[:probes]
     blocks = gram[:, :probes].reshape(groups, probes * probes)

time: 127 us -> 123 us (0.969)
  waiting for transfers between devices: 20.9 us -> 0.01 us
  other arithmetic: 2.57 us -> 10.4 us
  Pallas kernels: 68.7 us -> 75 us
  blocking collectives: 11.3 us -> 14.3 us
    all_to_all x1, waiting for transfers between devices: 20.9 us -> 0.01 us  [shards(): lax.all_to_all(fine_send, 'leaf', split_axis=0, concat_axis=0, tiled=True)]
    pallas_call x0 -> x1, Pallas kernels: none -> 19.7 us  [shards(): pl.pallas_call(own_kernel, out_shape=(jax.ShapeDtypeStruct((px, points_fi...]
    pallas_call x1, Pallas kernels: 37.2 us -> 29.9 us  [shards(): pl.pallas_call(fine_kernel, out_shape=jax.ShapeDtypeStruct((px, points_fi...]
    pallas_call x1, Pallas kernels: 24 us -> 17.8 us  [shards(): pl.pallas_call(coarse_kernel, out_shape=(jax.ShapeDtypeStruct((px, points...]
    reduce_sum x0 -> x4, other arithmetic: none -> 4.19 us  [slot_list(): jnp.sum(jnp.where(moved, (slots - nothing)[:, :, None], 0), axis=1)]
    all_to_all x1, blocking collectives: 11.3 us -> 14.3 us  [shards(): lax.all_to_all(blocks, ('leaf', 'probe'), split_axis=0, concat_axis=0, ti...]
    add x0 -> x6, other arithmetic: none -> 2.8 us  [the longest x4 2.43 us: slot_list(): nothing + jnp.sum(jnp.where(moved, (slots - nothing)[:, :, None], 0), axi...]
    max x0 -> x4, other arithmetic: none -> 2.13 us  [slot_list(): return (index, jnp.maximum(turns, 1))]
  transfers between devices with their start and end apart: 3 -> 3, of which waited for: 1 -> 0; matrix products, arithmetic and copies ran while one was open for 3% -> 9% of each run, Pallas kernels for 33% -> 47%
where the time goes in v5:
time: 123 us; the launch traced here: 122 us
  Pallas kernels  75 us (61%)
  starting transfers between devices  16.8 us (14%)
  blocking collectives  14.3 us (12%)
  other arithmetic  10.4 us (8%)
  local copies, waits for them, and re-layouts  4.3 us (3%)
    pallas_call x1, Pallas kernels, shards(): pl.pallas_call(fine_kernel, out_shape=jax.ShapeDtypeStruct((px, points_fi...  29.9 us
    pallas_call x1, Pallas kernels, shards(): pl.pallas_call(own_kernel, out_shape=(jax.ShapeDtypeStruct((px, points_fi...  19.7 us
    pallas_call x1, Pallas kernels, shards(): pl.pallas_call(coarse_kernel, out_shape=(jax.ShapeDtypeStruct((px, points...  17.8 us
    all_to_all x1, blocking collectives, shards(): lax.all_to_all(blocks, ('leaf', 'probe'), split_axis=0, concat_axis=0, ti...  14.3 us
    all_to_all x1, starting transfers between devices, shards(): lax.all_to_all(coarse_send, 'leaf', split_axis=0, concat_axis=0, tiled=True)  7.75 us
    all_to_all x1, starting transfers between devices, shards(): lax.all_to_all(fine_send, 'leaf', split_axis=0, concat_axis=0, tiled=True)  6.05 us
    pallas_call x1, Pallas kernels, shards(): pl.pallas_call(pack_coarse_kernel, out_shape=(jax.ShapeDtypeStruct((owner...  4.22 us
    reduce_sum x4, other arithmetic, slot_list(): jnp.sum(jnp.where(moved, (slots - nothing)[:, :, None], 0), axis=1)  4.19 us
  transfers between devices with their start and end apart: 3, of which 0 were waited for; matrix products, arithmetic and copies ran while one was open for 9% of the time, Pallas kernels for 47%

profile of v5, /device:TPU:0, one launch (start us, length us, event | category | flops | bytes accessed | tf_op | source)
XLA Modules:
  0.0 122.2 jit_solution(16717384895149455363)
XLA Ops:
  0.6 3.0 %collective-permute-start = (bf16[32,4096]{1,0:T(8,128)(2,1)}, bf16[32,4096]{1,0:T(8,128)(2,1)S(1)}, u32[]{:S(2)}, u32[]{:S(2)}) collective-permute-start(bf16[32,4096]{1,0:T(8,128)(2,1)} %fine_coef_ref.1), channel_id=1, source_target_pairs={{0,1},{1,0},{2,3},{3,2},{4,5},{5,4},{6,7},{7,6},{8,9},{9,8},{10,11... | collective-permute-start | bytes 786440 | tf_op jit(solution)/shard_map/ppermute | solution.py:421
  3.7 3.3 %pack_fine.1 = (bf16[16,320,128]{2,1,0:T(8,128)(2,1)}, f32[8,4096]{1,0:T(8,128)}) custom-call(s32[16,16]{1,0:T(8,128)} %bitcast.22, bf16[32,4096]{1,0:T(8,128)(2,1)} %fine_coef_ref.1, f32[3,4096]{1,0:T(4,128)} %points_ref.3), custom_call_target="tpu_custom_call" | custom-call | tf_op jit(solution)/shard_map/pack_fine/pallas_call | solution.py:424
  7.0 0.0 copy-start.3
  7.0 0.0 copy-start.4
  7.0 0.0 copy-start.7
  7.0 0.0 copy-start.6
  7.0 0.0 copy-start.5
  7.0 6.1 %all-to-all-start.1 = ((bf16[16,320,128]{2,1,0:T(8,128)(2,1)}), bf16[16,320,128]{2,1,0:T(8,128)(2,1)S(1)}, u32[]{:S(2)}, u32[]{:S(2)}) async-start(bf16[16,320,128]{2,1,0:T(8,128)(2,1)} %get-tuple-element.20), calls=%async_computation.1 | async-start | bytes 2621440 | tf_op jit(solution)/shard_map/all_to_all | solution.py:439
  13.1 0.0 copy-done.3
  13.1 0.1 copy.39
  13.2 0.0 copy-done.4
  13.2 0.0 copy-done.7
  13.2 0.1 fusion.20
  13.3 0.1 broadcast_select_fusion.2
  13.4 0.2 fusion.10
  13.6 0.5 fusion.27.coarse_turns_ref
  14.2 0.0 copy-done.6
  14.2 0.1 broadcast_select_fusion.1
  14.3 0.6 fusion.28.fine_turns_ref
  14.9 0.7 select_reduce_fusion.2
  15.6 0.1 broadcast_select_fusion
  15.7 0.0 copy-done.5
  15.8 0.7 copy.38.send_ref
  16.4 0.1 copy.42
  16.5 0.1 copy.40
  16.6 4.2 %pack_coarse.1 = (bf16[16,160,128]{2,1,0:T(8,128)(2,1)}, f32[8,2048]{1,0:T(8,128)}, bf16[32,2048]{1,0:T(8,128)(2,1)}) custom-call(s32[16,8]{1,0:T(8,128)} %copy.38.send_ref, bf16[32,4096]{1,0:T(8,128)(2,1)} %fine_coef_ref.1, bf16[64,4096]{1,0:T(8,128)(2,1)} %transfer_ref.3, f32[3,2048]{1,0:T(4,128)} %points_ref.2), custom_call_target="tpu_custom_call" | custom-call | tf_op jit(solution)/shard_map/pack_coarse/pallas_call | solution.py:441
  20.8 1.4 %select_reduce_fusion.1 = s32[64,72]{1,0:T(8,128)S(1)} fusion(s32[64,64]{1,0:T(8,128)S(1)} %get-tuple-element.27, s32[64,64]{1,0:T(8,128)S(1)} %copy.40), kind=kLoop, calls=%fused_computation.3 | loop fusion | flops 880128 | bytes 51200 | tf_op jit(solution)/shard_map/reduce_sum | solution.py:378
  22.2 0.6 broadcast_add_fusion.4.coarse_index_ref
  22.8 0.6 broadcast_add_fusion.2.fine_index_ref
  23.4 19.7 %own_sweep.1 = (f32[32,4096]{1,0:T(8,128)}, f32[32,2048]{1,0:T(8,128)}) custom-call(s32[64,72]{1,0:T(8,128)} %broadcast_add_fusion.2.fine_index_ref, s32[64]{0:T(128)} %fusion.28.fine_turns_ref, s32[32,72]{1,0:T(8,128)} %broadcast_add_fusion.4.coarse_index_ref, s32[32]{0:T(128)} %fusion.27.coarse_turns_ref, bf16[32,4096]{1,0:T(8,128)(2,1)} %fine_coef_ref.1, ...), custom_call_target="tpu_custom_call" | custom-call | flops 10000000000 | bytes 10000000 | tf_op jit(solution)/shard_map/own_sweep/pallas_call | solution.py:463
  43.1 0.0 copy-start.2
  43.1 0.1 broadcast_select_fusion.3
  43.2 0.2 fusion.11
  43.4 0.7 select_reduce_fusion.3
  44.1 1.4 %select_reduce_fusion = s32[64,72]{1,0:T(8,128)S(1)} fusion(s32[64,64]{1,0:T(8,128)S(1)} %get-tuple-element.26, s32[64,64]{1,0:T(8,128)S(1)} %copy.42), kind=kLoop, calls=%fused_computation.1 | loop fusion | flops 880128 | bytes 51200 | tf_op jit(solution)/shard_map/reduce_sum | solution.py:378
  45.6 0.5 fusion.26.turns_ref
  46.0 0.0 all-to-all-done.1.recv_ref
  46.1 0.0 copy-start
  46.1 7.7 %all-to-all-start = ((bf16[16,160,128]{2,1,0:T(8,128)(2,1)}), bf16[16,160,128]{2,1,0:T(8,128)(2,1)S(1)}, u32[]{:S(2)}, u32[]{:S(2)}) async-start(bf16[16,160,128]{2,1,0:T(8,128)(2,1)} %get-tuple-element.18), calls=%async_computation | async-start | bytes 1310720 | tf_op jit(solution)/shard_map/all_to_all | solution.py:478
  53.8 0.5 fusion.29.turns_ref
  54.3 0.6 broadcast_add_fusion.6.index_ref
  54.9 0.6 broadcast_add_fusion.index_ref
  55.5 0.0 collective-permute-done
  55.5 0.0 copy-done.2
  55.5 0.8 pad_maximum_fusion.probes_ref
  56.4 0.0 copy-done
  56.4 29.9 %fine_sweep.1.fine_ref = f32[32,4096]{1,0:T(8,128)} custom-call(s32[64,72]{1,0:T(8,128)} %broadcast_add_fusion.index_ref, s32[64]{0:T(128)} %fusion.26.turns_ref, bf16[16,320,128]{2,1,0:T(8,128)(2,1)} %copy-done, f32[8,4096]{1,0:T(8,128)} %get-tuple-element.14.fine_rows_ref.rows_ref, f32[32,4096]{1,0:T(8,128)} %get-tuple-element.21.own_ref), custom_call_target="tpu_custom_call" | custom-call | tf_op jit(solution)/shard_map/fine_sweep/pallas_call | solution.py:480
  86.3 0.0 all-to-all-done.recv_ref
  86.3 0.0 copy-start.1
  86.3 0.8 copy-done.1
  87.2 17.8 %coarse_sweep.1 = (f32[32,4096]{1,0:T(8,128)}, f32[64,32]{1,0:T(8,128)}) custom-call(s32[32,72]{1,0:T(8,128)} %broadcast_add_fusion.6.index_ref, s32[32]{0:T(128)} %fusion.29.turns_ref, bf16[16,160,128]{2,1,0:T(8,128)(2,1)} %copy-done.1, f32[8,2048]{1,0:T(8,128)} %get-tuple-element.16.coarse_rows_ref.rows_ref, f32[32,2048]{1,0:T(8,128)} %get-tuple-element.19.own_ref, ...), custom_call_target="tpu_custom_call" | custom-call | tf_op jit(solution)/shard_map/coarse_sweep/pallas_call | solution.py:490
  105.0 0.8 reshape.92
  105.8 0.6 gather_fusion
  106.4 0.2 reshape.93
  106.6 14.3 %all_to_all.15 = f32[32,1,1024]{2,1,0:T(1,128)S(1)} all-to-all(f32[32,1,1024]{2,1,0:T(1,128)S(1)} %reshape.93), channel_id=1, replica_groups=mesh['leaf'=16,'probe'=2] {'leaf','probe'}, dimensions={0} | all-to-all | bytes 262144 | tf_op jit(solution)/shard_map/all_to_all | solution.py:508
  120.9 0.3 reduce.2
  121.2 0.2 reshape.94
  121.4 0.1 reduce_sum.49
  121.5 0.7 mul.15
  (8 shorter events, 0.1 us)
Async XLA Ops:
  0.6 54.9 %collective-permute-start = (bf16[32,4096]{1,0:T(8,128)(2,1)}, bf16[32,4096]{1,0:T(8,128)(2,1)S(1)}, u32[]{:S(2)}, u32[]{:S(2)}) collective-permute-start(bf16[32,4096]{1,0:T(8,128)(2,1)} %fine_coef_ref.1), channel_id=1, source_target_pairs={{0,1},{1,0},{2,3},{3,2},{4,5},{5,4},{6,7},{7,6},{8,9},{9,8},{10,11... | collective-permute-start | bytes 786440 | tf_op jit(solution)/shard_map/ppermute | solution.py:421
  7.0 6.1 %copy-start.3 = (s32[64,64]{1,0:T(8,128)S(1)}, s32[64,64]{1,0:T(8,128)}, u32[]{:S(2)}) copy-start(s32[64,64]{1,0:T(8,128)} %param.15) | copy-start | bytes 49156
  7.0 6.2 %copy-start.4 = (s32[32,64]{1,0:T(8,128)S(1)}, s32[32,64]{1,0:T(8,128)}, u32[]{:S(2)}) copy-start(s32[32,64]{1,0:T(8,128)} %param.18) | copy-start | bytes 24580
  7.0 6.2 %copy-start.7 = (s32[32]{0:T(128)S(1)}, s32[32]{0:T(128)}, u32[]{:S(2)}) copy-start(s32[32]{0:T(128)} %param.19) | copy-start | bytes 388
  7.0 7.2 %copy-start.6 = (s32[64]{0:T(128)S(1)}, s32[64]{0:T(128)}, u32[]{:S(2)}) copy-start(s32[64]{0:T(128)} %param.16) | copy-start | bytes 772
  7.0 8.7 %copy-start.5 = (s32[1,16,8]{1,2,0:T(8,128)S(1)}, s32[1,16,8]{1,2,0:T(8,128)}, u32[]{:S(2)}) copy-start(s32[1,16,8]{1,2,0:T(8,128)} %param.17) | copy-start | bytes 1540
  7.0 39.0 %all-to-all-start.1 = ((bf16[16,320,128]{2,1,0:T(8,128)(2,1)}), bf16[16,320,128]{2,1,0:T(8,128)(2,1)S(1)}, u32[]{:S(2)}, u32[]{:S(2)}) async-start(bf16[16,320,128]{2,1,0:T(8,128)(2,1)} %get-tuple-element.20), calls=%async_computation.1 | async-start | bytes 2621440 | tf_op jit(solution)/shard_map/all_to_all | solution.py:439
  43.1 12.5 %copy-start.2 = (bf16[32,4096]{1,0:T(8,128)(2,1)S(1)}, bf16[32,4096]{1,0:T(8,128)(2,1)}, u32[]{:S(2)}) copy-start(bf16[32,4096]{1,0:T(8,128)(2,1)} %fine_coef_ref.1) | copy-start | bytes 786436
  46.1 10.3 %copy-start = (bf16[16,320,128]{2,1,0:T(8,128)(2,1)}, bf16[16,320,128]{2,1,0:T(8,128)(2,1)S(1)}, u32[]{:S(2)}) copy-start(bf16[16,320,128]{2,1,0:T(8,128)(2,1)S(1)} %all-to-all-done.1.recv_ref) | copy-start | bytes 3932164
  46.1 40.3 %all-to-all-start = ((bf16[16,160,128]{2,1,0:T(8,128)(2,1)}), bf16[16,160,128]{2,1,0:T(8,128)(2,1)S(1)}, u32[]{:S(2)}, u32[]{:S(2)}) async-start(bf16[16,160,128]{2,1,0:T(8,128)(2,1)} %get-tuple-element.18), calls=%async_computation | async-start | bytes 1310720 | tf_op jit(solution)/shard_map/all_to_all | solution.py:478
  86.3 0.8 copy-start.1

commit v6 on v5

--- a/solution.py
+++ b/solution.py
@@ -9,7 +9,7 @@
 from jax.sharding import PartitionSpec as P
 
 KERNEL_RATE = 1.5
-POINT_SCALE = math.sqrt(2.0 * KERNEL_RATE * math.log2(math.e))
+POINT_SCALE = math.sqrt(2.0 * KERNEL_RATE)
 LANES = 128
 UNITS = 8
 QUAD = 4
@@ -129,20 +129,27 @@
     pack_send(send_ref, out_ref, dup_coef, dup_rows, owners, capacity, px)
 
 
+def turned(rows):
+    row = lax.broadcasted_iota(jnp.int32, (LANES, LANES), 0)
+    column = lax.broadcasted_iota(jnp.int32, (LANES, LANES), 1)
+    unit = jnp.where(row == column, 1.0, 0.0).astype(jnp.bfloat16)
+    return bdot(unit, rows, NT).astype(jnp.bfloat16)
+
+
 def put_pair(entry, coef, rows, coef_table, feature_table):
     a, b = halves(coef.astype(jnp.float32))
     coef_table[entry] = a.astype(jnp.bfloat16)
     coef_table[entry + 1] = b.astype(jnp.bfloat16)
-    a, b = halves(source_features(rows))
-    feature_table[entry] = a.astype(jnp.bfloat16)
-    feature_table[entry + 1] = b.astype(jnp.bfloat16)
+    features = turned(jnp.concatenate([source_features(rows).astype(jnp.bfloat16)] * 8, axis=0))
+    feature_table[entry] = features[:64]
+    feature_table[entry + 1] = features[64:]
 
 
 def put_nothing(entry, coef_table, feature_table):
     coef_table[entry] = jnp.zeros(coef_table.shape[1:], jnp.bfloat16)
     place = lax.broadcasted_iota(jnp.int32, (8, LANES), 0)
-    nothing = source_features(jnp.where(place == 3, FAR_AWAY, 0.0))
-    feature_table[entry] = nothing.astype(jnp.bfloat16)
+    nothing = source_features(jnp.where(place == 3, FAR_AWAY, 0.0)).astype(jnp.bfloat16)
+    feature_table[entry] = turned(jnp.concatenate([nothing] * 8, axis=0))[:64]
 
 
 def build_own(coef_ref, rows_ref, coef_table, feature_table):
@@ -182,15 +189,10 @@
 
 
 def build_targets(rows_ref, target_table):
-    row = lax.broadcasted_iota(jnp.int32, (LANES, LANES), 0)
-    column = lax.broadcasted_iota(jnp.int32, (LANES, LANES), 1)
-    unit = jnp.where(row == column, 1.0, 0.0).astype(jnp.bfloat16)
-
     def one_tile(index, carry):
-        features = target_features(rows_ref[:, lane_tile(index)]).astype(jnp.bfloat16)
-        turned = bdot(unit, jnp.concatenate([features] * 8, axis=0), NT)[:, :16 * QUAD]
-        target_table[2 * index] = turned[:64].astype(jnp.bfloat16)
-        target_table[2 * index + 1] = turned[64:].astype(jnp.bfloat16)
+        a, b = halves(target_features(rows_ref[:, lane_tile(index)]))
+        target_table[2 * index] = a.astype(jnp.bfloat16)
+        target_table[2 * index + 1] = b.astype(jnp.bfloat16)
         return carry
 
     lax.fori_loop(0, rows_ref.shape[1] // LANES, one_tile, 0, unroll=4)
@@ -200,37 +202,51 @@
     clusters = turns_ref.shape[0]
     px = coef_table.shape[1]
     slots_end = index_ref.shape[1] // CHUNK - 1
-    lane = lax.broadcasted_iota(jnp.int32, (16, LANES), 1) < 64
+    lane = lax.broadcasted_iota(jnp.int32, (64, LANES), 1) // 16
+    lane_t = lax.broadcasted_iota(jnp.int32, (16, LANES), 1) // 64
     lane_x = lax.broadcasted_iota(jnp.int32, (px, LANES), 1) < 64
-    owner = lax.broadcasted_iota(jnp.int32, (64, 16 * QUAD), 1) // 16
-    blank = jnp.zeros((64, 16 * QUAD), jnp.bfloat16)
+    blank = jnp.zeros((16, LANES), jnp.bfloat16)
     acc[...] = jnp.zeros_like(acc)
 
-    def pairs_of(unit, table, low):
+    def partners(unit):
         target, turn = unit
-        ids = [index_ref[target, turn * CHUNK + m] for m in range(CHUNK)]
-        return jnp.concatenate(
-            [jnp.where(low, table[ids[m]], table[ids[m + 1]]) for m in range(0, CHUNK, 2)], axis=1
-        )
+        return [index_ref[target, turn * CHUNK + m] for m in range(CHUNK)]
 
     def tiles(units, buffer):
         for start in range(0, UNITS, QUAD):
             quad = units[start:start + QUAD]
-            targets = jnp.concatenate(
-                [jnp.where(owner == u, target_table[quad[u][0]], blank) for u in range(QUAD)], axis=0
-            )
-            sources = jnp.concatenate([pairs_of(unit, feature_table, lane) for unit in quad], axis=0)
-            for part in range(0, CHUNK * 64, 256):
-                power = bdot(targets, sources[:, part:part + 256], NN)
-                buffer[start * 64:(start + QUAD) * 64, part:part + 256] = jnp.exp2(power).astype(
-                    jnp.bfloat16
-                )
+            weights = []
+            for u in range(QUAD):
+                own = jnp.where(lane_t == u % 2, target_table[quad[u][0]], blank)
+                weights.append(jnp.concatenate([own if v == u // 2 else blank for v in range(QUAD // 2)], axis=1))
+            weights = jnp.concatenate(weights, axis=0)
+            ids = [partners(unit) for unit in quad]
+            for part in range(0, CHUNK, 4):
+                rows = []
+                for m in range(part, part + 4):
+                    tile = feature_table[ids[0][m]]
+                    for u in range(1, QUAD):
+                        tile = jnp.where(lane == u, feature_table[ids[u][m]], tile)
+                    rows.append(tile[:, :16 * QUAD])
+                power = bdot(jnp.concatenate(rows, axis=0), weights, NN)
+                buffer[start // QUAD, part * 64:(part + 4) * 64] = jnp.exp(power).astype(jnp.bfloat16)
 
     def products(units, buffer):
         for start in range(0, UNITS, QUAD):
             quad = units[start:start + QUAD]
-            coefs = jnp.concatenate([pairs_of(unit, coef_table, lane_x) for unit in quad], axis=0)
-            product = bdot(coefs, buffer[start * 64:(start + QUAD) * 64], NT)
+            coefs = []
+            for unit in quad:
+                ids = partners(unit)
+                coefs.append(
+                    jnp.concatenate(
+                        [
+                            jnp.where(lane_x, coef_table[ids[m]], coef_table[ids[m + 1]])
+                            for m in range(0, CHUNK, 2)
+                        ],
+                        axis=1,
+                    )
+                )
+            product = bdot(jnp.concatenate(coefs, axis=0), buffer[start // QUAD], NN)
             for u in range(QUAD):
                 side = (u // 2) * LANES
                 acc[u % 2, quad[u][0]] += product[u * px:(u + 1) * px, side:side + LANES]
@@ -361,10 +377,10 @@
 def sweep_scratch(total, clusters, px):
     return [
         pltpu.VMEM((total + 1, px, LANES), jnp.bfloat16),
-        pltpu.VMEM((total + 1, 16, LANES), jnp.bfloat16),
-        pltpu.VMEM((clusters, 64, 16 * QUAD), jnp.bfloat16),
-        pltpu.VMEM((UNITS * 64, CHUNK * 64), jnp.bfloat16),
-        pltpu.VMEM((UNITS * 64, CHUNK * 64), jnp.bfloat16),
+        pltpu.VMEM((total + 1, 64, LANES), jnp.bfloat16),
+        pltpu.VMEM((clusters, 16, LANES), jnp.bfloat16),
+        pltpu.VMEM((UNITS // QUAD, CHUNK * 64, QUAD * 64), jnp.bfloat16),
+        pltpu.VMEM((UNITS // QUAD, CHUNK * 64, QUAD * 64), jnp.bfloat16),
         pltpu.VMEM((2, clusters, px, LANES), jnp.float32),
     ]
 

time: 123 us -> 121 us (0.984); the launches traced: 122 us -> 123 us
  blocking collectives: 14.3 us -> 16.8 us
    pallas_call x1, Pallas kernels: 29.9 us -> 26.6 us  [shards(): pl.pallas_call(fine_kernel, out_shape=jax.ShapeDtypeStruct((px, points_fi...]
    all_to_all x1, blocking collectives: 14.3 us -> 16.8 us  [shards(): lax.all_to_all(blocks, ('leaf', 'probe'), split_axis=0, concat_axis=0, ti...]
    pallas_call x1, Pallas kernels: 17.8 us -> 20.2 us  [shards(): pl.pallas_call(coarse_kernel, out_shape=(jax.ShapeDtypeStruct((px, points...]
  transfers between devices with their start and end apart: 3 -> 3, of which waited for: 0 -> 0; matrix products, arithmetic and copies ran while one was open for 9% -> 9% of each run, Pallas kernels for 47% -> 43%
where the time goes in v6:
time: 121 us; the launch traced here: 123 us
  Pallas kernels  73.8 us (61%)
  blocking collectives  16.8 us (14%)
  starting transfers between devices  16.6 us (14%)
  other arithmetic  10.4 us (9%)
  local copies, waits for them, and re-layouts  4.3 us (4%)
    pallas_call x1, Pallas kernels, shards(): pl.pallas_call(fine_kernel, out_shape=jax.ShapeDtypeStruct((px, points_fi...  26.6 us
    pallas_call x1, Pallas kernels, shards(): pl.pallas_call(coarse_kernel, out_shape=(jax.ShapeDtypeStruct((px, points...  20.2 us
    pallas_call x1, Pallas kernels, shards(): pl.pallas_call(own_kernel, out_shape=(jax.ShapeDtypeStruct((px, points_fi...  19.4 us
    all_to_all x1, blocking collectives, shards(): lax.all_to_all(blocks, ('leaf', 'probe'), split_axis=0, concat_axis=0, ti...  16.8 us
    all_to_all x1, starting transfers between devices, shards(): lax.all_to_all(coarse_send, 'leaf', split_axis=0, concat_axis=0, tiled=True)  7.54 us
    all_to_all x1, starting transfers between devices, shards(): lax.all_to_all(fine_send, 'leaf', split_axis=0, concat_axis=0, tiled=True)  6.05 us
    pallas_call x1, Pallas kernels, shards(): pl.pallas_call(pack_coarse_kernel, out_shape=(jax.ShapeDtypeStruct((owner...  4.22 us
    reduce_sum x4, other arithmetic, slot_list(): jnp.sum(jnp.where(moved, (slots - nothing)[:, :, None], 0), axis=1)  4.19 us
  transfers between devices with their start and end apart: 3, of which 0 were waited for; matrix products, arithmetic and copies ran while one was open for 9% of the time, Pallas kernels for 43%

profile of v6, /device:TPU:0, one launch (start us, length us, event | category | flops | bytes accessed | tf_op | source)
XLA Modules:
  0.0 123.3 jit_solution(16688993335022555321)
XLA Ops:
  0.6 3.0 %collective-permute-start = (bf16[32,4096]{1,0:T(8,128)(2,1)}, bf16[32,4096]{1,0:T(8,128)(2,1)S(1)}, u32[]{:S(2)}, u32[]{:S(2)}) collective-permute-start(bf16[32,4096]{1,0:T(8,128)(2,1)} %fine_coef_ref.1), channel_id=1, source_target_pairs={{0,1},{1,0},{2,3},{3,2},{4,5},{5,4},{6,7},{7,6},{8,9},{9,8},{10,11... | collective-permute-start | bytes 786440 | tf_op jit(solution)/shard_map/ppermute | solution.py:437
  3.7 3.3 %pack_fine.1 = (bf16[16,320,128]{2,1,0:T(8,128)(2,1)}, f32[8,4096]{1,0:T(8,128)}) custom-call(s32[16,16]{1,0:T(8,128)} %bitcast.22, bf16[32,4096]{1,0:T(8,128)(2,1)} %fine_coef_ref.1, f32[3,4096]{1,0:T(4,128)} %points_ref.3), custom_call_target="tpu_custom_call" | custom-call | tf_op jit(solution)/shard_map/pack_fine/pallas_call | solution.py:440
  7.0 0.0 copy-start.3
  7.0 0.0 copy-start.4
  7.0 0.0 copy-start.7
  7.0 0.0 copy-start.6
  7.0 0.0 copy-start.5
  7.0 6.1 %all-to-all-start.1 = ((bf16[16,320,128]{2,1,0:T(8,128)(2,1)}), bf16[16,320,128]{2,1,0:T(8,128)(2,1)S(1)}, u32[]{:S(2)}, u32[]{:S(2)}) async-start(bf16[16,320,128]{2,1,0:T(8,128)(2,1)} %get-tuple-element.20), calls=%async_computation.1 | async-start | bytes 2621440 | tf_op jit(solution)/shard_map/all_to_all | solution.py:455
  13.1 0.0 copy-done.3
  13.1 0.1 copy.39
  13.2 0.0 copy-done.4
  13.2 0.0 copy-done.7
  13.2 0.1 fusion.20
  13.3 0.1 broadcast_select_fusion.2
  13.4 0.2 fusion.10
  13.6 0.5 fusion.27.coarse_turns_ref
  14.2 0.0 copy-done.6
  14.2 0.1 broadcast_select_fusion.1
  14.3 0.6 fusion.28.fine_turns_ref
  14.9 0.7 select_reduce_fusion.2
  15.6 0.1 broadcast_select_fusion
  15.7 0.0 copy-done.5
  15.8 0.7 copy.38.send_ref
  16.4 0.1 copy.42
  16.5 0.1 copy.40
  16.6 4.2 %pack_coarse.1 = (bf16[16,160,128]{2,1,0:T(8,128)(2,1)}, f32[8,2048]{1,0:T(8,128)}, bf16[32,2048]{1,0:T(8,128)(2,1)}) custom-call(s32[16,8]{1,0:T(8,128)} %copy.38.send_ref, bf16[32,4096]{1,0:T(8,128)(2,1)} %fine_coef_ref.1, bf16[64,4096]{1,0:T(8,128)(2,1)} %transfer_ref.3, f32[3,2048]{1,0:T(4,128)} %points_ref.2), custom_call_target="tpu_custom_call" | custom-call | tf_op jit(solution)/shard_map/pack_coarse/pallas_call | solution.py:457
  20.8 1.4 %select_reduce_fusion.1 = s32[64,72]{1,0:T(8,128)S(1)} fusion(s32[64,64]{1,0:T(8,128)S(1)} %get-tuple-element.27, s32[64,64]{1,0:T(8,128)S(1)} %copy.40), kind=kLoop, calls=%fused_computation.3 | loop fusion | flops 880128 | bytes 51200 | tf_op jit(solution)/shard_map/reduce_sum | solution.py:394
  22.2 0.6 broadcast_add_fusion.4.coarse_index_ref
  22.8 0.6 broadcast_add_fusion.2.fine_index_ref
  23.4 19.4 %own_sweep.1 = (f32[32,4096]{1,0:T(8,128)}, f32[32,2048]{1,0:T(8,128)}) custom-call(s32[64,72]{1,0:T(8,128)} %broadcast_add_fusion.2.fine_index_ref, s32[64]{0:T(128)} %fusion.28.fine_turns_ref, s32[32,72]{1,0:T(8,128)} %broadcast_add_fusion.4.coarse_index_ref, s32[32]{0:T(128)} %fusion.27.coarse_turns_ref, bf16[32,4096]{1,0:T(8,128)(2,1)} %fine_coef_ref.1, ...), custom_call_target="tpu_custom_call" | custom-call | flops 10000000000 | bytes 10000000 | tf_op jit(solution)/shard_map/own_sweep/pallas_call | solution.py:479
  42.8 0.0 copy-start.2
  42.8 0.1 broadcast_select_fusion.3
  43.0 0.2 fusion.11
  43.2 0.7 select_reduce_fusion.3
  43.9 1.4 %select_reduce_fusion = s32[64,72]{1,0:T(8,128)S(1)} fusion(s32[64,64]{1,0:T(8,128)S(1)} %get-tuple-element.26, s32[64,64]{1,0:T(8,128)S(1)} %copy.42), kind=kLoop, calls=%fused_computation.1 | loop fusion | flops 880128 | bytes 51200 | tf_op jit(solution)/shard_map/reduce_sum | solution.py:394
  45.3 0.5 fusion.26.turns_ref
  45.8 0.0 all-to-all-done.1.recv_ref
  45.8 0.0 copy-start
  45.8 7.5 %all-to-all-start = ((bf16[16,160,128]{2,1,0:T(8,128)(2,1)}), bf16[16,160,128]{2,1,0:T(8,128)(2,1)S(1)}, u32[]{:S(2)}, u32[]{:S(2)}) async-start(bf16[16,160,128]{2,1,0:T(8,128)(2,1)} %get-tuple-element.18), calls=%async_computation | async-start | bytes 1310720 | tf_op jit(solution)/shard_map/all_to_all | solution.py:494
  53.3 0.5 fusion.29.turns_ref
  53.8 0.6 broadcast_add_fusion.6.index_ref
  54.5 0.6 broadcast_add_fusion.index_ref
  55.1 0.0 collective-permute-done
  55.1 0.0 copy-done.2
  55.1 0.8 pad_maximum_fusion.probes_ref
  55.9 0.0 copy-done
  55.9 26.6 %fine_sweep.1.fine_ref = f32[32,4096]{1,0:T(8,128)} custom-call(s32[64,72]{1,0:T(8,128)} %broadcast_add_fusion.index_ref, s32[64]{0:T(128)} %fusion.26.turns_ref, bf16[16,320,128]{2,1,0:T(8,128)(2,1)} %copy-done, f32[8,4096]{1,0:T(8,128)} %get-tuple-element.14.fine_rows_ref.rows_ref, f32[32,4096]{1,0:T(8,128)} %get-tuple-element.21.own_ref), custom_call_target="tpu_custom_call" | custom-call | tf_op jit(solution)/shard_map/fine_sweep/pallas_call | solution.py:496
  82.5 0.0 all-to-all-done.recv_ref
  82.5 0.0 copy-start.1
  82.6 0.8 copy-done.1
  83.4 20.2 %coarse_sweep.1 = (f32[32,4096]{1,0:T(8,128)}, f32[64,32]{1,0:T(8,128)}) custom-call(s32[32,72]{1,0:T(8,128)} %broadcast_add_fusion.6.index_ref, s32[32]{0:T(128)} %fusion.29.turns_ref, bf16[16,160,128]{2,1,0:T(8,128)(2,1)} %copy-done.1, f32[8,2048]{1,0:T(8,128)} %get-tuple-element.16.coarse_rows_ref.rows_ref, f32[32,2048]{1,0:T(8,128)} %get-tuple-element.19.own_ref, ...), custom_call_target="tpu_custom_call" | custom-call | tf_op jit(solution)/shard_map/coarse_sweep/pallas_call | solution.py:506
  103.6 0.8 reshape.92
  104.4 0.6 gather_fusion
  105.0 0.2 reshape.93
  105.3 16.8 %all_to_all.15 = f32[32,1,1024]{2,1,0:T(1,128)S(1)} all-to-all(f32[32,1,1024]{2,1,0:T(1,128)S(1)} %reshape.93), channel_id=1, replica_groups=mesh['leaf'=16,'probe'=2] {'leaf','probe'}, dimensions={0} | all-to-all | bytes 262144 | tf_op jit(solution)/shard_map/all_to_all | solution.py:524
  122.1 0.3 reduce.2
  122.4 0.2 reshape.94
  122.5 0.1 reduce_sum.49
  122.7 0.7 mul.15
  (8 shorter events, 0.1 us)
Async XLA Ops:
  0.6 54.4 %collective-permute-start = (bf16[32,4096]{1,0:T(8,128)(2,1)}, bf16[32,4096]{1,0:T(8,128)(2,1)S(1)}, u32[]{:S(2)}, u32[]{:S(2)}) collective-permute-start(bf16[32,4096]{1,0:T(8,128)(2,1)} %fine_coef_ref.1), channel_id=1, source_target_pairs={{0,1},{1,0},{2,3},{3,2},{4,5},{5,4},{6,7},{7,6},{8,9},{9,8},{10,11... | collective-permute-start | bytes 786440 | tf_op jit(solution)/shard_map/ppermute | solution.py:437
  7.0 6.1 %copy-start.3 = (s32[64,64]{1,0:T(8,128)S(1)}, s32[64,64]{1,0:T(8,128)}, u32[]{:S(2)}) copy-start(s32[64,64]{1,0:T(8,128)} %param.15) | copy-start | bytes 49156
  7.0 6.2 %copy-start.4 = (s32[32,64]{1,0:T(8,128)S(1)}, s32[32,64]{1,0:T(8,128)}, u32[]{:S(2)}) copy-start(s32[32,64]{1,0:T(8,128)} %param.18) | copy-start | bytes 24580
  7.0 6.2 %copy-start.7 = (s32[32]{0:T(128)S(1)}, s32[32]{0:T(128)}, u32[]{:S(2)}) copy-start(s32[32]{0:T(128)} %param.19) | copy-start | bytes 388
  7.0 7.2 %copy-start.6 = (s32[64]{0:T(128)S(1)}, s32[64]{0:T(128)}, u32[]{:S(2)}) copy-start(s32[64]{0:T(128)} %param.16) | copy-start | bytes 772
  7.0 8.7 %copy-start.5 = (s32[1,16,8]{1,2,0:T(8,128)S(1)}, s32[1,16,8]{1,2,0:T(8,128)}, u32[]{:S(2)}) copy-start(s32[1,16,8]{1,2,0:T(8,128)} %param.17) | copy-start | bytes 1540
  7.0 38.8 %all-to-all-start.1 = ((bf16[16,320,128]{2,1,0:T(8,128)(2,1)}), bf16[16,320,128]{2,1,0:T(8,128)(2,1)S(1)}, u32[]{:S(2)}, u32[]{:S(2)}) async-start(bf16[16,320,128]{2,1,0:T(8,128)(2,1)} %get-tuple-element.20), calls=%async_computation.1 | async-start | bytes 2621440 | tf_op jit(solution)/shard_map/all_to_all | solution.py:455
  42.8 12.2 %copy-start.2 = (bf16[32,4096]{1,0:T(8,128)(2,1)S(1)}, bf16[32,4096]{1,0:T(8,128)(2,1)}, u32[]{:S(2)}) copy-start(bf16[32,4096]{1,0:T(8,128)(2,1)} %fine_coef_ref.1) | copy-start | bytes 786436
  45.8 10.1 %copy-start = (bf16[16,320,128]{2,1,0:T(8,128)(2,1)}, bf16[16,320,128]{2,1,0:T(8,128)(2,1)S(1)}, u32[]{:S(2)}) copy-start(bf16[16,320,128]{2,1,0:T(8,128)(2,1)S(1)} %all-to-all-done.1.recv_ref) | copy-start | bytes 3932164
  45.8 36.8 %all-to-all-start = ((bf16[16,160,128]{2,1,0:T(8,128)(2,1)}), bf16[16,160,128]{2,1,0:T(8,128)(2,1)S(1)}, u32[]{:S(2)}, u32[]{:S(2)}) async-start(bf16[16,160,128]{2,1,0:T(8,128)(2,1)} %get-tuple-element.18), calls=%async_computation | async-start | bytes 1310720 | tf_op jit(solution)/shard_map/all_to_all | solution.py:494
  82.5 0.8 copy-start.1

commit v7 on v6

--- a/solution.py
+++ b/solution.py
@@ -1,3 +1,4 @@
+import functools
 import functools
 import math
 
@@ -11,10 +12,12 @@
 KERNEL_RATE = 1.5
 POINT_SCALE = math.sqrt(2.0 * KERNEL_RATE)
 LANES = 128
-UNITS = 8
+UNITS = 16
 QUAD = 4
-CHUNK = 8
+CHUNK = 4
 FAR_AWAY = -30000.0
+SLOTS = 64
+TURNS = LANES - 1
 VMEM = 56 * 1024 * 1024
 
 NT = (((1,), (1,)), ((), ()))
@@ -58,6 +61,39 @@
     return pl.ds(pl.multiple_of(index * LANES, LANES), LANES)
 
 
+def list_slots(slots_ref, counts_ref, out_ref, entries):
+    clusters, width = slots_ref.shape
+    slots = slots_ref[...]
+    place = lax.broadcasted_iota(jnp.int32, slots.shape, 1)
+    live = place < counts_ref[...]
+    own = live & (slots < clusters)
+    received = live & (slots >= clusters)
+    row = lax.broadcasted_iota(jnp.int32, (width, width), 0)
+    column = lax.broadcasted_iota(jnp.int32, (width, width), 1)
+    upto = jnp.where(row <= column, 1.0, 0.0).astype(jnp.bfloat16)
+    rank = [
+        bdot(jnp.where(chosen, 1.0, 0.0).astype(jnp.bfloat16), upto, NN).astype(jnp.int32)
+        for chosen in (own, received)
+    ]
+    spot = jnp.where(own, rank[0] - 1, jnp.where(received, rank[1] + (LANES - 1), -1))
+    value = jnp.where(own, slots - clusters, slots - clusters - entries)
+    lane = lax.broadcasted_iota(jnp.int32, (clusters, 2 * LANES), 1)
+    table = jnp.where(lane < LANES, clusters, entries)
+    for m in range(width):
+        table = table + jnp.where(lane == spot[:, m:m + 1], value[:, m:m + 1], 0)
+    for side in range(2):
+        turns = jnp.maximum((rank[side][:, width - 1:] + CHUNK - 1) // CHUNK, 1)
+        table = jnp.where(lane == side * LANES + TURNS, turns, table)
+    out_ref[...] = table
+
+
+def list_slots_kernel(
+    fine_slots_ref, fine_counts_ref, coarse_slots_ref, coarse_counts_ref, fine_out_ref, coarse_out_ref, *, entries
+):
+    list_slots(fine_slots_ref, fine_counts_ref, fine_out_ref, entries[0])
+    list_slots(coarse_slots_ref, coarse_counts_ref, coarse_out_ref, entries[1])
+
+
 def pack_send(send_ref, out_ref, dup_coef, dup_rows, owners, capacity, px):
     pairs = capacity // 2
     lane = lax.broadcasted_iota(jnp.int32, (px, LANES), 1) < LANES // 2
@@ -66,8 +102,8 @@
     def one_owner(owner, carry):
         before = None
         for pair in range(pairs):
-            first = send_ref[owner, 2 * pair]
-            second = send_ref[owner, 2 * pair + 1]
+            first = send_ref[0, owner, 2 * pair]
+            second = send_ref[0, owner, 2 * pair + 1]
             out_ref[owner, pair * px:(pair + 1) * px, :] = jnp.where(
                 lane, dup_coef[first], dup_coef[second]
             ).astype(jnp.bfloat16)
@@ -85,7 +121,7 @@
 
 
 def pack_fine_kernel(send_ref, coef_ref, points_ref, out_ref, rows_ref, dup_coef, dup_rows):
-    owners, capacity = send_ref.shape
+    _, owners, capacity = send_ref.shape
     px = coef_ref.shape[0]
     rows_ref[...] = split_rows(points_ref[...])
 
@@ -105,7 +141,7 @@
 def pack_coarse_kernel(
     send_ref, coef_ref, transfer_ref, points_ref, out_ref, rows_ref, coarse_ref, dup_coef, dup_rows
 ):
-    owners, capacity = send_ref.shape
+    _, owners, capacity = send_ref.shape
     px = coef_ref.shape[0]
     rows_ref[...] = split_rows(points_ref[...])
 
@@ -198,10 +234,10 @@
     lax.fori_loop(0, rows_ref.shape[1] // LANES, one_tile, 0, unroll=4)
 
 
-def sweep(index_ref, turns_ref, coef_table, feature_table, target_table, first_buffer, second_buffer, acc):
-    clusters = turns_ref.shape[0]
+def sweep(index_ref, base, coef_table, feature_table, target_table, first_buffer, second_buffer, acc):
+    clusters = index_ref.shape[0]
     px = coef_table.shape[1]
-    slots_end = index_ref.shape[1] // CHUNK - 1
+    slots_end = SLOTS // CHUNK
     lane = lax.broadcasted_iota(jnp.int32, (64, LANES), 1) // 16
     lane_t = lax.broadcasted_iota(jnp.int32, (16, LANES), 1) // 64
     lane_x = lax.broadcasted_iota(jnp.int32, (px, LANES), 1) < 64
@@ -210,7 +246,7 @@
 
     def partners(unit):
         target, turn = unit
-        return [index_ref[target, turn * CHUNK + m] for m in range(CHUNK)]
+        return [index_ref[target, base + turn * CHUNK + m] for m in range(CHUNK)]
 
     def tiles(units, buffer):
         for start in range(0, UNITS, QUAD):
@@ -253,7 +289,7 @@
 
     def following(unit):
         target, turn = unit
-        over = turn + 1 >= turns_ref[target]
+        over = turn + 1 >= index_ref[target, base + TURNS]
         later = jnp.where(over, target + 1, target)
         end = later >= clusters
         turn = jnp.where(end, slots_end, jnp.where(over, 0, turn + 1))
@@ -275,7 +311,7 @@
         products(second, second_buffer)
         return third
 
-    total = lax.fori_loop(0, clusters, lambda c, n: n + turns_ref[c], jnp.int32(0))
+    total = lax.fori_loop(0, clusters, lambda c, n: n + index_ref[c, base + TURNS], jnp.int32(0))
     unit = (jnp.int32(0), jnp.int32(0))
     start = (unit,) + next_units(unit)[:-1]
     tiles(start, first_buffer)
@@ -301,10 +337,8 @@
 
 
 def own_kernel(
-    fine_index_ref,
-    fine_turns_ref,
-    coarse_index_ref,
-    coarse_turns_ref,
+    fine_list_ref,
+    coarse_list_ref,
     fine_coef_ref,
     fine_rows_ref,
     coarse_coef_ref,
@@ -313,45 +347,37 @@
     coarse_out_ref,
     *scratch,
 ):
-    acc = scratch[-1]
-    for index_ref, turns_ref, coef_ref, rows_ref, out_ref in (
-        (fine_index_ref, fine_turns_ref, fine_coef_ref, fine_rows_ref, fine_out_ref),
-        (coarse_index_ref, coarse_turns_ref, coarse_coef_ref, coarse_rows_ref, coarse_out_ref),
+    for list_ref, coef_ref, rows_ref, out_ref in (
+        (fine_list_ref, fine_coef_ref, fine_rows_ref, fine_out_ref),
+        (coarse_list_ref, coarse_coef_ref, coarse_rows_ref, coarse_out_ref),
     ):
         build_own(coef_ref, rows_ref, *scratch[:2])
         build_targets(rows_ref, scratch[2])
-        sweep(index_ref, turns_ref, *scratch)
-        put_sums(acc, turns_ref.shape[0], out_ref)
-
-
-def fine_kernel(index_ref, turns_ref, recv_ref, rows_ref, own_ref, out_ref, *scratch):
+        sweep(list_ref, 0, *scratch)
+        put_sums(scratch[-1], list_ref.shape[0], out_ref)
+
+
+def fine_kernel(list_ref, recv_ref, rows_ref, own_ref, out_ref, *scratch):
     build_received(recv_ref, *scratch[:2])
     build_targets(rows_ref, scratch[2])
-    sweep(index_ref, turns_ref, *scratch)
-    put_sums(scratch[-1], turns_ref.shape[0], out_ref, own_ref)
-
-
-def coarse_kernel(
-    index_ref,
-    turns_ref,
-    recv_ref,
-    rows_ref,
-    own_ref,
-    fine_ref,
-    transfer_ref,
-    probes_ref,
-    out_ref,
-    gram_ref,
-    *scratch,
-):
+    sweep(list_ref, LANES, *scratch)
+    put_sums(scratch[-1], list_ref.shape[0], out_ref, own_ref)
+
+
+def coarse_kernel(groups, *refs):
+    list_ref, recv_ref, rows_ref, own_ref, fine_ref, transfer_ref = refs[:6]
+    probes_refs = refs[6:6 + groups]
+    out_ref, terms_ref = refs[6 + groups:8 + groups]
+    gram_ref, *scratch = refs[8 + groups:]
+    probes = probes_refs[0].shape[0]
     acc = scratch[-1]
     build_received(recv_ref, *scratch[:2])
     build_targets(rows_ref, scratch[2])
-    sweep(index_ref, turns_ref, *scratch)
+    sweep(list_ref, LANES, *scratch)
     gram_ref[...] = jnp.zeros_like(gram_ref)
 
     def one_group(group, carry):
-        gram = None
+        grams = [None] * groups
         for part in range(4):
             q = group * 4 + part
             own = halves(own_ref[:, lane_tile(group * 2 + part // 2)])[part % 2]
@@ -365,13 +391,38 @@
             out_ref[:, lane_tile(q)] = total
             high = total.astype(jnp.bfloat16)
             rest = (total - high.astype(jnp.float32)).astype(jnp.bfloat16)
-            probes = probes_ref[:, lane_tile(q)]
-            term = bdot(probes, high, NT) + bdot(probes, rest, NT)
-            gram = term if gram is None else gram + term
-        gram_ref[...] += gram
-        return carry
-
-    lax.fori_loop(0, turns_ref.shape[0] // 4, one_group, 0)
+            for block, probes_ref in enumerate(probes_refs):
+                tile = probes_ref[:, lane_tile(q)]
+                term = bdot(tile, high, NT) + bdot(tile, rest, NT)
+                grams[block] = term if grams[block] is None else grams[block] + term
+        for block in range(groups):
+            gram_ref[block] += grams[block]
+        return carry
+
+    lax.fori_loop(0, list_ref.shape[0] // 4, one_group, 0)
+    place = lax.axis_index("probe")
+    for b in range(groups):
+        block = gram_ref[lax.rem(place - b + groups, groups)]
+        packed = jnp.concatenate([block[i:i + 8, :probes] for i in range(0, probes, 8)], axis=1)
+
+        def one_owner(owner, carry):
+            terms_ref[owner * groups + b] = packed
+            return carry
+
+        lax.fori_loop(0, terms_ref.shape[0] // groups, one_owner, 0)
+
+
+def gram_kernel(terms_ref, out_ref, *, groups, scale):
+    probes = out_ref.shape[0]
+    columns = []
+    for b in range(groups):
+        total = terms_ref[b]
+        for owner in range(1, terms_ref.shape[0] // groups):
+            total = total + terms_ref[owner * groups + b]
+        columns.append(
+            jnp.concatenate([total[:, i * probes:(i + 1) * probes] for i in range(probes // 8)], axis=0)
+        )
+    out_ref[...] = jnp.concatenate(columns, axis=1) * scale
 
 
 def sweep_scratch(total, clusters, px):
@@ -383,25 +434,6 @@
         pltpu.VMEM((UNITS // QUAD, CHUNK * 64, QUAD * 64), jnp.bfloat16),
         pltpu.VMEM((2, clusters, px, LANES), jnp.float32),
     ]
-
-
-def slot_list(slots, chosen, nothing):
-    width = slots.shape[1]
-    before = jnp.tril(jnp.ones((width, width), jnp.float32)).T
-    rank = jnp.dot(chosen.astype(jnp.float32), before).astype(jnp.int32) - 1
-    place = lax.broadcasted_iota(jnp.int32, (1, 1, width + CHUNK), 2)
-    moved = jnp.where(chosen, rank, -1)[:, :, None] == place
-    index = nothing + jnp.sum(jnp.where(moved, (slots - nothing)[:, :, None], 0), axis=1)
-    turns = (rank[:, -1] + CHUNK) // CHUNK
-    return index, jnp.maximum(turns, 1)
-
-
-def slot_lists(slots, counts, entries):
-    clusters, width = slots.shape
-    live = lax.broadcasted_iota(jnp.int32, slots.shape, 1) < counts[:, None]
-    own = slot_list(slots, live & (slots < clusters), clusters)
-    received = slot_list(slots - clusters, live & (slots >= clusters), entries)
-    return own, received
 
 
 def shards(
@@ -423,10 +455,8 @@
     groups = lax.axis_size("probe")
     px = -(-probes // 16) * 16
     coef = coef_fine if px == probes else jnp.pad(coef_fine, ((0, px - probes), (0, 0)))
-    send_fine = send_fine.reshape(owners, -1)
-    send_coarse = send_coarse.reshape(owners, -1)
-    cap_fine = send_fine.shape[1]
-    cap_coarse = send_coarse.shape[1]
+    cap_fine = send_fine.shape[2]
+    cap_coarse = send_coarse.shape[2]
     params = pltpu.CompilerParams(vmem_limit_bytes=VMEM)
     smem = pl.BlockSpec(memory_space=pltpu.SMEM)
     vmem = pl.BlockSpec(memory_space=pltpu.VMEM)
@@ -435,7 +465,6 @@
     turned = [coef_fine]
     for step in range(1, groups):
         turned.append(lax.ppermute(coef_fine, "probe", [(i, (i + step) % groups) for i in range(groups)]))
-    all_probes = jnp.concatenate(turned, axis=0)
 
     fine_send, fine_rows = pl.pallas_call(
         pack_fine_kernel,
@@ -472,23 +501,30 @@
     )(send_coarse, coef, transfer, points_coarse)
     fine_total = owners * cap_fine
     coarse_total = owners * cap_coarse
-    (fine_own, fine_own_turns), (fine_index, fine_turns) = slot_lists(slots_fine, counts_fine, fine_total)
-    (coarse_own, coarse_own_turns), (coarse_index, coarse_turns) = slot_lists(
-        slots_coarse, counts_coarse, coarse_total
-    )
+    fine_list, coarse_list = pl.pallas_call(
+        functools.partial(list_slots_kernel, entries=(fine_total, coarse_total)),
+        out_shape=(
+            jax.ShapeDtypeStruct((fine_count, 2 * LANES), jnp.int32),
+            jax.ShapeDtypeStruct((coarse_count, 2 * LANES), jnp.int32),
+        ),
+        in_specs=[vmem] * 4,
+        out_specs=[vmem, vmem],
+        compiler_params=params,
+        name="list_slots",
+    )(slots_fine, counts_fine[:, None], slots_coarse, counts_coarse[:, None])
     fine_sums, coarse_sums = pl.pallas_call(
         own_kernel,
         out_shape=(
             jax.ShapeDtypeStruct((px, points_fine.shape[1]), f32),
             jax.ShapeDtypeStruct((px, points_coarse.shape[1]), f32),
         ),
-        in_specs=[smem] * 4 + [vmem] * 4,
+        in_specs=[smem] * 2 + [vmem] * 4,
         out_specs=[vmem, vmem],
         scratch_shapes=sweep_scratch(fine_count, fine_count, px),
         compiler_params=params,
         cost_estimate=pl.CostEstimate(flops=10**10, bytes_accessed=10**7, transcendentals=10**7),
         name="own_sweep",
-    )(fine_own, fine_own_turns, coarse_own, coarse_own_turns, coef, fine_rows, coarse_coef, coarse_rows)
+    )(fine_list, coarse_list, coef, fine_rows, coarse_coef, coarse_rows)
 
     coarse_send, coarse_sums = lax.optimization_barrier((coarse_send, coarse_sums))
     coarse_recv = lax.all_to_all(coarse_send, "leaf", split_axis=0, concat_axis=0, tiled=True)
@@ -496,36 +532,39 @@
     fine_far = pl.pallas_call(
         fine_kernel,
         out_shape=jax.ShapeDtypeStruct((px, points_fine.shape[1]), f32),
-        in_specs=[smem, smem, vmem, vmem, vmem],
+        in_specs=[smem, vmem, vmem, vmem],
         out_specs=vmem,
         scratch_shapes=sweep_scratch(fine_total, fine_count, px),
         compiler_params=params,
         name="fine_sweep",
-    )(fine_index, fine_turns, fine_recv, fine_rows, fine_sums)
-
-    far, gram = pl.pallas_call(
-        coarse_kernel,
+    )(fine_list, fine_recv, fine_rows, fine_sums)
+
+    term_shape = (owners * groups, 8, probes * probes // 8)
+    far, terms = pl.pallas_call(
+        functools.partial(coarse_kernel, groups),
         out_shape=(
             jax.ShapeDtypeStruct((px, points_fine.shape[1]), f32),
-            jax.ShapeDtypeStruct((all_probes.shape[0], px), f32),
-        ),
-        in_specs=[smem, smem] + [vmem] * 6,
+            jax.ShapeDtypeStruct(term_shape, f32),
+        ),
+        in_specs=[smem] + [vmem] * (5 + groups),
         out_specs=[vmem, vmem],
-        scratch_shapes=sweep_scratch(coarse_total, coarse_count, px),
+        scratch_shapes=[pltpu.VMEM((groups, probes, px), f32)]
+        + sweep_scratch(coarse_total, coarse_count, px),
         compiler_params=params,
         name="coarse_sweep",
-    )(coarse_index, coarse_turns, coarse_recv, coarse_rows, coarse_sums, fine_far, transfer, all_probes)
-
-    far_field = far[:probes]
-    blocks = gram[:, :probes].reshape(groups, probes * probes)
-    blocks = blocks[(lax.axis_index("probe") - jnp.arange(groups)) % groups]
-    blocks = jnp.broadcast_to(blocks[None], (owners, groups, probes * probes))
-    blocks = blocks.reshape(owners * groups, 1, probes * probes)
-    blocks = lax.all_to_all(blocks, ("leaf", "probe"), split_axis=0, concat_axis=0, tiled=True)
-    total = jnp.sum(blocks.reshape(owners, groups, probes, probes), axis=0)
-    gram_scale = 1.0 / math.sqrt(owners * fine_count * 64)
-    probe_gram = total.transpose(1, 0, 2).reshape(probes, groups * probes) * gram_scale
-    return (far_field, probe_gram)
+    )(coarse_list, coarse_recv, coarse_rows, coarse_sums, fine_far, transfer, *turned)
+
+    terms = lax.all_to_all(terms, ("leaf", "probe"), split_axis=0, concat_axis=0, tiled=True)
+    probe_gram = pl.pallas_call(
+        functools.partial(
+            gram_kernel, groups=groups, scale=1.0 / math.sqrt(owners * fine_count * 64)
+        ),
+        out_shape=jax.ShapeDtypeStruct((probes, groups * probes), f32),
+        in_specs=[vmem],
+        out_specs=vmem,
+        name="gram_sum",
+    )(terms)
+    return (far[:probes], probe_gram)
 
 
 def solution(mesh):

time: 121 us -> 129 us (1.066); the launches traced: 123 us -> 127 us
  Pallas kernels: 73.8 us -> 89.6 us
  other arithmetic: 10.4 us -> 0 us
    pallas_call x1 -> x3, Pallas kernels: 20.2 us -> 31 us  [the longest x1 24.7 us: shards(): pl.pallas_call(functools.partial(coarse_kernel, groups), out_shape=(jax.S...]
    reduce_sum x5 -> x0, other arithmetic: 4.24 us -> none  [the longest x4 4.19 us: slot_list(): jnp.sum(jnp.where(moved, (slots - nothing)[:, :, None], 0), axis=1)]
    add x6 -> x0, other arithmetic: 2.8 us -> none  [the longest x4 2.43 us: slot_list(): nothing + jnp.sum(jnp.where(moved, (slots - nothing)[:, :, None], 0), axi...]
    pallas_call x1, Pallas kernels: 19.4 us -> 22.1 us  [shards(): pl.pallas_call(own_kernel, out_shape=(jax.ShapeDtypeStruct((px, points_fi...]
    pallas_call x1, Pallas kernels: 26.6 us -> 29 us  [shards(): pl.pallas_call(fine_kernel, out_shape=jax.ShapeDtypeStruct((px, points_fi...]
    max x4 -> x0, other arithmetic: 2.13 us -> none  [slot_list(): return (index, jnp.maximum(turns, 1))]
    reshape x4 -> x0, local copies, waits for them, and re-layouts: 1.88 us -> none  [the longest x1 0.84 us: shards(): blocks = gram[:, :probes].reshape(groups, probes * probes)]
    all_to_all x1, starting transfers between devices: 6.05 us -> 7.5 us  [shards(): lax.all_to_all(fine_send, 'leaf', split_axis=0, concat_axis=0, tiled=True)]
  transfers between devices with their start and end apart: 3 -> 3, of which waited for: 0 -> 0; matrix products, arithmetic and copies ran while one was open for 9% -> 2% of each run, Pallas kernels for 43% -> 47%
where the time goes in v7:
time: 129 us; the launch traced here: 127 us
  Pallas kernels  89.6 us (69%)
  blocking collectives  17.8 us (14%)
  starting transfers between devices  15.6 us (12%)
  local copies, waits for them, and re-layouts  3.62 us (3%)
    pallas_call x1, Pallas kernels, shards(): pl.pallas_call(fine_kernel, out_shape=jax.ShapeDtypeStruct((px, points_fi...  29 us
    pallas_call x1, Pallas kernels, shards(): pl.pallas_call(functools.partial(coarse_kernel, groups), out_shape=(jax.S...  24.7 us
    pallas_call x1, Pallas kernels, shards(): pl.pallas_call(own_kernel, out_shape=(jax.ShapeDtypeStruct((px, points_fi...  22.1 us
    all_to_all x1, blocking collectives, shards(): lax.all_to_all(terms, ('leaf', 'probe'), split_axis=0, concat_axis=0, til...  17.8 us
    all_to_all x1, starting transfers between devices, shards(): lax.all_to_all(fine_send, 'leaf', split_axis=0, concat_axis=0, tiled=True)  7.5 us
    all_to_all x1, starting transfers between devices, shards(): lax.all_to_all(coarse_send, 'leaf', split_axis=0, concat_axis=0, tiled=True)  6.47 us
    pallas_call x1, Pallas kernels, shards(): pl.pallas_call(functools.partial(list_slots_kernel, entries=(fine_total,...  4.65 us
    pallas_call x1, Pallas kernels, shards(): pl.pallas_call(pack_coarse_kernel, out_shape=(jax.ShapeDtypeStruct((owner...  4.17 us
  transfers between devices with their start and end apart: 3, of which 0 were waited for; matrix products, arithmetic and copies ran while one was open for 2% of the time, Pallas kernels for 47%

profile of v7, /device:TPU:0, one launch (start us, length us, event | category | flops | bytes accessed | tf_op | source)
XLA Modules:
  0.0 127.3 jit_solution(13876462074809570512)
XLA Ops:
  0.6 3.3 %pack_fine.1 = (bf16[16,320,128]{2,1,0:T(8,128)(2,1)}, f32[8,4096]{1,0:T(8,128)}) custom-call(s32[1,16,16]{2,1,0:T(8,128)} %send_ref.2, bf16[32,4096]{1,0:T(8,128)(2,1)} %refs_6_.1, f32[3,4096]{1,0:T(4,128)} %points_ref.3), custom_call_target="tpu_custom_call" | custom-call | tf_op jit(solution)/shard_map/pack_fine/pallas_call | solution.py:469
  3.9 0.0 copy-start.4
  3.9 0.0 copy-start.6
  3.9 0.0 copy-start.5
  3.9 7.5 %all-to-all-start.1 = ((bf16[16,320,128]{2,1,0:T(8,128)(2,1)}), bf16[16,320,128]{2,1,0:T(8,128)(2,1)S(1)}, u32[]{:S(2)}, u32[]{:S(2)}) async-start(bf16[16,320,128]{2,1,0:T(8,128)(2,1)} %get-tuple-element.24), calls=%async_computation.1 | async-start | bytes 2621440 | tf_op jit(solution)/shard_map/all_to_all | solution.py:484
  11.5 0.0 copy-done.4
  11.5 0.7 copy.14.send_ref
  12.1 0.0 copy-done.6
  12.1 0.7 copy.13.coarse_counts_ref
  12.8 0.0 copy-done.5
  12.8 0.7 copy.12.fine_counts_ref
  13.5 4.2 %pack_coarse.1 = (bf16[16,160,128]{2,1,0:T(8,128)(2,1)}, f32[8,2048]{1,0:T(8,128)}, bf16[32,2048]{1,0:T(8,128)(2,1)}) custom-call(s32[1,16,8]{2,1,0:T(8,128)} %copy.14.send_ref, bf16[32,4096]{1,0:T(8,128)(2,1)} %refs_6_.1, bf16[64,4096]{1,0:T(8,128)(2,1)} %refs_5_.1, f32[3,2048]{1,0:T(4,128)} %points_ref.2), custom_call_target="tpu_custom_call" | custom-call | tf_op jit(solution)/shard_map/pack_coarse/pallas_call | solution.py:486
  17.7 4.6 %list_slots.1 = (s32[64,256]{1,0:T(8,128)}, s32[32,256]{1,0:T(8,128)}) custom-call(s32[64,64]{1,0:T(8,128)} %fine_slots_ref.1, s32[64,1]{1,0:T(8,128)} %copy.12.fine_counts_ref, s32[32,64]{1,0:T(8,128)} %coarse_slots_ref.1, s32[32,1]{1,0:T(8,128)} %copy.13.coarse_counts_ref), custom_call_target="tpu_custom_call" | custom-call | tf_op jit(solution)/shard_map/list_slots/pallas_call | solution.py:504
  22.3 22.1 %own_sweep.1 = (f32[32,4096]{1,0:T(8,128)}, f32[32,2048]{1,0:T(8,128)}) custom-call(s32[64,256]{1,0:T(8,128)} %get-tuple-element.17.fine_list_ref.list_ref, s32[32,256]{1,0:T(8,128)} %get-tuple-element.15.coarse_list_ref.refs_0_, bf16[32,4096]{1,0:T(8,128)(2,1)} %refs_6_.1, f32[8,4096]{1,0:T(8,128)} %get-tuple-element.18.fine_rows_ref.rows_ref, ...), custom_call_target="tpu_custom_call" | custom-call | flops 10000000000 | bytes 10000000 | tf_op jit(solution)/shard_map/own_sweep/pallas_call | solution.py:515
  44.5 0.0 copy-start.2
  44.5 0.0 all-to-all-done.1.recv_ref
  44.5 0.0 copy-start
  44.5 6.5 %all-to-all-start = ((bf16[16,160,128]{2,1,0:T(8,128)(2,1)}), bf16[16,160,128]{2,1,0:T(8,128)(2,1)S(1)}, u32[]{:S(2)}, u32[]{:S(2)}) async-start(bf16[16,160,128]{2,1,0:T(8,128)(2,1)} %get-tuple-element.22), calls=%async_computation | async-start | bytes 1310720 | tf_op jit(solution)/shard_map/all_to_all | solution.py:530
  50.9 0.0 copy-done.2
  51.0 1.6 %collective-permute-start = (bf16[32,4096]{1,0:T(8,128)(2,1)S(1)}, bf16[32,4096]{1,0:T(8,128)(2,1)S(1)}, u32[]{:S(2)}, u32[]{:S(2)}) collective-permute-start(bf16[32,4096]{1,0:T(8,128)(2,1)S(1)} %copy-done.2), channel_id=1, source_target_pairs={{0,1},{1,0},{2,3},{3,2},{4,5},{5,4},{6,7},{7,6},{8,9},{9,8},{10,11... | collective-permute-start | bytes 786440 | tf_op jit(solution)/shard_map/ppermute | solution.py:467
  52.6 0.0 copy-done
  52.6 29.0 %fine_sweep.1.refs_4_ = f32[32,4096]{1,0:T(8,128)} custom-call(s32[64,256]{1,0:T(8,128)} %get-tuple-element.17.fine_list_ref.list_ref, bf16[16,320,128]{2,1,0:T(8,128)(2,1)} %copy-done, f32[8,4096]{1,0:T(8,128)} %get-tuple-element.18.fine_rows_ref.rows_ref, f32[32,4096]{1,0:T(8,128)} %get-tuple-element.25.own_ref), custom_call_target="tpu_custom_call" | custom-call | tf_op jit(solution)/shard_map/fine_sweep/pallas_call | solution.py:532
  81.5 0.0 collective-permute-done.refs_7_
  81.5 0.0 copy-start.3
  81.5 0.0 all-to-all-done.refs_1_
  81.5 0.7 copy-done.3
  82.2 0.0 copy-start.1
  82.2 0.8 copy-done.1
  83.1 24.7 %coarse_sweep.1 = (f32[32,4096]{1,0:T(8,128)}, f32[32,8,128]{2,1,0:T(8,128)}) custom-call(s32[32,256]{1,0:T(8,128)} %get-tuple-element.15.coarse_list_ref.refs_0_, bf16[16,160,128]{2,1,0:T(8,128)(2,1)} %copy-done.1, f32[8,2048]{1,0:T(8,128)} %get-tuple-element.20.coarse_rows_ref.refs_2_, f32[32,2048]{1,0:T(8,128)} %get-tuple-element.23.refs_3_, ...), custom_call_target="tpu_custom_call" | custom-call | tf_op jit(solution)/shard_map/coarse_sweep/pallas_call | solution.py:543
  107.8 17.8 %all_to_all.15.terms_ref = f32[32,8,128]{2,1,0:T(8,128)} all-to-all(f32[32,8,128]{2,1,0:T(8,128)} %get-tuple-element.27), channel_id=1, replica_groups=mesh['leaf'=16,'probe'=2] {'leaf','probe'}, dimensions={0} | all-to-all | bytes 262144 | tf_op jit(solution)/shard_map/all_to_all | solution.py:557
  125.6 1.7 %gram_sum.1 = f32[32,64]{1,0:T(8,128)} custom-call(f32[32,8,128]{2,1,0:T(8,128)} %all_to_all.15.terms_ref), custom_call_target="tpu_custom_call" | custom-call | tf_op jit(solution)/shard_map/gram_sum/pallas_call | solution.py:558
Async XLA Ops:
  3.9 7.5 %copy-start.4 = (s32[1,16,8]{1,2,0:T(8,128)S(1)}, s32[1,16,8]{1,2,0:T(8,128)}, u32[]{:S(2)}) copy-start(s32[1,16,8]{1,2,0:T(8,128)} %param.17) | copy-start | bytes 1540
  3.9 8.2 %copy-start.6 = (s32[32]{0:T(128)S(1)}, s32[32]{0:T(128)}, u32[]{:S(2)}) copy-start(s32[32]{0:T(128)} %param.19) | copy-start | bytes 388
  3.9 8.9 %copy-start.5 = (s32[64]{0:T(128)S(1)}, s32[64]{0:T(128)}, u32[]{:S(2)}) copy-start(s32[64]{0:T(128)} %param.16) | copy-start | bytes 772
  3.9 40.5 %all-to-all-start.1 = ((bf16[16,320,128]{2,1,0:T(8,128)(2,1)}), bf16[16,320,128]{2,1,0:T(8,128)(2,1)S(1)}, u32[]{:S(2)}, u32[]{:S(2)}) async-start(bf16[16,320,128]{2,1,0:T(8,128)(2,1)} %get-tuple-element.24), calls=%async_computation.1 | async-start | bytes 2621440 | tf_op jit(solution)/shard_map/all_to_all | solution.py:484
  44.5 6.5 %copy-start.2 = (bf16[32,4096]{1,0:T(8,128)(2,1)S(1)}, bf16[32,4096]{1,0:T(8,128)(2,1)}, u32[]{:S(2)}) copy-start(bf16[32,4096]{1,0:T(8,128)(2,1)} %refs_6_.1) | copy-start | bytes 786436
  44.5 8.1 %copy-start = (bf16[16,320,128]{2,1,0:T(8,128)(2,1)}, bf16[16,320,128]{2,1,0:T(8,128)(2,1)S(1)}, u32[]{:S(2)}) copy-start(bf16[16,320,128]{2,1,0:T(8,128)(2,1)S(1)} %all-to-all-done.1.recv_ref) | copy-start | bytes 3932164
  44.5 37.1 %all-to-all-start = ((bf16[16,160,128]{2,1,0:T(8,128)(2,1)}), bf16[16,160,128]{2,1,0:T(8,128)(2,1)S(1)}, u32[]{:S(2)}, u32[]{:S(2)}) async-start(bf16[16,160,128]{2,1,0:T(8,128)(2,1)} %get-tuple-element.22), calls=%async_computation | async-start | bytes 1310720 | tf_op jit(solution)/shard_map/all_to_all | solution.py:530
  51.0 30.6 %collective-permute-start = (bf16[32,4096]{1,0:T(8,128)(2,1)S(1)}, bf16[32,4096]{1,0:T(8,128)(2,1)S(1)}, u32[]{:S(2)}, u32[]{:S(2)}) collective-permute-start(bf16[32,4096]{1,0:T(8,128)(2,1)S(1)} %copy-done.2), channel_id=1, source_target_pairs={{0,1},{1,0},{2,3},{3,2},{4,5},{5,4},{6,7},{7,6},{8,9},{9,8},{10,11... | collective-permute-start | bytes 786440 | tf_op jit(solution)/shard_map/ppermute | solution.py:467
  81.5 0.7 copy-start.3
  82.2 0.8 copy-start.1

commit v8 on v7

--- a/solution.py
+++ b/solution.py
@@ -12,13 +12,13 @@
 KERNEL_RATE = 1.5
 POINT_SCALE = math.sqrt(2.0 * KERNEL_RATE)
 LANES = 128
-UNITS = 16
+UNITS = 8
 QUAD = 4
-CHUNK = 4
+CHUNK = 8
 FAR_AWAY = -30000.0
 SLOTS = 64
-TURNS = LANES - 1
-VMEM = 56 * 1024 * 1024
+RECEIVED = SLOTS + CHUNK
+SPARE = 6 * 1024 * 1024
 
 NT = (((1,), (1,)), ((), ()))
 NN = (((1,), (0,)), ((), ()))
@@ -61,40 +61,70 @@
     return pl.ds(pl.multiple_of(index * LANES, LANES), LANES)
 
 
-def list_slots(slots_ref, counts_ref, out_ref, entries):
-    clusters, width = slots_ref.shape
-    slots = slots_ref[...]
-    place = lax.broadcasted_iota(jnp.int32, slots.shape, 1)
-    live = place < counts_ref[...]
+def list_slots_kernel(
+    fine_slots_ref, fine_counts_ref, coarse_slots_ref, coarse_counts_ref, out_ref, *units_refs, entries
+):
+    fine, coarse = fine_slots_ref.shape[0], coarse_slots_ref.shape[0]
+    spare = LANES - fine - coarse
+    slots = jnp.concatenate(
+        [fine_slots_ref[...], coarse_slots_ref[...], jnp.zeros((spare, SLOTS), jnp.int32)], axis=0
+    )
+    slots = slots.astype(jnp.float32).T.astype(jnp.int32)
+    counts = jnp.concatenate(
+        [fine_counts_ref[...], coarse_counts_ref[...], jnp.zeros((1, spare), jnp.int32)], axis=1
+    )
+    shape = (SLOTS, LANES)
+    in_fine = lax.broadcasted_iota(jnp.int32, shape, 1) < fine
+    clusters = jnp.where(in_fine, fine, coarse)
+    nothing = jnp.where(in_fine, entries[0], entries[1])
+    live = lax.broadcasted_iota(jnp.int32, shape, 0) < counts
     own = live & (slots < clusters)
     received = live & (slots >= clusters)
-    row = lax.broadcasted_iota(jnp.int32, (width, width), 0)
-    column = lax.broadcasted_iota(jnp.int32, (width, width), 1)
-    upto = jnp.where(row <= column, 1.0, 0.0).astype(jnp.bfloat16)
-    rank = [
-        bdot(jnp.where(chosen, 1.0, 0.0).astype(jnp.bfloat16), upto, NN).astype(jnp.int32)
-        for chosen in (own, received)
-    ]
-    spot = jnp.where(own, rank[0] - 1, jnp.where(received, rank[1] + (LANES - 1), -1))
-    value = jnp.where(own, slots - clusters, slots - clusters - entries)
-    lane = lax.broadcasted_iota(jnp.int32, (clusters, 2 * LANES), 1)
-    table = jnp.where(lane < LANES, clusters, entries)
-    for m in range(width):
-        table = table + jnp.where(lane == spot[:, m:m + 1], value[:, m:m + 1], 0)
+    row = lax.broadcasted_iota(jnp.int32, (SLOTS, SLOTS), 0)
+    column = lax.broadcasted_iota(jnp.int32, (SLOTS, SLOTS), 1)
+    upto = jnp.where(column <= row, 1.0, 0.0).astype(jnp.bfloat16)
+    turns = []
+    for start, chosen, value, blank in (
+        (0, own, slots, clusters),
+        (RECEIVED, received, slots - clusters, nothing),
+    ):
+        rank = bdot(upto, jnp.where(chosen, 1.0, 0.0).astype(jnp.bfloat16), NN).astype(jnp.int32)
+        spot = jnp.where(chosen, rank - 1, -1)
+        value = value - blank
+        for first in range(0, SLOTS, 8):
+            rows = [
+                blank[:1] + jnp.sum(jnp.where(spot == place, value, 0), axis=0, keepdims=True)
+                for place in range(first, first + 8)
+            ]
+            out_ref[start + first:start + first + 8] = jnp.concatenate(rows, axis=0)
+        out_ref[start + SLOTS:start + SLOTS + CHUNK] = jnp.broadcast_to(blank[:1], (CHUNK, LANES))
+        turns.append(jnp.maximum((rank[SLOTS - 1:] + CHUNK - 1) // CHUNK, 1))
+    turns = jnp.concatenate(turns + [jnp.zeros((6, LANES), jnp.int32)], axis=0).astype(jnp.float32).T
+    row = lax.broadcasted_iota(jnp.int32, (LANES, LANES), 0)
+    column = lax.broadcasted_iota(jnp.int32, (LANES, LANES), 1)
+    upto = (column <= row) & ((row < fine) == (column < fine))
+    ends = bdot(jnp.where(upto, 1.0, 0.0).astype(jnp.bfloat16), turns.astype(jnp.bfloat16), NN)
+    ends, turns = ends.astype(jnp.int32), turns.astype(jnp.int32)
     for side in range(2):
-        turns = jnp.maximum((rank[side][:, width - 1:] + CHUNK - 1) // CHUNK, 1)
-        table = jnp.where(lane == side * LANES + TURNS, turns, table)
-    out_ref[...] = table
-
-
-def list_slots_kernel(
-    fine_slots_ref, fine_counts_ref, coarse_slots_ref, coarse_counts_ref, fine_out_ref, coarse_out_ref, *, entries
-):
-    list_slots(fine_slots_ref, fine_counts_ref, fine_out_ref, entries[0])
-    list_slots(coarse_slots_ref, coarse_counts_ref, coarse_out_ref, entries[1])
-
-
-def pack_send(send_ref, out_ref, dup_coef, dup_rows, owners, capacity, px):
+        for level, (low, count) in enumerate(((0, fine), (fine, coarse))):
+            units_ref = units_refs[2 * side + level]
+            end = ends[low:low + count, side:side + 1]
+            took = turns[low:low + count, side:side + 1]
+            lane = lax.broadcasted_iota(jnp.int32, (1, LANES), 1)
+            for tile in range(units_ref.shape[0]):
+                place = tile * LANES + lane
+                passed = end <= place
+                target = jnp.sum(jnp.where(passed, 1, 0), axis=0, keepdims=True)
+                turn = place - jnp.sum(jnp.where(passed, took, 0), axis=0, keepdims=True)
+                over = target >= count
+                start = side * RECEIVED + jnp.where(over, SLOTS, turn * CHUNK)
+                code = start * LANES + low + jnp.where(over, count - 1, target)
+                if tile == units_ref.shape[0] - 1:
+                    code = jnp.where(lane == LANES - 1, end[count - 1:], code)
+                units_ref[tile:tile + 1] = code
+
+
+def pack_send(send_ref, out_ref, dup_coef, dup_rows, owners, capacity, px, entry_first=False):
     pairs = capacity // 2
     lane = lax.broadcasted_iota(jnp.int32, (px, LANES), 1) < LANES // 2
     lane8 = lax.broadcasted_iota(jnp.int32, (8, LANES), 1) < LANES // 2
@@ -102,8 +132,10 @@
     def one_owner(owner, carry):
         before = None
         for pair in range(pairs):
-            first = send_ref[0, owner, 2 * pair]
-            second = send_ref[0, owner, 2 * pair + 1]
+            first, second = [
+                send_ref[0, entry, owner] if entry_first else send_ref[0, owner, entry]
+                for entry in (2 * pair, 2 * pair + 1)
+            ]
             out_ref[owner, pair * px:(pair + 1) * px, :] = jnp.where(
                 lane, dup_coef[first], dup_coef[second]
             ).astype(jnp.bfloat16)
@@ -141,7 +173,7 @@
 def pack_coarse_kernel(
     send_ref, coef_ref, transfer_ref, points_ref, out_ref, rows_ref, coarse_ref, dup_coef, dup_rows
 ):
-    _, owners, capacity = send_ref.shape
+    _, capacity, owners = send_ref.shape
     px = coef_ref.shape[0]
     rows_ref[...] = split_rows(points_ref[...])
 
@@ -162,7 +194,7 @@
         return carry
 
     lax.fori_loop(0, coef_ref.shape[1] // (2 * LANES), one_tile, 0, unroll=2)
-    pack_send(send_ref, out_ref, dup_coef, dup_rows, owners, capacity, px)
+    pack_send(send_ref, out_ref, dup_coef, dup_rows, owners, capacity, px, entry_first=True)
 
 
 def turned(rows):
@@ -176,7 +208,7 @@
     a, b = halves(coef.astype(jnp.float32))
     coef_table[entry] = a.astype(jnp.bfloat16)
     coef_table[entry + 1] = b.astype(jnp.bfloat16)
-    features = turned(jnp.concatenate([source_features(rows).astype(jnp.bfloat16)] * 8, axis=0))
+    features = turned(jnp.concatenate([source_features(rows).astype(jnp.bfloat16)] * QUAD, axis=0))
     feature_table[entry] = features[:64]
     feature_table[entry + 1] = features[64:]
 
@@ -185,7 +217,7 @@
     coef_table[entry] = jnp.zeros(coef_table.shape[1:], jnp.bfloat16)
     place = lax.broadcasted_iota(jnp.int32, (8, LANES), 0)
     nothing = source_features(jnp.where(place == 3, FAR_AWAY, 0.0)).astype(jnp.bfloat16)
-    feature_table[entry] = turned(jnp.concatenate([nothing] * 8, axis=0))[:64]
+    feature_table[entry] = turned(jnp.concatenate([nothing] * QUAD, axis=0))[:64]
 
 
 def build_own(coef_ref, rows_ref, coef_table, feature_table):
@@ -234,26 +266,28 @@
     lax.fori_loop(0, rows_ref.shape[1] // LANES, one_tile, 0, unroll=4)
 
 
-def sweep(index_ref, base, coef_table, feature_table, target_table, first_buffer, second_buffer, acc):
-    clusters = index_ref.shape[0]
+def sweep(list_ref, units_ref, first, coef_table, feature_table, target_table, first_buffer, second_buffer, acc):
     px = coef_table.shape[1]
-    slots_end = SLOTS // CHUNK
-    lane = lax.broadcasted_iota(jnp.int32, (64, LANES), 1) // 16
+    lane = lax.broadcasted_iota(jnp.int32, (64, 16 * QUAD), 1) // 16
     lane_t = lax.broadcasted_iota(jnp.int32, (16, LANES), 1) // 64
     lane_x = lax.broadcasted_iota(jnp.int32, (px, LANES), 1) < 64
     blank = jnp.zeros((16, LANES), jnp.bfloat16)
     acc[...] = jnp.zeros_like(acc)
 
     def partners(unit):
-        target, turn = unit
-        return [index_ref[target, base + turn * CHUNK + m] for m in range(CHUNK)]
+        row, column = unit
+        return [list_ref[row + m, column] for m in range(CHUNK)]
+
+    def units_of(place):
+        codes = [units_ref[place >> 7, (place & (LANES - 1)) + u] for u in range(UNITS)]
+        return [(code >> 7, code & (LANES - 1)) for code in codes]
 
     def tiles(units, buffer):
         for start in range(0, UNITS, QUAD):
             quad = units[start:start + QUAD]
             weights = []
             for u in range(QUAD):
-                own = jnp.where(lane_t == u % 2, target_table[quad[u][0]], blank)
+                own = jnp.where(lane_t == u % 2, target_table[quad[u][1] - first], blank)
                 weights.append(jnp.concatenate([own if v == u // 2 else blank for v in range(QUAD // 2)], axis=1))
             weights = jnp.concatenate(weights, axis=0)
             ids = [partners(unit) for unit in quad]
@@ -263,7 +297,7 @@
                     tile = feature_table[ids[0][m]]
                     for u in range(1, QUAD):
                         tile = jnp.where(lane == u, feature_table[ids[u][m]], tile)
-                    rows.append(tile[:, :16 * QUAD])
+                    rows.append(tile)
                 power = bdot(jnp.concatenate(rows, axis=0), weights, NN)
                 buffer[start // QUAD, part * 64:(part + 4) * 64] = jnp.exp(power).astype(jnp.bfloat16)
 
@@ -285,37 +319,20 @@
             product = bdot(jnp.concatenate(coefs, axis=0), buffer[start // QUAD], NN)
             for u in range(QUAD):
                 side = (u // 2) * LANES
-                acc[u % 2, quad[u][0]] += product[u * px:(u + 1) * px, side:side + LANES]
-
-    def following(unit):
-        target, turn = unit
-        over = turn + 1 >= index_ref[target, base + TURNS]
-        later = jnp.where(over, target + 1, target)
-        end = later >= clusters
-        turn = jnp.where(end, slots_end, jnp.where(over, 0, turn + 1))
-        return jnp.minimum(later, clusters - 1), turn
-
-    def next_units(unit):
-        units = []
-        for _ in range(UNITS):
-            unit = following(unit)
-            units.append(unit)
-        return tuple(units)
-
-    def two_sets(_, units):
-        second = next_units(units[-1])
-        third = next_units(second[-1])
+                acc[u % 2, quad[u][1] - first] += product[u * px:(u + 1) * px, side:side + LANES]
+
+    def two_sets(index, carry):
+        here = index * (2 * UNITS)
+        second = units_of(here + UNITS)
         tiles(second, second_buffer)
-        products(units, first_buffer)
-        tiles(third, first_buffer)
+        products(units_of(here), first_buffer)
+        tiles(units_of(here + 2 * UNITS), first_buffer)
         products(second, second_buffer)
-        return third
-
-    total = lax.fori_loop(0, clusters, lambda c, n: n + index_ref[c, base + TURNS], jnp.int32(0))
-    unit = (jnp.int32(0), jnp.int32(0))
-    start = (unit,) + next_units(unit)[:-1]
-    tiles(start, first_buffer)
-    lax.fori_loop(0, (total + 2 * UNITS - 1) // (2 * UNITS), two_sets, start)
+        return carry
+
+    total = units_ref[units_ref.shape[0] - 1, LANES - 1]
+    tiles(units_of(0), first_buffer)
+    lax.fori_loop(0, (total + 2 * UNITS - 1) // (2 * UNITS), two_sets, 0)
 
 
 def summed(acc, target):
@@ -337,8 +354,9 @@
 
 
 def own_kernel(
-    fine_list_ref,
-    coarse_list_ref,
+    list_ref,
+    fine_units_ref,
+    coarse_units_ref,
     fine_coef_ref,
     fine_rows_ref,
     coarse_coef_ref,
@@ -347,33 +365,37 @@
     coarse_out_ref,
     *scratch,
 ):
-    for list_ref, coef_ref, rows_ref, out_ref in (
-        (fine_list_ref, fine_coef_ref, fine_rows_ref, fine_out_ref),
-        (coarse_list_ref, coarse_coef_ref, coarse_rows_ref, coarse_out_ref),
+    first = 0
+    for units_ref, coef_ref, rows_ref, out_ref in (
+        (fine_units_ref, fine_coef_ref, fine_rows_ref, fine_out_ref),
+        (coarse_units_ref, coarse_coef_ref, coarse_rows_ref, coarse_out_ref),
     ):
+        clusters = rows_ref.shape[1] // 64
         build_own(coef_ref, rows_ref, *scratch[:2])
         build_targets(rows_ref, scratch[2])
-        sweep(list_ref, 0, *scratch)
-        put_sums(scratch[-1], list_ref.shape[0], out_ref)
-
-
-def fine_kernel(list_ref, recv_ref, rows_ref, own_ref, out_ref, *scratch):
+        sweep(list_ref, units_ref, first, *scratch)
+        put_sums(scratch[-1], clusters, out_ref)
+        first += clusters
+
+
+def fine_kernel(list_ref, units_ref, recv_ref, rows_ref, own_ref, out_ref, *scratch):
     build_received(recv_ref, *scratch[:2])
     build_targets(rows_ref, scratch[2])
-    sweep(list_ref, LANES, *scratch)
-    put_sums(scratch[-1], list_ref.shape[0], out_ref, own_ref)
+    sweep(list_ref, units_ref, 0, *scratch)
+    put_sums(scratch[-1], rows_ref.shape[1] // 64, out_ref, own_ref)
 
 
 def coarse_kernel(groups, *refs):
-    list_ref, recv_ref, rows_ref, own_ref, fine_ref, transfer_ref = refs[:6]
-    probes_refs = refs[6:6 + groups]
-    out_ref, terms_ref = refs[6 + groups:8 + groups]
-    gram_ref, *scratch = refs[8 + groups:]
+    list_ref, units_ref, recv_ref, rows_ref, own_ref, fine_ref, transfer_ref = refs[:7]
+    probes_refs = refs[7:7 + groups]
+    out_ref, terms_ref = refs[7 + groups:9 + groups]
+    gram_ref, *scratch = refs[9 + groups:]
+    clusters = rows_ref.shape[1] // 64
     probes = probes_refs[0].shape[0]
     acc = scratch[-1]
     build_received(recv_ref, *scratch[:2])
     build_targets(rows_ref, scratch[2])
-    sweep(list_ref, LANES, *scratch)
+    sweep(list_ref, units_ref, fine_ref.shape[1] // 64, *scratch)
     gram_ref[...] = jnp.zeros_like(gram_ref)
 
     def one_group(group, carry):
@@ -399,7 +421,7 @@
             gram_ref[block] += grams[block]
         return carry
 
-    lax.fori_loop(0, list_ref.shape[0] // 4, one_group, 0)
+    lax.fori_loop(0, clusters // 4, one_group, 0)
     place = lax.axis_index("probe")
     for b in range(groups):
         block = gram_ref[lax.rem(place - b + groups, groups)]
@@ -428,7 +450,7 @@
 def sweep_scratch(total, clusters, px):
     return [
         pltpu.VMEM((total + 1, px, LANES), jnp.bfloat16),
-        pltpu.VMEM((total + 1, 64, LANES), jnp.bfloat16),
+        pltpu.VMEM((total + 1, 64, 16 * QUAD), jnp.bfloat16),
         pltpu.VMEM((clusters, 16, LANES), jnp.bfloat16),
         pltpu.VMEM((UNITS // QUAD, CHUNK * 64, QUAD * 64), jnp.bfloat16),
         pltpu.VMEM((UNITS // QUAD, CHUNK * 64, QUAD * 64), jnp.bfloat16),
@@ -457,7 +479,24 @@
     coef = coef_fine if px == probes else jnp.pad(coef_fine, ((0, px - probes), (0, 0)))
     cap_fine = send_fine.shape[2]
     cap_coarse = send_coarse.shape[2]
-    params = pltpu.CompilerParams(vmem_limit_bytes=VMEM)
+
+    def params(scratch, blocks):
+        size = SPARE + blocks * px * points_fine.shape[1] * 4
+        for ref in scratch:
+            size += math.prod(ref.shape[:-1]) * -(-ref.shape[-1] // LANES) * LANES * ref.dtype.itemsize
+        return pltpu.CompilerParams(vmem_limit_bytes=size)
+
+    fine_pack = [
+        pltpu.VMEM((fine_count, px, LANES), jnp.float32),
+        pltpu.VMEM((fine_count, 8, LANES), jnp.float32),
+    ]
+    coarse_pack = [
+        pltpu.VMEM((coarse_count, px, LANES), jnp.float32),
+        pltpu.VMEM((coarse_count, 8, LANES), jnp.float32),
+    ]
+    own_scratch = sweep_scratch(fine_count, fine_count, px)
+    fine_scratch = sweep_scratch(owners * cap_fine, fine_count, px)
+    coarse_scratch = sweep_scratch(owners * cap_coarse, coarse_count, px)
     smem = pl.BlockSpec(memory_space=pltpu.SMEM)
     vmem = pl.BlockSpec(memory_space=pltpu.VMEM)
     bf16, f32 = jnp.bfloat16, jnp.float32
@@ -474,11 +513,8 @@
         ),
         in_specs=[smem, vmem, vmem],
         out_specs=[vmem, vmem],
-        scratch_shapes=[
-            pltpu.VMEM((fine_count, px, LANES), f32),
-            pltpu.VMEM((fine_count, 8, LANES), f32),
-        ],
-        compiler_params=params,
+        scratch_shapes=fine_pack,
+        compiler_params=params(fine_pack, owners // 4),
         name="pack_fine",
     )(send_fine, coef, points_fine)
     fine_recv = lax.all_to_all(fine_send, "leaf", split_axis=0, concat_axis=0, tiled=True)
@@ -492,39 +528,34 @@
         ),
         in_specs=[smem, vmem, vmem, vmem],
         out_specs=[vmem, vmem, vmem],
-        scratch_shapes=[
-            pltpu.VMEM((coarse_count, px, LANES), f32),
-            pltpu.VMEM((coarse_count, 8, LANES), f32),
-        ],
-        compiler_params=params,
+        scratch_shapes=coarse_pack,
+        compiler_params=params(coarse_pack, owners // 4),
         name="pack_coarse",
-    )(send_coarse, coef, transfer, points_coarse)
+    )(jnp.swapaxes(send_coarse, 1, 2), coef, transfer, points_coarse)
     fine_total = owners * cap_fine
     coarse_total = owners * cap_coarse
-    fine_list, coarse_list = pl.pallas_call(
+    unit_rows = [-(-(count * (SLOTS // CHUNK) + 2 * UNITS + 1) // LANES) for count in (fine_count, coarse_count)]
+    slot_list, fine_own, coarse_own, fine_units, coarse_units = pl.pallas_call(
         functools.partial(list_slots_kernel, entries=(fine_total, coarse_total)),
-        out_shape=(
-            jax.ShapeDtypeStruct((fine_count, 2 * LANES), jnp.int32),
-            jax.ShapeDtypeStruct((coarse_count, 2 * LANES), jnp.int32),
-        ),
+        out_shape=[jax.ShapeDtypeStruct((RECEIVED + SLOTS + CHUNK, LANES), jnp.int32)]
+        + [jax.ShapeDtypeStruct((rows, LANES), jnp.int32) for rows in unit_rows * 2],
         in_specs=[vmem] * 4,
-        out_specs=[vmem, vmem],
-        compiler_params=params,
+        out_specs=[vmem] * 5,
         name="list_slots",
-    )(slots_fine, counts_fine[:, None], slots_coarse, counts_coarse[:, None])
+    )(slots_fine, counts_fine.reshape(1, -1), slots_coarse, counts_coarse.reshape(1, -1))
     fine_sums, coarse_sums = pl.pallas_call(
         own_kernel,
         out_shape=(
             jax.ShapeDtypeStruct((px, points_fine.shape[1]), f32),
             jax.ShapeDtypeStruct((px, points_coarse.shape[1]), f32),
         ),
-        in_specs=[smem] * 2 + [vmem] * 4,
+        in_specs=[smem] * 3 + [vmem] * 4,
         out_specs=[vmem, vmem],
-        scratch_shapes=sweep_scratch(fine_count, fine_count, px),
-        compiler_params=params,
+        scratch_shapes=own_scratch,
+        compiler_params=params(own_scratch, 4),
         cost_estimate=pl.CostEstimate(flops=10**10, bytes_accessed=10**7, transcendentals=10**7),
         name="own_sweep",
-    )(fine_list, coarse_list, coef, fine_rows, coarse_coef, coarse_rows)
+    )(slot_list, fine_own, coarse_own, coef, fine_rows, coarse_coef, coarse_rows)
 
     coarse_send, coarse_sums = lax.optimization_barrier((coarse_send, coarse_sums))
     coarse_recv = lax.all_to_all(coarse_send, "leaf", split_axis=0, concat_axis=0, tiled=True)
@@ -532,12 +563,12 @@
     fine_far = pl.pallas_call(
         fine_kernel,
         out_shape=jax.ShapeDtypeStruct((px, points_fine.shape[1]), f32),
-        in_specs=[smem, vmem, vmem, vmem],
+        in_specs=[smem] * 2 + [vmem] * 3,
         out_specs=vmem,
-        scratch_shapes=sweep_scratch(fine_total, fine_count, px),
-        compiler_params=params,
+        scratch_shapes=fine_scratch,
+        compiler_params=params(fine_scratch, owners // 4 + 4),
         name="fine_sweep",
-    )(fine_list, fine_recv, fine_rows, fine_sums)
+    )(slot_list, fine_units, fine_recv, fine_rows, fine_sums)
 
     term_shape = (owners * groups, 8, probes * probes // 8)
     far, terms = pl.pallas_call(
@@ -546,13 +577,12 @@
             jax.ShapeDtypeStruct((px, points_fine.shape[1]), f32),
             jax.ShapeDtypeStruct(term_shape, f32),
         ),
-        in_specs=[smem] + [vmem] * (5 + groups),
+        in_specs=[smem] * 2 + [vmem] * (5 + groups),
         out_specs=[vmem, vmem],
-        scratch_shapes=[pltpu.VMEM((groups, probes, px), f32)]
-        + sweep_scratch(coarse_total, coarse_count, px),
-        compiler_params=params,
+        scratch_shapes=[pltpu.VMEM((groups, probes, px), f32)] + coarse_scratch,
+        compiler_params=params(coarse_scratch, owners // 4 + 6),
         name="coarse_sweep",
-    )(coarse_list, coarse_recv, coarse_rows, coarse_sums, fine_far, transfer, *turned)
+    )(slot_list, coarse_units, coarse_recv, coarse_rows, coarse_sums, fine_far, transfer, *turned)
 
     terms = lax.all_to_all(terms, ("leaf", "probe"), split_axis=0, concat_axis=0, tiled=True)
     probe_gram = pl.pallas_call(

time: 129 us -> 115 us (0.89)
  Pallas kernels: 89.6 us -> 68.6 us
  local copies, waits for them, and re-layouts: 3.62 us -> 9.88 us
  starting transfers between devices: 15.6 us -> 17.1 us
    pallas_call x1, Pallas kernels: 24.7 us -> 17 us  [shards(): pl.pallas_call(functools.partial(coarse_kernel, groups), out_shape=(jax.S...]
    unnamed x15 -> x38, local copies, waits for them, and re-layouts: 2.22 us -> 9.88 us
    pallas_call x1, Pallas kernels: 29 us -> 23.7 us  [shards(): pl.pallas_call(fine_kernel, out_shape=jax.ShapeDtypeStruct((px, points_fi...]
    pallas_call x1, Pallas kernels: 22.1 us -> 17.3 us  [shards(): pl.pallas_call(own_kernel, out_shape=(jax.ShapeDtypeStruct((px, points_fi...]
    pallas_call x1, Pallas kernels: 4.65 us -> 2.36 us  [shards(): pl.pallas_call(functools.partial(list_slots_kernel, entries=(fine_total,...]
    all_to_all x1, starting transfers between devices: 6.47 us -> 8.01 us  [shards(): lax.all_to_all(coarse_send, 'leaf', split_axis=0, concat_axis=0, tiled=True)]
    broadcast_in_dim x2 -> x0, local copies, waits for them, and re-layouts: 1.4 us -> none  [the longest x1 0.71 us: shards(): counts_fine[:, None]]
  transfers between devices with their start and end apart: 3 -> 3, of which waited for: 0 -> 1; matrix products, arithmetic and copies ran while one was open for 2% -> 0% of each run, Pallas kernels for 47% -> 41%
where the time goes in v8:
time: 115 us; the launch traced here: 114 us
  Pallas kernels  68.6 us (60%)
  blocking collectives  17.8 us (15%)
  starting transfers between devices  17.1 us (15%)
  local copies, waits for them, and re-layouts  9.88 us (9%)
    pallas_call x1, Pallas kernels, shards(): pl.pallas_call(fine_kernel, out_shape=jax.ShapeDtypeStruct((px, points_fi...  23.7 us
    all_to_all x1, blocking collectives, shards(): lax.all_to_all(terms, ('leaf', 'probe'), split_axis=0, concat_axis=0, til...  17.8 us
    pallas_call x1, Pallas kernels, shards(): pl.pallas_call(own_kernel, out_shape=(jax.ShapeDtypeStruct((px, points_fi...  17.3 us
    pallas_call x1, Pallas kernels, shards(): pl.pallas_call(functools.partial(coarse_kernel, groups), out_shape=(jax.S...  17 us
    unnamed x38, local copies, waits for them, and re-layouts  9.88 us
    all_to_all x1, starting transfers between devices, shards(): lax.all_to_all(coarse_send, 'leaf', split_axis=0, concat_axis=0, tiled=True)  8.01 us
    all_to_all x1, starting transfers between devices, shards(): lax.all_to_all(fine_send, 'leaf', split_axis=0, concat_axis=0, tiled=True)  7.5 us
    pallas_call x1, Pallas kernels, shards(): pl.pallas_call(pack_coarse_kernel, out_shape=(jax.ShapeDtypeStruct((owner...  3.62 us
  transfers between devices with their start and end apart: 3, of which 1 were waited for; matrix products, arithmetic and copies ran while one was open for 0% of the time, Pallas kernels for 41%

profile of v8, /device:TPU:0, one launch (start us, length us, event | category | flops | bytes accessed | tf_op | source)
XLA Modules:
  0.0 114.5 jit_solution(13854762142115485507)
XLA Ops:
  0.6 0.0 copy-start
  0.6 0.9 copy-done
  1.6 0.0 copy-start.11
  1.6 0.8 copy-done.11
  2.4 0.0 copy-start.13
  2.4 0.7 copy-done.13
  3.1 3.0 %pack_fine.1 = (bf16[16,320,128]{2,1,0:T(8,128)(2,1)}, f32[8,4096]{1,0:T(8,128)S(1)}) custom-call(s32[1,16,16]{2,1,0:T(8,128)S(1)} %copy-done.13, bf16[32,4096]{1,0:T(8,128)(2,1)S(1)} %copy-done, f32[3,4096]{1,0:T(4,128)S(1)} %copy-done.11), custom_call_target="tpu_custom_call" | custom-call | tf_op jit(solution)/shard_map/pack_fine/pallas_call | solution.py:508
  6.1 0.0 copy-start.1
  6.1 0.0 copy-start.2
  6.1 0.0 copy-start.12
  6.1 0.0 copy-start.14
  6.1 7.5 %all-to-all-start.1 = ((bf16[16,320,128]{2,1,0:T(8,128)(2,1)}), bf16[16,320,128]{2,1,0:T(8,128)(2,1)S(1)}, u32[]{:S(2)}, u32[]{:S(2)}) async-start(bf16[16,320,128]{2,1,0:T(8,128)(2,1)} %get-tuple-element.30), calls=%async_computation.1 | async-start | bytes 2621440 | tf_op jit(solution)/shard_map/all_to_all | solution.py:520
  13.6 0.0 copy-done.1
  13.6 0.0 copy-done.2
  13.6 0.0 copy-done.12
  13.6 0.0 copy-done.14
  13.7 3.6 %pack_coarse.1 = (bf16[16,160,128]{2,1,0:T(8,128)(2,1)}, f32[8,2048]{1,0:T(8,128)S(1)}, bf16[32,2048]{1,0:T(8,128)(2,1)S(1)}) custom-call(s32[1,8,16]{2,1,0:T(8,128)S(1)} %bitcast.3, bf16[32,4096]{1,0:T(8,128)(2,1)S(1)} %copy-done.1, bf16[64,4096]{1,0:T(8,128)(2,1)S(1)} %copy-done.2, f32[3,2048]{1,0:T(4,128)S(1)} %copy-done.12), custom_call_target="tpu_custom_call" | custom-call | tf_op jit(solution)/shard_map/pack_coarse/pallas_call | solution.py:522
  17.3 2.4 %list_slots.1 = (s32[144,128]{1,0:T(8,128)}, s32[5,128]{1,0:T(8,128)}, s32[3,128]{1,0:T(4,128)}, s32[5,128]{1,0:T(8,128)}, s32[3,128]{1,0:T(4,128)}) custom-call(s32[64,64]{1,0:T(8,128)} %fine_slots_ref.1, s32[1,64]{1,0:T(1,128)} %bitcast.4, s32[32,64]{1,0:T(8,128)} %coarse_slots_ref.1, s32[1,32]{1,0:T(1,128)} %bitcast.5), custom_call_target="tpu_custom_call" | custom-call | tf_op jit(solution)/shard_map/list_slots/pallas_call | solution.py:538
  19.6 0.0 copy-start.5
  19.6 0.9 copy-done.5
  20.5 0.0 copy-start.17
  20.5 0.7 copy-done.17
  21.2 0.0 copy-start.18
  21.2 0.7 copy-done.18
  21.9 17.3 %own_sweep.1 = (f32[32,4096]{1,0:T(8,128)S(1)}, f32[32,2048]{1,0:T(8,128)S(1)}) custom-call(s32[144,128]{1,0:T(8,128)S(1)} %copy-done.5, s32[5,128]{1,0:T(8,128)S(1)} %copy-done.17, s32[3,128]{1,0:T(4,128)S(1)} %copy-done.18, bf16[32,4096]{1,0:T(8,128)(2,1)S(1)} %copy-done.1, f32[8,4096]{1,0:T(8,128)S(1)} %get-tuple-element.23.fine_rows_ref.rows_ref, ...), custom_call_target="tpu_custom_call" | custom-call | flops 10000000000 | bytes 10000000 | tf_op jit(solution)/shard_map/own_sweep/pallas_call | solution.py:546
  39.2 0.0 copy-start.3
  39.2 0.8 copy-done.3
  40.0 0.0 copy-start.7
  40.0 0.7 copy-done.7
  40.7 0.0 copy-start.6
  40.7 0.0 copy-start.15
  40.7 0.3 all-to-all-done.1.recv_ref
  41.0 8.0 %all-to-all-start = ((bf16[16,160,128]{2,1,0:T(8,128)(2,1)}), bf16[16,160,128]{2,1,0:T(8,128)(2,1)S(1)}, u32[]{:S(2)}, u32[]{:S(2)}) async-start(bf16[16,160,128]{2,1,0:T(8,128)(2,1)} %get-tuple-element.27), calls=%async_computation | async-start | bytes 1310720 | tf_op jit(solution)/shard_map/all_to_all | solution.py:561
  49.0 0.0 copy-start.16
  49.1 1.6 %collective-permute-start = (bf16[32,4096]{1,0:T(8,128)(2,1)S(1)}, bf16[32,4096]{1,0:T(8,128)(2,1)S(1)}, u32[]{:S(2)}, u32[]{:S(2)}) collective-permute-start(bf16[32,4096]{1,0:T(8,128)(2,1)S(1)} %copy-done.1), channel_id=1, source_target_pairs={{0,1},{1,0},{2,3},{3,2},{4,5},{5,4},{6,7},{7,6},{8,9},{9,8},{10,11... | collective-permute-start | bytes 786440 | tf_op jit(solution)/shard_map/ppermute | solution.py:506
  50.6 0.0 copy-done.6
  50.6 0.0 copy-done.15
  50.7 0.0 copy-start.4
  50.7 1.0 copy-done.4
  51.7 23.7 %fine_sweep.1.refs_5_ = f32[32,4096]{1,0:T(8,128)S(1)} custom-call(s32[144,128]{1,0:T(8,128)S(1)} %copy-done.6, s32[5,128]{1,0:T(8,128)S(1)} %copy-done.15, bf16[16,320,128]{2,1,0:T(8,128)(2,1)S(1)} %all-to-all-done.1.recv_ref, f32[8,4096]{1,0:T(8,128)S(1)} %get-tuple-element.23.fine_rows_ref.rows_ref, f32[32,4096]{1,0:T(8,128)S(1)} %copy-done.4), custom_call_target="tpu_custom_call" | custom-call | tf_op jit(solution)/shard_map/fine_sweep/pallas_call | solution.py:563
  75.4 0.0 collective-permute-done.refs_8_
  75.4 0.0 copy-start.9
  75.4 0.7 copy-done.9
  76.1 0.0 all-to-all-done.refs_2_
  76.1 0.0 copy-done.16
  76.1 0.0 copy-start.8
  76.1 0.9 copy-done.8
  77.1 0.0 copy-start.10
  77.1 0.9 copy-done.10
  78.0 17.0 %coarse_sweep.1 = (f32[32,4096]{1,0:T(8,128)}, f32[32,8,128]{2,1,0:T(8,128)S(1)}) custom-call(s32[144,128]{1,0:T(8,128)S(1)} %copy-done.6, s32[3,128]{1,0:T(4,128)S(1)} %copy-done.16, bf16[16,160,128]{2,1,0:T(8,128)(2,1)S(1)} %all-to-all-done.refs_2_, f32[8,2048]{1,0:T(8,128)S(1)} %get-tuple-element.25.coarse_rows_ref.refs_3_, f32[32,2048]{1,0:T(8,128)S(1)} %copy-done.8, ...), custom_call_target="tpu_custom_call" | custom-call | tf_op jit(solution)/shard_map/coarse_sweep/pallas_call | solution.py:574
  95.0 17.8 %all_to_all.15.terms_ref = f32[32,8,128]{2,1,0:T(8,128)} all-to-all(f32[32,8,128]{2,1,0:T(8,128)S(1)} %get-tuple-element.33), channel_id=1, replica_groups=mesh['leaf'=16,'probe'=2] {'leaf','probe'}, dimensions={0} | all-to-all | bytes 262144 | tf_op jit(solution)/shard_map/all_to_all | solution.py:587
  112.8 1.7 %gram_sum.1 = f32[32,64]{1,0:T(8,128)} custom-call(f32[32,8,128]{2,1,0:T(8,128)} %all_to_all.15.terms_ref), custom_call_target="tpu_custom_call" | custom-call | tf_op jit(solution)/shard_map/gram_sum/pallas_call | solution.py:588
Async XLA Ops:
  0.6 1.0 copy-start
  1.6 0.8 copy-start.11
  2.4 0.7 copy-start.13
  6.1 7.5 %copy-start.1 = (bf16[32,4096]{1,0:T(8,128)(2,1)S(1)}, bf16[32,4096]{1,0:T(8,128)(2,1)}, u32[]{:S(2)}) copy-start(bf16[32,4096]{1,0:T(8,128)(2,1)} %refs_7_.1) | copy-start | bytes 786436
  6.1 7.5 %copy-start.2 = (bf16[64,4096]{1,0:T(8,128)(2,1)S(1)}, bf16[64,4096]{1,0:T(8,128)(2,1)}, u32[]{:S(2)}) copy-start(bf16[64,4096]{1,0:T(8,128)(2,1)} %refs_6_.1) | copy-start | bytes 1572868
  6.1 7.5 %copy-start.12 = (f32[3,2048]{1,0:T(4,128)S(1)}, f32[3,2048]{1,0:T(4,128)}, u32[]{:S(2)}) copy-start(f32[3,2048]{1,0:T(4,128)} %points_ref.2) | copy-start | bytes 73732
  6.1 7.5 %copy-start.14 = (s32[1,16,8]{1,2,0:T(8,128)S(1)}, s32[1,16,8]{1,2,0:T(8,128)}, u32[]{:S(2)}) copy-start(s32[1,16,8]{1,2,0:T(8,128)} %param.17) | copy-start | bytes 1540
  6.1 34.9 %all-to-all-start.1 = ((bf16[16,320,128]{2,1,0:T(8,128)(2,1)}), bf16[16,320,128]{2,1,0:T(8,128)(2,1)S(1)}, u32[]{:S(2)}, u32[]{:S(2)}) async-start(bf16[16,320,128]{2,1,0:T(8,128)(2,1)} %get-tuple-element.30), calls=%async_computation.1 | async-start | bytes 2621440 | tf_op jit(solution)/shard_map/all_to_all | solution.py:520
  19.6 0.9 copy-start.5
  20.5 0.7 copy-start.17
  21.2 0.7 copy-start.18
  39.2 0.8 copy-start.3
  40.0 0.7 copy-start.7
  40.7 10.0 %copy-start.6 = (s32[144,128]{1,0:T(8,128)S(1)}, s32[144,128]{1,0:T(8,128)}, u32[]{:S(2)}) copy-start(s32[144,128]{1,0:T(8,128)} %get-tuple-element.18.list_ref.refs_0_) | copy-start | bytes 221188
  40.7 10.0 %copy-start.15 = (s32[5,128]{1,0:T(8,128)S(1)}, s32[5,128]{1,0:T(8,128)}, u32[]{:S(2)}) copy-start(s32[5,128]{1,0:T(8,128)} %get-tuple-element.29.units_ref) | copy-start | bytes 7684
  41.0 35.1 %all-to-all-start = ((bf16[16,160,128]{2,1,0:T(8,128)(2,1)}), bf16[16,160,128]{2,1,0:T(8,128)(2,1)S(1)}, u32[]{:S(2)}, u32[]{:S(2)}) async-start(bf16[16,160,128]{2,1,0:T(8,128)(2,1)} %get-tuple-element.27), calls=%async_computation | async-start | bytes 1310720 | tf_op jit(solution)/shard_map/all_to_all | solution.py:561
  49.0 27.1 %copy-start.16 = (s32[3,128]{1,0:T(4,128)S(1)}, s32[3,128]{1,0:T(4,128)}, u32[]{:S(2)}) copy-start(s32[3,128]{1,0:T(4,128)} %get-tuple-element.19.refs_1_) | copy-start | bytes 4612
  49.1 26.4 %collective-permute-start = (bf16[32,4096]{1,0:T(8,128)(2,1)S(1)}, bf16[32,4096]{1,0:T(8,128)(2,1)S(1)}, u32[]{:S(2)}, u32[]{:S(2)}) collective-permute-start(bf16[32,4096]{1,0:T(8,128)(2,1)S(1)} %copy-done.1), channel_id=1, source_target_pairs={{0,1},{1,0},{2,3},{3,2},{4,5},{5,4},{6,7},{7,6},{8,9},{9,8},{10,11... | collective-permute-start | bytes 786440 | tf_op jit(solution)/shard_map/ppermute | solution.py:506
  50.7 1.0 copy-start.4
  75.4 0.7 copy-start.9
  76.1 1.0 copy-start.8
  77.1 0.9 copy-start.10

commit v9 on v8

--- a/solution.py
+++ b/solution.py
@@ -18,6 +18,7 @@
 FAR_AWAY = -30000.0
 SLOTS = 64
 RECEIVED = SLOTS + CHUNK
+VMEM = 56 * 1024 * 1024
 SPARE = 6 * 1024 * 1024
 
 NT = (((1,), (1,)), ((), ()))
@@ -61,7 +62,7 @@
     return pl.ds(pl.multiple_of(index * LANES, LANES), LANES)
 
 
-def list_slots_kernel(
+def list_slots(
     fine_slots_ref, fine_counts_ref, coarse_slots_ref, coarse_counts_ref, out_ref, *units_refs, entries
 ):
     fine, coarse = fine_slots_ref.shape[0], coarse_slots_ref.shape[0]
@@ -149,7 +150,7 @@
                 ).astype(jnp.bfloat16)
         return carry
 
-    lax.fori_loop(0, owners, one_owner, 0)
+    lax.fori_loop(0, owners, one_owner, 0, unroll=4)
 
 
 def pack_fine_kernel(send_ref, coef_ref, points_ref, out_ref, rows_ref, dup_coef, dup_rows):
@@ -166,11 +167,11 @@
         dup_rows[2 * index + 1] = b
         return carry
 
-    lax.fori_loop(0, coef_ref.shape[1] // LANES, one_tile, 0, unroll=4)
+    lax.fori_loop(0, coef_ref.shape[1] // LANES, one_tile, 0, unroll=8)
     pack_send(send_ref, out_ref, dup_coef, dup_rows, owners, capacity, px)
 
 
-def pack_coarse_kernel(
+def pack_coarse(
     send_ref, coef_ref, transfer_ref, points_ref, out_ref, rows_ref, coarse_ref, dup_coef, dup_rows
 ):
     _, capacity, owners = send_ref.shape
@@ -193,7 +194,7 @@
         dup_rows[2 * index + 1] = b
         return carry
 
-    lax.fori_loop(0, coef_ref.shape[1] // (2 * LANES), one_tile, 0, unroll=2)
+    lax.fori_loop(0, coef_ref.shape[1] // (2 * LANES), one_tile, 0, unroll=8)
     pack_send(send_ref, out_ref, dup_coef, dup_rows, owners, capacity, px, entry_first=True)
 
 
@@ -228,7 +229,7 @@
         put_pair(2 * index, coef_ref[:, tile], rows_ref[:, tile], coef_table, feature_table)
         return carry
 
-    lax.fori_loop(0, tiles, one_tile, 0, unroll=4)
+    lax.fori_loop(0, tiles, one_tile, 0, unroll=16)
     put_nothing(2 * tiles, coef_table, feature_table)
 
 
@@ -252,7 +253,7 @@
                 )
         return carry
 
-    lax.fori_loop(0, owners, one_owner, 0)
+    lax.fori_loop(0, owners, one_owner, 0, unroll=32 // pairs)
     put_nothing(owners * pairs * 2, coef_table, feature_table)
 
 
@@ -263,7 +264,7 @@
         target_table[2 * index + 1] = b.astype(jnp.bfloat16)
         return carry
 
-    lax.fori_loop(0, rows_ref.shape[1] // LANES, one_tile, 0, unroll=4)
+    lax.fori_loop(0, rows_ref.shape[1] // LANES, one_tile, 0, unroll=16)
 
 
 def sweep(list_ref, units_ref, first, coef_table, feature_table, target_table, first_buffer, second_buffer, acc):
@@ -350,28 +351,79 @@
         out_ref[:, tile] = sums if before_ref is None else before_ref[:, tile] + sums
         return carry
 
-    lax.fori_loop(0, clusters // 2, one_tile, 0, unroll=4)
+    lax.fori_loop(0, clusters // 2, one_tile, 0, unroll=8)
 
 
 def own_kernel(
-    list_ref,
+    send_ref,
+    fine_slots_ref,
+    fine_counts_ref,
+    coarse_slots_ref,
+    coarse_counts_ref,
+    coef_ref,
+    transfer_ref,
+    points_ref,
+    fine_rows_ref,
+    send_out_ref,
+    coarse_rows_ref,
+    list_out_ref,
     fine_units_ref,
     coarse_units_ref,
-    fine_coef_ref,
-    fine_rows_ref,
-    coarse_coef_ref,
-    coarse_rows_ref,
     fine_out_ref,
     coarse_out_ref,
+    coarse_coef_ref,
+    dup_coef,
+    dup_rows,
+    fine_own_units,
+    coarse_own_units,
+    list_ref,
+    fine_own_ref,
+    coarse_own_ref,
+    list_sem,
+    fine_sem,
+    coarse_sem,
     *scratch,
+    entries,
 ):
+    list_slots(
+        fine_slots_ref,
+        fine_counts_ref,
+        coarse_slots_ref,
+        coarse_counts_ref,
+        list_out_ref,
+        fine_own_units,
+        coarse_own_units,
+        fine_units_ref,
+        coarse_units_ref,
+        entries=entries,
+    )
+    copies = [
+        pltpu.make_async_copy(list_out_ref, list_ref, list_sem),
+        pltpu.make_async_copy(fine_own_units, fine_own_ref, fine_sem),
+        pltpu.make_async_copy(coarse_own_units, coarse_own_ref, coarse_sem),
+    ]
+    for copy in copies:
+        copy.start()
+    pack_coarse(
+        send_ref,
+        coef_ref,
+        transfer_ref,
+        points_ref,
+        send_out_ref,
+        coarse_rows_ref,
+        coarse_coef_ref,
+        dup_coef,
+        dup_rows,
+    )
+    for copy in copies:
+        copy.wait()
     first = 0
-    for units_ref, coef_ref, rows_ref, out_ref in (
-        (fine_units_ref, fine_coef_ref, fine_rows_ref, fine_out_ref),
-        (coarse_units_ref, coarse_coef_ref, coarse_rows_ref, coarse_out_ref),
+    for units_ref, source_ref, rows_ref, out_ref in (
+        (fine_own_ref, coef_ref, fine_rows_ref, fine_out_ref),
+        (coarse_own_ref, coarse_coef_ref, coarse_rows_ref, coarse_out_ref),
     ):
         clusters = rows_ref.shape[1] // 64
-        build_own(coef_ref, rows_ref, *scratch[:2])
+        build_own(source_ref, rows_ref, *scratch[:2])
         build_targets(rows_ref, scratch[2])
         sweep(list_ref, units_ref, first, *scratch)
         put_sums(scratch[-1], clusters, out_ref)
@@ -389,39 +441,35 @@
     list_ref, units_ref, recv_ref, rows_ref, own_ref, fine_ref, transfer_ref = refs[:7]
     probes_refs = refs[7:7 + groups]
     out_ref, terms_ref = refs[7 + groups:9 + groups]
-    gram_ref, *scratch = refs[9 + groups:]
+    gram_ref, split_ref, *scratch = refs[9 + groups:]
     clusters = rows_ref.shape[1] // 64
+    px = split_ref.shape[0] // 2
     probes = probes_refs[0].shape[0]
     acc = scratch[-1]
     build_received(recv_ref, *scratch[:2])
     build_targets(rows_ref, scratch[2])
     sweep(list_ref, units_ref, fine_ref.shape[1] // 64, *scratch)
-    gram_ref[...] = jnp.zeros_like(gram_ref)
-
-    def one_group(group, carry):
-        grams = [None] * groups
-        for part in range(4):
-            q = group * 4 + part
-            own = halves(own_ref[:, lane_tile(group * 2 + part // 2)])[part % 2]
-            twice = (summed(acc, q) + own).astype(jnp.bfloat16)
-            matrix = transfer_ref[:, lane_tile(q)].astype(jnp.float32)
-            low = lax.broadcasted_iota(jnp.int32, matrix.shape, 1) < 64
-            matrix = jnp.concatenate(
-                [jnp.where(low, matrix, 0.0), jnp.where(low, 0.0, matrix)], axis=0
-            ).astype(jnp.bfloat16)
-            total = fine_ref[:, lane_tile(q)] + bdot(twice, matrix, NT)
-            out_ref[:, lane_tile(q)] = total
-            high = total.astype(jnp.bfloat16)
-            rest = (total - high.astype(jnp.float32)).astype(jnp.bfloat16)
-            for block, probes_ref in enumerate(probes_refs):
-                tile = probes_ref[:, lane_tile(q)]
-                term = bdot(tile, high, NT) + bdot(tile, rest, NT)
-                grams[block] = term if grams[block] is None else grams[block] + term
-        for block in range(groups):
-            gram_ref[block] += grams[block]
-        return carry
-
-    lax.fori_loop(0, clusters // 4, one_group, 0)
+
+    def one_parent(q, carry):
+        own = halves(own_ref[:, lane_tile(q >> 1)])
+        own = jnp.where((q & 1) == 0, own[0], own[1])
+        twice = (summed(acc, q) + own).astype(jnp.bfloat16)
+        matrix = transfer_ref[:, lane_tile(q)].astype(jnp.float32)
+        low = lax.broadcasted_iota(jnp.int32, matrix.shape, 1) < 64
+        matrix = jnp.concatenate(
+            [jnp.where(low, matrix, 0.0), jnp.where(low, 0.0, matrix)], axis=0
+        ).astype(jnp.bfloat16)
+        total = fine_ref[:, lane_tile(q)] + bdot(twice, matrix, NT)
+        out_ref[:, lane_tile(q)] = total
+        high = total.astype(jnp.bfloat16)
+        split_ref[:px, lane_tile(q)] = high
+        split_ref[px:, lane_tile(q)] = (total - high.astype(jnp.float32)).astype(jnp.bfloat16)
+        return carry
+
+    lax.fori_loop(0, clusters, one_parent, 0, unroll=8)
+    for block, probes_ref in enumerate(probes_refs):
+        term = bdot(probes_ref[...], split_ref[...], NT)
+        gram_ref[block] = term[:, :px] + term[:, px:]
     place = lax.axis_index("probe")
     for b in range(groups):
         block = gram_ref[lax.rem(place - b + groups, groups)]
@@ -486,15 +534,7 @@
             size += math.prod(ref.shape[:-1]) * -(-ref.shape[-1] // LANES) * LANES * ref.dtype.itemsize
         return pltpu.CompilerParams(vmem_limit_bytes=size)
 
-    fine_pack = [
-        pltpu.VMEM((fine_count, px, LANES), jnp.float32),
-        pltpu.VMEM((fine_count, 8, LANES), jnp.float32),
-    ]
-    coarse_pack = [
-        pltpu.VMEM((coarse_count, px, LANES), jnp.float32),
-        pltpu.VMEM((coarse_count, 8, LANES), jnp.float32),
-    ]
-    own_scratch = sweep_scratch(fine_count, fine_count, px)
+    whole_vmem = pltpu.CompilerParams(vmem_limit_bytes=VMEM)
     fine_scratch = sweep_scratch(owners * cap_fine, fine_count, px)
     coarse_scratch = sweep_scratch(owners * cap_coarse, coarse_count, px)
     smem = pl.BlockSpec(memory_space=pltpu.SMEM)
@@ -513,49 +553,61 @@
         ),
         in_specs=[smem, vmem, vmem],
         out_specs=[vmem, vmem],
-        scratch_shapes=fine_pack,
-        compiler_params=params(fine_pack, owners // 4),
+        scratch_shapes=[
+            pltpu.VMEM((fine_count, px, LANES), f32),
+            pltpu.VMEM((fine_count, 8, LANES), f32),
+        ],
+        compiler_params=whole_vmem,
         name="pack_fine",
     )(send_fine, coef, points_fine)
     fine_recv = lax.all_to_all(fine_send, "leaf", split_axis=0, concat_axis=0, tiled=True)
 
-    coarse_send, coarse_rows, coarse_coef = pl.pallas_call(
-        pack_coarse_kernel,
+    fine_total = owners * cap_fine
+    coarse_total = owners * cap_coarse
+    unit_rows = [-(-(count * (SLOTS // CHUNK) + 2 * UNITS + 1) // LANES) for count in (fine_count, coarse_count)]
+    list_shape = (RECEIVED + SLOTS + CHUNK, LANES)
+    i32 = jnp.int32
+    coarse_send, coarse_rows, slot_list, fine_units, coarse_units, fine_sums, coarse_sums = pl.pallas_call(
+        functools.partial(own_kernel, entries=(fine_total, coarse_total)),
         out_shape=(
             jax.ShapeDtypeStruct((owners, (cap_coarse // 2) * (px + 8), LANES), bf16),
             jax.ShapeDtypeStruct((8, points_coarse.shape[1]), f32),
-            jax.ShapeDtypeStruct((px, points_coarse.shape[1]), bf16),
-        ),
-        in_specs=[smem, vmem, vmem, vmem],
-        out_specs=[vmem, vmem, vmem],
-        scratch_shapes=coarse_pack,
-        compiler_params=params(coarse_pack, owners // 4),
-        name="pack_coarse",
-    )(jnp.swapaxes(send_coarse, 1, 2), coef, transfer, points_coarse)
-    fine_total = owners * cap_fine
-    coarse_total = owners * cap_coarse
-    unit_rows = [-(-(count * (SLOTS // CHUNK) + 2 * UNITS + 1) // LANES) for count in (fine_count, coarse_count)]
-    slot_list, fine_own, coarse_own, fine_units, coarse_units = pl.pallas_call(
-        functools.partial(list_slots_kernel, entries=(fine_total, coarse_total)),
-        out_shape=[jax.ShapeDtypeStruct((RECEIVED + SLOTS + CHUNK, LANES), jnp.int32)]
-        + [jax.ShapeDtypeStruct((rows, LANES), jnp.int32) for rows in unit_rows * 2],
-        in_specs=[vmem] * 4,
-        out_specs=[vmem] * 5,
-        name="list_slots",
-    )(slots_fine, counts_fine.reshape(1, -1), slots_coarse, counts_coarse.reshape(1, -1))
-    fine_sums, coarse_sums = pl.pallas_call(
-        own_kernel,
-        out_shape=(
+            jax.ShapeDtypeStruct(list_shape, i32),
+            jax.ShapeDtypeStruct((unit_rows[0], LANES), i32),
+            jax.ShapeDtypeStruct((unit_rows[1], LANES), i32),
             jax.ShapeDtypeStruct((px, points_fine.shape[1]), f32),
             jax.ShapeDtypeStruct((px, points_coarse.shape[1]), f32),
         ),
-        in_specs=[smem] * 3 + [vmem] * 4,
-        out_specs=[vmem, vmem],
-        scratch_shapes=own_scratch,
-        compiler_params=params(own_scratch, 4),
+        in_specs=[smem] + [vmem] * 8,
+        out_specs=[vmem] * 7,
+        scratch_shapes=[
+            pltpu.VMEM((px, points_coarse.shape[1]), bf16),
+            pltpu.VMEM((coarse_count, px, LANES), f32),
+            pltpu.VMEM((coarse_count, 8, LANES), f32),
+            pltpu.VMEM((unit_rows[0], LANES), i32),
+            pltpu.VMEM((unit_rows[1], LANES), i32),
+            pltpu.SMEM(list_shape, i32),
+            pltpu.SMEM((unit_rows[0], LANES), i32),
+            pltpu.SMEM((unit_rows[1], LANES), i32),
+            pltpu.SemaphoreType.DMA,
+            pltpu.SemaphoreType.DMA,
+            pltpu.SemaphoreType.DMA,
+        ]
+        + sweep_scratch(fine_count, fine_count, px),
+        compiler_params=whole_vmem,
         cost_estimate=pl.CostEstimate(flops=10**10, bytes_accessed=10**7, transcendentals=10**7),
         name="own_sweep",
-    )(slot_list, fine_own, coarse_own, coef, fine_rows, coarse_coef, coarse_rows)
+    )(
+        jnp.swapaxes(send_coarse, 1, 2),
+        slots_fine,
+        counts_fine.reshape(1, -1),
+        slots_coarse,
+        counts_coarse.reshape(1, -1),
+        coef,
+        transfer,
+        points_coarse,
+        fine_rows,
+    )
 
     coarse_send, coarse_sums = lax.optimization_barrier((coarse_send, coarse_sums))
     coarse_recv = lax.all_to_all(coarse_send, "leaf", split_axis=0, concat_axis=0, tiled=True)
@@ -579,7 +631,11 @@
         ),
         in_specs=[smem] * 2 + [vmem] * (5 + groups),
         out_specs=[vmem, vmem],
-        scratch_shapes=[pltpu.VMEM((groups, probes, px), f32)] + coarse_scratch,
+        scratch_shapes=[
+            pltpu.VMEM((groups, probes, px), f32),
+            pltpu.VMEM((2 * px, points_fine.shape[1]), bf16),
+        ]
+        + coarse_scratch,
         compiler_params=params(coarse_scratch, owners // 4 + 6),
         name="coarse_sweep",
     )(slot_list, coarse_units, coarse_recv, coarse_rows, coarse_sums, fine_far, transfer, *turned)

time: 115 us -> 104 us (0.904)
  Pallas kernels: 68.6 us -> 58.2 us
  waiting for transfers between devices: 0.35 us -> 8.8 us
  local copies, waits for them, and re-layouts: 9.88 us -> 3.67 us
  blocking collectives: 17.8 us -> 15.2 us
    all_to_all x1, waiting for transfers between devices: 0.34 us -> 8.79 us  [shards(): lax.all_to_all(fine_send, 'leaf', split_axis=0, concat_axis=0, tiled=True)]
    unnamed x38 -> x22, local copies, waits for them, and re-layouts: 9.88 us -> 3.67 us
    pallas_call x3 -> x1, Pallas kernels: 23.3 us -> 18.6 us  [shards(): pl.pallas_call(functools.partial(own_kernel, entries=(fine_total, coarse_...]
    pallas_call x1, Pallas kernels: 17 us -> 13.7 us  [shards(): pl.pallas_call(functools.partial(coarse_kernel, groups), out_shape=(jax.S...]
    all_to_all x1, blocking collectives: 17.8 us -> 15.2 us  [shards(): lax.all_to_all(terms, ('leaf', 'probe'), split_axis=0, concat_axis=0, til...]
    pallas_call x1, Pallas kernels: 23.7 us -> 21.3 us  [shards(): pl.pallas_call(fine_kernel, out_shape=jax.ShapeDtypeStruct((px, points_fi...]
  transfers between devices with their start and end apart: 3 -> 3, of which waited for: 1 -> 1; matrix products, arithmetic and copies ran while one was open for 0% -> 0% of each run, Pallas kernels for 41% -> 38%
where the time goes in v9:
time: 104 us
  Pallas kernels  58.2 us (56%)
  starting transfers between devices  16.9 us (16%)
  blocking collectives  15.2 us (15%)
  waiting for transfers between devices  8.8 us (8%)
  local copies, waits for them, and re-layouts  3.67 us (4%)
    pallas_call x1, Pallas kernels, shards(): pl.pallas_call(fine_kernel, out_shape=jax.ShapeDtypeStruct((px, points_fi...  21.3 us
    pallas_call x1, Pallas kernels, shards(): pl.pallas_call(functools.partial(own_kernel, entries=(fine_total, coarse_...  18.6 us
    all_to_all x1, blocking collectives, shards(): lax.all_to_all(terms, ('leaf', 'probe'), split_axis=0, concat_axis=0, til...  15.2 us
    pallas_call x1, Pallas kernels, shards(): pl.pallas_call(functools.partial(coarse_kernel, groups), out_shape=(jax.S...  13.7 us
    all_to_all x1, waiting for transfers between devices, shards(): lax.all_to_all(fine_send, 'leaf', split_axis=0, concat_axis=0, tiled=True)  8.79 us
    all_to_all x1, starting transfers between devices, shards(): lax.all_to_all(coarse_send, 'leaf', split_axis=0, concat_axis=0, tiled=True)  8.01 us
    all_to_all x1, starting transfers between devices, shards(): lax.all_to_all(fine_send, 'leaf', split_axis=0, concat_axis=0, tiled=True)  7.35 us
    unnamed x22, local copies, waits for them, and re-layouts  3.67 us
  transfers between devices with their start and end apart: 3, of which 1 were waited for; matrix products, arithmetic and copies ran while one was open for 0% of the time, Pallas kernels for 38%

profile of v9, /device:TPU:0, one launch (start us, length us, event | category | flops | bytes accessed | tf_op | source)
XLA Modules:
  0.0 103.6 jit_solution(6448966129461872266)
XLA Ops:
  0.6 3.0 %pack_fine.1 = (bf16[16,320,128]{2,1,0:T(8,128)(2,1)}, f32[8,4096]{1,0:T(8,128)}) custom-call(s32[1,16,16]{2,1,0:T(8,128)} %send_ref.1, bf16[32,4096]{1,0:T(8,128)(2,1)} %refs_7_.1, f32[3,4096]{1,0:T(4,128)} %points_ref.2), custom_call_target="tpu_custom_call" | custom-call | tf_op jit(solution)/shard_map/pack_fine/pallas_call | solution.py:548
  3.6 7.4 %all-to-all-start.1 = ((bf16[16,320,128]{2,1,0:T(8,128)(2,1)}), bf16[16,320,128]{2,1,0:T(8,128)(2,1)S(1)}, u32[]{:S(2)}, u32[]{:S(2)}) async-start(bf16[16,320,128]{2,1,0:T(8,128)(2,1)} %get-tuple-element.24), calls=%async_computation.1 | async-start | bytes 2621440 | tf_op jit(solution)/shard_map/all_to_all | solution.py:563
  11.0 18.6 %own_sweep.1 = (bf16[16,160,128]{2,1,0:T(8,128)(2,1)}, f32[8,2048]{1,0:T(8,128)}, s32[144,128]{1,0:T(8,128)}, s32[5,128]{1,0:T(8,128)}, s32[3,128]{1,0:T(4,128)}...) custom-call(s32[1,8,16]{2,1,0:T(8,128)} %bitcast.3, s32[64,64]{1,0:T(8,128)} %fine_slots_ref.1, s32[1,64]{1,0:T(1,128)} %bitcast.4, ...), custom_call_target="tpu_custom_call" | custom-call | flops 10000000000 | bytes 10000000 | tf_op jit(solution)/shard_map/own_sweep/pallas_call | solution.py:570
  29.5 0.0 copy-start
  29.5 0.0 copy-start.1
  29.6 0.0 copy-start.3
  29.6 0.0 copy-start.7
  29.6 0.0 copy-start.9
  29.6 8.8 %all-to-all-done.1.recv_ref = bf16[16,320,128]{2,1,0:T(8,128)(2,1)S(1)} async-done(((bf16[16,320,128]{2,1,0:T(8,128)(2,1)}), bf16[16,320,128]{2,1,0:T(8,128)(2,1)S(1)}, u32[]{:S(2)}, u32[]{:S(2)}) %all-to-all-start.1) | async-done | bytes 1310752 | tf_op jit(solution)/shard_map/all_to_all | solution.py:563
  38.4 8.0 %all-to-all-start = ((bf16[16,160,128]{2,1,0:T(8,128)(2,1)}), bf16[16,160,128]{2,1,0:T(8,128)(2,1)S(1)}, u32[]{:S(2)}, u32[]{:S(2)}) async-start(bf16[16,160,128]{2,1,0:T(8,128)(2,1)} %get-tuple-element.20), calls=%async_computation | async-start | bytes 1310720 | tf_op jit(solution)/shard_map/all_to_all | solution.py:613
  46.4 0.0 copy-done
  46.4 0.0 copy-start.8
  46.4 0.0 copy-start.10
  46.4 1.6 %collective-permute-start = (bf16[32,4096]{1,0:T(8,128)(2,1)S(1)}, bf16[32,4096]{1,0:T(8,128)(2,1)S(1)}, u32[]{:S(2)}, u32[]{:S(2)}) collective-permute-start(bf16[32,4096]{1,0:T(8,128)(2,1)S(1)} %copy-done), channel_id=1, source_target_pairs={{0,1},{1,0},{2,3},{3,2},{4,5},{5,4},{6,7},{7,6},{8,9},{9,8},{10,11... | collective-permute-start | bytes 786440 | tf_op jit(solution)/shard_map/ppermute | solution.py:546
  48.0 0.0 copy-done.1
  48.0 0.0 copy-done.3
  48.0 0.0 copy-done.7
  48.0 0.0 copy-done.9
  48.0 21.3 %fine_sweep.1.refs_5_ = f32[32,4096]{1,0:T(8,128)S(1)} custom-call(s32[144,128]{1,0:T(8,128)S(1)} %copy-done.3, s32[5,128]{1,0:T(8,128)S(1)} %copy-done.9, bf16[16,320,128]{2,1,0:T(8,128)(2,1)S(1)} %all-to-all-done.1.recv_ref, f32[8,4096]{1,0:T(8,128)S(1)} %copy-done.7, f32[32,4096]{1,0:T(8,128)S(1)} %copy-done.1), custom_call_target="tpu_custom_call" | custom-call | tf_op jit(solution)/shard_map/fine_sweep/pallas_call | solution.py:615
  69.3 0.0 collective-permute-done.refs_8_
  69.4 0.0 copy-start.5
  69.4 0.7 copy-done.5
  70.1 0.0 all-to-all-done.refs_2_
  70.1 0.0 copy-done.8
  70.1 0.0 copy-done.10
  70.1 0.0 copy-start.2
  70.1 1.0 copy-done.2
  71.1 0.0 copy-start.4
  71.1 0.9 copy-done.4
  72.1 0.0 copy-start.6
  72.1 0.9 copy-done.6
  73.0 13.7 %coarse_sweep.1 = (f32[32,4096]{1,0:T(8,128)}, f32[32,8,128]{2,1,0:T(8,128)S(1)}) custom-call(s32[144,128]{1,0:T(8,128)S(1)} %copy-done.3, s32[3,128]{1,0:T(4,128)S(1)} %copy-done.10, bf16[16,160,128]{2,1,0:T(8,128)(2,1)S(1)} %all-to-all-done.refs_2_, f32[8,2048]{1,0:T(8,128)S(1)} %copy-done.8, f32[32,2048]{1,0:T(8,128)S(1)} %copy-done.4, ...), custom_call_target="tpu_custom_call" | custom-call | tf_op jit(solution)/shard_map/coarse_sweep/pallas_call | solution.py:626
  86.7 15.2 %all_to_all.15.terms_ref = f32[32,8,128]{2,1,0:T(8,128)} all-to-all(f32[32,8,128]{2,1,0:T(8,128)S(1)} %get-tuple-element.27), channel_id=1, replica_groups=mesh['leaf'=16,'probe'=2] {'leaf','probe'}, dimensions={0} | all-to-all | bytes 262144 | tf_op jit(solution)/shard_map/all_to_all | solution.py:643
  101.9 1.7 %gram_sum.1 = f32[32,64]{1,0:T(8,128)} custom-call(f32[32,8,128]{2,1,0:T(8,128)} %all_to_all.15.terms_ref), custom_call_target="tpu_custom_call" | custom-call | tf_op jit(solution)/shard_map/gram_sum/pallas_call | solution.py:644
Async XLA Ops:
  3.6 34.8 %all-to-all-start.1 = ((bf16[16,320,128]{2,1,0:T(8,128)(2,1)}), bf16[16,320,128]{2,1,0:T(8,128)(2,1)S(1)}, u32[]{:S(2)}, u32[]{:S(2)}) async-start(bf16[16,320,128]{2,1,0:T(8,128)(2,1)} %get-tuple-element.24), calls=%async_computation.1 | async-start | bytes 2621440 | tf_op jit(solution)/shard_map/all_to_all | solution.py:563
  29.5 16.9 %copy-start = (bf16[32,4096]{1,0:T(8,128)(2,1)S(1)}, bf16[32,4096]{1,0:T(8,128)(2,1)}, u32[]{:S(2)}) copy-start(bf16[32,4096]{1,0:T(8,128)(2,1)} %refs_7_.1) | copy-start | bytes 786436
  29.5 18.5 %copy-start.1 = (f32[32,4096]{1,0:T(8,128)S(1)}, f32[32,4096]{1,0:T(8,128)}, u32[]{:S(2)}) copy-start(f32[32,4096]{1,0:T(8,128)} %get-tuple-element.25.own_ref) | copy-start | bytes 1572868
  29.6 18.5 %copy-start.3 = (s32[144,128]{1,0:T(8,128)S(1)}, s32[144,128]{1,0:T(8,128)}, u32[]{:S(2)}) copy-start(s32[144,128]{1,0:T(8,128)} %get-tuple-element.16.list_ref.refs_0_) | copy-start | bytes 221188
  29.6 18.5 %copy-start.7 = (f32[8,4096]{1,0:T(8,128)S(1)}, f32[8,4096]{1,0:T(8,128)}, u32[]{:S(2)}) copy-start(f32[8,4096]{1,0:T(8,128)} %get-tuple-element.15.fine_rows_ref.rows_ref) | copy-start | bytes 393220
  29.6 18.5 %copy-start.9 = (s32[5,128]{1,0:T(8,128)S(1)}, s32[5,128]{1,0:T(8,128)}, u32[]{:S(2)}) copy-start(s32[5,128]{1,0:T(8,128)} %get-tuple-element.23.units_ref) | copy-start | bytes 7684
  38.4 31.7 %all-to-all-start = ((bf16[16,160,128]{2,1,0:T(8,128)(2,1)}), bf16[16,160,128]{2,1,0:T(8,128)(2,1)S(1)}, u32[]{:S(2)}, u32[]{:S(2)}) async-start(bf16[16,160,128]{2,1,0:T(8,128)(2,1)} %get-tuple-element.20), calls=%async_computation | async-start | bytes 1310720 | tf_op jit(solution)/shard_map/all_to_all | solution.py:613
  46.4 23.6 %copy-start.8 = (f32[8,2048]{1,0:T(8,128)S(1)}, f32[8,2048]{1,0:T(8,128)}, u32[]{:S(2)}) copy-start(f32[8,2048]{1,0:T(8,128)} %get-tuple-element.21.refs_3_) | copy-start | bytes 196612
  46.4 23.6 %copy-start.10 = (s32[3,128]{1,0:T(4,128)S(1)}, s32[3,128]{1,0:T(4,128)}, u32[]{:S(2)}) copy-start(s32[3,128]{1,0:T(4,128)} %get-tuple-element.17.refs_1_) | copy-start | bytes 4612
  46.4 22.9 %collective-permute-start = (bf16[32,4096]{1,0:T(8,128)(2,1)S(1)}, bf16[32,4096]{1,0:T(8,128)(2,1)S(1)}, u32[]{:S(2)}, u32[]{:S(2)}) collective-permute-start(bf16[32,4096]{1,0:T(8,128)(2,1)S(1)} %copy-done), channel_id=1, source_target_pairs={{0,1},{1,0},{2,3},{3,2},{4,5},{5,4},{6,7},{7,6},{8,9},{9,8},{10,11... | collective-permute-start | bytes 786440 | tf_op jit(solution)/shard_map/ppermute | solution.py:546
  69.4 0.7 copy-start.5
  70.1 1.0 %copy-start.2 = (bf16[64,4096]{1,0:T(8,128)(2,1)S(1)}, bf16[64,4096]{1,0:T(8,128)(2,1)}, u32[]{:S(2)}) copy-start(bf16[64,4096]{1,0:T(8,128)(2,1)} %refs_6_.1) | copy-start | bytes 1572868
  71.1 0.9 copy-start.4
  72.1 0.9 copy-start.6

commit v10 on v9

--- a/solution.py
+++ b/solution.py
@@ -12,7 +12,7 @@
 KERNEL_RATE = 1.5
 POINT_SCALE = math.sqrt(2.0 * KERNEL_RATE)
 LANES = 128
-UNITS = 8
+UNITS = 16
 QUAD = 4
 CHUNK = 8
 FAR_AWAY = -30000.0
@@ -137,9 +137,7 @@
                 send_ref[0, entry, owner] if entry_first else send_ref[0, owner, entry]
                 for entry in (2 * pair, 2 * pair + 1)
             ]
-            out_ref[owner, pair * px:(pair + 1) * px, :] = jnp.where(
-                lane, dup_coef[first], dup_coef[second]
-            ).astype(jnp.bfloat16)
+            out_ref[owner, pair * px:(pair + 1) * px, :] = jnp.where(lane, dup_coef[first], dup_coef[second])
             rows = jnp.where(lane8, dup_rows[first], dup_rows[second])
             if pair % 2 == 0:
                 before = rows
@@ -160,8 +158,8 @@
 
     def one_tile(index, carry):
         a, b = halves(coef_ref[:, lane_tile(index)].astype(jnp.float32))
-        dup_coef[2 * index] = a
-        dup_coef[2 * index + 1] = b
+        dup_coef[2 * index] = a.astype(jnp.bfloat16)
+        dup_coef[2 * index + 1] = b.astype(jnp.bfloat16)
         a, b = halves(rows_ref[:, lane_tile(index)])
         dup_rows[2 * index] = a
         dup_rows[2 * index + 1] = b
@@ -184,11 +182,11 @@
             q = 2 * index + part
             a, b = halves(transfer_ref[:, lane_tile(q)].astype(jnp.float32))
             matrix = jnp.concatenate([a, b], axis=0).astype(jnp.bfloat16)
-            block = bdot(coef_ref[:, lane_tile(q)], matrix, NN)
+            block = bdot(coef_ref[:, lane_tile(q)], matrix, NN).astype(jnp.bfloat16)
             dup_coef[q] = block
             doubled.append(block)
         lane = lax.broadcasted_iota(jnp.int32, (px, LANES), 1) < LANES // 2
-        coarse_ref[:, lane_tile(index)] = jnp.where(lane, doubled[0], doubled[1]).astype(jnp.bfloat16)
+        coarse_ref[:, lane_tile(index)] = jnp.where(lane, doubled[0], doubled[1])
         a, b = halves(rows_ref[:, lane_tile(index)])
         dup_rows[2 * index] = a
         dup_rows[2 * index + 1] = b
@@ -438,10 +436,16 @@
 
 
 def coarse_kernel(groups, *refs):
-    list_ref, units_ref, recv_ref, rows_ref, own_ref, fine_ref, transfer_ref = refs[:7]
-    probes_refs = refs[7:7 + groups]
-    out_ref, terms_ref = refs[7 + groups:9 + groups]
-    gram_ref, split_ref, *scratch = refs[9 + groups:]
+    late = 3 + groups
+    list_ref, units_ref, recv_ref, rows_ref = refs[:4]
+    out_ref, terms_ref = refs[4 + late:6 + late]
+    late_refs = refs[6 + late:6 + 2 * late]
+    late_sems = refs[6 + 2 * late:6 + 3 * late]
+    gram_ref, split_ref, *scratch = refs[6 + 3 * late:]
+    copies = [pltpu.make_async_copy(*pair) for pair in zip(refs[4:4 + late], late_refs, late_sems)]
+    for copy in copies:
+        copy.start()
+    own_ref, fine_ref, transfer_ref, *probes_refs = late_refs
     clusters = rows_ref.shape[1] // 64
     px = split_ref.shape[0] // 2
     probes = probes_refs[0].shape[0]
@@ -449,6 +453,8 @@
     build_received(recv_ref, *scratch[:2])
     build_targets(rows_ref, scratch[2])
     sweep(list_ref, units_ref, fine_ref.shape[1] // 64, *scratch)
+    for copy in copies:
+        copy.wait()
 
     def one_parent(q, carry):
         own = halves(own_ref[:, lane_tile(q >> 1)])
@@ -541,10 +547,6 @@
     vmem = pl.BlockSpec(memory_space=pltpu.VMEM)
     bf16, f32 = jnp.bfloat16, jnp.float32
 
-    turned = [coef_fine]
-    for step in range(1, groups):
-        turned.append(lax.ppermute(coef_fine, "probe", [(i, (i + step) % groups) for i in range(groups)]))
-
     fine_send, fine_rows = pl.pallas_call(
         pack_fine_kernel,
         out_shape=(
@@ -554,7 +556,7 @@
         in_specs=[smem, vmem, vmem],
         out_specs=[vmem, vmem],
         scratch_shapes=[
-            pltpu.VMEM((fine_count, px, LANES), f32),
+            pltpu.VMEM((fine_count, px, LANES), bf16),
             pltpu.VMEM((fine_count, 8, LANES), f32),
         ],
         compiler_params=whole_vmem,
@@ -582,7 +584,7 @@
         out_specs=[vmem] * 7,
         scratch_shapes=[
             pltpu.VMEM((px, points_coarse.shape[1]), bf16),
-            pltpu.VMEM((coarse_count, px, LANES), f32),
+            pltpu.VMEM((coarse_count, px, LANES), bf16),
             pltpu.VMEM((coarse_count, 8, LANES), f32),
             pltpu.VMEM((unit_rows[0], LANES), i32),
             pltpu.VMEM((unit_rows[1], LANES), i32),
@@ -609,7 +611,9 @@
         fine_rows,
     )
 
-    coarse_send, coarse_sums = lax.optimization_barrier((coarse_send, coarse_sums))
+    turned = [coef_fine]
+    for step in range(1, groups):
+        turned.append(lax.ppermute(coef_fine, "probe", [(i, (i + step) % groups) for i in range(groups)]))
     coarse_recv = lax.all_to_all(coarse_send, "leaf", split_axis=0, concat_axis=0, tiled=True)
 
     fine_far = pl.pallas_call(
@@ -622,6 +626,7 @@
         name="fine_sweep",
     )(slot_list, fine_units, fine_recv, fine_rows, fine_sums)
 
+    late = (coarse_sums, fine_far, transfer, *turned)
     term_shape = (owners * groups, 8, probes * probes // 8)
     far, terms = pl.pallas_call(
         functools.partial(coarse_kernel, groups),
@@ -629,16 +634,18 @@
             jax.ShapeDtypeStruct((px, points_fine.shape[1]), f32),
             jax.ShapeDtypeStruct(term_shape, f32),
         ),
-        in_specs=[smem] * 2 + [vmem] * (5 + groups),
+        in_specs=[smem] * 2 + [vmem] * 2 + [pl.BlockSpec(memory_space=pl.ANY)] * (3 + groups),
         out_specs=[vmem, vmem],
-        scratch_shapes=[
+        scratch_shapes=[pltpu.VMEM(operand.shape, operand.dtype) for operand in late]
+        + [pltpu.SemaphoreType.DMA] * len(late)
+        + [
             pltpu.VMEM((groups, probes, px), f32),
             pltpu.VMEM((2 * px, points_fine.shape[1]), bf16),
         ]
         + coarse_scratch,
-        compiler_params=params(coarse_scratch, owners // 4 + 6),
+        compiler_params=whole_vmem,
         name="coarse_sweep",
-    )(slot_list, coarse_units, coarse_recv, coarse_rows, coarse_sums, fine_far, transfer, *turned)
+    )(slot_list, coarse_units, coarse_recv, coarse_rows, *late)
 
     terms = lax.all_to_all(terms, ("leaf", "probe"), split_axis=0, concat_axis=0, tiled=True)
     probe_gram = pl.pallas_call(

time: 104 us -> 103 us (level); the launches traced: 104 us -> 104 us
  blocking collectives: 15.2 us -> 19.1 us
  local copies, waits for them, and re-layouts: 3.67 us -> 1.75 us
  Pallas kernels: 58.2 us -> 56.9 us
    all_to_all x1, blocking collectives: 15.2 us -> 19.1 us  [shards(): lax.all_to_all(terms, ('leaf', 'probe'), split_axis=0, concat_axis=0, til...]
    unnamed x22 -> x16, local copies, waits for them, and re-layouts: 3.67 us -> 1.75 us
    pallas_call x1, Pallas kernels: 21.3 us -> 20.2 us  [shards(): pl.pallas_call(fine_kernel, out_shape=jax.ShapeDtypeStruct((px, points_fi...]
  transfers between devices with their start and end apart: 3 -> 3, of which waited for: 1 -> 1; matrix products, arithmetic and copies ran while one was open for 0% -> 0% of each run, Pallas kernels for 38% -> 37%
where the time goes in v10:
time: 103 us; the launch traced here: 104 us
  Pallas kernels  56.9 us (55%)
  blocking collectives  19.1 us (19%)
  starting transfers between devices  17 us (17%)
  waiting for transfers between devices  8.58 us (8%)
  local copies, waits for them, and re-layouts  1.75 us (2%)
    pallas_call x1, Pallas kernels, shards(): pl.pallas_call(fine_kernel, out_shape=jax.ShapeDtypeStruct((px, points_fi...  20.2 us
    all_to_all x1, blocking collectives, shards(): lax.all_to_all(terms, ('leaf', 'probe'), split_axis=0, concat_axis=0, til...  19.1 us
    pallas_call x1, Pallas kernels, shards(): pl.pallas_call(functools.partial(own_kernel, entries=(fine_total, coarse_...  18.8 us
    pallas_call x1, Pallas kernels, shards(): pl.pallas_call(functools.partial(coarse_kernel, groups), out_shape=(jax.S...  13.1 us
    all_to_all x1, waiting for transfers between devices, shards(): lax.all_to_all(fine_send, 'leaf', split_axis=0, concat_axis=0, tiled=True)  8.57 us
    all_to_all x1, starting transfers between devices, shards(): lax.all_to_all(coarse_send, 'leaf', split_axis=0, concat_axis=0, tiled=True)  8.01 us
    all_to_all x1, starting transfers between devices, shards(): lax.all_to_all(fine_send, 'leaf', split_axis=0, concat_axis=0, tiled=True)  7.36 us
    pallas_call x1, Pallas kernels, shards(): pl.pallas_call(pack_fine_kernel, out_shape=(jax.ShapeDtypeStruct((owners,...  3.13 us
  transfers between devices with their start and end apart: 3, of which 1 were waited for; matrix products, arithmetic and copies ran while one was open for 0% of the time, Pallas kernels for 37%

profile of v10, /device:TPU:0, one launch (start us, length us, event | category | flops | bytes accessed | tf_op | source)
XLA Modules:
  0.0 104.0 jit_solution(155290900197141900)
XLA Ops:
  0.6 3.1 %pack_fine.1 = (bf16[16,320,128]{2,1,0:T(8,128)(2,1)}, f32[8,4096]{1,0:T(8,128)}) custom-call(s32[1,16,16]{2,1,0:T(8,128)} %send_ref.1, bf16[32,4096]{1,0:T(8,128)(2,1)} %refs_7_.1, f32[3,4096]{1,0:T(4,128)} %points_ref.2), custom_call_target="tpu_custom_call" | custom-call | tf_op jit(solution)/shard_map/pack_fine/pallas_call | solution.py:550
  3.8 7.4 %all-to-all-start.1 = ((bf16[16,320,128]{2,1,0:T(8,128)(2,1)}), bf16[16,320,128]{2,1,0:T(8,128)(2,1)S(1)}, u32[]{:S(2)}, u32[]{:S(2)}) async-start(bf16[16,320,128]{2,1,0:T(8,128)(2,1)} %get-tuple-element.20), calls=%async_computation.1 | async-start | bytes 2621440 | tf_op jit(solution)/shard_map/all_to_all | solution.py:565
  11.1 18.8 %own_sweep.1 = (bf16[16,160,128]{2,1,0:T(8,128)(2,1)}, f32[8,2048]{1,0:T(8,128)}, s32[144,128]{1,0:T(8,128)}, s32[5,128]{1,0:T(8,128)}, s32[3,128]{1,0:T(4,128)}...) custom-call(s32[1,8,16]{2,1,0:T(8,128)} %bitcast.3, s32[64,64]{1,0:T(8,128)} %fine_slots_ref.1, s32[1,64]{1,0:T(1,128)} %bitcast.4, ...), custom_call_target="tpu_custom_call" | custom-call | flops 10000000000 | bytes 10000000 | tf_op jit(solution)/shard_map/own_sweep/pallas_call | solution.py:572
  29.9 0.0 copy-start.6
  29.9 0.0 copy-start.1
  29.9 0.0 copy-start.2
  29.9 0.0 copy-start.3
  30.0 0.0 copy-start.4
  30.0 8.6 %all-to-all-done.1.recv_ref = bf16[16,320,128]{2,1,0:T(8,128)(2,1)S(1)} async-done(((bf16[16,320,128]{2,1,0:T(8,128)(2,1)}), bf16[16,320,128]{2,1,0:T(8,128)(2,1)S(1)}, u32[]{:S(2)}, u32[]{:S(2)}) %all-to-all-start.1) | async-done | bytes 1310752 | tf_op jit(solution)/shard_map/all_to_all | solution.py:565
  38.5 8.0 %all-to-all-start = ((bf16[16,160,128]{2,1,0:T(8,128)(2,1)}), bf16[16,160,128]{2,1,0:T(8,128)(2,1)S(1)}, u32[]{:S(2)}, u32[]{:S(2)}) async-start(bf16[16,160,128]{2,1,0:T(8,128)(2,1)} %get-tuple-element.16), calls=%async_computation | async-start | bytes 1310720 | tf_op jit(solution)/shard_map/all_to_all | solution.py:617
  46.6 0.0 copy-done.6
  46.6 1.6 %collective-permute-start = (bf16[32,4096]{1,0:T(8,128)(2,1)S(1)}, bf16[32,4096]{1,0:T(8,128)(2,1)S(1)}, u32[]{:S(2)}, u32[]{:S(2)}) collective-permute-start(bf16[32,4096]{1,0:T(8,128)(2,1)S(1)} %copy-done.6), channel_id=1, source_target_pairs={{0,1},{1,0},{2,3},{3,2},{4,5},{5,4},{6,7},{7,6},{8,9},{9,8},{10,11... | collective-permute-start | bytes 786440 | tf_op jit(solution)/shard_map/ppermute | solution.py:616
  48.2 0.0 copy-done.1
  48.2 0.0 copy-done.2
  48.2 0.0 copy-done.3
  48.2 0.0 copy-done.4
  48.2 20.2 %fine_sweep.1.refs_5_ = f32[32,4096]{1,0:T(8,128)S(1)} custom-call(s32[144,128]{1,0:T(8,128)S(1)} %copy-done.2, s32[5,128]{1,0:T(8,128)S(1)} %copy-done.4, bf16[16,320,128]{2,1,0:T(8,128)(2,1)S(1)} %all-to-all-done.1.recv_ref, f32[8,4096]{1,0:T(8,128)S(1)} %copy-done.3, f32[32,4096]{1,0:T(8,128)S(1)} %copy-done.1), custom_call_target="tpu_custom_call" | custom-call | tf_op jit(solution)/shard_map/fine_sweep/pallas_call | solution.py:619
  68.4 0.0 copy-start
  68.4 0.8 copy-done
  69.2 0.0 collective-permute-done.refs_8_
  69.2 0.0 copy-start.7
  69.2 0.0 all-to-all-done.refs_2_
  69.2 0.0 copy-start.5
  69.2 0.7 copy-done.7
  69.9 0.2 copy-done.5
  70.1 13.1 %coarse_sweep.1 = (f32[32,4096]{1,0:T(8,128)}, f32[32,8,128]{2,1,0:T(8,128)}) custom-call(s32[144,128]{1,0:T(8,128)} %get-tuple-element.14.list_ref.refs_0_, s32[3,128]{1,0:T(4,128)} %get-tuple-element.15.refs_1_, bf16[16,160,128]{2,1,0:T(8,128)(2,1)} %copy-done.5, f32[8,2048]{1,0:T(8,128)} %get-tuple-element.17.refs_3_, ...), custom_call_target="tpu_custom_call" | custom-call | tf_op jit(solution)/shard_map/coarse_sweep/pallas_call | solution.py:631
  83.2 19.1 %all_to_all.15.terms_ref = f32[32,8,128]{2,1,0:T(8,128)} all-to-all(f32[32,8,128]{2,1,0:T(8,128)} %get-tuple-element.23), channel_id=1, replica_groups=mesh['leaf'=16,'probe'=2] {'leaf','probe'}, dimensions={0} | all-to-all | bytes 262144 | tf_op jit(solution)/shard_map/all_to_all | solution.py:650
  102.3 1.7 %gram_sum.1 = f32[32,64]{1,0:T(8,128)} custom-call(f32[32,8,128]{2,1,0:T(8,128)} %all_to_all.15.terms_ref), custom_call_target="tpu_custom_call" | custom-call | tf_op jit(solution)/shard_map/gram_sum/pallas_call | solution.py:651
Async XLA Ops:
  3.8 34.8 %all-to-all-start.1 = ((bf16[16,320,128]{2,1,0:T(8,128)(2,1)}), bf16[16,320,128]{2,1,0:T(8,128)(2,1)S(1)}, u32[]{:S(2)}, u32[]{:S(2)}) async-start(bf16[16,320,128]{2,1,0:T(8,128)(2,1)} %get-tuple-element.20), calls=%async_computation.1 | async-start | bytes 2621440 | tf_op jit(solution)/shard_map/all_to_all | solution.py:565
  29.9 16.7 %copy-start.6 = (bf16[32,4096]{1,0:T(8,128)(2,1)S(1)}, bf16[32,4096]{1,0:T(8,128)(2,1)}, u32[]{:S(2)}) copy-start(bf16[32,4096]{1,0:T(8,128)(2,1)} %refs_7_.1) | copy-start | bytes 786436
  29.9 18.2 %copy-start.1 = (f32[32,4096]{1,0:T(8,128)S(1)}, f32[32,4096]{1,0:T(8,128)}, u32[]{:S(2)}) copy-start(f32[32,4096]{1,0:T(8,128)} %get-tuple-element.21.own_ref) | copy-start | bytes 1572868
  29.9 18.2 %copy-start.2 = (s32[144,128]{1,0:T(8,128)S(1)}, s32[144,128]{1,0:T(8,128)}, u32[]{:S(2)}) copy-start(s32[144,128]{1,0:T(8,128)} %get-tuple-element.14.list_ref.refs_0_) | copy-start | bytes 221188
  29.9 18.2 %copy-start.3 = (f32[8,4096]{1,0:T(8,128)S(1)}, f32[8,4096]{1,0:T(8,128)}, u32[]{:S(2)}) copy-start(f32[8,4096]{1,0:T(8,128)} %get-tuple-element.13.fine_rows_ref.rows_ref) | copy-start | bytes 393220
  30.0 18.2 %copy-start.4 = (s32[5,128]{1,0:T(8,128)S(1)}, s32[5,128]{1,0:T(8,128)}, u32[]{:S(2)}) copy-start(s32[5,128]{1,0:T(8,128)} %get-tuple-element.19.units_ref) | copy-start | bytes 7684
  38.5 30.7 %all-to-all-start = ((bf16[16,160,128]{2,1,0:T(8,128)(2,1)}), bf16[16,160,128]{2,1,0:T(8,128)(2,1)S(1)}, u32[]{:S(2)}, u32[]{:S(2)}) async-start(bf16[16,160,128]{2,1,0:T(8,128)(2,1)} %get-tuple-element.16), calls=%async_computation | async-start | bytes 1310720 | tf_op jit(solution)/shard_map/all_to_all | solution.py:617
  46.6 22.6 %collective-permute-start = (bf16[32,4096]{1,0:T(8,128)(2,1)S(1)}, bf16[32,4096]{1,0:T(8,128)(2,1)S(1)}, u32[]{:S(2)}, u32[]{:S(2)}) collective-permute-start(bf16[32,4096]{1,0:T(8,128)(2,1)S(1)} %copy-done.6), channel_id=1, source_target_pairs={{0,1},{1,0},{2,3},{3,2},{4,5},{5,4},{6,7},{7,6},{8,9},{9,8},{10,11... | collective-permute-start | bytes 786440 | tf_op jit(solution)/shard_map/ppermute | solution.py:616
  68.4 0.8 copy-start
  69.2 0.7 copy-start.7
  69.2 0.9 copy-start.5

commit v11 on v10

--- a/solution.py
+++ b/solution.py
@@ -19,7 +19,6 @@
 SLOTS = 64
 RECEIVED = SLOTS + CHUNK
 VMEM = 56 * 1024 * 1024
-SPARE = 6 * 1024 * 1024
 
 NT = (((1,), (1,)), ((), ()))
 NN = (((1,), (0,)), ((), ()))
@@ -151,7 +150,7 @@
     lax.fori_loop(0, owners, one_owner, 0, unroll=4)
 
 
-def pack_fine_kernel(send_ref, coef_ref, points_ref, out_ref, rows_ref, dup_coef, dup_rows):
+def pack_fine(send_ref, coef_ref, points_ref, out_ref, rows_ref, dup_coef, dup_rows):
     _, owners, capacity = send_ref.shape
     px = coef_ref.shape[0]
     rows_ref[...] = split_rows(points_ref[...])
@@ -330,8 +329,22 @@
         return carry
 
     total = units_ref[units_ref.shape[0] - 1, LANES - 1]
+    sets = (total + UNITS - 1) // UNITS
+    bodies = (sets - 1) // 2
+    last = bodies * (2 * UNITS)
     tiles(units_of(0), first_buffer)
-    lax.fori_loop(0, (total + 2 * UNITS - 1) // (2 * UNITS), two_sets, 0)
+    lax.fori_loop(0, bodies, two_sets, 0)
+
+    @pl.when(sets == 2 * bodies + 2)
+    def _():
+        second = units_of(last + UNITS)
+        tiles(second, second_buffer)
+        products(units_of(last), first_buffer)
+        products(second, second_buffer)
+
+    @pl.when(sets == 2 * bodies + 1)
+    def _():
+        products(units_of(last), first_buffer)
 
 
 def summed(acc, target):
@@ -352,34 +365,30 @@
     lax.fori_loop(0, clusters // 2, one_tile, 0, unroll=8)
 
 
-def own_kernel(
+def prepare_kernel(
     send_ref,
     fine_slots_ref,
     fine_counts_ref,
     coarse_slots_ref,
     coarse_counts_ref,
     coef_ref,
-    transfer_ref,
     points_ref,
+    coarse_coef_ref,
+    coarse_rows_ref,
+    send_out_ref,
     fine_rows_ref,
-    send_out_ref,
-    coarse_rows_ref,
     list_out_ref,
+    fine_own_ref,
     fine_units_ref,
     coarse_units_ref,
-    fine_out_ref,
     coarse_out_ref,
-    coarse_coef_ref,
     dup_coef,
     dup_rows,
-    fine_own_units,
-    coarse_own_units,
+    coarse_own_ref,
     list_ref,
-    fine_own_ref,
-    coarse_own_ref,
+    units_ref,
     list_sem,
-    fine_sem,
-    coarse_sem,
+    units_sem,
     *scratch,
     entries,
 ):
@@ -389,53 +398,52 @@
         coarse_slots_ref,
         coarse_counts_ref,
         list_out_ref,
-        fine_own_units,
-        coarse_own_units,
+        fine_own_ref,
+        coarse_own_ref,
         fine_units_ref,
         coarse_units_ref,
         entries=entries,
     )
     copies = [
         pltpu.make_async_copy(list_out_ref, list_ref, list_sem),
-        pltpu.make_async_copy(fine_own_units, fine_own_ref, fine_sem),
-        pltpu.make_async_copy(coarse_own_units, coarse_own_ref, coarse_sem),
+        pltpu.make_async_copy(coarse_own_ref, units_ref, units_sem),
     ]
     for copy in copies:
         copy.start()
-    pack_coarse(
-        send_ref,
-        coef_ref,
-        transfer_ref,
-        points_ref,
-        send_out_ref,
-        coarse_rows_ref,
-        coarse_coef_ref,
-        dup_coef,
-        dup_rows,
-    )
+    pack_fine(send_ref, coef_ref, points_ref, send_out_ref, fine_rows_ref, dup_coef, dup_rows)
+    build_own(coarse_coef_ref, coarse_rows_ref, *scratch[:2])
+    build_targets(coarse_rows_ref, scratch[2])
     for copy in copies:
         copy.wait()
-    first = 0
-    for units_ref, source_ref, rows_ref, out_ref in (
-        (fine_own_ref, coef_ref, fine_rows_ref, fine_out_ref),
-        (coarse_own_ref, coarse_coef_ref, coarse_rows_ref, coarse_out_ref),
-    ):
-        clusters = rows_ref.shape[1] // 64
-        build_own(source_ref, rows_ref, *scratch[:2])
-        build_targets(rows_ref, scratch[2])
-        sweep(list_ref, units_ref, first, *scratch)
-        put_sums(scratch[-1], clusters, out_ref)
-        first += clusters
-
-
-def fine_kernel(list_ref, units_ref, recv_ref, rows_ref, own_ref, out_ref, *scratch):
+    sweep(list_ref, units_ref, fine_rows_ref.shape[1] // 64, *scratch)
+    put_sums(scratch[-1], coarse_rows_ref.shape[1] // 64, coarse_out_ref)
+
+
+def coarse_kernel(
+    list_ref,
+    own_units_ref,
+    units_ref,
+    coef_ref,
+    fine_rows_ref,
+    recv_ref,
+    rows_ref,
+    own_ref,
+    fine_out_ref,
+    out_ref,
+    *scratch,
+):
+    fine = fine_rows_ref.shape[1] // 64
+    build_own(coef_ref, fine_rows_ref, *scratch[:2])
+    build_targets(fine_rows_ref, scratch[2])
+    sweep(list_ref, own_units_ref, 0, *scratch)
+    put_sums(scratch[-1], fine, fine_out_ref)
     build_received(recv_ref, *scratch[:2])
     build_targets(rows_ref, scratch[2])
-    sweep(list_ref, units_ref, 0, *scratch)
+    sweep(list_ref, units_ref, fine, *scratch)
     put_sums(scratch[-1], rows_ref.shape[1] // 64, out_ref, own_ref)
 
 
-def coarse_kernel(groups, *refs):
+def fine_kernel(groups, *refs):
     late = 3 + groups
     list_ref, units_ref, recv_ref, rows_ref = refs[:4]
     out_ref, terms_ref = refs[4 + late:6 + late]
@@ -445,34 +453,34 @@
     copies = [pltpu.make_async_copy(*pair) for pair in zip(refs[4:4 + late], late_refs, late_sems)]
     for copy in copies:
         copy.start()
-    own_ref, fine_ref, transfer_ref, *probes_refs = late_refs
-    clusters = rows_ref.shape[1] // 64
+    own_ref, coarse_ref, transfer_ref, *probes_refs = late_refs
     px = split_ref.shape[0] // 2
     probes = probes_refs[0].shape[0]
     acc = scratch[-1]
     build_received(recv_ref, *scratch[:2])
     build_targets(rows_ref, scratch[2])
-    sweep(list_ref, units_ref, fine_ref.shape[1] // 64, *scratch)
+    sweep(list_ref, units_ref, 0, *scratch)
     for copy in copies:
         copy.wait()
+    low_x = lax.broadcasted_iota(jnp.int32, (px, LANES), 1) < 64
 
     def one_parent(q, carry):
-        own = halves(own_ref[:, lane_tile(q >> 1)])
-        own = jnp.where((q & 1) == 0, own[0], own[1])
-        twice = (summed(acc, q) + own).astype(jnp.bfloat16)
+        far = halves(coarse_ref[:, lane_tile(q >> 1)])
+        twice = jnp.where((q & 1) == 0, far[0], far[1]).astype(jnp.bfloat16)
         matrix = transfer_ref[:, lane_tile(q)].astype(jnp.float32)
         low = lax.broadcasted_iota(jnp.int32, matrix.shape, 1) < 64
         matrix = jnp.concatenate(
             [jnp.where(low, matrix, 0.0), jnp.where(low, 0.0, matrix)], axis=0
         ).astype(jnp.bfloat16)
-        total = fine_ref[:, lane_tile(q)] + bdot(twice, matrix, NT)
+        sums = jnp.where(low_x, summed(acc, 2 * q), summed(acc, 2 * q + 1))
+        total = own_ref[:, lane_tile(q)] + sums + bdot(twice, matrix, NT)
         out_ref[:, lane_tile(q)] = total
         high = total.astype(jnp.bfloat16)
         split_ref[:px, lane_tile(q)] = high
         split_ref[px:, lane_tile(q)] = (total - high.astype(jnp.float32)).astype(jnp.bfloat16)
         return carry
 
-    lax.fori_loop(0, clusters, one_parent, 0, unroll=8)
+    lax.fori_loop(0, coarse_ref.shape[1] // 64, one_parent, 0, unroll=8)
     for block, probes_ref in enumerate(probes_refs):
         term = bdot(probes_ref[...], split_ref[...], NT)
         gram_ref[block] = term[:, :px] + term[:, px:]
@@ -534,102 +542,97 @@
     cap_fine = send_fine.shape[2]
     cap_coarse = send_coarse.shape[2]
 
-    def params(scratch, blocks):
-        size = SPARE + blocks * px * points_fine.shape[1] * 4
-        for ref in scratch:
-            size += math.prod(ref.shape[:-1]) * -(-ref.shape[-1] // LANES) * LANES * ref.dtype.itemsize
-        return pltpu.CompilerParams(vmem_limit_bytes=size)
-
     whole_vmem = pltpu.CompilerParams(vmem_limit_bytes=VMEM)
-    fine_scratch = sweep_scratch(owners * cap_fine, fine_count, px)
-    coarse_scratch = sweep_scratch(owners * cap_coarse, coarse_count, px)
     smem = pl.BlockSpec(memory_space=pltpu.SMEM)
     vmem = pl.BlockSpec(memory_space=pltpu.VMEM)
     bf16, f32 = jnp.bfloat16, jnp.float32
-
-    fine_send, fine_rows = pl.pallas_call(
-        pack_fine_kernel,
-        out_shape=(
-            jax.ShapeDtypeStruct((owners, (cap_fine // 2) * (px + 8), LANES), bf16),
-            jax.ShapeDtypeStruct((8, points_fine.shape[1]), f32),
-        ),
-        in_specs=[smem, vmem, vmem],
-        out_specs=[vmem, vmem],
-        scratch_shapes=[
-            pltpu.VMEM((fine_count, px, LANES), bf16),
-            pltpu.VMEM((fine_count, 8, LANES), f32),
-        ],
-        compiler_params=whole_vmem,
-        name="pack_fine",
-    )(send_fine, coef, points_fine)
-    fine_recv = lax.all_to_all(fine_send, "leaf", split_axis=0, concat_axis=0, tiled=True)
 
     fine_total = owners * cap_fine
     coarse_total = owners * cap_coarse
     unit_rows = [-(-(count * (SLOTS // CHUNK) + 2 * UNITS + 1) // LANES) for count in (fine_count, coarse_count)]
     list_shape = (RECEIVED + SLOTS + CHUNK, LANES)
     i32 = jnp.int32
-    coarse_send, coarse_rows, slot_list, fine_units, coarse_units, fine_sums, coarse_sums = pl.pallas_call(
-        functools.partial(own_kernel, entries=(fine_total, coarse_total)),
+    fine_columns, coarse_columns = points_fine.shape[1], points_coarse.shape[1]
+
+    coarse_send, coarse_rows, coarse_coef = pl.pallas_call(
+        pack_coarse,
         out_shape=(
             jax.ShapeDtypeStruct((owners, (cap_coarse // 2) * (px + 8), LANES), bf16),
-            jax.ShapeDtypeStruct((8, points_coarse.shape[1]), f32),
+            jax.ShapeDtypeStruct((8, coarse_columns), f32),
+            jax.ShapeDtypeStruct((px, coarse_columns), bf16),
+        ),
+        in_specs=[smem, vmem, vmem, vmem],
+        out_specs=[vmem] * 3,
+        scratch_shapes=[
+            pltpu.VMEM((coarse_count, px, LANES), bf16),
+            pltpu.VMEM((coarse_count, 8, LANES), f32),
+        ],
+        compiler_params=whole_vmem,
+        name="pack_coarse",
+    )(jnp.swapaxes(send_coarse, 1, 2), coef, transfer, points_coarse)
+    coarse_recv = lax.all_to_all(coarse_send, "leaf", split_axis=0, concat_axis=0, tiled=True)
+
+    turned = [coef_fine]
+    for step in range(1, groups):
+        turned.append(lax.ppermute(coef_fine, "probe", [(i, (i + step) % groups) for i in range(groups)]))
+
+    fine_send, fine_rows, slot_list, fine_own, fine_units, coarse_units, coarse_own_sums = pl.pallas_call(
+        functools.partial(prepare_kernel, entries=(fine_total, coarse_total)),
+        out_shape=(
+            jax.ShapeDtypeStruct((owners, (cap_fine // 2) * (px + 8), LANES), bf16),
+            jax.ShapeDtypeStruct((8, fine_columns), f32),
             jax.ShapeDtypeStruct(list_shape, i32),
             jax.ShapeDtypeStruct((unit_rows[0], LANES), i32),
+            jax.ShapeDtypeStruct((unit_rows[0], LANES), i32),
             jax.ShapeDtypeStruct((unit_rows[1], LANES), i32),
-            jax.ShapeDtypeStruct((px, points_fine.shape[1]), f32),
-            jax.ShapeDtypeStruct((px, points_coarse.shape[1]), f32),
+            jax.ShapeDtypeStruct((px, coarse_columns), f32),
         ),
         in_specs=[smem] + [vmem] * 8,
         out_specs=[vmem] * 7,
         scratch_shapes=[
-            pltpu.VMEM((px, points_coarse.shape[1]), bf16),
-            pltpu.VMEM((coarse_count, px, LANES), bf16),
-            pltpu.VMEM((coarse_count, 8, LANES), f32),
-            pltpu.VMEM((unit_rows[0], LANES), i32),
+            pltpu.VMEM((fine_count, px, LANES), bf16),
+            pltpu.VMEM((fine_count, 8, LANES), f32),
             pltpu.VMEM((unit_rows[1], LANES), i32),
             pltpu.SMEM(list_shape, i32),
-            pltpu.SMEM((unit_rows[0], LANES), i32),
             pltpu.SMEM((unit_rows[1], LANES), i32),
             pltpu.SemaphoreType.DMA,
             pltpu.SemaphoreType.DMA,
-            pltpu.SemaphoreType.DMA,
         ]
-        + sweep_scratch(fine_count, fine_count, px),
+        + sweep_scratch(coarse_count, coarse_count, px),
         compiler_params=whole_vmem,
         cost_estimate=pl.CostEstimate(flops=10**10, bytes_accessed=10**7, transcendentals=10**7),
-        name="own_sweep",
+        name="prepare",
     )(
-        jnp.swapaxes(send_coarse, 1, 2),
+        send_fine,
         slots_fine,
         counts_fine.reshape(1, -1),
         slots_coarse,
         counts_coarse.reshape(1, -1),
         coef,
-        transfer,
-        points_coarse,
-        fine_rows,
+        points_fine,
+        coarse_coef,
+        coarse_rows,
     )
-
-    turned = [coef_fine]
-    for step in range(1, groups):
-        turned.append(lax.ppermute(coef_fine, "probe", [(i, (i + step) % groups) for i in range(groups)]))
-    coarse_recv = lax.all_to_all(coarse_send, "leaf", split_axis=0, concat_axis=0, tiled=True)
-
-    fine_far = pl.pallas_call(
-        fine_kernel,
-        out_shape=jax.ShapeDtypeStruct((px, points_fine.shape[1]), f32),
-        in_specs=[smem] * 2 + [vmem] * 3,
-        out_specs=vmem,
-        scratch_shapes=fine_scratch,
-        compiler_params=params(fine_scratch, owners // 4 + 4),
-        name="fine_sweep",
-    )(slot_list, fine_units, fine_recv, fine_rows, fine_sums)
-
-    late = (coarse_sums, fine_far, transfer, *turned)
+    fine_recv = lax.all_to_all(fine_send, "leaf", split_axis=0, concat_axis=0, tiled=True)
+
+    fine_sums, coarse_far = pl.pallas_call(
+        coarse_kernel,
+        out_shape=(
+            jax.ShapeDtypeStruct((px, fine_columns), f32),
+            jax.ShapeDtypeStruct((px, coarse_columns), f32),
+        ),
+        in_specs=[smem] * 3 + [vmem] * 5,
+        out_specs=[vmem, vmem],
+        scratch_shapes=sweep_scratch(max(fine_count, coarse_total), fine_count, px),
+        compiler_params=whole_vmem,
+        cost_estimate=pl.CostEstimate(flops=10**10, bytes_accessed=10**7, transcendentals=10**7),
+        name="coarse_sweep",
+    )(slot_list, fine_own, coarse_units, coef, fine_rows, coarse_recv, coarse_rows, coarse_own_sums)
+
+    late = (fine_sums, coarse_far, transfer, *turned)
     term_shape = (owners * groups, 8, probes * probes // 8)
     far, terms = pl.pallas_call(
-        functools.partial(coarse_kernel, groups),
+        functools.partial(fine_kernel, groups),
         out_shape=(
             jax.ShapeDtypeStruct((px, points_fine.shape[1]), f32),
             jax.ShapeDtypeStruct(term_shape, f32),
@@ -642,10 +645,10 @@
             pltpu.VMEM((groups, probes, px), f32),
             pltpu.VMEM((2 * px, points_fine.shape[1]), bf16),
         ]
-        + coarse_scratch,
+        + sweep_scratch(fine_total, fine_count, px),
         compiler_params=whole_vmem,
-        name="coarse_sweep",
-    )(slot_list, coarse_units, coarse_recv, coarse_rows, *late)
+        name="fine_sweep",
+    )(slot_list, fine_units, fine_recv, fine_rows, *late)
 
     terms = lax.all_to_all(terms, ("leaf", "probe"), split_axis=0, concat_axis=0, tiled=True)
     probe_gram = pl.pallas_call(

time: 103 us -> 105 us (1.019); the launches traced: 104 us -> 104 us
  waiting for transfers between devices: 8.58 us -> 15.8 us
  Pallas kernels: 56.9 us -> 50.2 us
  starting transfers between devices: 17 us -> 13.7 us
  blocking collectives: 19.1 us -> 21.5 us
    all_to_all x1, waiting for transfers between devices: 0.01 us -> 7.79 us  [shards(): lax.all_to_all(coarse_send, 'leaf', split_axis=0, concat_axis=0, tiled=True)]
    pallas_call x4, Pallas kernels: 55.2 us -> 48.6 us  [the longest x1 18.9 us: shards(): pl.pallas_call(functools.partial(fine_kernel, groups), out_shape=(jax.Sha...]
    all_to_all x1, starting transfers between devices: 7.36 us -> 4.77 us  [shards(): lax.all_to_all(fine_send, 'leaf', split_axis=0, concat_axis=0, tiled=True)]
    all_to_all x1, blocking collectives: 19.1 us -> 21.5 us  [shards(): lax.all_to_all(terms, ('leaf', 'probe'), split_axis=0, concat_axis=0, til...]
  transfers between devices with their start and end apart: 3 -> 3, of which waited for: 1 -> 2; matrix products, arithmetic and copies ran while one was open for 0% -> 0% of each run, Pallas kernels for 37% -> 26%
where the time goes in v11:
time: 105 us; the launch traced here: 104 us
  Pallas kernels  50.2 us (48%)
  blocking collectives  21.5 us (20%)
  waiting for transfers between devices  15.8 us (15%)
  starting transfers between devices  13.7 us (13%)
  local copies, waits for them, and re-layouts  1.91 us (2%)
    all_to_all x1, blocking collectives, shards(): lax.all_to_all(terms, ('leaf', 'probe'), split_axis=0, concat_axis=0, til...  21.5 us
    pallas_call x1, Pallas kernels, shards(): pl.pallas_call(functools.partial(fine_kernel, groups), out_shape=(jax.Sha...  18.9 us
    pallas_call x1, Pallas kernels, shards(): pl.pallas_call(coarse_kernel, out_shape=(jax.ShapeDtypeStruct((px, fine_c...  17.8 us
    pallas_call x1, Pallas kernels, shards(): pl.pallas_call(functools.partial(prepare_kernel, entries=(fine_total, coa...  8.8 us
    all_to_all x1, waiting for transfers between devices, shards(): lax.all_to_all(fine_send, 'leaf', split_axis=0, concat_axis=0, tiled=True)  7.99 us
    all_to_all x1, waiting for transfers between devices, shards(): lax.all_to_all(coarse_send, 'leaf', split_axis=0, concat_axis=0, tiled=True)  7.79 us
    all_to_all x1, starting transfers between devices, shards(): lax.all_to_all(coarse_send, 'leaf', split_axis=0, concat_axis=0, tiled=True)  7.36 us
    all_to_all x1, starting transfers between devices, shards(): lax.all_to_all(fine_send, 'leaf', split_axis=0, concat_axis=0, tiled=True)  4.77 us
  transfers between devices with their start and end apart: 3, of which 2 were waited for; matrix products, arithmetic and copies ran while one was open for 0% of the time, Pallas kernels for 26%

profile of v11, /device:TPU:0, one launch (start us, length us, event | category | flops | bytes accessed | tf_op | source)
XLA Modules:
  0.0 103.8 jit_solution(14718584327030588536)
XLA Ops:
  0.6 3.1 %pack_coarse.1 = (bf16[16,160,128]{2,1,0:T(8,128)(2,1)}, f32[8,2048]{1,0:T(8,128)}, bf16[32,2048]{1,0:T(8,128)(2,1)}) custom-call(s32[1,8,16]{2,1,0:T(8,128)} %bitcast.3, bf16[32,4096]{1,0:T(8,128)(2,1)} %refs_7_.1, bf16[64,4096]{1,0:T(8,128)(2,1)} %refs_6_.1, f32[3,2048]{1,0:T(4,128)} %points_ref.2), custom_call_target="tpu_custom_call" | custom-call | tf_op jit(solution)/shard_map/pack_coarse/pallas_call | solution.py:557
  3.7 7.4 %all-to-all-start.1 = ((bf16[16,160,128]{2,1,0:T(8,128)(2,1)}), bf16[16,160,128]{2,1,0:T(8,128)(2,1)S(1)}, u32[]{:S(2)}, u32[]{:S(2)}) async-start(bf16[16,160,128]{2,1,0:T(8,128)(2,1)} %get-tuple-element.24), calls=%async_computation.1 | async-start | bytes 1310720 | tf_op jit(solution)/shard_map/all_to_all | solution.py:573
  11.0 8.8 %prepare.1 = (bf16[16,320,128]{2,1,0:T(8,128)(2,1)}, f32[8,4096]{1,0:T(8,128)}, s32[144,128]{1,0:T(8,128)}, s32[5,128]{1,0:T(8,128)}, s32[5,128]{1,0:T(8,128)}, /*index=5*/s32[3,128]{1,0:T(4,128)}, f32[32,2048]{1,0:T(8,128)}) custom-call(s32[1,16,16]{2,1,0:T(8,128)} %send_ref.1, s32[64,64]{1,0:T(8,128)} %fine_slots_ref.1, s32[1,64]{1,0:T(1,128)} %bitcast.4, ...), custom_call_target="tpu_custom_call" | custom-call | flops 10000000000 | bytes 10000000 | tf_op jit(solution)/shard_map/prepare/pallas_call | solution.py:579
  19.9 7.8 %all-to-all-done.1.recv_ref = bf16[16,160,128]{2,1,0:T(8,128)(2,1)S(1)} async-done(((bf16[16,160,128]{2,1,0:T(8,128)(2,1)}), bf16[16,160,128]{2,1,0:T(8,128)(2,1)S(1)}, u32[]{:S(2)}, u32[]{:S(2)}) %all-to-all-start.1) | async-done | bytes 655392 | tf_op jit(solution)/shard_map/all_to_all | solution.py:573
  27.6 0.0 copy-start.2
  27.7 0.0 copy-start.1
  27.7 0.8 copy-done.2
  28.5 4.8 %all-to-all-start = ((bf16[16,320,128]{2,1,0:T(8,128)(2,1)}), bf16[16,320,128]{2,1,0:T(8,128)(2,1)S(1)}, u32[]{:S(2)}, u32[]{:S(2)}) async-start(bf16[16,320,128]{2,1,0:T(8,128)(2,1)} %get-tuple-element.20), calls=%async_computation | async-start | bytes 2621440 | tf_op jit(solution)/shard_map/all_to_all | solution.py:616
  33.3 0.0 copy-done.1
  33.3 1.6 %collective-permute-start = (bf16[32,4096]{1,0:T(8,128)(2,1)S(1)}, bf16[32,4096]{1,0:T(8,128)(2,1)S(1)}, u32[]{:S(2)}, u32[]{:S(2)}) collective-permute-start(bf16[32,4096]{1,0:T(8,128)(2,1)S(1)} %copy-done.1), channel_id=1, source_target_pairs={{0,1},{1,0},{2,3},{3,2},{4,5},{5,4},{6,7},{7,6},{8,9},{9,8},{10,11... | collective-permute-start | bytes 786440 | tf_op jit(solution)/shard_map/ppermute | solution.py:577
  34.9 17.8 %coarse_sweep.1 = (f32[32,4096]{1,0:T(8,128)}, f32[32,2048]{1,0:T(8,128)}) custom-call(s32[144,128]{1,0:T(8,128)} %get-tuple-element.18.list_ref.refs_0_, s32[5,128]{1,0:T(8,128)} %get-tuple-element.22.own_units_ref, s32[3,128]{1,0:T(4,128)} %get-tuple-element.23.units_ref, bf16[32,4096]{1,0:T(8,128)(2,1)} %refs_7_.1, ...), custom_call_target="tpu_custom_call" | custom-call | flops 10000000000 | bytes 10000000 | tf_op jit(solution)/shard_map/coarse_sweep/pallas_call | solution.py:618
  52.7 0.0 collective-permute-done.refs_8_
  52.7 0.0 copy-start.3
  52.7 8.0 %all-to-all-done.refs_2_ = bf16[16,320,128]{2,1,0:T(8,128)(2,1)S(1)} async-done(((bf16[16,320,128]{2,1,0:T(8,128)(2,1)}), bf16[16,320,128]{2,1,0:T(8,128)(2,1)S(1)}, u32[]{:S(2)}, u32[]{:S(2)}) %all-to-all-start) | async-done | bytes 1310752 | tf_op jit(solution)/shard_map/all_to_all | solution.py:616
  60.7 0.0 copy-start
  60.7 0.0 copy-done.3
  60.7 1.1 %copy-done = bf16[16,320,128]{2,1,0:T(8,128)(2,1)} copy-done((bf16[16,320,128]{2,1,0:T(8,128)(2,1)}, bf16[16,320,128]{2,1,0:T(8,128)(2,1)S(1)}, u32[]{:S(2)}) %copy-start) | copy-done | bytes 1310744
  61.8 18.9 %fine_sweep.1 = (f32[32,4096]{1,0:T(8,128)}, f32[32,8,128]{2,1,0:T(8,128)}) custom-call(s32[144,128]{1,0:T(8,128)} %get-tuple-element.18.list_ref.refs_0_, s32[5,128]{1,0:T(8,128)} %get-tuple-element.19.refs_1_, bf16[16,320,128]{2,1,0:T(8,128)(2,1)} %copy-done, f32[8,4096]{1,0:T(8,128)} %get-tuple-element.21.fine_rows_ref.refs_3_, ...), custom_call_target="tpu_custom_call" | custom-call | tf_op jit(solution)/shard_map/fine_sweep/pallas_call | solution.py:634
  80.7 21.5 %all_to_all.15.terms_ref = f32[32,8,128]{2,1,0:T(8,128)} all-to-all(f32[32,8,128]{2,1,0:T(8,128)} %get-tuple-element.29), channel_id=1, replica_groups=mesh['leaf'=16,'probe'=2] {'leaf','probe'}, dimensions={0} | all-to-all | bytes 262144 | tf_op jit(solution)/shard_map/all_to_all | solution.py:653
  102.1 1.7 %gram_sum.1 = f32[32,64]{1,0:T(8,128)} custom-call(f32[32,8,128]{2,1,0:T(8,128)} %all_to_all.15.terms_ref), custom_call_target="tpu_custom_call" | custom-call | tf_op jit(solution)/shard_map/gram_sum/pallas_call | solution.py:654
Async XLA Ops:
  3.7 24.0 %all-to-all-start.1 = ((bf16[16,160,128]{2,1,0:T(8,128)(2,1)}), bf16[16,160,128]{2,1,0:T(8,128)(2,1)S(1)}, u32[]{:S(2)}, u32[]{:S(2)}) async-start(bf16[16,160,128]{2,1,0:T(8,128)(2,1)} %get-tuple-element.24), calls=%async_computation.1 | async-start | bytes 1310720 | tf_op jit(solution)/shard_map/all_to_all | solution.py:573
  27.6 0.8 copy-start.2
  27.7 5.6 %copy-start.1 = (bf16[32,4096]{1,0:T(8,128)(2,1)S(1)}, bf16[32,4096]{1,0:T(8,128)(2,1)}, u32[]{:S(2)}) copy-start(bf16[32,4096]{1,0:T(8,128)(2,1)} %refs_7_.1) | copy-start | bytes 786436
  28.5 32.2 %all-to-all-start = ((bf16[16,320,128]{2,1,0:T(8,128)(2,1)}), bf16[16,320,128]{2,1,0:T(8,128)(2,1)S(1)}, u32[]{:S(2)}, u32[]{:S(2)}) async-start(bf16[16,320,128]{2,1,0:T(8,128)(2,1)} %get-tuple-element.20), calls=%async_computation | async-start | bytes 2621440 | tf_op jit(solution)/shard_map/all_to_all | solution.py:616
  33.3 19.4 %collective-permute-start = (bf16[32,4096]{1,0:T(8,128)(2,1)S(1)}, bf16[32,4096]{1,0:T(8,128)(2,1)S(1)}, u32[]{:S(2)}, u32[]{:S(2)}) collective-permute-start(bf16[32,4096]{1,0:T(8,128)(2,1)S(1)} %copy-done.1), channel_id=1, source_target_pairs={{0,1},{1,0},{2,3},{3,2},{4,5},{5,4},{6,7},{7,6},{8,9},{9,8},{10,11... | collective-permute-start | bytes 786440 | tf_op jit(solution)/shard_map/ppermute | solution.py:577
  52.7 8.0 %copy-start.3 = (bf16[32,4096]{1,0:T(8,128)(2,1)}, bf16[32,4096]{1,0:T(8,128)(2,1)S(1)}, u32[]{:S(2)}) copy-start(bf16[32,4096]{1,0:T(8,128)(2,1)S(1)} %collective-permute-done.refs_8_) | copy-start | bytes 786436
  60.7 1.1 %copy-start = (bf16[16,320,128]{2,1,0:T(8,128)(2,1)}, bf16[16,320,128]{2,1,0:T(8,128)(2,1)S(1)}, u32[]{:S(2)}) copy-start(bf16[16,320,128]{2,1,0:T(8,128)(2,1)S(1)} %all-to-all-done.refs_2_) | copy-start | bytes 3932164

commit v12 on v11

--- a/solution.py
+++ b/solution.py
@@ -17,7 +17,8 @@
 CHUNK = 8
 FAR_AWAY = -30000.0
 SLOTS = 64
-RECEIVED = SLOTS + CHUNK
+SECTION = SLOTS + CHUNK
+EARLY = 3
 VMEM = 56 * 1024 * 1024
 
 NT = (((1,), (1,)), ((), ()))
@@ -62,7 +63,7 @@
 
 
 def list_slots(
-    fine_slots_ref, fine_counts_ref, coarse_slots_ref, coarse_counts_ref, out_ref, *units_refs, entries
+    fine_slots_ref, fine_counts_ref, coarse_slots_ref, coarse_counts_ref, out_ref, *units_refs, owners, caps, splits
 ):
     fine, coarse = fine_slots_ref.shape[0], coarse_slots_ref.shape[0]
     spare = LANES - fine - coarse
@@ -75,19 +76,31 @@
     )
     shape = (SLOTS, LANES)
     in_fine = lax.broadcasted_iota(jnp.int32, shape, 1) < fine
-    clusters = jnp.where(in_fine, fine, coarse)
-    nothing = jnp.where(in_fine, entries[0], entries[1])
+
+    def by_level(values):
+        return jnp.where(in_fine, values[0], values[1])
+
+    clusters = by_level((fine, coarse))
+    split = by_level(splits)
     live = lax.broadcasted_iota(jnp.int32, shape, 0) < counts
     own = live & (slots < clusters)
     received = live & (slots >= clusters)
+    entry = slots - clusters
+    source = by_level([entry >> (cap.bit_length() - 1) for cap in caps])
+    within = by_level([entry & (cap - 1) for cap in caps])
+    later = by_level([cap - first for cap, first in zip(caps, splits)])
     row = lax.broadcasted_iota(jnp.int32, (SLOTS, SLOTS), 0)
     column = lax.broadcasted_iota(jnp.int32, (SLOTS, SLOTS), 1)
     upto = jnp.where(column <= row, 1.0, 0.0).astype(jnp.bfloat16)
     turns = []
-    for start, chosen, value, blank in (
-        (0, own, slots, clusters),
-        (RECEIVED, received, slots - clusters, nothing),
+    for side, (chosen, value, blank) in enumerate(
+        (
+            (own, slots, clusters),
+            (received & (within < split), source * split + within, owners * split),
+            (received & (within >= split), source * later + within - split, owners * later),
+        )
     ):
+        start = side * SECTION
         rank = bdot(upto, jnp.where(chosen, 1.0, 0.0).astype(jnp.bfloat16), NN).astype(jnp.int32)
         spot = jnp.where(chosen, rank - 1, -1)
         value = value - blank
@@ -99,14 +112,16 @@
             out_ref[start + first:start + first + 8] = jnp.concatenate(rows, axis=0)
         out_ref[start + SLOTS:start + SLOTS + CHUNK] = jnp.broadcast_to(blank[:1], (CHUNK, LANES))
         turns.append(jnp.maximum((rank[SLOTS - 1:] + CHUNK - 1) // CHUNK, 1))
-    turns = jnp.concatenate(turns + [jnp.zeros((6, LANES), jnp.int32)], axis=0).astype(jnp.float32).T
+    turns = jnp.concatenate(turns + [jnp.zeros((5, LANES), jnp.int32)], axis=0).astype(jnp.float32).T
     row = lax.broadcasted_iota(jnp.int32, (LANES, LANES), 0)
     column = lax.broadcasted_iota(jnp.int32, (LANES, LANES), 1)
     upto = (column <= row) & ((row < fine) == (column < fine))
     ends = bdot(jnp.where(upto, 1.0, 0.0).astype(jnp.bfloat16), turns.astype(jnp.bfloat16), NN)
     ends, turns = ends.astype(jnp.int32), turns.astype(jnp.int32)
-    for side in range(2):
+    for side in range(3):
         for level, (low, count) in enumerate(((0, fine), (fine, coarse))):
+            if side == 2 and level == 1:
+                continue
             units_ref = units_refs[2 * side + level]
             end = ends[low:low + count, side:side + 1]
             took = turns[low:low + count, side:side + 1]
@@ -117,44 +132,46 @@
                 target = jnp.sum(jnp.where(passed, 1, 0), axis=0, keepdims=True)
                 turn = place - jnp.sum(jnp.where(passed, took, 0), axis=0, keepdims=True)
                 over = target >= count
-                start = side * RECEIVED + jnp.where(over, SLOTS, turn * CHUNK)
+                start = side * SECTION + jnp.where(over, SLOTS, turn * CHUNK)
                 code = start * LANES + low + jnp.where(over, count - 1, target)
                 if tile == units_ref.shape[0] - 1:
                     code = jnp.where(lane == LANES - 1, end[count - 1:], code)
                 units_ref[tile:tile + 1] = code
 
 
-def pack_send(send_ref, out_ref, dup_coef, dup_rows, owners, capacity, px, entry_first=False):
-    pairs = capacity // 2
+def sent_rows(pairs, px):
+    return pairs * px + -(-pairs // 2) * 16
+
+
+def pack_send(send_ref, out_ref, dup_coef, dup_rows, px, pairs, base=0, entry_first=False):
+    owners = out_ref.shape[0]
+    points = base + len(pairs) * px
     lane = lax.broadcasted_iota(jnp.int32, (px, LANES), 1) < LANES // 2
     lane8 = lax.broadcasted_iota(jnp.int32, (8, LANES), 1) < LANES // 2
 
     def one_owner(owner, carry):
-        before = None
-        for pair in range(pairs):
+        rows = []
+        for place, pair in enumerate(pairs):
             first, second = [
                 send_ref[0, entry, owner] if entry_first else send_ref[0, owner, entry]
                 for entry in (2 * pair, 2 * pair + 1)
             ]
-            out_ref[owner, pair * px:(pair + 1) * px, :] = jnp.where(lane, dup_coef[first], dup_coef[second])
-            rows = jnp.where(lane8, dup_rows[first], dup_rows[second])
-            if pair % 2 == 0:
-                before = rows
-            else:
-                start = pairs * px + (pair - 1) * 8
-                out_ref[owner, start:start + 16, :] = jnp.concatenate(
-                    [before, rows], axis=0
-                ).astype(jnp.bfloat16)
+            start = base + place * px
+            out_ref[owner, start:start + px, :] = jnp.where(lane, dup_coef[first], dup_coef[second])
+            rows.append(jnp.where(lane8, dup_rows[first], dup_rows[second]))
+        if len(rows) % 2:
+            rows.append(rows[-1])
+        for place in range(0, len(rows), 2):
+            start = points + place * 8
+            out_ref[owner, start:start + 16, :] = jnp.concatenate(rows[place:place + 2], axis=0).astype(
+                jnp.bfloat16
+            )
         return carry
 
     lax.fori_loop(0, owners, one_owner, 0, unroll=4)
 
 
-def pack_fine(send_ref, coef_ref, points_ref, out_ref, rows_ref, dup_coef, dup_rows):
-    _, owners, capacity = send_ref.shape
-    px = coef_ref.shape[0]
-    rows_ref[...] = split_rows(points_ref[...])
-
+def double_fine(coef_ref, rows_ref, dup_coef, dup_rows):
     def one_tile(index, carry):
         a, b = halves(coef_ref[:, lane_tile(index)].astype(jnp.float32))
         dup_coef[2 * index] = a.astype(jnp.bfloat16)
@@ -165,15 +182,31 @@
         return carry
 
     lax.fori_loop(0, coef_ref.shape[1] // LANES, one_tile, 0, unroll=8)
-    pack_send(send_ref, out_ref, dup_coef, dup_rows, owners, capacity, px)
-
-
-def pack_coarse(
-    send_ref, coef_ref, transfer_ref, points_ref, out_ref, rows_ref, coarse_ref, dup_coef, dup_rows
+
+
+def pack_kernel(
+    send_ref,
+    send_fine_ref,
+    coef_ref,
+    transfer_ref,
+    points_ref,
+    points_fine_ref,
+    out_ref,
+    rows_ref,
+    coarse_ref,
+    fine_rows_ref,
+    dup_coef,
+    dup_rows,
+    dup_fine,
+    dup_fine_rows,
+    *,
+    early,
 ):
-    _, capacity, owners = send_ref.shape
     px = coef_ref.shape[0]
+    pairs = send_ref.shape[1] // 2
     rows_ref[...] = split_rows(points_ref[...])
+    fine_rows_ref[...] = split_rows(points_fine_ref[...])
+    double_fine(coef_ref, fine_rows_ref, dup_fine, dup_fine_rows)
 
     def one_tile(index, carry):
         doubled = []
@@ -192,7 +225,8 @@
         return carry
 
     lax.fori_loop(0, coef_ref.shape[1] // (2 * LANES), one_tile, 0, unroll=8)
-    pack_send(send_ref, out_ref, dup_coef, dup_rows, owners, capacity, px, entry_first=True)
+    pack_send(send_ref, out_ref, dup_coef, dup_rows, px, range(pairs), entry_first=True)
+    pack_send(send_fine_ref, out_ref, dup_fine, dup_fine_rows, px, range(early), base=sent_rows(pairs, px))
 
 
 def turned(rows):
@@ -230,27 +264,28 @@
     put_nothing(2 * tiles, coef_table, feature_table)
 
 
-def build_received(recv_ref, coef_table, feature_table):
-    owners, recv_rows, _ = recv_ref.shape
+def build_received(recv_ref, base, pairs, coef_table, feature_table):
+    owners = recv_ref.shape[0]
     px = coef_table.shape[1]
-    pairs = recv_rows // (px + 8)
+    points = base + pairs * px
 
     def one_owner(owner, carry):
         for pair in range(0, pairs, 2):
-            start = pairs * px + pair * 8
+            start = points + pair * 8
             both = recv_ref[owner, start:start + 16, :].astype(jnp.float32)
-            for part in range(2):
+            for part in range(min(2, pairs - pair)):
                 where = pair + part
+                start = base + where * px
                 put_pair(
                     owner * (2 * pairs) + 2 * where,
-                    recv_ref[owner, where * px:(where + 1) * px, :],
+                    recv_ref[owner, start:start + px, :],
                     both[8 * part:8 * part + 8],
                     coef_table,
                     feature_table,
                 )
         return carry
 
-    lax.fori_loop(0, owners, one_owner, 0, unroll=32 // pairs)
+    lax.fori_loop(0, owners, one_owner, 0, unroll=8 if pairs <= 4 else 4)
     put_nothing(owners * pairs * 2, coef_table, feature_table)
 
 
@@ -372,25 +407,30 @@
     coarse_slots_ref,
     coarse_counts_ref,
     coef_ref,
-    points_ref,
+    fine_rows_ref,
     coarse_coef_ref,
     coarse_rows_ref,
     send_out_ref,
-    fine_rows_ref,
     list_out_ref,
-    fine_own_ref,
+    early_units_ref,
+    coarse_units_ref,
     fine_units_ref,
-    coarse_units_ref,
+    fine_out_ref,
     coarse_out_ref,
     dup_coef,
     dup_rows,
+    fine_own_ref,
     coarse_own_ref,
     list_ref,
-    units_ref,
+    fine_own_units,
+    coarse_own_units,
     list_sem,
-    units_sem,
+    fine_sem,
+    coarse_sem,
     *scratch,
-    entries,
+    owners,
+    caps,
+    splits,
 ):
     list_slots(
         fine_slots_ref,
@@ -400,50 +440,67 @@
         list_out_ref,
         fine_own_ref,
         coarse_own_ref,
+        early_units_ref,
+        coarse_units_ref,
         fine_units_ref,
-        coarse_units_ref,
-        entries=entries,
+        owners=owners,
+        caps=caps,
+        splits=splits,
     )
     copies = [
         pltpu.make_async_copy(list_out_ref, list_ref, list_sem),
-        pltpu.make_async_copy(coarse_own_ref, units_ref, units_sem),
+        pltpu.make_async_copy(fine_own_ref, fine_own_units, fine_sem),
+        pltpu.make_async_copy(coarse_own_ref, coarse_own_units, coarse_sem),
     ]
     for copy in copies:
         copy.start()
-    pack_fine(send_ref, coef_ref, points_ref, send_out_ref, fine_rows_ref, dup_coef, dup_rows)
-    build_own(coarse_coef_ref, coarse_rows_ref, *scratch[:2])
-    build_targets(coarse_rows_ref, scratch[2])
+    double_fine(coef_ref, fine_rows_ref, dup_coef, dup_rows)
+    pack_send(
+        send_ref, send_out_ref, dup_coef, dup_rows, coef_ref.shape[0], range(splits[0] // 2, caps[0] // 2)
+    )
     for copy in copies:
         copy.wait()
-    sweep(list_ref, units_ref, fine_rows_ref.shape[1] // 64, *scratch)
-    put_sums(scratch[-1], coarse_rows_ref.shape[1] // 64, coarse_out_ref)
-
-
-def coarse_kernel(
+    first = 0
+    for units_ref, source_ref, rows_ref, out_ref in (
+        (fine_own_units, coef_ref, fine_rows_ref, fine_out_ref),
+        (coarse_own_units, coarse_coef_ref, coarse_rows_ref, coarse_out_ref),
+    ):
+        clusters = rows_ref.shape[1] // 64
+        build_own(source_ref, rows_ref, *scratch[:2])
+        build_targets(rows_ref, scratch[2])
+        sweep(list_ref, units_ref, first, *scratch)
+        put_sums(scratch[-1], clusters, out_ref)
+        first += clusters
+
+
+def first_kernel(
     list_ref,
-    own_units_ref,
+    early_units_ref,
     units_ref,
-    coef_ref,
+    recv_ref,
     fine_rows_ref,
-    recv_ref,
     rows_ref,
+    fine_own_ref,
     own_ref,
     fine_out_ref,
     out_ref,
     *scratch,
+    pairs,
+    early,
 ):
+    px = own_ref.shape[0]
     fine = fine_rows_ref.shape[1] // 64
-    build_own(coef_ref, fine_rows_ref, *scratch[:2])
-    build_targets(fine_rows_ref, scratch[2])
-    sweep(list_ref, own_units_ref, 0, *scratch)
-    put_sums(scratch[-1], fine, fine_out_ref)
-    build_received(recv_ref, *scratch[:2])
+    build_received(recv_ref, 0, pairs, *scratch[:2])
     build_targets(rows_ref, scratch[2])
     sweep(list_ref, units_ref, fine, *scratch)
     put_sums(scratch[-1], rows_ref.shape[1] // 64, out_ref, own_ref)
-
-
-def fine_kernel(groups, *refs):
+    build_received(recv_ref, sent_rows(pairs, px), early, *scratch[:2])
+    build_targets(fine_rows_ref, scratch[2])
+    sweep(list_ref, early_units_ref, 0, *scratch)
+    put_sums(scratch[-1], fine, fine_out_ref, fine_own_ref)
+
+
+def fine_kernel(groups, pairs, *refs):
     late = 3 + groups
     list_ref, units_ref, recv_ref, rows_ref = refs[:4]
     out_ref, terms_ref = refs[4 + late:6 + late]
@@ -457,7 +514,7 @@
     px = split_ref.shape[0] // 2
     probes = probes_refs[0].shape[0]
     acc = scratch[-1]
-    build_received(recv_ref, *scratch[:2])
+    build_received(recv_ref, 0, pairs, *scratch[:2])
     build_targets(rows_ref, scratch[2])
     sweep(list_ref, units_ref, 0, *scratch)
     for copy in copies:
@@ -547,44 +604,60 @@
     vmem = pl.BlockSpec(memory_space=pltpu.VMEM)
     bf16, f32 = jnp.bfloat16, jnp.float32
 
-    fine_total = owners * cap_fine
+    coarse_pairs = cap_coarse // 2
+    early_pairs = EARLY * (cap_fine // 2) // 8
+    late_pairs = cap_fine // 2 - early_pairs
+    early_total = owners * 2 * early_pairs
+    late_total = owners * 2 * late_pairs
     coarse_total = owners * cap_coarse
     unit_rows = [-(-(count * (SLOTS // CHUNK) + 2 * UNITS + 1) // LANES) for count in (fine_count, coarse_count)]
-    list_shape = (RECEIVED + SLOTS + CHUNK, LANES)
+    list_shape = (3 * SECTION, LANES)
     i32 = jnp.int32
+    fine_units_shape, coarse_units_shape = [(rows, LANES) for rows in unit_rows]
     fine_columns, coarse_columns = points_fine.shape[1], points_coarse.shape[1]
-
-    coarse_send, coarse_rows, coarse_coef = pl.pallas_call(
-        pack_coarse,
+    heavy = pl.CostEstimate(flops=10**10, bytes_accessed=10**7, transcendentals=10**7)
+
+    first_send, coarse_rows, coarse_coef, fine_rows = pl.pallas_call(
+        functools.partial(pack_kernel, early=early_pairs),
         out_shape=(
-            jax.ShapeDtypeStruct((owners, (cap_coarse // 2) * (px + 8), LANES), bf16),
+            jax.ShapeDtypeStruct(
+                (owners, sent_rows(coarse_pairs, px) + sent_rows(early_pairs, px), LANES), bf16
+            ),
             jax.ShapeDtypeStruct((8, coarse_columns), f32),
             jax.ShapeDtypeStruct((px, coarse_columns), bf16),
+            jax.ShapeDtypeStruct((8, fine_columns), f32),
         ),
-        in_specs=[smem, vmem, vmem, vmem],
-        out_specs=[vmem] * 3,
+        in_specs=[smem] * 2 + [vmem] * 4,
+        out_specs=[vmem] * 4,
         scratch_shapes=[
             pltpu.VMEM((coarse_count, px, LANES), bf16),
             pltpu.VMEM((coarse_count, 8, LANES), f32),
+            pltpu.VMEM((fine_count, px, LANES), bf16),
+            pltpu.VMEM((fine_count, 8, LANES), f32),
         ],
         compiler_params=whole_vmem,
-        name="pack_coarse",
-    )(jnp.swapaxes(send_coarse, 1, 2), coef, transfer, points_coarse)
-    coarse_recv = lax.all_to_all(coarse_send, "leaf", split_axis=0, concat_axis=0, tiled=True)
+        name="pack_first",
+    )(jnp.swapaxes(send_coarse, 1, 2), send_fine, coef, transfer, points_coarse, points_fine)
+    first_recv = lax.all_to_all(first_send, "leaf", split_axis=0, concat_axis=0, tiled=True)
 
     turned = [coef_fine]
     for step in range(1, groups):
         turned.append(lax.ppermute(coef_fine, "probe", [(i, (i + step) % groups) for i in range(groups)]))
 
-    fine_send, fine_rows, slot_list, fine_own, fine_units, coarse_units, coarse_own_sums = pl.pallas_call(
-        functools.partial(prepare_kernel, entries=(fine_total, coarse_total)),
+    fine_send, slot_list, early_units, coarse_units, fine_units, fine_own_sums, coarse_own_sums = pl.pallas_call(
+        functools.partial(
+            prepare_kernel,
+            owners=owners,
+            caps=(cap_fine, cap_coarse),
+            splits=(2 * early_pairs, cap_coarse),
+        ),
         out_shape=(
-            jax.ShapeDtypeStruct((owners, (cap_fine // 2) * (px + 8), LANES), bf16),
-            jax.ShapeDtypeStruct((8, fine_columns), f32),
+            jax.ShapeDtypeStruct((owners, sent_rows(late_pairs, px), LANES), bf16),
             jax.ShapeDtypeStruct(list_shape, i32),
-            jax.ShapeDtypeStruct((unit_rows[0], LANES), i32),
-            jax.ShapeDtypeStruct((unit_rows[0], LANES), i32),
-            jax.ShapeDtypeStruct((unit_rows[1], LANES), i32),
+            jax.ShapeDtypeStruct(fine_units_shape, i32),
+            jax.ShapeDtypeStruct(coarse_units_shape, i32),
+            jax.ShapeDtypeStruct(fine_units_shape, i32),
+            jax.ShapeDtypeStruct((px, fine_columns), f32),
             jax.ShapeDtypeStruct((px, coarse_columns), f32),
         ),
         in_specs=[smem] + [vmem] * 8,
@@ -592,15 +665,18 @@
         scratch_shapes=[
             pltpu.VMEM((fine_count, px, LANES), bf16),
             pltpu.VMEM((fine_count, 8, LANES), f32),
-            pltpu.VMEM((unit_rows[1], LANES), i32),
+            pltpu.VMEM(fine_units_shape, i32),
+            pltpu.VMEM(coarse_units_shape, i32),
             pltpu.SMEM(list_shape, i32),
-            pltpu.SMEM((unit_rows[1], LANES), i32),
+            pltpu.SMEM(fine_units_shape, i32),
+            pltpu.SMEM(coarse_units_shape, i32),
+            pltpu.SemaphoreType.DMA,
             pltpu.SemaphoreType.DMA,
             pltpu.SemaphoreType.DMA,
         ]
-        + sweep_scratch(coarse_count, coarse_count, px),
+        + sweep_scratch(fine_count, fine_count, px),
         compiler_params=whole_vmem,
-        cost_estimate=pl.CostEstimate(flops=10**10, bytes_accessed=10**7, transcendentals=10**7),
+        cost_estimate=heavy,
         name="prepare",
     )(
         send_fine,
@@ -609,30 +685,30 @@
         slots_coarse,
         counts_coarse.reshape(1, -1),
         coef,
-        points_fine,
+        fine_rows,
         coarse_coef,
         coarse_rows,
     )
     fine_recv = lax.all_to_all(fine_send, "leaf", split_axis=0, concat_axis=0, tiled=True)
 
     fine_sums, coarse_far = pl.pallas_call(
-        coarse_kernel,
+        functools.partial(first_kernel, pairs=coarse_pairs, early=early_pairs),
         out_shape=(
             jax.ShapeDtypeStruct((px, fine_columns), f32),
             jax.ShapeDtypeStruct((px, coarse_columns), f32),
         ),
         in_specs=[smem] * 3 + [vmem] * 5,
         out_specs=[vmem, vmem],
-        scratch_shapes=sweep_scratch(max(fine_count, coarse_total), fine_count, px),
+        scratch_shapes=sweep_scratch(max(early_total, coarse_total), fine_count, px),
         compiler_params=whole_vmem,
-        cost_estimate=pl.CostEstimate(flops=10**10, bytes_accessed=10**7, transcendentals=10**7),
-        name="coarse_sweep",
-    )(slot_list, fine_own, coarse_units, coef, fine_rows, coarse_recv, coarse_rows, coarse_own_sums)
+        cost_estimate=heavy,
+        name="first_sweep",
+    )(slot_list, early_units, coarse_units, first_recv, fine_rows, coarse_rows, fine_own_sums, coarse_own_sums)
 
     late = (fine_sums, coarse_far, transfer, *turned)
     term_shape = (owners * groups, 8, probes * probes // 8)
     far, terms = pl.pallas_call(
-        functools.partial(fine_kernel, groups),
+        functools.partial(fine_kernel, groups, late_pairs),
         out_shape=(
             jax.ShapeDtypeStruct((px, points_fine.shape[1]), f32),
             jax.ShapeDtypeStruct(term_shape, f32),
@@ -645,7 +721,7 @@
             pltpu.VMEM((groups, probes, px), f32),
             pltpu.VMEM((2 * px, points_fine.shape[1]), bf16),
         ]
-        + sweep_scratch(fine_total, fine_count, px),
+        + sweep_scratch(late_total, fine_count, px),
         compiler_params=whole_vmem,
         name="fine_sweep",
     )(slot_list, fine_units, fine_recv, fine_rows, *late)

time: 105 us -> 102 us (0.971); the launches traced: 104 us -> 102 us
  Pallas kernels: 50.2 us -> 64.8 us
  waiting for transfers between devices: 15.8 us -> 5.55 us
  blocking collectives: 21.5 us -> 13.7 us
  starting transfers between devices: 13.7 us -> 16.4 us
    pallas_call x4, Pallas kernels: 48.6 us -> 63.1 us  [the longest x1 21.4 us: shards(): pl.pallas_call(functools.partial(first_kernel, pairs=coarse_pairs, early=...]
    all_to_all x1, waiting for transfers between devices: 7.99 us -> 0.01 us  [shards(): lax.all_to_all(fine_send, 'leaf', split_axis=0, concat_axis=0, tiled=True)]
    all_to_all x1, blocking collectives: 21.5 us -> 13.7 us  [shards(): lax.all_to_all(terms, ('leaf', 'probe'), split_axis=0, concat_axis=0, til...]
    all_to_all x1, starting transfers between devices: 4.77 us -> 7.49 us  [shards(): lax.all_to_all(fine_send, 'leaf', split_axis=0, concat_axis=0, tiled=True)]
    all_to_all x1, waiting for transfers between devices: 7.79 us -> 5.55 us  [shards(): lax.all_to_all(first_send, 'leaf', split_axis=0, concat_axis=0, tiled=True)]
  transfers between devices with their start and end apart: 3 -> 3, of which waited for: 2 -> 1; matrix products, arithmetic and copies ran while one was open for 0% -> 0% of each run, Pallas kernels for 26% -> 40%
where the time goes in v12:
time: 102 us
  Pallas kernels  64.8 us (64%)
  starting transfers between devices  16.4 us (16%)
  blocking collectives  13.7 us (13%)
  waiting for transfers between devices  5.55 us (5%)
    pallas_call x1, Pallas kernels, shards(): pl.pallas_call(functools.partial(first_kernel, pairs=coarse_pairs, early=...  21.4 us
    pallas_call x1, Pallas kernels, shards(): pl.pallas_call(functools.partial(prepare_kernel, owners=owners, caps=(cap...  19.6 us
    pallas_call x1, Pallas kernels, shards(): pl.pallas_call(functools.partial(fine_kernel, groups, late_pairs), out_sh...  18.2 us
    all_to_all x1, blocking collectives, shards(): lax.all_to_all(terms, ('leaf', 'probe'), split_axis=0, concat_axis=0, til...  13.7 us
    all_to_all x1, starting transfers between devices, shards(): lax.all_to_all(fine_send, 'leaf', split_axis=0, concat_axis=0, tiled=True)  7.49 us
    all_to_all x1, starting transfers between devices, shards(): lax.all_to_all(first_send, 'leaf', split_axis=0, concat_axis=0, tiled=True)  7.36 us
    all_to_all x1, waiting for transfers between devices, shards(): lax.all_to_all(first_send, 'leaf', split_axis=0, concat_axis=0, tiled=True)  5.55 us
    pallas_call x1, Pallas kernels, shards(): pl.pallas_call(functools.partial(pack_kernel, early=early_pairs), out_sha...  3.95 us
  transfers between devices with their start and end apart: 3, of which 1 were waited for; matrix products, arithmetic and copies ran while one was open for 0% of the time, Pallas kernels for 40%

profile of v12, /device:TPU:0, one launch (start us, length us, event | category | flops | bytes accessed | tf_op | source)
XLA Modules:
  0.0 102.1 jit_solution(4303728826759236946)
XLA Ops:
  0.6 4.0 %pack_first.1 = (bf16[16,288,128]{2,1,0:T(8,128)(2,1)}, f32[8,2048]{1,0:T(8,128)}, bf16[32,2048]{1,0:T(8,128)(2,1)}, f32[8,4096]{1,0:T(8,128)}) custom-call(s32[1,8,16]{2,1,0:T(8,128)} %bitcast.3, s32[1,16,16]{2,1,0:T(8,128)} %send_ref.1, bf16[32,4096]{1,0:T(8,128)(2,1)} %refs_7_.1, bf16[64,4096]{1,0:T(8,128)(2,1)} %refs_6_.1, f32[3,2048]{1,0:T(4,128)} %points_ref.1, ...), custom_call_target="tpu_custom_call" | custom-call | tf_op jit(solution)/shard_map/pack_first/pallas_call | solution.py:620
  4.6 7.4 %all-to-all-start.1 = ((bf16[16,288,128]{2,1,0:T(8,128)(2,1)}), bf16[16,288,128]{2,1,0:T(8,128)(2,1)S(1)}, u32[]{:S(2)}, u32[]{:S(2)}) async-start(bf16[16,288,128]{2,1,0:T(8,128)(2,1)} %get-tuple-element.25), calls=%async_computation.1 | async-start | bytes 2359296 | tf_op jit(solution)/shard_map/all_to_all | solution.py:641
  11.9 19.6 %prepare.1 = (bf16[16,208,128]{2,1,0:T(8,128)(2,1)}, s32[216,128]{1,0:T(8,128)}, s32[5,128]{1,0:T(8,128)}, s32[3,128]{1,0:T(4,128)}, s32[5,128]{1,0:T(8,128)}, /*index=5*/f32[32,4096]{1,0:T(8,128)}, f32[32,2048]{1,0:T(8,128)}) custom-call(s32[1,16,16]{2,1,0:T(8,128)} %send_ref.1, s32[64,64]{1,0:T(8,128)} %fine_slots_ref.1, s32[1,64]{1,0:T(1,128)} %bitcast.4, ...), custom_call_target="tpu_custom_call" | custom-call | flops 10000000000 | bytes 10000000 | tf_op jit(solution)/shard_map/prepare/pallas_call | solution.py:647
  31.5 0.0 copy-start.2
  31.5 5.5 %all-to-all-done.1.recv_ref = bf16[16,288,128]{2,1,0:T(8,128)(2,1)S(1)} async-done(((bf16[16,288,128]{2,1,0:T(8,128)(2,1)}), bf16[16,288,128]{2,1,0:T(8,128)(2,1)S(1)}, u32[]{:S(2)}, u32[]{:S(2)}) %all-to-all-start.1) | async-done | bytes 1179680 | tf_op jit(solution)/shard_map/all_to_all | solution.py:641
  37.1 0.0 copy-start.1
  37.1 7.5 %all-to-all-start = ((bf16[16,208,128]{2,1,0:T(8,128)(2,1)}), bf16[16,208,128]{2,1,0:T(8,128)(2,1)S(1)}, u32[]{:S(2)}, u32[]{:S(2)}) async-start(bf16[16,208,128]{2,1,0:T(8,128)(2,1)} %get-tuple-element.22), calls=%async_computation | async-start | bytes 1703936 | tf_op jit(solution)/shard_map/all_to_all | solution.py:692
  44.6 0.0 copy-done.2
  44.6 1.6 %collective-permute-start = (bf16[32,4096]{1,0:T(8,128)(2,1)S(1)}, bf16[32,4096]{1,0:T(8,128)(2,1)S(1)}, u32[]{:S(2)}, u32[]{:S(2)}) collective-permute-start(bf16[32,4096]{1,0:T(8,128)(2,1)S(1)} %copy-done.2), channel_id=1, source_target_pairs={{0,1},{1,0},{2,3},{3,2},{4,5},{5,4},{6,7},{7,6},{8,9},{9,8},{10,11... | collective-permute-start | bytes 786440 | tf_op jit(solution)/shard_map/ppermute | solution.py:645
  46.2 0.0 copy-done.1
  46.2 21.4 %first_sweep.1 = (f32[32,4096]{1,0:T(8,128)}, f32[32,2048]{1,0:T(8,128)}) custom-call(s32[216,128]{1,0:T(8,128)} %get-tuple-element.20.list_ref.refs_0_, s32[5,128]{1,0:T(8,128)} %get-tuple-element.23.early_units_ref, s32[3,128]{1,0:T(4,128)} %get-tuple-element.24.units_ref, bf16[16,288,128]{2,1,0:T(8,128)(2,1)} %copy-done.1, ...), custom_call_target="tpu_custom_call" | custom-call | flops 10000000000 | bytes 10000000 | tf_op jit(solution)/shard_map/first_sweep/pallas_call | solution.py:694
  67.6 0.0 collective-permute-done.refs_8_
  67.6 0.0 copy-start.3
  67.6 0.0 all-to-all-done.refs_2_
  67.6 0.0 copy-start
  67.6 0.7 copy-done.3
  68.3 0.3 copy-done
  68.6 18.2 %fine_sweep.1 = (f32[32,4096]{1,0:T(8,128)}, f32[32,8,128]{2,1,0:T(8,128)}) custom-call(s32[216,128]{1,0:T(8,128)} %get-tuple-element.20.list_ref.refs_0_, s32[5,128]{1,0:T(8,128)} %get-tuple-element.21.refs_1_, bf16[16,208,128]{2,1,0:T(8,128)(2,1)} %copy-done, f32[8,4096]{1,0:T(8,128)} %get-tuple-element.17.fine_rows_ref.refs_3_, ...), custom_call_target="tpu_custom_call" | custom-call | tf_op jit(solution)/shard_map/fine_sweep/pallas_call | solution.py:710
  86.8 13.7 %all_to_all.15.terms_ref = f32[32,8,128]{2,1,0:T(8,128)} all-to-all(f32[32,8,128]{2,1,0:T(8,128)} %get-tuple-element.31), channel_id=1, replica_groups=mesh['leaf'=16,'probe'=2] {'leaf','probe'}, dimensions={0} | all-to-all | bytes 262144 | tf_op jit(solution)/shard_map/all_to_all | solution.py:729
  100.5 1.7 %gram_sum.1 = f32[32,64]{1,0:T(8,128)} custom-call(f32[32,8,128]{2,1,0:T(8,128)} %all_to_all.15.terms_ref), custom_call_target="tpu_custom_call" | custom-call | tf_op jit(solution)/shard_map/gram_sum/pallas_call | solution.py:730
Async XLA Ops:
  4.6 32.5 %all-to-all-start.1 = ((bf16[16,288,128]{2,1,0:T(8,128)(2,1)}), bf16[16,288,128]{2,1,0:T(8,128)(2,1)S(1)}, u32[]{:S(2)}, u32[]{:S(2)}) async-start(bf16[16,288,128]{2,1,0:T(8,128)(2,1)} %get-tuple-element.25), calls=%async_computation.1 | async-start | bytes 2359296 | tf_op jit(solution)/shard_map/all_to_all | solution.py:641
  31.5 13.1 %copy-start.2 = (bf16[32,4096]{1,0:T(8,128)(2,1)S(1)}, bf16[32,4096]{1,0:T(8,128)(2,1)}, u32[]{:S(2)}) copy-start(bf16[32,4096]{1,0:T(8,128)(2,1)} %refs_7_.1) | copy-start | bytes 786436
  37.1 9.1 %copy-start.1 = (bf16[16,288,128]{2,1,0:T(8,128)(2,1)}, bf16[16,288,128]{2,1,0:T(8,128)(2,1)S(1)}, u32[]{:S(2)}) copy-start(bf16[16,288,128]{2,1,0:T(8,128)(2,1)S(1)} %all-to-all-done.1.recv_ref) | copy-start | bytes 3538948
  37.1 30.5 %all-to-all-start = ((bf16[16,208,128]{2,1,0:T(8,128)(2,1)}), bf16[16,208,128]{2,1,0:T(8,128)(2,1)S(1)}, u32[]{:S(2)}, u32[]{:S(2)}) async-start(bf16[16,208,128]{2,1,0:T(8,128)(2,1)} %get-tuple-element.22), calls=%async_computation | async-start | bytes 1703936 | tf_op jit(solution)/shard_map/all_to_all | solution.py:692
  44.6 23.0 %collective-permute-start = (bf16[32,4096]{1,0:T(8,128)(2,1)S(1)}, bf16[32,4096]{1,0:T(8,128)(2,1)S(1)}, u32[]{:S(2)}, u32[]{:S(2)}) collective-permute-start(bf16[32,4096]{1,0:T(8,128)(2,1)S(1)} %copy-done.2), channel_id=1, source_target_pairs={{0,1},{1,0},{2,3},{3,2},{4,5},{5,4},{6,7},{7,6},{8,9},{9,8},{10,11... | collective-permute-start | bytes 786440 | tf_op jit(solution)/shard_map/ppermute | solution.py:645
  67.6 0.7 copy-start.3
  67.6 1.0 copy-start

commit v13 on v12

--- a/solution.py
+++ b/solution.py
@@ -10,7 +10,7 @@
 from jax.sharding import PartitionSpec as P
 
 KERNEL_RATE = 1.5
-POINT_SCALE = math.sqrt(2.0 * KERNEL_RATE)
+POINT_SCALE = math.sqrt(2.0 * KERNEL_RATE * math.log2(math.e))
 LANES = 128
 UNITS = 16
 QUAD = 4
@@ -18,7 +18,7 @@
 FAR_AWAY = -30000.0
 SLOTS = 64
 SECTION = SLOTS + CHUNK
-EARLY = 3
+EARLY = 2
 VMEM = 56 * 1024 * 1024
 
 NT = (((1,), (1,)), ((), ()))
@@ -332,7 +332,7 @@
                         tile = jnp.where(lane == u, feature_table[ids[u][m]], tile)
                     rows.append(tile)
                 power = bdot(jnp.concatenate(rows, axis=0), weights, NN)
-                buffer[start // QUAD, part * 64:(part + 4) * 64] = jnp.exp(power).astype(jnp.bfloat16)
+                buffer[start // QUAD, part * 64:(part + 4) * 64] = jnp.exp2(power).astype(jnp.bfloat16)
 
     def products(units, buffer):
         for start in range(0, UNITS, QUAD):

time: 102 us -> 101 us (level)
  Pallas kernels: 64.8 us -> 58.3 us
  blocking collectives: 13.7 us -> 17.1 us
  waiting for transfers between devices: 5.55 us -> 6.62 us
    all_to_all x1, blocking collectives: 13.7 us -> 17.1 us  [shards(): lax.all_to_all(terms, ('leaf', 'probe'), split_axis=0, concat_axis=0, til...]
    pallas_call x1, Pallas kernels: 21.4 us -> 18.5 us  [shards(): pl.pallas_call(functools.partial(first_kernel, pairs=coarse_pairs, early=...]
    pallas_call x1, Pallas kernels: 19.6 us -> 17 us  [shards(): pl.pallas_call(functools.partial(prepare_kernel, owners=owners, caps=(cap...]
    all_to_all x1, waiting for transfers between devices: 0.01 us -> 1.77 us  [shards(): lax.all_to_all(fine_send, 'leaf', split_axis=0, concat_axis=0, tiled=True)]
  transfers between devices with their start and end apart: 3 -> 3, of which waited for: 1 -> 2; matrix products, arithmetic and copies ran while one was open for 0% -> 0% of each run, Pallas kernels for 40% -> 35%
where the time goes in v13:
time: 101 us; the launch traced here: 100 us
  Pallas kernels  58.3 us (58%)
  blocking collectives  17.1 us (17%)
  starting transfers between devices  15.5 us (15%)
  waiting for transfers between devices  6.62 us (7%)
  local copies, waits for them, and re-layouts  1.94 us (2%)
    pallas_call x1, Pallas kernels, shards(): pl.pallas_call(functools.partial(first_kernel, pairs=coarse_pairs, early=...  18.5 us
    pallas_call x1, Pallas kernels, shards(): pl.pallas_call(functools.partial(fine_kernel, groups, late_pairs), out_sh...  17.3 us
    all_to_all x1, blocking collectives, shards(): lax.all_to_all(terms, ('leaf', 'probe'), split_axis=0, concat_axis=0, til...  17.1 us
    pallas_call x1, Pallas kernels, shards(): pl.pallas_call(functools.partial(prepare_kernel, owners=owners, caps=(cap...  17 us
    all_to_all x1, starting transfers between devices, shards(): lax.all_to_all(first_send, 'leaf', split_axis=0, concat_axis=0, tiled=True)  7.36 us
    all_to_all x1, starting transfers between devices, shards(): lax.all_to_all(fine_send, 'leaf', split_axis=0, concat_axis=0, tiled=True)  6.53 us
    all_to_all x1, waiting for transfers between devices, shards(): lax.all_to_all(first_send, 'leaf', split_axis=0, concat_axis=0, tiled=True)  4.85 us
    pallas_call x1, Pallas kernels, shards(): pl.pallas_call(functools.partial(pack_kernel, early=early_pairs), out_sha...  3.83 us
  transfers between devices with their start and end apart: 3, of which 2 were waited for; matrix products, arithmetic and copies ran while one was open for 0% of the time, Pallas kernels for 35%

profile of v13, /device:TPU:0, one launch (start us, length us, event | category | flops | bytes accessed | tf_op | source)
XLA Modules:
  0.0 100.1 jit_solution(11368384232654317928)
XLA Ops:
  0.6 3.8 %pack_first.1 = (bf16[16,240,128]{2,1,0:T(8,128)(2,1)}, f32[8,2048]{1,0:T(8,128)}, bf16[32,2048]{1,0:T(8,128)(2,1)}, f32[8,4096]{1,0:T(8,128)}) custom-call(s32[1,8,16]{2,1,0:T(8,128)} %bitcast.3, s32[1,16,16]{2,1,0:T(8,128)} %send_ref.1, bf16[32,4096]{1,0:T(8,128)(2,1)} %refs_7_.1, bf16[64,4096]{1,0:T(8,128)(2,1)} %refs_6_.1, f32[3,2048]{1,0:T(4,128)} %points_ref.1, ...), custom_call_target="tpu_custom_call" | custom-call | tf_op jit(solution)/shard_map/pack_first/pallas_call | solution.py:620
  4.5 7.4 %all-to-all-start.1 = ((bf16[16,240,128]{2,1,0:T(8,128)(2,1)}), bf16[16,240,128]{2,1,0:T(8,128)(2,1)S(1)}, u32[]{:S(2)}, u32[]{:S(2)}) async-start(bf16[16,240,128]{2,1,0:T(8,128)(2,1)} %get-tuple-element.25), calls=%async_computation.1 | async-start | bytes 1966080 | tf_op jit(solution)/shard_map/all_to_all | solution.py:641
  11.8 17.0 %prepare.1 = (bf16[16,240,128]{2,1,0:T(8,128)(2,1)}, s32[216,128]{1,0:T(8,128)}, s32[5,128]{1,0:T(8,128)}, s32[3,128]{1,0:T(4,128)}, s32[5,128]{1,0:T(8,128)}, /*index=5*/f32[32,4096]{1,0:T(8,128)}, f32[32,2048]{1,0:T(8,128)}) custom-call(s32[1,16,16]{2,1,0:T(8,128)} %send_ref.1, s32[64,64]{1,0:T(8,128)} %fine_slots_ref.1, s32[1,64]{1,0:T(1,128)} %bitcast.4, ...), custom_call_target="tpu_custom_call" | custom-call | flops 10000000000 | bytes 10000000 | tf_op jit(solution)/shard_map/prepare/pallas_call | solution.py:647
  28.8 4.8 %all-to-all-done.1.recv_ref = bf16[16,240,128]{2,1,0:T(8,128)(2,1)S(1)} async-done(((bf16[16,240,128]{2,1,0:T(8,128)(2,1)}), bf16[16,240,128]{2,1,0:T(8,128)(2,1)S(1)}, u32[]{:S(2)}, u32[]{:S(2)}) %all-to-all-start.1) | async-done | bytes 983072 | tf_op jit(solution)/shard_map/all_to_all | solution.py:641
  33.7 0.0 copy-start.2
  33.7 0.0 copy-start.1
  33.7 1.0 copy-done.2
  34.7 6.5 %all-to-all-start = ((bf16[16,240,128]{2,1,0:T(8,128)(2,1)}), bf16[16,240,128]{2,1,0:T(8,128)(2,1)S(1)}, u32[]{:S(2)}, u32[]{:S(2)}) async-start(bf16[16,240,128]{2,1,0:T(8,128)(2,1)} %get-tuple-element.22), calls=%async_computation | async-start | bytes 1966080 | tf_op jit(solution)/shard_map/all_to_all | solution.py:692
  41.2 0.0 copy-done.1
  41.2 1.6 %collective-permute-start = (bf16[32,4096]{1,0:T(8,128)(2,1)S(1)}, bf16[32,4096]{1,0:T(8,128)(2,1)S(1)}, u32[]{:S(2)}, u32[]{:S(2)}) collective-permute-start(bf16[32,4096]{1,0:T(8,128)(2,1)S(1)} %copy-done.1), channel_id=1, source_target_pairs={{0,1},{1,0},{2,3},{3,2},{4,5},{5,4},{6,7},{7,6},{8,9},{9,8},{10,11... | collective-permute-start | bytes 786440 | tf_op jit(solution)/shard_map/ppermute | solution.py:645
  42.8 18.5 %first_sweep.1 = (f32[32,4096]{1,0:T(8,128)}, f32[32,2048]{1,0:T(8,128)}) custom-call(s32[216,128]{1,0:T(8,128)} %get-tuple-element.20.list_ref.refs_0_, s32[5,128]{1,0:T(8,128)} %get-tuple-element.23.early_units_ref, s32[3,128]{1,0:T(4,128)} %get-tuple-element.24.units_ref, bf16[16,240,128]{2,1,0:T(8,128)(2,1)} %copy-done.2, ...), custom_call_target="tpu_custom_call" | custom-call | flops 10000000000 | bytes 10000000 | tf_op jit(solution)/shard_map/first_sweep/pallas_call | solution.py:694
  61.3 0.0 collective-permute-done.refs_8_
  61.3 0.0 copy-start.3
  61.3 1.8 %all-to-all-done.refs_2_ = bf16[16,240,128]{2,1,0:T(8,128)(2,1)S(1)} async-done(((bf16[16,240,128]{2,1,0:T(8,128)(2,1)}), bf16[16,240,128]{2,1,0:T(8,128)(2,1)S(1)}, u32[]{:S(2)}, u32[]{:S(2)}) %all-to-all-start) | async-done | bytes 983072 | tf_op jit(solution)/shard_map/all_to_all | solution.py:692
  63.1 0.0 copy-start
  63.1 0.0 copy-done.3
  63.1 0.9 copy-done
  64.0 17.3 %fine_sweep.1 = (f32[32,4096]{1,0:T(8,128)}, f32[32,8,128]{2,1,0:T(8,128)}) custom-call(s32[216,128]{1,0:T(8,128)} %get-tuple-element.20.list_ref.refs_0_, s32[5,128]{1,0:T(8,128)} %get-tuple-element.21.refs_1_, bf16[16,240,128]{2,1,0:T(8,128)(2,1)} %copy-done, f32[8,4096]{1,0:T(8,128)} %get-tuple-element.17.fine_rows_ref.refs_3_, ...), custom_call_target="tpu_custom_call" | custom-call | tf_op jit(solution)/shard_map/fine_sweep/pallas_call | solution.py:710
  81.4 17.1 %all_to_all.15.terms_ref = f32[32,8,128]{2,1,0:T(8,128)} all-to-all(f32[32,8,128]{2,1,0:T(8,128)} %get-tuple-element.31), channel_id=1, replica_groups=mesh['leaf'=16,'probe'=2] {'leaf','probe'}, dimensions={0} | all-to-all | bytes 262144 | tf_op jit(solution)/shard_map/all_to_all | solution.py:729
  98.5 1.7 %gram_sum.1 = f32[32,64]{1,0:T(8,128)} custom-call(f32[32,8,128]{2,1,0:T(8,128)} %all_to_all.15.terms_ref), custom_call_target="tpu_custom_call" | custom-call | tf_op jit(solution)/shard_map/gram_sum/pallas_call | solution.py:730
Async XLA Ops:
  4.5 29.2 %all-to-all-start.1 = ((bf16[16,240,128]{2,1,0:T(8,128)(2,1)}), bf16[16,240,128]{2,1,0:T(8,128)(2,1)S(1)}, u32[]{:S(2)}, u32[]{:S(2)}) async-start(bf16[16,240,128]{2,1,0:T(8,128)(2,1)} %get-tuple-element.25), calls=%async_computation.1 | async-start | bytes 1966080 | tf_op jit(solution)/shard_map/all_to_all | solution.py:641
  33.7 1.0 copy-start.2
  33.7 7.5 %copy-start.1 = (bf16[32,4096]{1,0:T(8,128)(2,1)S(1)}, bf16[32,4096]{1,0:T(8,128)(2,1)}, u32[]{:S(2)}) copy-start(bf16[32,4096]{1,0:T(8,128)(2,1)} %refs_7_.1) | copy-start | bytes 786436
  34.7 28.4 %all-to-all-start = ((bf16[16,240,128]{2,1,0:T(8,128)(2,1)}), bf16[16,240,128]{2,1,0:T(8,128)(2,1)S(1)}, u32[]{:S(2)}, u32[]{:S(2)}) async-start(bf16[16,240,128]{2,1,0:T(8,128)(2,1)} %get-tuple-element.22), calls=%async_computation | async-start | bytes 1966080 | tf_op jit(solution)/shard_map/all_to_all | solution.py:692
  41.2 20.1 %collective-permute-start = (bf16[32,4096]{1,0:T(8,128)(2,1)S(1)}, bf16[32,4096]{1,0:T(8,128)(2,1)S(1)}, u32[]{:S(2)}, u32[]{:S(2)}) collective-permute-start(bf16[32,4096]{1,0:T(8,128)(2,1)S(1)} %copy-done.1), channel_id=1, source_target_pairs={{0,1},{1,0},{2,3},{3,2},{4,5},{5,4},{6,7},{7,6},{8,9},{9,8},{10,11... | collective-permute-start | bytes 786440 | tf_op jit(solution)/shard_map/ppermute | solution.py:645
  61.3 1.8 %copy-start.3 = (bf16[32,4096]{1,0:T(8,128)(2,1)}, bf16[32,4096]{1,0:T(8,128)(2,1)S(1)}, u32[]{:S(2)}) copy-start(bf16[32,4096]{1,0:T(8,128)(2,1)S(1)} %collective-permute-done.refs_8_) | copy-start | bytes 786436
  63.1 0.9 copy-start

commit v14 on v13

--- a/solution.py
+++ b/solution.py
@@ -315,8 +315,8 @@
         codes = [units_ref[place >> 7, (place & (LANES - 1)) + u] for u in range(UNITS)]
         return [(code >> 7, code & (LANES - 1)) for code in codes]
 
-    def tiles(units, buffer):
-        for start in range(0, UNITS, QUAD):
+    def tiles(units, buffer, starts=range(0, UNITS, QUAD)):
+        for start in starts:
             quad = units[start:start + QUAD]
             weights = []
             for u in range(QUAD):
@@ -334,8 +334,8 @@
                 power = bdot(jnp.concatenate(rows, axis=0), weights, NN)
                 buffer[start // QUAD, part * 64:(part + 4) * 64] = jnp.exp2(power).astype(jnp.bfloat16)
 
-    def products(units, buffer):
-        for start in range(0, UNITS, QUAD):
+    def products(units, buffer, starts=range(0, UNITS, QUAD)):
+        for start in starts:
             quad = units[start:start + QUAD]
             coefs = []
             for unit in quad:
@@ -354,13 +354,16 @@
                 side = (u // 2) * LANES
                 acc[u % 2, quad[u][1] - first] += product[u * px:(u + 1) * px, side:side + LANES]
 
+    def phase(later, later_buffer, units, buffer):
+        for start in range(0, UNITS, QUAD):
+            tiles(later, later_buffer, [start])
+            products(units, buffer, [start])
+
     def two_sets(index, carry):
         here = index * (2 * UNITS)
         second = units_of(here + UNITS)
-        tiles(second, second_buffer)
-        products(units_of(here), first_buffer)
-        tiles(units_of(here + 2 * UNITS), first_buffer)
-        products(second, second_buffer)
+        phase(second, second_buffer, units_of(here), first_buffer)
+        phase(units_of(here + 2 * UNITS), first_buffer, second, second_buffer)
         return carry
 
     total = units_ref[units_ref.shape[0] - 1, LANES - 1]
@@ -373,8 +376,7 @@
     @pl.when(sets == 2 * bodies + 2)
     def _():
         second = units_of(last + UNITS)
-        tiles(second, second_buffer)
-        products(units_of(last), first_buffer)
+        phase(second, second_buffer, units_of(last), first_buffer)
         products(second, second_buffer)
 
     @pl.when(sets == 2 * bodies + 1)

time: 101 us -> 102 us (level)
  transfers between devices with their start and end apart: 3 -> 3, of which waited for: 2 -> 2; matrix products, arithmetic and copies ran while one was open for 0% -> 0% of each run, Pallas kernels for 35% -> 36%
where the time goes in v14:
time: 102 us; the launch traced here: 101 us
  Pallas kernels  59.1 us (58%)
  blocking collectives  17.9 us (18%)
  starting transfers between devices  15.5 us (15%)
  waiting for transfers between devices  5.78 us (6%)
  local copies, waits for them, and re-layouts  1.94 us (2%)
    pallas_call x1, Pallas kernels, shards(): pl.pallas_call(functools.partial(first_kernel, pairs=coarse_pairs, early=...  19.1 us
    all_to_all x1, blocking collectives, shards(): lax.all_to_all(terms, ('leaf', 'probe'), split_axis=0, concat_axis=0, til...  17.9 us
    pallas_call x1, Pallas kernels, shards(): pl.pallas_call(functools.partial(fine_kernel, groups, late_pairs), out_sh...  17.3 us
    pallas_call x1, Pallas kernels, shards(): pl.pallas_call(functools.partial(prepare_kernel, owners=owners, caps=(cap...  17.2 us
    all_to_all x1, starting transfers between devices, shards(): lax.all_to_all(first_send, 'leaf', split_axis=0, concat_axis=0, tiled=True)  7.36 us
    all_to_all x1, starting transfers between devices, shards(): lax.all_to_all(fine_send, 'leaf', split_axis=0, concat_axis=0, tiled=True)  6.53 us
    all_to_all x1, waiting for transfers between devices, shards(): lax.all_to_all(first_send, 'leaf', split_axis=0, concat_axis=0, tiled=True)  4.63 us
    pallas_call x1, Pallas kernels, shards(): pl.pallas_call(functools.partial(pack_kernel, early=early_pairs), out_sha...  3.83 us
  transfers between devices with their start and end apart: 3, of which 2 were waited for; matrix products, arithmetic and copies ran while one was open for 0% of the time, Pallas kernels for 36%

profile of v14, /device:TPU:0, one launch (start us, length us, event | category | flops | bytes accessed | tf_op | source)
XLA Modules:
  0.0 100.9 jit_solution(16392741319020712412)
XLA Ops:
  0.6 3.8 %pack_first.1 = (bf16[16,240,128]{2,1,0:T(8,128)(2,1)}, f32[8,2048]{1,0:T(8,128)}, bf16[32,2048]{1,0:T(8,128)(2,1)}, f32[8,4096]{1,0:T(8,128)}) custom-call(s32[1,8,16]{2,1,0:T(8,128)} %bitcast.3, s32[1,16,16]{2,1,0:T(8,128)} %send_ref.1, bf16[32,4096]{1,0:T(8,128)(2,1)} %refs_7_.1, bf16[64,4096]{1,0:T(8,128)(2,1)} %refs_6_.1, f32[3,2048]{1,0:T(4,128)} %points_ref.1, ...), custom_call_target="tpu_custom_call" | custom-call | tf_op jit(solution)/shard_map/pack_first/pallas_call | solution.py:622
  4.5 7.4 %all-to-all-start.1 = ((bf16[16,240,128]{2,1,0:T(8,128)(2,1)}), bf16[16,240,128]{2,1,0:T(8,128)(2,1)S(1)}, u32[]{:S(2)}, u32[]{:S(2)}) async-start(bf16[16,240,128]{2,1,0:T(8,128)(2,1)} %get-tuple-element.25), calls=%async_computation.1 | async-start | bytes 1966080 | tf_op jit(solution)/shard_map/all_to_all | solution.py:643
  11.8 17.2 %prepare.1 = (bf16[16,240,128]{2,1,0:T(8,128)(2,1)}, s32[216,128]{1,0:T(8,128)}, s32[5,128]{1,0:T(8,128)}, s32[3,128]{1,0:T(4,128)}, s32[5,128]{1,0:T(8,128)}, /*index=5*/f32[32,4096]{1,0:T(8,128)}, f32[32,2048]{1,0:T(8,128)}) custom-call(s32[1,16,16]{2,1,0:T(8,128)} %send_ref.1, s32[64,64]{1,0:T(8,128)} %fine_slots_ref.1, s32[1,64]{1,0:T(1,128)} %bitcast.4, ...), custom_call_target="tpu_custom_call" | custom-call | flops 10000000000 | bytes 10000000 | tf_op jit(solution)/shard_map/prepare/pallas_call | solution.py:649
  29.1 4.6 %all-to-all-done.1.recv_ref = bf16[16,240,128]{2,1,0:T(8,128)(2,1)S(1)} async-done(((bf16[16,240,128]{2,1,0:T(8,128)(2,1)}), bf16[16,240,128]{2,1,0:T(8,128)(2,1)S(1)}, u32[]{:S(2)}, u32[]{:S(2)}) %all-to-all-start.1) | async-done | bytes 983072 | tf_op jit(solution)/shard_map/all_to_all | solution.py:643
  33.7 0.0 copy-start.2
  33.7 0.0 copy-start.1
  33.7 1.0 copy-done.2
  34.7 6.5 %all-to-all-start = ((bf16[16,240,128]{2,1,0:T(8,128)(2,1)}), bf16[16,240,128]{2,1,0:T(8,128)(2,1)S(1)}, u32[]{:S(2)}, u32[]{:S(2)}) async-start(bf16[16,240,128]{2,1,0:T(8,128)(2,1)} %get-tuple-element.22), calls=%async_computation | async-start | bytes 1966080 | tf_op jit(solution)/shard_map/all_to_all | solution.py:694
  41.2 0.0 copy-done.1
  41.2 1.6 %collective-permute-start = (bf16[32,4096]{1,0:T(8,128)(2,1)S(1)}, bf16[32,4096]{1,0:T(8,128)(2,1)S(1)}, u32[]{:S(2)}, u32[]{:S(2)}) collective-permute-start(bf16[32,4096]{1,0:T(8,128)(2,1)S(1)} %copy-done.1), channel_id=1, source_target_pairs={{0,1},{1,0},{2,3},{3,2},{4,5},{5,4},{6,7},{7,6},{8,9},{9,8},{10,11... | collective-permute-start | bytes 786440 | tf_op jit(solution)/shard_map/ppermute | solution.py:647
  42.8 19.1 %first_sweep.1 = (f32[32,4096]{1,0:T(8,128)}, f32[32,2048]{1,0:T(8,128)}) custom-call(s32[216,128]{1,0:T(8,128)} %get-tuple-element.20.list_ref.refs_0_, s32[5,128]{1,0:T(8,128)} %get-tuple-element.23.early_units_ref, s32[3,128]{1,0:T(4,128)} %get-tuple-element.24.units_ref, bf16[16,240,128]{2,1,0:T(8,128)(2,1)} %copy-done.2, ...), custom_call_target="tpu_custom_call" | custom-call | flops 10000000000 | bytes 10000000 | tf_op jit(solution)/shard_map/first_sweep/pallas_call | solution.py:696
  61.9 0.0 collective-permute-done.refs_8_
  61.9 0.0 copy-start.3
  61.9 1.1 %all-to-all-done.refs_2_ = bf16[16,240,128]{2,1,0:T(8,128)(2,1)S(1)} async-done(((bf16[16,240,128]{2,1,0:T(8,128)(2,1)}), bf16[16,240,128]{2,1,0:T(8,128)(2,1)S(1)}, u32[]{:S(2)}, u32[]{:S(2)}) %all-to-all-start) | async-done | bytes 983072 | tf_op jit(solution)/shard_map/all_to_all | solution.py:694
  63.1 0.0 copy-start
  63.1 0.0 copy-done.3
  63.1 0.9 copy-done
  64.0 17.3 %fine_sweep.1 = (f32[32,4096]{1,0:T(8,128)}, f32[32,8,128]{2,1,0:T(8,128)}) custom-call(s32[216,128]{1,0:T(8,128)} %get-tuple-element.20.list_ref.refs_0_, s32[5,128]{1,0:T(8,128)} %get-tuple-element.21.refs_1_, bf16[16,240,128]{2,1,0:T(8,128)(2,1)} %copy-done, f32[8,4096]{1,0:T(8,128)} %get-tuple-element.17.fine_rows_ref.refs_3_, ...), custom_call_target="tpu_custom_call" | custom-call | tf_op jit(solution)/shard_map/fine_sweep/pallas_call | solution.py:712
  81.4 17.9 %all_to_all.15.terms_ref = f32[32,8,128]{2,1,0:T(8,128)} all-to-all(f32[32,8,128]{2,1,0:T(8,128)} %get-tuple-element.31), channel_id=1, replica_groups=mesh['leaf'=16,'probe'=2] {'leaf','probe'}, dimensions={0} | all-to-all | bytes 262144 | tf_op jit(solution)/shard_map/all_to_all | solution.py:731
  99.2 1.7 %gram_sum.1 = f32[32,64]{1,0:T(8,128)} custom-call(f32[32,8,128]{2,1,0:T(8,128)} %all_to_all.15.terms_ref), custom_call_target="tpu_custom_call" | custom-call | tf_op jit(solution)/shard_map/gram_sum/pallas_call | solution.py:732
Async XLA Ops:
  4.5 29.2 %all-to-all-start.1 = ((bf16[16,240,128]{2,1,0:T(8,128)(2,1)}), bf16[16,240,128]{2,1,0:T(8,128)(2,1)S(1)}, u32[]{:S(2)}, u32[]{:S(2)}) async-start(bf16[16,240,128]{2,1,0:T(8,128)(2,1)} %get-tuple-element.25), calls=%async_computation.1 | async-start | bytes 1966080 | tf_op jit(solution)/shard_map/all_to_all | solution.py:643
  33.7 1.0 copy-start.2
  33.7 7.5 %copy-start.1 = (bf16[32,4096]{1,0:T(8,128)(2,1)S(1)}, bf16[32,4096]{1,0:T(8,128)(2,1)}, u32[]{:S(2)}) copy-start(bf16[32,4096]{1,0:T(8,128)(2,1)} %refs_7_.1) | copy-start | bytes 786436
  34.7 28.4 %all-to-all-start = ((bf16[16,240,128]{2,1,0:T(8,128)(2,1)}), bf16[16,240,128]{2,1,0:T(8,128)(2,1)S(1)}, u32[]{:S(2)}, u32[]{:S(2)}) async-start(bf16[16,240,128]{2,1,0:T(8,128)(2,1)} %get-tuple-element.22), calls=%async_computation | async-start | bytes 1966080 | tf_op jit(solution)/shard_map/all_to_all | solution.py:694
  41.2 20.7 %collective-permute-start = (bf16[32,4096]{1,0:T(8,128)(2,1)S(1)}, bf16[32,4096]{1,0:T(8,128)(2,1)S(1)}, u32[]{:S(2)}, u32[]{:S(2)}) collective-permute-start(bf16[32,4096]{1,0:T(8,128)(2,1)S(1)} %copy-done.1), channel_id=1, source_target_pairs={{0,1},{1,0},{2,3},{3,2},{4,5},{5,4},{6,7},{7,6},{8,9},{9,8},{10,11... | collective-permute-start | bytes 786440 | tf_op jit(solution)/shard_map/ppermute | solution.py:647
  61.9 1.2 %copy-start.3 = (bf16[32,4096]{1,0:T(8,128)(2,1)}, bf16[32,4096]{1,0:T(8,128)(2,1)S(1)}, u32[]{:S(2)}) copy-start(bf16[32,4096]{1,0:T(8,128)(2,1)S(1)} %collective-permute-done.refs_8_) | copy-start | bytes 786436
  63.1 0.9 copy-start

commit v15 on v13

--- a/solution.py
+++ b/solution.py
@@ -324,15 +324,15 @@
                 weights.append(jnp.concatenate([own if v == u // 2 else blank for v in range(QUAD // 2)], axis=1))
             weights = jnp.concatenate(weights, axis=0)
             ids = [partners(unit) for unit in quad]
-            for part in range(0, CHUNK, 4):
+            for part in range(0, CHUNK, CHUNK):
                 rows = []
-                for m in range(part, part + 4):
+                for m in range(part, part + CHUNK):
                     tile = feature_table[ids[0][m]]
                     for u in range(1, QUAD):
                         tile = jnp.where(lane == u, feature_table[ids[u][m]], tile)
                     rows.append(tile)
                 power = bdot(jnp.concatenate(rows, axis=0), weights, NN)
-                buffer[start // QUAD, part * 64:(part + 4) * 64] = jnp.exp2(power).astype(jnp.bfloat16)
+                buffer[start // QUAD, part * 64:(part + CHUNK) * 64] = jnp.exp2(power).astype(jnp.bfloat16)
 
     def products(units, buffer):
         for start in range(0, UNITS, QUAD):

time: 101 us -> 101 us (level)
  blocking collectives: 17.1 us -> 18.5 us
    all_to_all x1, blocking collectives: 17.1 us -> 18.5 us  [shards(): lax.all_to_all(terms, ('leaf', 'probe'), split_axis=0, concat_axis=0, til...]
  transfers between devices with their start and end apart: 3 -> 3, of which waited for: 2 -> 2; matrix products, arithmetic and copies ran while one was open for 0% -> 0% of each run, Pallas kernels for 35% -> 36%
where the time goes in v15:
time: 101 us
  Pallas kernels  57.8 us (57%)
  blocking collectives  18.5 us (18%)
  starting transfers between devices  15.5 us (15%)
  waiting for transfers between devices  6.24 us (6%)
  local copies, waits for them, and re-layouts  1.94 us (2%)
    all_to_all x1, blocking collectives, shards(): lax.all_to_all(terms, ('leaf', 'probe'), split_axis=0, concat_axis=0, til...  18.5 us
    pallas_call x1, Pallas kernels, shards(): pl.pallas_call(functools.partial(first_kernel, pairs=coarse_pairs, early=...  18.3 us
    pallas_call x1, Pallas kernels, shards(): pl.pallas_call(functools.partial(prepare_kernel, owners=owners, caps=(cap...  17.5 us
    pallas_call x1, Pallas kernels, shards(): pl.pallas_call(functools.partial(fine_kernel, groups, late_pairs), out_sh...  16.5 us
    all_to_all x1, starting transfers between devices, shards(): lax.all_to_all(first_send, 'leaf', split_axis=0, concat_axis=0, tiled=True)  7.36 us
    all_to_all x1, starting transfers between devices, shards(): lax.all_to_all(fine_send, 'leaf', split_axis=0, concat_axis=0, tiled=True)  6.54 us
    all_to_all x1, waiting for transfers between devices, shards(): lax.all_to_all(first_send, 'leaf', split_axis=0, concat_axis=0, tiled=True)  4.31 us
    pallas_call x1, Pallas kernels, shards(): pl.pallas_call(functools.partial(pack_kernel, early=early_pairs), out_sha...  3.83 us
  transfers between devices with their start and end apart: 3, of which 2 were waited for; matrix products, arithmetic and copies ran while one was open for 0% of the time, Pallas kernels for 36%

profile of v15, /device:TPU:0, one launch (start us, length us, event | category | flops | bytes accessed | tf_op | source)
XLA Modules:
  0.0 100.7 jit_solution(5952403881650718831)
XLA Ops:
  0.6 3.8 %pack_first.1 = (bf16[16,240,128]{2,1,0:T(8,128)(2,1)}, f32[8,2048]{1,0:T(8,128)}, bf16[32,2048]{1,0:T(8,128)(2,1)}, f32[8,4096]{1,0:T(8,128)}) custom-call(s32[1,8,16]{2,1,0:T(8,128)} %bitcast.3, s32[1,16,16]{2,1,0:T(8,128)} %send_ref.1, bf16[32,4096]{1,0:T(8,128)(2,1)} %refs_7_.1, bf16[64,4096]{1,0:T(8,128)(2,1)} %refs_6_.1, f32[3,2048]{1,0:T(4,128)} %points_ref.1, ...), custom_call_target="tpu_custom_call" | custom-call | tf_op jit(solution)/shard_map/pack_first/pallas_call | solution.py:620
  4.5 7.4 %all-to-all-start.1 = ((bf16[16,240,128]{2,1,0:T(8,128)(2,1)}), bf16[16,240,128]{2,1,0:T(8,128)(2,1)S(1)}, u32[]{:S(2)}, u32[]{:S(2)}) async-start(bf16[16,240,128]{2,1,0:T(8,128)(2,1)} %get-tuple-element.25), calls=%async_computation.1 | async-start | bytes 1966080 | tf_op jit(solution)/shard_map/all_to_all | solution.py:641
  11.8 17.5 %prepare.1 = (bf16[16,240,128]{2,1,0:T(8,128)(2,1)}, s32[216,128]{1,0:T(8,128)}, s32[5,128]{1,0:T(8,128)}, s32[3,128]{1,0:T(4,128)}, s32[5,128]{1,0:T(8,128)}, /*index=5*/f32[32,4096]{1,0:T(8,128)}, f32[32,2048]{1,0:T(8,128)}) custom-call(s32[1,16,16]{2,1,0:T(8,128)} %send_ref.1, s32[64,64]{1,0:T(8,128)} %fine_slots_ref.1, s32[1,64]{1,0:T(1,128)} %bitcast.4, ...), custom_call_target="tpu_custom_call" | custom-call | flops 10000000000 | bytes 10000000 | tf_op jit(solution)/shard_map/prepare/pallas_call | solution.py:647
  29.4 4.3 %all-to-all-done.1.recv_ref = bf16[16,240,128]{2,1,0:T(8,128)(2,1)S(1)} async-done(((bf16[16,240,128]{2,1,0:T(8,128)(2,1)}), bf16[16,240,128]{2,1,0:T(8,128)(2,1)S(1)}, u32[]{:S(2)}, u32[]{:S(2)}) %all-to-all-start.1) | async-done | bytes 983072 | tf_op jit(solution)/shard_map/all_to_all | solution.py:641
  33.7 0.0 copy-start.2
  33.7 0.0 copy-start.1
  33.7 1.0 copy-done.2
  34.7 6.5 %all-to-all-start = ((bf16[16,240,128]{2,1,0:T(8,128)(2,1)}), bf16[16,240,128]{2,1,0:T(8,128)(2,1)S(1)}, u32[]{:S(2)}, u32[]{:S(2)}) async-start(bf16[16,240,128]{2,1,0:T(8,128)(2,1)} %get-tuple-element.22), calls=%async_computation | async-start | bytes 1966080 | tf_op jit(solution)/shard_map/all_to_all | solution.py:692
  41.2 0.0 copy-done.1
  41.2 1.6 %collective-permute-start = (bf16[32,4096]{1,0:T(8,128)(2,1)S(1)}, bf16[32,4096]{1,0:T(8,128)(2,1)S(1)}, u32[]{:S(2)}, u32[]{:S(2)}) collective-permute-start(bf16[32,4096]{1,0:T(8,128)(2,1)S(1)} %copy-done.1), channel_id=1, source_target_pairs={{0,1},{1,0},{2,3},{3,2},{4,5},{5,4},{6,7},{7,6},{8,9},{9,8},{10,11... | collective-permute-start | bytes 786440 | tf_op jit(solution)/shard_map/ppermute | solution.py:645
  42.8 18.3 %first_sweep.1 = (f32[32,4096]{1,0:T(8,128)}, f32[32,2048]{1,0:T(8,128)}) custom-call(s32[216,128]{1,0:T(8,128)} %get-tuple-element.20.list_ref.refs_0_, s32[5,128]{1,0:T(8,128)} %get-tuple-element.23.early_units_ref, s32[3,128]{1,0:T(4,128)} %get-tuple-element.24.units_ref, bf16[16,240,128]{2,1,0:T(8,128)(2,1)} %copy-done.2, ...), custom_call_target="tpu_custom_call" | custom-call | flops 10000000000 | bytes 10000000 | tf_op jit(solution)/shard_map/first_sweep/pallas_call | solution.py:694
  61.2 0.0 collective-permute-done.refs_8_
  61.2 0.0 copy-start.3
  61.2 1.9 %all-to-all-done.refs_2_ = bf16[16,240,128]{2,1,0:T(8,128)(2,1)S(1)} async-done(((bf16[16,240,128]{2,1,0:T(8,128)(2,1)}), bf16[16,240,128]{2,1,0:T(8,128)(2,1)S(1)}, u32[]{:S(2)}, u32[]{:S(2)}) %all-to-all-start) | async-done | bytes 983072 | tf_op jit(solution)/shard_map/all_to_all | solution.py:692
  63.1 0.0 copy-start
  63.1 0.0 copy-done.3
  63.1 0.9 copy-done
  64.0 16.5 %fine_sweep.1 = (f32[32,4096]{1,0:T(8,128)}, f32[32,8,128]{2,1,0:T(8,128)}) custom-call(s32[216,128]{1,0:T(8,128)} %get-tuple-element.20.list_ref.refs_0_, s32[5,128]{1,0:T(8,128)} %get-tuple-element.21.refs_1_, bf16[16,240,128]{2,1,0:T(8,128)(2,1)} %copy-done, f32[8,4096]{1,0:T(8,128)} %get-tuple-element.17.fine_rows_ref.refs_3_, ...), custom_call_target="tpu_custom_call" | custom-call | tf_op jit(solution)/shard_map/fine_sweep/pallas_call | solution.py:710
  80.5 18.5 %all_to_all.15.terms_ref = f32[32,8,128]{2,1,0:T(8,128)} all-to-all(f32[32,8,128]{2,1,0:T(8,128)} %get-tuple-element.31), channel_id=1, replica_groups=mesh['leaf'=16,'probe'=2] {'leaf','probe'}, dimensions={0} | all-to-all | bytes 262144 | tf_op jit(solution)/shard_map/all_to_all | solution.py:729
  99.0 1.7 %gram_sum.1 = f32[32,64]{1,0:T(8,128)} custom-call(f32[32,8,128]{2,1,0:T(8,128)} %all_to_all.15.terms_ref), custom_call_target="tpu_custom_call" | custom-call | tf_op jit(solution)/shard_map/gram_sum/pallas_call | solution.py:730
Async XLA Ops:
  4.5 29.2 %all-to-all-start.1 = ((bf16[16,240,128]{2,1,0:T(8,128)(2,1)}), bf16[16,240,128]{2,1,0:T(8,128)(2,1)S(1)}, u32[]{:S(2)}, u32[]{:S(2)}) async-start(bf16[16,240,128]{2,1,0:T(8,128)(2,1)} %get-tuple-element.25), calls=%async_computation.1 | async-start | bytes 1966080 | tf_op jit(solution)/shard_map/all_to_all | solution.py:641
  33.7 1.0 copy-start.2
  33.7 7.5 %copy-start.1 = (bf16[32,4096]{1,0:T(8,128)(2,1)S(1)}, bf16[32,4096]{1,0:T(8,128)(2,1)}, u32[]{:S(2)}) copy-start(bf16[32,4096]{1,0:T(8,128)(2,1)} %refs_7_.1) | copy-start | bytes 786436
  34.7 28.4 %all-to-all-start = ((bf16[16,240,128]{2,1,0:T(8,128)(2,1)}), bf16[16,240,128]{2,1,0:T(8,128)(2,1)S(1)}, u32[]{:S(2)}, u32[]{:S(2)}) async-start(bf16[16,240,128]{2,1,0:T(8,128)(2,1)} %get-tuple-element.22), calls=%async_computation | async-start | bytes 1966080 | tf_op jit(solution)/shard_map/all_to_all | solution.py:692
  41.2 19.9 %collective-permute-start = (bf16[32,4096]{1,0:T(8,128)(2,1)S(1)}, bf16[32,4096]{1,0:T(8,128)(2,1)S(1)}, u32[]{:S(2)}, u32[]{:S(2)}) collective-permute-start(bf16[32,4096]{1,0:T(8,128)(2,1)S(1)} %copy-done.1), channel_id=1, source_target_pairs={{0,1},{1,0},{2,3},{3,2},{4,5},{5,4},{6,7},{7,6},{8,9},{9,8},{10,11... | collective-permute-start | bytes 786440 | tf_op jit(solution)/shard_map/ppermute | solution.py:645
  61.2 1.9 %copy-start.3 = (bf16[32,4096]{1,0:T(8,128)(2,1)}, bf16[32,4096]{1,0:T(8,128)(2,1)S(1)}, u32[]{:S(2)}) copy-start(bf16[32,4096]{1,0:T(8,128)(2,1)S(1)} %collective-permute-done.refs_8_) | copy-start | bytes 786436
  63.1 0.9 copy-start
